TPU v7x, 32 devices: a whole 2x2x4 slice. The times are simulated.
32 devices in a mesh: dp: 4 (over z), fsdp: 8 (over y, x, core).
Axes of the slice: x: 2, y: 2, z: 4, core: 2. Of those that a mesh axis runs over, the one named last changes fastest.
Arguments:
- tokens: bfloat16 [4096, 2048], P(('dp', 'fsdp')), may hold values from -6 to 6
- out_grad: bfloat16 [4096, 2048], P(('dp', 'fsdp')), may hold values from -6 to 6
- seq_lengths: int32 [4, 3], P('dp'), may hold values from 1 to 896, as said below
- query_weight: float32 [2048, 2048], P(('dp', 'fsdp')), may hold values from -0.125 to 0.125
- query_first: float32 [2048, 2048], P(('dp', 'fsdp')), may hold values from -384 to 384
- query_second: float32 [2048, 2048], P(('dp', 'fsdp')), may hold values from 2048 to 32768
- key_weight: float32 [2048, 256], P(('dp', 'fsdp')), may hold values from -0.125 to 0.125
- key_first: float32 [2048, 256], P(('dp', 'fsdp')), may hold values from -1024 to 1024
- key_second: float32 [2048, 256], P(('dp', 'fsdp')), may hold values from 18432 to 294912
- value_weight: float32 [2048, 256], P(('dp', 'fsdp')), may hold values from -0.125 to 0.125
- value_first: float32 [2048, 256], P(('dp', 'fsdp')), may hold values from -1024 to 1024
- value_second: float32 [2048, 256], P(('dp', 'fsdp')), may hold values from 18432 to 294912
- output_weight: float32 [2048, 2048], P(('dp', 'fsdp')), may hold values from -1.5 to 1.5
- output_first: float32 [2048, 2048], P(('dp', 'fsdp')), may hold values from -32 to 32
- output_second: float32 [2048, 2048], P(('dp', 'fsdp')), may hold values from 18 to 292
- gate_weight: float32 [2048, 5632], P(('dp', 'fsdp')), may hold values from -0.125 to 0.125
- gate_first: float32 [2048, 5632], P(('dp', 'fsdp')), may hold values from -224 to 224
- gate_second: float32 [2048, 5632], P(('dp', 'fsdp')), may hold values from 737.28 to 11796.48
- up_weight: float32 [2048, 5632], P(('dp', 'fsdp')), may hold values from -0.125 to 0.125
- up_first: float32 [2048, 5632], P(('dp', 'fsdp')), may hold values from -224 to 224
- up_second: float32 [2048, 5632], P(('dp', 'fsdp')), may hold values from 737.28 to 11796.48
- down_weight: float32 [5632, 2048], P(('dp', 'fsdp')), may hold values from -0.078125 to 0.078125
- down_first: float32 [5632, 2048], P(('dp', 'fsdp')), may hold values from -224 to 224
- down_second: float32 [5632, 2048], P(('dp', 'fsdp')), may hold values from 737.28 to 11796.48
- norm_gains: float32 [2, 2048], P(None, ('dp', 'fsdp')), may hold values from 0.5 to 1.5
- gains_first: float32 [2, 2048], P(None, ('dp', 'fsdp')), may hold values from -512 to 512
- gains_second: float32 [2, 2048], P(None, ('dp', 'fsdp')), may hold values from 4608 to 73728
Outputs:
- result: bfloat16 [4096, 2048], P(('dp', 'fsdp'))
- grad_tokens: float32 [4096, 2048], P(('dp', 'fsdp'))
- query_weight_next: float32 [2048, 2048], P(('dp', 'fsdp'))
- query_first_next: float32 [2048, 2048], P(('dp', 'fsdp'))
- query_second_next: float32 [2048, 2048], P(('dp', 'fsdp'))
- key_weight_next: float32 [2048, 256], P(('dp', 'fsdp'))
- key_first_next: float32 [2048, 256], P(('dp', 'fsdp'))
- key_second_next: float32 [2048, 256], P(('dp', 'fsdp'))
- value_weight_next: float32 [2048, 256], P(('dp', 'fsdp'))
- value_first_next: float32 [2048, 256], P(('dp', 'fsdp'))
- value_second_next: float32 [2048, 256], P(('dp', 'fsdp'))
- output_weight_next: float32 [2048, 2048], P(('dp', 'fsdp'))
- output_first_next: float32 [2048, 2048], P(('dp', 'fsdp'))
- output_second_next: float32 [2048, 2048], P(('dp', 'fsdp'))
- gate_weight_next: float32 [2048, 5632], P(('dp', 'fsdp'))
- gate_first_next: float32 [2048, 5632], P(('dp', 'fsdp'))
- gate_second_next: float32 [2048, 5632], P(('dp', 'fsdp'))
- up_weight_next: float32 [2048, 5632], P(('dp', 'fsdp'))
- up_first_next: float32 [2048, 5632], P(('dp', 'fsdp'))
- up_second_next: float32 [2048, 5632], P(('dp', 'fsdp'))
- down_weight_next: float32 [5632, 2048], P(('dp', 'fsdp'))
- down_first_next: float32 [5632, 2048], P(('dp', 'fsdp'))
- down_second_next: float32 [5632, 2048], P(('dp', 'fsdp'))
- norm_gains_next: float32 [2, 2048], P(None, ('dp', 'fsdp'))
- gains_first_next: float32 [2, 2048], P(None, ('dp', 'fsdp'))
- gains_second_next: float32 [2, 2048], P(None, ('dp', 'fsdp'))
Inputs may be any that keep to these rules, and one draw needn't show every extreme that they name: `seq_lengths`: row b holds, in token order, the lengths of the 3 sequences of batch b; each row sums to 1024; the middle sequence has 896 tokens and the other two together 128.
All inputs are finite; a program needn't handle non-finite values.
Results may differ from a plain program's by a relative error of at most 0.014.
Values may be sent and summed in bfloat16 or wider, within the bound.
No kernel may reach another device: no remote copies, remote signals or barrier semaphores. Data moves between devices by JAX's collectives and lax.ppermute only.
A program may use at most 288 MiB of HBM per device.

v0:
```python
import math

import jax
import jax.numpy as jnp
from jax import lax
from jax.sharding import PartitionSpec as P

HEADS = 32
KV_HEADS = 4
HEAD_DIM = 64
STEP = 3


NORM_EPS = 1e-05
ROPE_BASE = 10000.0
BETA = 0.5
ADAM_EPS = 1e-08
DECAY = 0.1
RATES = (0.02, 0.02, 0.02, 0.1, 0.02, 0.02, 0.02, 0.2)
MASKED = -1e30


def matmul(left, right):
    return jnp.dot(left, right, preferred_element_type=jnp.float32)


def matmul_tn(left, right):
    return lax.dot_general(
        left, right, (((0,), (0,)), ((), ())), preferred_element_type=jnp.float32
    )


def matmul_nt(left, right):
    return lax.dot_general(
        left, right, (((1,), (1,)), ((), ())), preferred_element_type=jnp.float32
    )


def rms_scale(values):
    return lax.rsqrt(jnp.mean(values * values, -1, keepdims=True) + NORM_EPS)


def rope_tables(places, head_size):
    half = head_size // 2
    freqs = jnp.exp(jnp.arange(half, dtype=jnp.float32) * (-2.0 * math.log(ROPE_BASE) / head_size))
    angles = places.astype(jnp.float32)[:, None] * freqs[None, :]
    cosine = jnp.cos(angles)
    sine = jnp.sin(angles)
    return (jnp.concatenate([cosine, cosine], 1), jnp.concatenate([sine, sine], 1))


def rotate(values, cosine, sine):
    half = values.shape[-1] // 2
    turned = jnp.concatenate([-values[..., half:], values[..., :half]], -1)
    return values * cosine[:, None, :] + turned * sine[:, None, :]


def segment_info(lengths_row, places):
    ends = jnp.cumsum(lengths_row, dtype=jnp.int32)
    starts = ends - lengths_row
    segments = jnp.sum((places[:, None] >= ends[None, :]).astype(jnp.int32), 1, dtype=jnp.int32)
    which_seq = segments[:, None] == jnp.arange(lengths_row.shape[0], dtype=jnp.int32)[None, :]
    first_place = jnp.sum(jnp.where(which_seq, starts[None, :], 0), 1, dtype=jnp.int32)
    return (segments, places - first_place)


def adam_step(master, first_moment, second_moment, gradient, rate):
    first_new = BETA * first_moment + (1.0 - BETA) * gradient
    second_new = BETA * second_moment + (1.0 - BETA) * gradient * gradient
    correction = 1.0 - BETA**STEP
    master_new = master - rate * (
        first_new / correction / (jnp.sqrt(second_new / correction) + ADAM_EPS) + DECAY * master
    )
    return (master_new, first_new, second_new)


def forward_pass(tokens_f, attn_set, ffn_set, cosine, sine, allowed):
    w_query, w_key, w_value, w_output, gains = attn_set
    w_gate, w_up, w_down = ffn_set
    row_count = tokens_f.shape[0]
    shared = HEADS // KV_HEADS
    score_scale = HEAD_DIM ** (-0.5)
    gain_one = gains[0].astype(jnp.float32)
    gain_two = gains[1].astype(jnp.float32)
    scale_one = rms_scale(tokens_f)
    normed = (tokens_f * scale_one * gain_one).astype(jnp.bfloat16)
    queries = rotate(
        matmul(normed, w_query).reshape(row_count, HEADS, HEAD_DIM), cosine, sine
    ).astype(jnp.bfloat16)
    keys_rot = rotate(
        matmul(normed, w_key).reshape(row_count, KV_HEADS, HEAD_DIM), cosine, sine
    ).astype(jnp.bfloat16)
    values = matmul(normed, w_value).astype(jnp.bfloat16)
    keys_full, values_full = (
        lax.all_gather(
            keys_rot.reshape(row_count, KV_HEADS * HEAD_DIM), "fsdp", axis=0, tiled=True
        ),
        lax.all_gather(values, "fsdp", axis=0, tiled=True),
    )
    query_sets = jnp.transpose(queries.reshape(row_count, KV_HEADS, shared, HEAD_DIM), (1, 0, 2, 3))
    key_sets = jnp.transpose(keys_full.reshape(-1, KV_HEADS, HEAD_DIM), (1, 0, 2))
    value_sets = jnp.transpose(values_full.reshape(-1, KV_HEADS, HEAD_DIM), (1, 0, 2))

    def attend(head_items):
        query_head, key_head, value_head = head_items
        scores = (
            jnp.einsum("tgd,kd->tgk", query_head, key_head, preferred_element_type=jnp.float32)
            * score_scale
        )
        scores = jnp.where(allowed, scores, MASKED)
        row_peak = jnp.max(scores, -1, keepdims=True)
        raised = jnp.exp(scores - row_peak)
        row_total = jnp.sum(raised, -1, keepdims=True)
        soft_weights = (raised / row_total).astype(jnp.bfloat16)
        mixture = jnp.einsum(
            "tgk,kd->tgd", soft_weights, value_head, preferred_element_type=jnp.float32
        )
        return (mixture.astype(jnp.bfloat16), row_peak[..., 0] + jnp.log(row_total[..., 0]))

    mixtures, log_totals = lax.map(attend, (query_sets, key_sets, value_sets))
    attended = jnp.transpose(mixtures, (1, 0, 2, 3)).reshape(row_count, HEADS * HEAD_DIM)
    resid_sum = tokens_f + matmul(attended, w_output)
    scale_two = rms_scale(resid_sum)
    normed_two = (resid_sum * scale_two * gain_two).astype(jnp.bfloat16)
    gate_value = matmul(normed_two, w_gate)
    up_value = matmul(normed_two, w_up)
    hidden = (jax.nn.silu(gate_value) * up_value).astype(jnp.bfloat16)
    result = resid_sum + matmul(hidden, w_down)
    saved = {
        "scale_one": scale_one,
        "gain_one": gain_one,
        "normed": normed,
        "query_sets": query_sets,
        "key_sets": key_sets,
        "value_sets": value_sets,
        "log_totals": log_totals,
        "attended": attended,
        "resid_sum": resid_sum,
        "scale_two": scale_two,
        "gain_two": gain_two,
        "normed_two": normed_two,
        "gate_value": gate_value,
        "up_value": up_value,
        "hidden": hidden,
    }
    return (result, saved)


def backward_pass(tokens_f, out_grad, attn_set, ffn_set, saved, cosine, sine, allowed):
    w_query, w_key, w_value, w_output, gains = attn_set
    w_gate, w_up, w_down = ffn_set
    row_count = tokens_f.shape[0]
    shared = HEADS // KV_HEADS
    score_scale = HEAD_DIM ** (-0.5)
    grad_out_f = out_grad.astype(jnp.float32)
    gate_value = saved["gate_value"]
    up_value = saved["up_value"]
    normed_two = saved["normed_two"]
    grad_down = matmul_tn(saved["hidden"], out_grad)
    grad_hidden = matmul_nt(out_grad, w_down)
    sigmoid_gate = jax.nn.sigmoid(gate_value)
    grad_gate = (
        grad_hidden * up_value * sigmoid_gate * (1.0 + gate_value * (1.0 - sigmoid_gate))
    ).astype(jnp.bfloat16)
    grad_up = (grad_hidden * gate_value * sigmoid_gate).astype(jnp.bfloat16)
    grad_wgate = matmul_tn(normed_two, grad_gate)
    grad_wup = matmul_tn(normed_two, grad_up)
    ffn_grads = (
        lax.psum_scatter(grad_wgate, ("dp", "fsdp"), scatter_dimension=0, tiled=True),
        lax.psum_scatter(grad_wup, ("dp", "fsdp"), scatter_dimension=0, tiled=True),
        lax.psum_scatter(grad_down, ("dp", "fsdp"), scatter_dimension=0, tiled=True),
    )
    grad_normed_two = matmul_nt(grad_gate, w_gate) + matmul_nt(grad_up, w_up)
    resid_sum = saved["resid_sum"]
    scale_two = saved["scale_two"]
    weighted_two = grad_normed_two * saved["gain_two"]
    grad_gain_two = jnp.sum(grad_normed_two * resid_sum * scale_two, 0)
    grad_resid = (
        grad_out_f
        + scale_two * weighted_two
        - resid_sum
        * (scale_two * scale_two * scale_two)
        * jnp.mean(weighted_two * resid_sum, -1, keepdims=True)
    )
    grad_attn_out = grad_resid.astype(jnp.bfloat16)
    grad_woutput = matmul_tn(saved["attended"], grad_attn_out)
    grad_mixed = matmul_nt(grad_attn_out, w_output).astype(jnp.bfloat16)
    grad_sets = jnp.transpose(
        grad_mixed.reshape(row_count, KV_HEADS, shared, HEAD_DIM), (1, 0, 2, 3)
    )

    def attend_back(head_items):
        query_head, key_head, value_head, grad_head, log_total = head_items
        scores = (
            jnp.einsum("tgd,kd->tgk", query_head, key_head, preferred_element_type=jnp.float32)
            * score_scale
        )
        scores = jnp.where(allowed, scores, MASKED)
        soft_weights = jnp.exp(scores - log_total[..., None])
        grad_value = jnp.einsum(
            "tgk,tgd->kd",
            soft_weights.astype(jnp.bfloat16),
            grad_head,
            preferred_element_type=jnp.float32,
        )
        grad_probs = jnp.einsum(
            "tgd,kd->tgk", grad_head, value_head, preferred_element_type=jnp.float32
        )
        centre = jnp.sum(soft_weights * grad_probs, -1, keepdims=True)
        grad_scores = (soft_weights * (grad_probs - centre) * score_scale).astype(jnp.bfloat16)
        grad_query = jnp.einsum(
            "tgk,kd->tgd", grad_scores, key_head, preferred_element_type=jnp.float32
        )
        grad_key = jnp.einsum(
            "tgk,tgd->kd", grad_scores, query_head, preferred_element_type=jnp.float32
        )
        return (grad_query, grad_key, grad_value)

    grad_query_sets, grad_key_sets, grad_value_sets = lax.map(
        attend_back,
        (
            saved["query_sets"],
            saved["key_sets"],
            saved["value_sets"],
            grad_sets,
            saved["log_totals"],
        ),
    )
    grad_query_rot = jnp.transpose(grad_query_sets, (1, 0, 2, 3)).reshape(
        row_count, HEADS, HEAD_DIM
    )
    grad_key_part = jnp.transpose(grad_key_sets, (1, 0, 2)).reshape(-1, KV_HEADS * HEAD_DIM)
    grad_value_part = jnp.transpose(grad_value_sets, (1, 0, 2)).reshape(-1, KV_HEADS * HEAD_DIM)
    grad_key_rot, grad_value_sum = (
        lax.psum_scatter(grad_key_part, "fsdp", scatter_dimension=0, tiled=True),
        lax.psum_scatter(grad_value_part, "fsdp", scatter_dimension=0, tiled=True),
    )
    grad_query = (
        rotate(grad_query_rot, cosine, -sine)
        .reshape(row_count, HEADS * HEAD_DIM)
        .astype(jnp.bfloat16)
    )
    grad_key = (
        rotate(grad_key_rot.reshape(row_count, KV_HEADS, HEAD_DIM), cosine, -sine)
        .reshape(row_count, KV_HEADS * HEAD_DIM)
        .astype(jnp.bfloat16)
    )
    grad_value = grad_value_sum.astype(jnp.bfloat16)
    normed = saved["normed"]
    grad_wquery = matmul_tn(normed, grad_query)
    grad_wkey = matmul_tn(normed, grad_key)
    grad_wvalue = matmul_tn(normed, grad_value)
    grad_normed = (
        matmul_nt(grad_query, w_query) + matmul_nt(grad_key, w_key) + matmul_nt(grad_value, w_value)
    )
    scale_one = saved["scale_one"]
    weighted_one = grad_normed * saved["gain_one"]
    grad_gain_one = jnp.sum(grad_normed * tokens_f * scale_one, 0)
    grad_tokens = (
        grad_resid
        + scale_one * weighted_one
        - tokens_f
        * (scale_one * scale_one * scale_one)
        * jnp.mean(weighted_one * tokens_f, -1, keepdims=True)
    )
    gain_grads = jnp.stack([grad_gain_one, grad_gain_two])
    attn_grads = (
        lax.psum_scatter(grad_wquery, ("dp", "fsdp"), scatter_dimension=0, tiled=True),
        lax.psum_scatter(grad_wkey, ("dp", "fsdp"), scatter_dimension=0, tiled=True),
        lax.psum_scatter(grad_wvalue, ("dp", "fsdp"), scatter_dimension=0, tiled=True),
        lax.psum_scatter(grad_woutput, ("dp", "fsdp"), scatter_dimension=0, tiled=True),
        lax.psum_scatter(gain_grads, ("dp", "fsdp"), scatter_dimension=1, tiled=True),
    )
    return (grad_tokens, attn_grads, ffn_grads)


def local(
    tokens,
    out_grad,
    seq_lengths,
    query_weight,
    query_first,
    query_second,
    key_weight,
    key_first,
    key_second,
    value_weight,
    value_first,
    value_second,
    output_weight,
    output_first,
    output_second,
    gate_weight,
    gate_first,
    gate_second,
    up_weight,
    up_first,
    up_second,
    down_weight,
    down_first,
    down_second,
    norm_gains,
    gains_first,
    gains_second,
):
    row_count = tokens.shape[0]
    members = lax.axis_size("fsdp")
    own_index = lax.axis_index("fsdp") * row_count + jnp.arange(row_count, dtype=jnp.int32)
    all_index = jnp.arange(row_count * members, dtype=jnp.int32)
    own_segments, own_places = segment_info(seq_lengths[0], own_index)
    all_segments = segment_info(seq_lengths[0], all_index)[0]
    allowed = (
        (own_segments[:, None] == all_segments[None, :])
        & (all_index[None, :] <= own_index[:, None])
    )[:, None, :]
    cosine, sine = rope_tables(own_places, HEAD_DIM)
    attn_local = (
        query_weight.astype(jnp.bfloat16),
        key_weight.astype(jnp.bfloat16),
        value_weight.astype(jnp.bfloat16),
        output_weight.astype(jnp.bfloat16),
        norm_gains.astype(jnp.bfloat16),
    )
    ffn_local = (
        gate_weight.astype(jnp.bfloat16),
        up_weight.astype(jnp.bfloat16),
        down_weight.astype(jnp.bfloat16),
    )
    attn_set = (
        lax.all_gather(attn_local[0], ("dp", "fsdp"), axis=0, tiled=True),
        lax.all_gather(attn_local[1], ("dp", "fsdp"), axis=0, tiled=True),
        lax.all_gather(attn_local[2], ("dp", "fsdp"), axis=0, tiled=True),
        lax.all_gather(attn_local[3], ("dp", "fsdp"), axis=0, tiled=True),
        lax.all_gather(attn_local[4], ("dp", "fsdp"), axis=1, tiled=True),
    )
    ffn_set = (
        lax.all_gather(ffn_local[0], ("dp", "fsdp"), axis=0, tiled=True),
        lax.all_gather(ffn_local[1], ("dp", "fsdp"), axis=0, tiled=True),
        lax.all_gather(ffn_local[2], ("dp", "fsdp"), axis=0, tiled=True),
    )
    tokens_f = tokens.astype(jnp.float32)
    result, saved = forward_pass(tokens_f, attn_set, ffn_set, cosine, sine, allowed)
    attn_set = (
        lax.all_gather(attn_local[0], ("dp", "fsdp"), axis=0, tiled=True),
        lax.all_gather(attn_local[1], ("dp", "fsdp"), axis=0, tiled=True),
        lax.all_gather(attn_local[2], ("dp", "fsdp"), axis=0, tiled=True),
        lax.all_gather(attn_local[3], ("dp", "fsdp"), axis=0, tiled=True),
        lax.all_gather(attn_local[4], ("dp", "fsdp"), axis=1, tiled=True),
    )
    ffn_set = (
        lax.all_gather(ffn_local[0], ("dp", "fsdp"), axis=0, tiled=True),
        lax.all_gather(ffn_local[1], ("dp", "fsdp"), axis=0, tiled=True),
        lax.all_gather(ffn_local[2], ("dp", "fsdp"), axis=0, tiled=True),
    )
    saved = forward_pass(tokens_f, attn_set, ffn_set, cosine, sine, allowed)[1]
    grad_tokens, attn_grads, ffn_grads = backward_pass(
        tokens_f, out_grad, attn_set, ffn_set, saved, cosine, sine, allowed
    )
    masters = (
        query_weight,
        key_weight,
        value_weight,
        output_weight,
        gate_weight,
        up_weight,
        down_weight,
        norm_gains,
    )
    firsts = (
        query_first,
        key_first,
        value_first,
        output_first,
        gate_first,
        up_first,
        down_first,
        gains_first,
    )
    seconds = (
        query_second,
        key_second,
        value_second,
        output_second,
        gate_second,
        up_second,
        down_second,
        gains_second,
    )
    gradients = (
        attn_grads[0],
        attn_grads[1],
        attn_grads[2],
        attn_grads[3],
        ffn_grads[0],
        ffn_grads[1],
        ffn_grads[2],
        attn_grads[4],
    )
    updated = [
        adam_step(
            masters[number], firsts[number], seconds[number], gradients[number], RATES[number]
        )
        for number in range(8)
    ]
    return (
        result.astype(jnp.bfloat16),
        grad_tokens,
        updated[0][0],
        updated[0][1],
        updated[0][2],
        updated[1][0],
        updated[1][1],
        updated[1][2],
        updated[2][0],
        updated[2][1],
        updated[2][2],
        updated[3][0],
        updated[3][1],
        updated[3][2],
        updated[4][0],
        updated[4][1],
        updated[4][2],
        updated[5][0],
        updated[5][1],
        updated[5][2],
        updated[6][0],
        updated[6][1],
        updated[6][2],
        updated[7][0],
        updated[7][1],
        updated[7][2],
    )


def solution(mesh):
    in_specs = (
        P(("dp", "fsdp"), None),
        P(("dp", "fsdp"), None),
        P("dp", None),
        P(("dp", "fsdp"), None),
        P(("dp", "fsdp"), None),
        P(("dp", "fsdp"), None),
        P(("dp", "fsdp"), None),
        P(("dp", "fsdp"), None),
        P(("dp", "fsdp"), None),
        P(("dp", "fsdp"), None),
        P(("dp", "fsdp"), None),
        P(("dp", "fsdp"), None),
        P(("dp", "fsdp"), None),
        P(("dp", "fsdp"), None),
        P(("dp", "fsdp"), None),
        P(("dp", "fsdp"), None),
        P(("dp", "fsdp"), None),
        P(("dp", "fsdp"), None),
        P(("dp", "fsdp"), None),
        P(("dp", "fsdp"), None),
        P(("dp", "fsdp"), None),
        P(("dp", "fsdp"), None),
        P(("dp", "fsdp"), None),
        P(("dp", "fsdp"), None),
        P(None, ("dp", "fsdp")),
        P(None, ("dp", "fsdp")),
        P(None, ("dp", "fsdp")),
    )
    out_specs = (
        P(("dp", "fsdp"), None),
        P(("dp", "fsdp"), None),
        P(("dp", "fsdp"), None),
        P(("dp", "fsdp"), None),
        P(("dp", "fsdp"), None),
        P(("dp", "fsdp"), None),
        P(("dp", "fsdp"), None),
        P(("dp", "fsdp"), None),
        P(("dp", "fsdp"), None),
        P(("dp", "fsdp"), None),
        P(("dp", "fsdp"), None),
        P(("dp", "fsdp"), None),
        P(("dp", "fsdp"), None),
        P(("dp", "fsdp"), None),
        P(("dp", "fsdp"), None),
        P(("dp", "fsdp"), None),
        P(("dp", "fsdp"), None),
        P(("dp", "fsdp"), None),
        P(("dp", "fsdp"), None),
        P(("dp", "fsdp"), None),
        P(("dp", "fsdp"), None),
        P(("dp", "fsdp"), None),
        P(("dp", "fsdp"), None),
        P(None, ("dp", "fsdp")),
        P(None, ("dp", "fsdp")),
        P(None, ("dp", "fsdp")),
    )
    return jax.shard_map(local, mesh=mesh, in_specs=in_specs, out_specs=out_specs, check_vma=False)
```

profile of v0, /device:TPU:0, one launch (start us, length us, event | category | flops | bytes accessed | tf_op | source)
XLA Modules:
  0.0 3251.6 jit_solution(2870744292713227820)
XLA Ops:
  16.3 43.0 %all-gather = bf16[32,64,2]{1,2,0:T(2,128)(2,1)S(1)} all-gather(bf16[1,64,2]{1,2,0:T(2,128)(2,1)S(1)} %convert_bitcast_fusion), channel_id=1, replica_groups=mesh['dp'=4,'fsdp'=8] {'dp','fsdp'}, dimensions={0}, use_global_device_ids=true | all-gather | bytes 8448 | tf_op jit(solution)/shard_map/all_gather | solution.py:334
  61.6 6.4 all-gather.11.cloned.1.call-done
  69.9 9.8 all_gather.43
  79.8 44.2 %all-gather.13.cloned.1.call-done = bf16[2048,256]{1,0:T(8,128)(2,1)} async-done(((bf16[64,256]{1,0:T(8,128)(2,1)}), bf16[2048,256]{1,0:T(8,128)(2,1)}) %all-gather.13.cloned.1.call-update) | async-done | bytes 1048592 | tf_op jit(solution)/shard_map/all_gather | solution.py:332
  125.6 9.8 all_gather.45
  135.7 68.3 %all-gather.9.cloned.1.call-done = bf16[2048,2048]{1,0:T(8,128)(2,1)} async-done(((bf16[64,2048]{1,0:T(8,128)(2,1)}), bf16[2048,2048]{1,0:T(8,128)(2,1)}) %all-gather.9.cloned.1.call-update) | async-done | bytes 8388624 | tf_op jit(solution)/shard_map/all_gather | solution.py:330
  204.0 6.9 fusion.175
  211.3 14.5 while.40
  225.8 57.4 %all-gather.15.cloned.1.call-done = bf16[2048,2048]{1,0:T(8,128)(2,1)} async-done(((bf16[64,2048]{1,0:T(8,128)(2,1)}), bf16[2048,2048]{1,0:T(8,128)(2,1)}) %all-gather.15.cloned.1.call-update) | async-done | bytes 8388624 | tf_op jit(solution)/shard_map/all_gather | solution.py:333
  289.9 139.8 %all-gather.19.cloned.1.call-done = bf16[2048,5632]{1,0:T(8,128)(2,1)} async-done(((bf16[64,5632]{1,0:T(8,128)(2,1)}), bf16[2048,5632]{1,0:T(8,128)(2,1)}) %all-gather.19.cloned.1.call-update) | async-done | bytes 23068688 | tf_op jit(solution)/shard_map/all_gather | solution.py:338
  429.7 9.4 fusion.194
  439.1 136.7 %all-gather.17.cloned.1.call-done = bf16[2048,5632]{1,0:T(8,128)(2,1)} async-done(((bf16[64,5632]{1,0:T(8,128)(2,1)}), bf16[2048,5632]{1,0:T(8,128)(2,1)}) %all-gather.17.cloned.1.call-update) | async-done | bytes 23068688 | tf_op jit(solution)/shard_map/all_gather | solution.py:337
  575.8 12.5 fusion.195
  588.3 19.6 fusion.129
  608.0 483.3 %reduce-scatter.29.cloned.1.call-done = f32[176,2048]{1,0:T(8,128)} async-done(((f32[5632,2048]{1,0:T(8,128)}), f32[176,2048]{1,0:T(8,128)}) %reduce-scatter.29.cloned.1.call-update) | async-done | bytes 1441808 | tf_op jit(solution)/shard_map/reduce_scatter | solution.py:171
  1091.3 6.3 multiply_subtract_fusion
  1097.6 152.7 %all-gather.21.cloned.1.call-done = bf16[5632,2048]{1,0:T(8,128)(2,1)} async-done(((bf16[176,2048]{1,0:T(8,128)(2,1)}), bf16[5632,2048]{1,0:T(8,128)(2,1)}) %all-gather.21.cloned.1.call-update) | async-done | bytes 23068688 | tf_op jit(solution)/shard_map/all_gather | solution.py:339
  1250.4 14.2 multiply_convert_fusion.2
  1264.6 13.1 fusion.196
  1277.7 12.5 multiply_reduce_fusion.1
  1290.6 7.1 convolution_convert_fusion
  1299.1 104.6 %while.41 = (s32[]{:T(128)}, f32[4,128,8,64]{1,3,2,0:T(8,128)}, f32[4,1024,64]{1,2,0:T(8,128)}, f32[4,1024,64]{1,2,0:T(8,128)}, bf16[4,128,8,64]{1,3,2,0:T(8,128...) while((s32[]{:T(128)}, f32[4,128,8,64]{1,3,2,0:T(8,128)}, ...), condition=%wide.region_18.19_spmd.clone, body=%wide.region_16.18_spmd.clone.sunk | while | flops 686166016 | bytes 48126088 | solution.py:219
  1306.3 7.9 fusion.283
  1314.2 7.8 fusion.284
  1332.3 7.9 fusion.283
  1340.3 7.8 fusion.284
  1358.4 7.9 fusion.283
  1366.4 7.8 fusion.284
  1384.5 7.9 fusion.283
  1392.4 7.8 fusion.284
  1405.9 6.4 fusion.197
  1412.4 25.7 reduce-scatter.13.cloned.1.call-done
  1442.6 35.1 %reduce-scatter.15.cloned.1.call-done = f32[128,256]{0,1:T(8,128)} async-done(((f32[1024,256]{0,1:T(8,128)}), f32[128,256]{0,1:T(8,128)}) %reduce-scatter.15.cloned.1.call-update) | async-done | bytes 131088 | tf_op jit(solution)/shard_map/reduce_scatter | solution.py:236
  1486.7 8.3 fusion.170
  1496.0 8.2 fusion.153
  1505.7 17.9 fusion.198
  1524.9 18.0 fusion.199
  1543.6 31.3 while.39
  1579.7 12.5 fusion.143
  1592.3 19.7 fusion.125
  1619.9 132.8 %reduce-scatter.19.cloned.1.call-done = f32[64,256]{1,0:T(8,128)} async-done(((f32[2048,256]{1,0:T(8,128)}), f32[64,256]{1,0:T(8,128)}) %reduce-scatter.19.cloned.1.call-update) | async-done | bytes 65552 | tf_op jit(solution)/shard_map/reduce_scatter | solution.py:269
  1754.2 133.4 %reduce-scatter.21.cloned.1.call-done = f32[64,256]{1,0:T(8,128)} async-done(((f32[2048,256]{1,0:T(8,128)}), f32[64,256]{1,0:T(8,128)}) %reduce-scatter.21.cloned.1.call-update) | async-done | bytes 65552 | tf_op jit(solution)/shard_map/reduce_scatter | solution.py:270
  1889.1 179.3 %reduce-scatter.17.cloned.1.call-done = f32[64,2048]{1,0:T(8,128)} async-done(((f32[2048,2048]{1,0:T(8,128)}), f32[64,2048]{1,0:T(8,128)}) %reduce-scatter.17.cloned.1.call-update) | async-done | bytes 524304 | tf_op jit(solution)/shard_map/reduce_scatter | solution.py:268
  2071.0 184.2 %reduce-scatter.23.cloned.1.call-done = f32[64,2048]{1,0:T(8,128)} async-done(((f32[2048,2048]{1,0:T(8,128)}), f32[64,2048]{1,0:T(8,128)}) %reduce-scatter.23.cloned.1.call-update) | async-done | bytes 524304 | tf_op jit(solution)/shard_map/reduce_scatter | solution.py:271
  2258.0 486.3 %reduce-scatter.25.cloned.1.call-done = f32[64,5632]{1,0:T(8,128)} async-done(((f32[2048,5632]{1,0:T(8,128)}), f32[64,5632]{1,0:T(8,128)}) %reduce-scatter.25.cloned.1.call-update) | async-done | bytes 1441808 | tf_op jit(solution)/shard_map/reduce_scatter | solution.py:169
  2744.3 5.0 multiply_subtract_fusion.2
  2749.3 490.3 %reduce-scatter.27.cloned.1.call-done = f32[64,5632]{1,0:T(8,128)} async-done(((f32[2048,5632]{1,0:T(8,128)}), f32[64,5632]{1,0:T(8,128)}) %reduce-scatter.27.cloned.1.call-update) | async-done | bytes 1441808 | tf_op jit(solution)/shard_map/reduce_scatter | solution.py:170
  3239.6 5.0 multiply_subtract_fusion.1
  (247 shorter events, 151.7 us)
Async XLA Ops:
  7.2 7.0 copy-start.15
  7.2 8.0 copy-start.13
  7.2 60.8 %all-gather.11.cloned.1.call-start = ((), (), s32[]{:S(2)}) async-start(), calls=%async_computation.11 | async-start | bytes 1081344 | tf_op jit(solution)/shard_map/all_gather | solution.py:331
  8.9 115.1 %all-gather.13.cloned.1.call-start = ((), (), s32[]{:S(2)}) async-start(), calls=%async_computation.12 | async-start | bytes 1081344 | tf_op jit(solution)/shard_map/all_gather | solution.py:332
  10.4 193.5 %all-gather.9.cloned.1.call-start = ((), (), s32[]{:S(2)}) async-start(), calls=%async_computation.10 | async-start | bytes 8650752 | tf_op jit(solution)/shard_map/all_gather | solution.py:330
  12.3 270.9 %all-gather.15.cloned.1.call-start = ((), (), s32[]{:S(2)}) async-start(), calls=%async_computation.13 | async-start | bytes 8650752 | tf_op jit(solution)/shard_map/all_gather | solution.py:333
  14.2 45.3 %copy-start.44 = (s32[1,3]{1,0:T(1,128)S(1)}, s32[1,3]{1,0:T(1,128)}, u32[]{:S(2)}) copy-start(s32[1,3]{1,0:T(1,128)} %param.35) | copy-start | bytes 40
  14.2 46.7 %copy-start = (bf16[128,2048]{1,0:T(8,128)(2,1)S(1)}, bf16[128,2048]{1,0:T(8,128)(2,1)}, u32[]{:S(2)}) copy-start(bf16[128,2048]{1,0:T(8,128)(2,1)} %param.33) | copy-start | bytes 1572868
  14.2 415.5 %all-gather.19.cloned.1.call-start = ((), (), s32[]{:S(2)}) async-start(), calls=%async_computation.15 | async-start | bytes 23789568 | tf_op jit(solution)/shard_map/all_gather | solution.py:338
  15.2 560.6 %all-gather.17.cloned.1.call-start = ((), (), s32[]{:S(2)}) async-start(), calls=%async_computation.14 | async-start | bytes 23789568 | tf_op jit(solution)/shard_map/all_gather | solution.py:337
  16.2 1075.0 %reduce-scatter.29.cloned.1.call-start = ((), (), s32[]{:S(2)}) async-start(), calls=%async_computation.25 | async-start | bytes 47579136 | tf_op jit(solution)/shard_map/reduce_scatter | solution.py:171
  60.0 150.9 %copy-start.22 = (f32[128,64]{0,1:T(8,128)}, f32[128,64]{0,1:T(8,128)S(1)}, u32[]{:S(2)}) copy-start(f32[128,64]{0,1:T(8,128)S(1)} %pad_maximum_fusion) | copy-start | bytes 98308
  61.5 142.4 %copy-start.39 = (f32[128]{0:T(128)}, f32[128]{0:T(128)S(1)}, u32[]{:S(2)}) copy-start(f32[128]{0:T(128)S(1)} %get-tuple-element.337) | copy-start | bytes 1540
  61.6 142.4 %copy-start.26 = (f32[1,2048]{1,0:T(1,128)}, f32[1,2048]{1,0:T(1,128)S(1)}, u32[]{:S(2)}) copy-start(f32[1,2048]{1,0:T(1,128)S(1)} %get-tuple-element.333) | copy-start | bytes 24580
  61.6 1228.6 %copy-start.29 = (f32[1,2048]{1,0:T(1,128)}, f32[1,2048]{1,0:T(1,128)S(1)}, u32[]{:S(2)}) copy-start(f32[1,2048]{1,0:T(1,128)S(1)} %get-tuple-element.332) | copy-start | bytes 24580
  225.8 62.2 %copy-start.7 = (bf16[4,128,8,64]{1,3,2,0:T(8,128)(2,1)}, bf16[4,128,8,64]{1,3,2,0:T(8,128)(2,1)S(1)}, u32[]{:S(2)}) copy-start(bf16[4,128,8,64]{1,3,2,0:T(8,128)(2,1)S(1)} %get-tuple-element.151) | copy-start | bytes 1572868
  225.8 62.2 %copy-start.9 = (bf16[4,1024,64]{1,2,0:T(8,128)(2,1)}, bf16[4,1024,64]{1,2,0:T(8,128)(2,1)S(1)}, u32[]{:S(2)}) copy-start(bf16[4,1024,64]{1,2,0:T(8,128)(2,1)S(1)} %get-tuple-element.662) | copy-start | bytes 1572868
  225.8 62.2 %copy-start.11 = (bf16[4,128,8,64]{1,3,2,0:T(8,128)(2,1)}, bf16[4,128,8,64]{1,3,2,0:T(8,128)(2,1)S(1)}, u32[]{:S(2)}) copy-start(bf16[4,128,8,64]{1,3,2,0:T(8,128)(2,1)S(1)} %get-tuple-element.664) | copy-start | bytes 1572868
  225.8 62.2 %copy-start.18 = (bf16[4,1024,64]{1,2,0:T(8,128)(2,1)}, bf16[4,1024,64]{1,2,0:T(8,128)(2,1)S(1)}, u32[]{:S(2)}) copy-start(bf16[4,1024,64]{1,2,0:T(8,128)(2,1)S(1)} %get-tuple-element.674) | copy-start | bytes 1572868
  607.9 642.4 %all-gather.21.cloned.1.call-start = ((), (), s32[]{:S(2)}) async-start(), calls=%async_computation.16 | async-start | bytes 23789568 | tf_op jit(solution)/shard_map/all_gather | solution.py:339
  1097.5 340.5 %reduce-scatter.13.cloned.1.call-start = ((), (), s32[]{:S(2)}) async-start(), calls=%async_computation.17 | async-start | bytes 1179648 | tf_op jit(solution)/shard_map/reduce_scatter | solution.py:235
  1264.6 13.1 copy-start.2
  1264.6 13.1 copy-start.5
  1277.7 12.5 copy-start.19
  1290.6 8.5 copy-start.10
  1290.6 8.5 copy-start.12
  1403.7 74.0 %reduce-scatter.15.cloned.1.call-start = ((), (), s32[]{:S(2)}) async-start(), calls=%async_computation.18 | async-start | bytes 1179648 | tf_op jit(solution)/shard_map/reduce_scatter | solution.py:236
  1404.3 213.4 %reduce-scatter.31.cloned.1.call-start = ((), (), s32[]{:S(2)}) async-start(), calls=%async_computation.26 | async-start | bytes 1081344
  1412.4 65.4 %copy-start.27 = (f32[1,2048]{1,0:T(1,128)S(1)}, f32[1,2048]{1,0:T(1,128)}, u32[]{:S(2)}) copy-start(f32[1,2048]{1,0:T(1,128)} %copy-done.26) | copy-start | bytes 24580
  1412.4 65.4 %copy-start.40 = (f32[128]{0:T(128)S(1)}, f32[128]{0:T(128)}, u32[]{:S(2)}) copy-start(f32[128]{0:T(128)} %copy-done.39) | copy-start | bytes 1540
  1482.7 269.9 %reduce-scatter.19.cloned.1.call-start = ((), (), s32[]{:S(2)}) async-start(), calls=%async_computation.20 | async-start | bytes 2162688 | tf_op jit(solution)/shard_map/reduce_scatter | solution.py:269
  1484.7 402.8 %reduce-scatter.21.cloned.1.call-start = ((), (), s32[]{:S(2)}) async-start(), calls=%async_computation.21 | async-start | bytes 2162688 | tf_op jit(solution)/shard_map/reduce_scatter | solution.py:270
  1486.7 581.8 %reduce-scatter.17.cloned.1.call-start = ((), (), s32[]{:S(2)}) async-start(), calls=%async_computation.19 | async-start | bytes 17301504 | tf_op jit(solution)/shard_map/reduce_scatter | solution.py:268
  1495.0 760.2 %reduce-scatter.23.cloned.1.call-start = ((), (), s32[]{:S(2)}) async-start(), calls=%async_computation.22 | async-start | bytes 17301504 | tf_op jit(solution)/shard_map/reduce_scatter | solution.py:271
  1504.2 1240.1 %reduce-scatter.25.cloned.1.call-start = ((), (), s32[]{:S(2)}) async-start(), calls=%async_computation.23 | async-start | bytes 47579136 | tf_op jit(solution)/shard_map/reduce_scatter | solution.py:169
  1523.6 1716.0 %reduce-scatter.27.cloned.1.call-start = ((), (), s32[]{:S(2)}) async-start(), calls=%async_computation.24 | async-start | bytes 47579136 | tf_op jit(solution)/shard_map/reduce_scatter | solution.py:170
  1592.3 20.6 copy-start.41
  1612.0 140.6 %copy-start.31 = (f32[64,256]{1,0:T(8,128)S(1)}, f32[64,256]{1,0:T(8,128)}, u32[]{:S(2)}) copy-start(f32[64,256]{1,0:T(8,128)} %param.39) | copy-start | bytes 196612
  1612.0 140.6 %copy-start.35 = (f32[64,256]{1,0:T(8,128)S(1)}, f32[64,256]{1,0:T(8,128)}, u32[]{:S(2)}) copy-start(f32[64,256]{1,0:T(8,128)} %param.40) | copy-start | bytes 196612
  1612.0 140.6 %copy-start.36 = (f32[64,256]{1,0:T(8,128)S(1)}, f32[64,256]{1,0:T(8,128)}, u32[]{:S(2)}) copy-start(f32[64,256]{1,0:T(8,128)} %param.41) | copy-start | bytes 196612
  1612.1 275.5 %copy-start.32 = (f32[64,256]{1,0:T(8,128)S(1)}, f32[64,256]{1,0:T(8,128)}, u32[]{:S(2)}) copy-start(f32[64,256]{1,0:T(8,128)} %param.42) | copy-start | bytes 196612
  1612.1 275.5 %copy-start.37 = (f32[64,256]{1,0:T(8,128)S(1)}, f32[64,256]{1,0:T(8,128)}, u32[]{:S(2)}) copy-start(f32[64,256]{1,0:T(8,128)} %param.43) | copy-start | bytes 196612
  1612.1 275.5 %copy-start.38 = (f32[64,256]{1,0:T(8,128)S(1)}, f32[64,256]{1,0:T(8,128)}, u32[]{:S(2)}) copy-start(f32[64,256]{1,0:T(8,128)} %param.44) | copy-start | bytes 196612
  1612.1 456.3 %copy-start.20 = (f32[64,2048]{1,0:T(8,128)S(1)}, f32[64,2048]{1,0:T(8,128)}, u32[]{:S(2)}) copy-start(f32[64,2048]{1,0:T(8,128)} %param.36) | copy-start | bytes 1572868
  1612.1 456.3 %copy-start.24 = (f32[64,2048]{1,0:T(8,128)S(1)}, f32[64,2048]{1,0:T(8,128)}, u32[]{:S(2)}) copy-start(f32[64,2048]{1,0:T(8,128)} %param.37) | copy-start | bytes 1572868
  1615.4 639.8 %copy-start.21 = (f32[64,2048]{1,0:T(8,128)S(1)}, f32[64,2048]{1,0:T(8,128)}, u32[]{:S(2)}) copy-start(f32[64,2048]{1,0:T(8,128)} %param.45) | copy-start | bytes 1572868
  1889.1 855.2 %copy-start.14 = (f32[64,5632]{1,0:T(8,128)S(1)}, f32[64,5632]{1,0:T(8,128)}, u32[]{:S(2)}) copy-start(f32[64,5632]{1,0:T(8,128)} %param.48) | copy-start | bytes 4325380
  2258.0 981.7 %copy-start.16 = (f32[64,5632]{1,0:T(8,128)S(1)}, f32[64,5632]{1,0:T(8,128)}, u32[]{:S(2)}) copy-start(f32[64,5632]{1,0:T(8,128)} %param.51) | copy-start | bytes 4325380
  (14 other events, 30.4 us)
Sparse Core Ops, SparseCore 0:
  11.5 56.4 all-gather.10
  71.4 52.5 all-gather.12
  127.5 76.4 all-gather.8
  207.2 75.9 all-gather.14
  286.5 143.1 all-gather.18
  433.0 142.7 all-gather.16
  608.1 483.1 reduce-scatter.28
  1097.7 152.6 all-gather.20
  1403.8 34.2 reduce-scatter.12
  1441.7 36.0 reduce-scatter.14
  1482.9 134.8 reduce-scatter.30
  1619.9 132.6 reduce-scatter.18
  1754.9 132.6 reduce-scatter.20
  1889.8 178.5 reduce-scatter.16
  2070.7 184.4 reduce-scatter.22
  2257.5 486.7 reduce-scatter.24
  2746.5 493.0 reduce-scatter.26
where the time goes:
time: 3270 us; the launch traced here: 3250 us
  waiting for transfers between devices  2760 us (84%)
  matrix products  352 us (11%)
  blocking collectives  62.6 us (2%)
  other arithmetic  51.7 us (2%)
    reduce_scatter x1, waiting for transfers between devices, backward_pass(): lax.psum_scatter(grad_wup, ('dp', 'fsdp'), scatter_dimension=0, tiled=True)  490 us
    reduce_scatter x1, waiting for transfers between devices, backward_pass(): lax.psum_scatter(grad_wgate, ('dp', 'fsdp'), scatter_dimension=0, tiled=T...  486 us
    reduce_scatter x1, waiting for transfers between devices, backward_pass(): lax.psum_scatter(grad_down, ('dp', 'fsdp'), scatter_dimension=0, tiled=True)  483 us
    reduce_scatter x1, waiting for transfers between devices, backward_pass(): lax.psum_scatter(grad_woutput, ('dp', 'fsdp'), scatter_dimension=0, tiled...  184 us
    reduce_scatter x1, waiting for transfers between devices, backward_pass(): lax.psum_scatter(grad_wquery, ('dp', 'fsdp'), scatter_dimension=0, tiled=...  179 us
    all_gather x1, waiting for transfers between devices, local(): lax.all_gather(ffn_local[2], ('dp', 'fsdp'), axis=0, tiled=True)  153 us
    all_gather x1, waiting for transfers between devices, local(): lax.all_gather(ffn_local[1], ('dp', 'fsdp'), axis=0, tiled=True)  140 us
    all_gather x1, waiting for transfers between devices, local(): lax.all_gather(ffn_local[0], ('dp', 'fsdp'), axis=0, tiled=True)  137 us
  transfers between devices with their start and end apart: 17, of which 17 were waited for; matrix products, arithmetic and copies ran while one was open for 6% of the time, Pallas kernels for 0%

commit v1 on v0

v1 whole, which is shorter than its diff:
```python
import functools
import math

import jax
import jax.numpy as jnp
from jax import lax
from jax.experimental import pallas as pl
from jax.experimental.pallas import tpu as pltpu
from jax.sharding import PartitionSpec as P

HEADS = 32
KV_HEADS = 4
HEAD_DIM = 64
STEP = 3

NORM_EPS = 1e-05
ROPE_BASE = 10000.0
BETA = 0.5
ADAM_EPS = 1e-08
DECAY = 0.1
MASKED = -1e30
PAIR = 2 * HEAD_DIM
BF16 = jnp.bfloat16
F32 = jnp.float32


def matmul(left, right):
    return jnp.dot(left, right, preferred_element_type=F32)


def matmul_tn(left, right):
    return lax.dot_general(left, right, (((0,), (0,)), ((), ())), preferred_element_type=F32)


def matmul_nt(left, right):
    return lax.dot_general(left, right, (((1,), (1,)), ((), ())), preferred_element_type=F32)


def rms_scale(values):
    return lax.rsqrt(jnp.mean(values * values, -1, keepdims=True) + NORM_EPS)


def adam_step(master, first_moment, second_moment, gradient, rate):
    first_new = BETA * first_moment + (1.0 - BETA) * gradient
    second_new = BETA * second_moment + (1.0 - BETA) * gradient * gradient
    correction = 1.0 - BETA**STEP
    master_new = master - rate * (
        first_new / correction / (jnp.sqrt(second_new / correction) + ADAM_EPS) + DECAY * master
    )
    return (master_new, first_new, second_new)


def core_swap(value):
    members = lax.axis_size("fsdp")
    return lax.ppermute(value, "fsdp", [(i, i ^ 1) for i in range(members)])


def chip_send(value, step):
    members = lax.axis_size("fsdp")
    return lax.ppermute(value, "fsdp", [(i, i ^ (2 * step)) for i in range(members)])


def plane_gather(own):
    chips = lax.axis_size("fsdp") // 2
    mine = jnp.stack([own] + [chip_send(own, step) for step in range(1, chips)])
    partner = core_swap(mine)
    return jnp.stack([mine, partner], 1).reshape((2 * chips,) + own.shape)


def plane_scatter(parts):
    members = parts.shape[0]
    chips = members // 2
    parts = parts.reshape((chips, 2) + parts.shape[1:])
    sums = parts[:, 0] + core_swap(parts[:, 1].astype(BF16)).astype(F32)
    total = sums[0]
    low = sums.astype(BF16)
    for step in range(1, chips):
        total = total + chip_send(low[step], step).astype(F32)
    return total


def plane_exchange(blocks):
    members = blocks.shape[0]
    chips = members // 2
    blocks = blocks.reshape((chips, 2) + blocks.shape[1:])
    mine, other = blocks[:, 0], core_swap(blocks[:, 1])
    pairs = jnp.stack([mine, other], 1)
    got = jnp.stack([pairs[0]] + [chip_send(pairs[step], step) for step in range(1, chips)])
    return got.reshape((members,) + blocks.shape[2:])


def by_offset(blocks, index):
    count = blocks.shape[0]
    return jnp.stack(
        [lax.dynamic_index_in_dim(blocks, j ^ index, 0, keepdims=False) for j in range(count)]
    )


def lane_ids(shape):
    return lax.broadcasted_iota(jnp.int32, shape, len(shape) - 1)


def turn(values, cosine, sine):
    low_half = lane_ids(values.shape) % HEAD_DIM < HEAD_DIM // 2
    shifted = jnp.where(
        low_half,
        pltpu.roll(values, PAIR - HEAD_DIM // 2, 1),
        pltpu.roll(values, HEAD_DIM // 2, 1),
    )
    return values * cosine + shifted * sine


def attend_kernel(
    members, pairs, index_ref, start_ref, cos_ref, sin_ref, qkv_ref, q_ref, kv_ref, o_ref
):
    length = qkv_ref.shape[0]
    rows = length // members
    index = index_ref[0]
    even = lane_ids((rows, PAIR)) < HEAD_DIM
    for j in range(members):
        there = pl.ds(pl.multiple_of((j ^ index) * rows, rows), rows)
        here = pl.ds(j * rows, rows)
        cosine = cos_ref[here, :]
        sine = sin_ref[here, :]
        for pair in range(pairs):
            lanes = pl.ds(pair * PAIR, PAIR)
            turned = turn(qkv_ref[there, lanes], cosine, sine)
            q_ref[here, lanes] = (turned.astype(BF16).astype(F32) * HEAD_DIM**-0.5).astype(BF16)
        both = qkv_ref[there, pl.ds(pairs * PAIR, PAIR)]
        both = jnp.where(even, turn(both, cosine, sine), both)
        kv_ref[here, :] = both.astype(BF16)
    block = min(2 * rows, 256)
    for first in range(0, length, block):
        reach = first + block
        both = kv_ref[:reach, :].astype(F32)
        left = lane_ids(both.shape) < HEAD_DIM
        keys_even = jnp.where(left, both, 0.0)
        values_odd = jnp.where(left, 0.0, both)
        keys = (keys_even.astype(BF16), pltpu.roll(keys_even, HEAD_DIM, 1).astype(BF16))
        values = (pltpu.roll(values_odd, HEAD_DIM, 1).astype(BF16), values_odd.astype(BF16))
        query_at = first + lax.broadcasted_iota(jnp.int32, (block, reach), 0)
        key_at = lax.broadcasted_iota(jnp.int32, (block, reach), 1)
        allowed = (key_at <= query_at) & (key_at >= start_ref[first:reach, :])
        for pair in range(pairs):
            lanes = pl.ds(pair * PAIR, PAIR)
            query = q_ref[first:reach, lanes]
            mixed = jnp.zeros((block, PAIR), F32)
            for side in range(2):
                scores = jnp.where(allowed, matmul_nt(query, keys[side]), MASKED)
                raised = jnp.exp(scores - jnp.max(scores, -1, keepdims=True))
                weights = raised * (1.0 / jnp.sum(raised, -1, keepdims=True))
                mixed = mixed + matmul(weights.astype(BF16), values[side])
            mixed = mixed.astype(BF16)
            for part in range(block // rows):
                j = first // rows + part
                there = pl.ds(pl.multiple_of((j ^ index) * rows, rows), rows)
                o_ref[there, lanes] = mixed[part * rows : (part + 1) * rows, :]


def attend(qkv, index, start, cosine, sine):
    length, width = qkv.shape
    pairs = width // PAIR - 1
    vmem = pl.BlockSpec(memory_space=pltpu.VMEM)
    return pl.pallas_call(
        functools.partial(attend_kernel, lax.axis_size("fsdp"), pairs),
        out_shape=(
            jax.ShapeDtypeStruct((length, pairs * PAIR), BF16),
            jax.ShapeDtypeStruct((length, PAIR), BF16),
            jax.ShapeDtypeStruct((length, pairs * PAIR), BF16),
        ),
        in_specs=[pl.BlockSpec(memory_space=pltpu.SMEM)] + [vmem] * 4,
        out_specs=(vmem,) * 3,
        compiler_params=pltpu.CompilerParams(vmem_limit_bytes=48 * 2**20),
        cost_estimate=pl.CostEstimate(
            flops=8 * length * length * pairs * PAIR // 3,
            bytes_accessed=length * pairs * PAIR * 12,
            transcendentals=length * length * pairs,
        ),
        name="attend",
    )(index, start, cosine, sine, qkv)


def attend_back_kernel(
    members,
    pairs,
    index_ref,
    start_ref,
    cos_ref,
    sin_ref,
    q_ref,
    kv_ref,
    do_ref,
    out_ref,
    dk_ref,
    dv_ref,
):
    length = q_ref.shape[0]
    rows = length // members
    index = index_ref[0]
    block = min(2 * rows, 256)
    dk_ref[...] = jnp.zeros_like(dk_ref)
    dv_ref[...] = jnp.zeros_like(dv_ref)
    for first in range(0, length, block):
        reach = first + block
        both = kv_ref[:reach, :].astype(F32)
        left = lane_ids(both.shape) < HEAD_DIM
        keys_even = jnp.where(left, both, 0.0)
        values_odd = jnp.where(left, 0.0, both)
        keys = (keys_even.astype(BF16), pltpu.roll(keys_even, HEAD_DIM, 1).astype(BF16))
        values = (pltpu.roll(values_odd, HEAD_DIM, 1).astype(BF16), values_odd.astype(BF16))
        key_at = lax.broadcasted_iota(jnp.int32, (reach, block), 0)
        query_at = first + lax.broadcasted_iota(jnp.int32, (reach, block), 1)
        allowed = (key_at <= query_at) & (key_at >= start_ref[:, first:reach])
        half = lane_ids((block, PAIR)) < HEAD_DIM
        for pair in range(pairs):
            lanes = pl.ds(pair * PAIR, PAIR)
            query = q_ref[first:reach, lanes]
            grad = jnp.concatenate(
                [
                    do_ref[
                        pl.ds(pl.multiple_of(((first // rows + part) ^ index) * rows, rows), rows),
                        lanes,
                    ]
                    for part in range(block // rows)
                ],
                0,
            )
            dq = jnp.zeros((block, PAIR), F32)
            for side in range(2):
                keep = half if side == 0 else ~half
                query_side = jnp.where(keep, query.astype(F32), 0.0).astype(BF16)
                grad_side = jnp.where(keep, grad.astype(F32), 0.0).astype(BF16)
                scores = jnp.where(allowed, matmul_nt(keys[side], query), MASKED)
                raised = jnp.exp(scores - jnp.max(scores, 0, keepdims=True))
                weights = raised * (1.0 / jnp.sum(raised, 0, keepdims=True))
                dp = matmul_nt(values[side], grad)
                centre = jnp.sum(weights * dp, 0, keepdims=True)
                ds = (weights * (dp - centre)).astype(BF16)
                dv_ref[:reach, :] += matmul(weights.astype(BF16), grad_side)
                dk_ref[:reach, :] += matmul(ds, query_side)
                dq = dq + matmul_tn(ds, keys[side])
            dq = dq * HEAD_DIM**-0.5
            for part in range(block // rows):
                j = first // rows + part
                piece = dq[part * rows : (part + 1) * rows, :]
                here = pl.ds(j * rows, rows)
                there = pl.ds(pl.multiple_of((j ^ index) * rows, rows), rows)
                out_ref[there, lanes] = turn(piece, cos_ref[here, :], -sin_ref[here, :]).astype(BF16)
    left = lane_ids((rows, PAIR)) < HEAD_DIM
    for j in range(members):
        here = pl.ds(j * rows, rows)
        there = pl.ds(pl.multiple_of((j ^ index) * rows, rows), rows)
        dk = dk_ref[here, :]
        dv = dv_ref[here, :]
        dk = turn(dk + pltpu.roll(dk, HEAD_DIM, 1), cos_ref[here, :], -sin_ref[here, :])
        dv = dv + pltpu.roll(dv, HEAD_DIM, 1)
        out_ref[there, pl.ds(pairs * PAIR, PAIR)] = jnp.where(left, dk, dv).astype(BF16)


def attend_back(queries, keys_values, grad, index, start, cosine, sine):
    length, width = queries.shape
    pairs = width // PAIR
    vmem = pl.BlockSpec(memory_space=pltpu.VMEM)
    return pl.pallas_call(
        functools.partial(attend_back_kernel, lax.axis_size("fsdp"), pairs),
        out_shape=jax.ShapeDtypeStruct((length, width + PAIR), BF16),
        in_specs=[pl.BlockSpec(memory_space=pltpu.SMEM)] + [vmem] * 6,
        out_specs=vmem,
        scratch_shapes=[pltpu.VMEM((length, PAIR), F32), pltpu.VMEM((length, PAIR), F32)],
        compiler_params=pltpu.CompilerParams(vmem_limit_bytes=48 * 2**20),
        cost_estimate=pl.CostEstimate(
            flops=20 * length * length * pairs * PAIR // 3,
            bytes_accessed=length * pairs * PAIR * 12,
            transcendentals=length * length * pairs,
        ),
        name="attend_back",
    )(index, start, cosine, sine, queries, keys_values, grad)


def segment_starts(lengths_row, length):
    count = lengths_row.shape[0]
    ahead = jnp.arange(count)[:, None] < jnp.arange(count)[None, :]
    starts = jnp.sum(jnp.where(ahead, lengths_row[:, None], 0), 0, dtype=jnp.int32)
    ends = starts + lengths_row
    places = jnp.arange(length, dtype=jnp.int32)
    within = (places[:, None] >= starts[None, :]) & (places[:, None] < ends[None, :])
    return jnp.sum(jnp.where(within, starts[None, :], 0), 1, dtype=jnp.int32)


def rope_tables(positions):
    half = HEAD_DIM // 2
    freqs = jnp.exp(jnp.arange(half, dtype=F32) * (-2.0 * math.log(ROPE_BASE) / HEAD_DIM))
    angles = positions.astype(F32)[:, None] * freqs[None, :]
    cosine = jnp.cos(angles)
    sine = jnp.sin(angles)
    return (
        jnp.concatenate([cosine] * 4, 1),
        jnp.concatenate([-sine, sine, -sine, sine], 1),
    )


def local(
    tokens,
    out_grad,
    seq_lengths,
    query_weight,
    query_first,
    query_second,
    key_weight,
    key_first,
    key_second,
    value_weight,
    value_first,
    value_second,
    output_weight,
    output_first,
    output_second,
    gate_weight,
    gate_first,
    gate_second,
    up_weight,
    up_first,
    up_second,
    down_weight,
    down_first,
    down_second,
    norm_gains,
    gains_first,
    gains_second,
):
    both = ("dp", "fsdp")
    planes = lax.axis_size("dp")
    members = lax.axis_size("fsdp")
    index = lax.axis_index("fsdp")
    index_ref = index.astype(jnp.int32)[None]
    count, width = tokens.shape
    length = count * members
    slice_rows = query_weight.shape[0]
    own_q = query_weight.shape[1] // members
    own_ff = gate_weight.shape[1] // members
    ff_piece = own_ff // planes
    sharing = members // KV_HEADS

    tokens_all = plane_gather(tokens).reshape(length, width)
    out_grad_all = plane_gather(out_grad).reshape(length, width)
    gains = lax.all_gather(norm_gains.astype(BF16), both, axis=1, tiled=True).astype(F32)

    start = segment_starts(seq_lengths[0], length)
    cosine, sine = rope_tables(jnp.arange(length, dtype=jnp.int32) - start)

    def head_columns(weight):
        return weight.reshape(slice_rows, -1, HEAD_DIM * HEADS // members)

    q_cols = query_weight.astype(BF16).reshape(slice_rows, members, own_q)
    k_cols = jnp.repeat(key_weight.astype(BF16).reshape(slice_rows, KV_HEADS, HEAD_DIM), sharing, 1)
    v_cols = jnp.repeat(value_weight.astype(BF16).reshape(slice_rows, KV_HEADS, HEAD_DIM), sharing, 1)
    qkv_cols = jnp.transpose(jnp.concatenate([q_cols, k_cols, v_cols], 2), (1, 0, 2))
    qkv_got = by_offset(plane_exchange(by_offset(qkv_cols, index)), index)
    w_qkv = lax.all_gather(qkv_got.reshape(members * slice_rows, -1), "dp", axis=0, tiled=True)

    hop = members // planes
    out_rows = lax.all_gather(output_weight.astype(BF16), "dp", axis=0, tiled=False)
    own_plane = index // hop

    def out_route(turn_no):
        return [
            (i, ((turn_no + i) % planes) * hop + i // planes) for i in range(members)
        ]

    w_output = jnp.zeros((planes, slice_rows, width), BF16)
    for turn_no in range(planes):
        sent = lax.dynamic_index_in_dim(out_rows, (turn_no + index) % planes, 0, keepdims=False)
        got = lax.ppermute(sent, "fsdp", out_route(turn_no))
        place = (own_plane + planes - turn_no) % planes
        w_output = lax.dynamic_update_index_in_dim(w_output, got, place, 0)
    w_output = w_output.reshape(planes * slice_rows, width)

    def ff_columns(weight):
        cols = weight.astype(BF16).reshape(slice_rows, planes, members, ff_piece)
        cols = jnp.transpose(cols, (2, 0, 1, 3)).reshape(members, slice_rows, own_ff)
        got = by_offset(plane_exchange(by_offset(cols, index)), index)
        return lax.all_gather(got.reshape(members * slice_rows, own_ff), "dp", axis=0, tiled=True)

    w_gate = ff_columns(gate_weight)
    w_up = ff_columns(up_weight)
    w_down = lax.all_gather(down_weight.astype(BF16), "dp", axis=0, tiled=True)

    tokens_f = tokens_all.astype(F32)
    scale_one_all = rms_scale(tokens_f)
    normed = (tokens_f * scale_one_all * gains[0]).astype(BF16)
    qkv = matmul(normed, w_qkv)
    queries, keys_values, attended = attend(qkv, index_ref, start[:, None], cosine, sine)
    own_tokens = tokens.astype(F32)
    mixed = matmul(attended, w_output)
    resid = own_tokens + plane_scatter(mixed.reshape(members, count, width))
    scale_two = rms_scale(resid)
    normed_two = plane_gather((resid * scale_two * gains[1]).astype(BF16)).reshape(length, width)
    gate_value = matmul(normed_two, w_gate)
    up_value = matmul(normed_two, w_up)
    sigmoid_gate = jax.nn.sigmoid(gate_value)
    hidden = (gate_value * sigmoid_gate * up_value).astype(BF16)

    grad_hidden = matmul_nt(out_grad_all, w_down)
    grad_gate = (
        grad_hidden * up_value * sigmoid_gate * (1.0 + gate_value * (1.0 - sigmoid_gate))
    ).astype(BF16)
    grad_up = (grad_hidden * gate_value * sigmoid_gate).astype(BF16)
    grad_normed_two = matmul_nt(grad_gate, w_gate) + matmul_nt(grad_up, w_up)
    grad_normed_two = plane_scatter(grad_normed_two.reshape(members, count, width))
    weighted_two = grad_normed_two * gains[1]
    grad_gain_two = jnp.sum(grad_normed_two * resid * scale_two, 0)
    grad_resid = (
        out_grad.astype(F32)
        + scale_two * weighted_two
        - resid
        * (scale_two * scale_two * scale_two)
        * jnp.mean(weighted_two * resid, -1, keepdims=True)
    )
    grad_attn_out = plane_gather(grad_resid.astype(BF16)).reshape(length, width)

    def ff_gradient(gradient):
        part = lax.psum_scatter(gradient.astype(BF16), "dp", scatter_dimension=0, tiled=True)
        blocks = by_offset(part.reshape(members, slice_rows, own_ff), index)
        got = by_offset(plane_exchange(blocks), index)
        got = got.reshape(members, slice_rows, planes, ff_piece)
        return jnp.transpose(got, (1, 2, 0, 3)).reshape(slice_rows, members * own_ff).astype(F32)

    grad_gate_weight = ff_gradient(matmul_tn(normed_two, grad_gate))
    grad_up_weight = ff_gradient(matmul_tn(normed_two, grad_up))
    grad_down_weight = lax.psum_scatter(
        matmul_tn(hidden, out_grad_all).astype(BF16), "dp", scatter_dimension=0, tiled=True
    ).astype(F32)
    result = resid + plane_scatter(matmul(hidden, w_down).reshape(members, count, width))

    grad_mixed = matmul_nt(grad_attn_out, w_output).astype(BF16)
    grad_qkv = attend_back(
        queries, keys_values, grad_mixed, index_ref, start[None, :], cosine, sine
    )
    grad_normed = plane_scatter(matmul_nt(grad_qkv, w_qkv).reshape(members, count, width))
    scale_one = rms_scale(own_tokens)
    weighted_one = grad_normed * gains[0]
    grad_gain_one = jnp.sum(grad_normed * own_tokens * scale_one, 0)
    grad_tokens = (
        grad_resid
        + scale_one * weighted_one
        - own_tokens
        * (scale_one * scale_one * scale_one)
        * jnp.mean(weighted_one * own_tokens, -1, keepdims=True)
    )

    grad_output = matmul_tn(attended, grad_attn_out).astype(BF16)
    grad_output = grad_output.reshape(planes, slice_rows, width)
    out_parts = jnp.zeros((planes, slice_rows, width), BF16)
    for turn_no in range(planes):
        place = (own_plane + planes - turn_no) % planes
        sent = lax.dynamic_index_in_dim(grad_output, place, 0, keepdims=False)
        got = lax.ppermute(sent, "fsdp", [(b, a) for a, b in out_route(turn_no)])
        out_parts = lax.dynamic_update_index_in_dim(out_parts, got, (turn_no + index) % planes, 0)
    grad_output_weight = lax.psum_scatter(
        out_parts.reshape(planes * slice_rows, width), "dp", scatter_dimension=0, tiled=True
    ).astype(F32)

    grad_w_qkv = lax.psum_scatter(
        matmul_tn(normed, grad_qkv).astype(BF16), "dp", scatter_dimension=0, tiled=True
    )
    blocks = by_offset(grad_w_qkv.reshape(members, slice_rows, -1), index)
    got = by_offset(plane_exchange(blocks), index).astype(F32)
    got = jnp.transpose(got, (1, 0, 2))
    grad_query_weight = got[:, :, :own_q].reshape(slice_rows, -1)
    grad_kv = got[:, :, own_q:].reshape(slice_rows, KV_HEADS, sharing, PAIR).sum(2)
    grad_key_weight = grad_kv[:, :, :HEAD_DIM].reshape(slice_rows, -1)
    grad_value_weight = grad_kv[:, :, HEAD_DIM:].reshape(slice_rows, -1)
    gain_grads = lax.psum_scatter(
        jnp.stack([grad_gain_one, grad_gain_two]), both, scatter_dimension=1, tiled=True
    )

    updated = (
        adam_step(query_weight, query_first, query_second, grad_query_weight, 0.02)
        + adam_step(key_weight, key_first, key_second, grad_key_weight, 0.02)
        + adam_step(value_weight, value_first, value_second, grad_value_weight, 0.02)
        + adam_step(output_weight, output_first, output_second, grad_output_weight, 0.1)
        + adam_step(gate_weight, gate_first, gate_second, grad_gate_weight, 0.02)
        + adam_step(up_weight, up_first, up_second, grad_up_weight, 0.02)
        + adam_step(down_weight, down_first, down_second, grad_down_weight, 0.02)
        + adam_step(norm_gains, gains_first, gains_second, gain_grads, 0.2)
    )
    return (result.astype(BF16), grad_tokens) + updated


def solution(mesh):
    rows = P(("dp", "fsdp"), None)
    columns = P(None, ("dp", "fsdp"))
    in_specs = (rows, rows, P("dp", None)) + (rows,) * 21 + (columns,) * 3
    out_specs = (rows, rows) + (rows,) * 21 + (columns,) * 3
    return jax.shard_map(local, mesh=mesh, in_specs=in_specs, out_specs=out_specs, check_vma=False)
```

time: 3270 us -> 708 us (0.22)
  waiting for transfers between devices: 2760 us -> 290 us
  matrix products: 352 us -> 72.7 us
  starting transfers between devices: 0.92 us -> 81.6 us
  local copies, waits for them, and re-layouts: 9.7 us -> 85.8 us
    reduce_scatter x9 -> x5, waiting for transfers between devices: 2150 us -> 0.04 us  [the longest x1 0.02 us: local(): lax.psum_scatter(matmul_tn(normed, grad_qkv).astype(BF16), 'dp', scatter_...]
    all_gather x7 -> x5, waiting for transfers between devices: 606 us -> 0.01 us  [the longest x2 0.01 us: ff_columns(): lax.all_gather(got.reshape(members * slice_rows, own_ff), 'dp', axis=0, t...]
    dot_general x41 -> x5, matrix products: 198 us -> 28.1 us  [matmul(): return jnp.dot(left, right, preferred_element_type=F32)]
    ppermute x0 -> x64, waiting for transfers between devices: none -> 166 us  [the longest x42 142 us: chip_send(): lax.ppermute(value, 'fsdp', [(i, i ^ 2 * step) for i in range(members)])]
    unnamed x18 -> x12, waiting for transfers between devices: 3.09 us -> 124 us
    ppermute x0 -> x64, starting transfers between devices: none -> 71.8 us  [the longest x42 50.2 us: chip_send(): lax.ppermute(value, 'fsdp', [(i, i ^ 2 * step) for i in range(members)])]
    dot_general x7 -> x5, matrix products: 75.7 us -> 18.4 us  [matmul_tn(): lax.dot_general(left, right, (((0,), (0,)), ((), ())), preferred_element_...]
    dot_general x7 -> x5, matrix products: 59.7 us -> 26.3 us  [matmul_nt(): lax.dot_general(left, right, (((1,), (1,)), ((), ())), preferred_element_...]
  transfers between devices with their start and end apart: 17 -> 75, of which waited for: 17 -> 37; matrix products, arithmetic and copies ran while one was open for 6% -> 28% of each run, Pallas kernels for 0% -> 3%
where the time goes in v1:
time: 708 us; the launch traced here: 699 us
  waiting for transfers between devices  290 us (41%)
  local copies, waits for them, and re-layouts  85.8 us (12%)
  starting transfers between devices  81.6 us (12%)
  other arithmetic  76.5 us (11%)
  matrix products  72.7 us (10%)
  blocking collectives  54.6 us (8%)
  Pallas kernels  21.4 us (3%)
  between operations  16 us (2%)
    ppermute x42, waiting for transfers between devices, chip_send(): lax.ppermute(value, 'fsdp', [(i, i ^ 2 * step) for i in range(members)])  142 us
    unnamed x12, waiting for transfers between devices  124 us
    all_gather x1, blocking collectives, local(): lax.all_gather(norm_gains.astype(BF16), both, axis=1, tiled=True)  54.6 us
    ppermute x42, starting transfers between devices, chip_send(): lax.ppermute(value, 'fsdp', [(i, i ^ 2 * step) for i in range(members)])  50.2 us
    unnamed x198, local copies, waits for them, and re-layouts  38.5 us
    dot_general x5, matrix products, matmul(): return jnp.dot(left, right, preferred_element_type=F32)  28.1 us
    dot_general x5, matrix products, matmul_nt(): lax.dot_general(left, right, (((1,), (1,)), ((), ())), preferred_element_...  26.3 us
    sub x8, other arithmetic, adam_step(): master - rate * (first_new / correction / (jnp.sqrt(second_new / correcti...  20.3 us
  transfers between devices with their start and end apart: 75, of which 37 were waited for; matrix products, arithmetic and copies ran while one was open for 28% of the time, Pallas kernels for 3%

profile of v1, /device:TPU:0, one launch (start us, length us, event | category | flops | bytes accessed | tf_op | source)
XLA Modules:
  0.0 698.8 jit_solution(286171818471219654)
XLA Ops:
  25.7 3.5 collective-permute-start.7
  45.9 5.2 collective-permute-done.23
  51.1 3.4 collective-permute-done.22
  60.6 54.6 %all-gather.1 = bf16[32,64,2]{1,2,0:T(2,128)(2,1)S(1)} all-gather(bf16[1,64,2]{1,2,0:T(2,128)(2,1)S(1)} %convert_bitcast_fusion.1), channel_id=1, replica_groups=mesh['dp'=4,'fsdp'=8] {'dp','fsdp'}, dimensions={0}, use_global_device_ids=true | all-gather | bytes 8448 | tf_op jit(solution)/shard_map/all_gather | solution.py:346
  119.5 3.4 collective-permute-start.25
  122.9 3.7 fusion.86
  138.8 5.5 collective-permute-start.9
  160.8 5.0 fusion.108.qkv_ref
  165.8 7.9 %attend.1 = (bf16[1024,256]{1,0:T(8,128)(2,1)S(1)}, bf16[1024,128]{1,0:T(8,128)(2,1)S(1)}, bf16[1024,256]{1,0:T(8,128)(2,1)S(1)}) custom-call(s32[1]{0:T(128)} %bitcast.index_ref, s32[1024,1]{1,0:T(8,128)S(1)} %copy.259.start_ref, f32[1024,128]{1,0:T(8,128)S(1)} %get-tuple-element.170.cos_ref, f32[1024,128]{1,0:T(8,128)S(1)} %get-tuple-element.171.sin_ref, ...), custom_call_target="tpu_custom_call" | custom-call | flops 715827904 | bytes 3145728 | tf_op jit(solution)/shard_map/attend/pallas_call | solution.py:164
  176.1 3.8 collective-permute-done.12
  191.2 8.8 %reduce-scatter.13.cloned.1.call-start = ((), (), s32[]{:S(2)}) async-start(), calls=%async_computation.12 | async-start | bytes 3604480 | tf_op jit(solution)/shard_map/reduce_scatter | solution.py:422
  200.8 10.4 %collective-permute-done.14 = bf16[128,2048]{1,0:T(8,128)(2,1)S(1)} collective-permute-done((bf16[128,2048]{1,0:T(8,128)(2,1)}, bf16[128,2048]{1,0:T(8,128)(2,1)S(1)}, u32[]{:S(2)}, u32[]{:S(2)}) %collective-permute-start.14) | collective-permute-done | bytes 524320 | tf_op jit(solution)/shard_map/ppermute | solution.py:60
  217.2 5.2 collective-permute-done.34
  223.0 10.7 %collective-permute-done.33 = bf16[128,2048]{1,0:T(8,128)(2,1)} collective-permute-done((bf16[128,2048]{1,0:T(8,128)(2,1)}, bf16[128,2048]{1,0:T(8,128)(2,1)}, u32[]{:S(2)}, u32[]{:S(2)}) %collective-permute-start.33) | collective-permute-done | bytes 524320 | tf_op jit(solution)/shard_map/ppermute | solution.py:60
  236.0 8.9 %collective-permute-done.18 = bf16[128,2048]{1,0:T(8,128)(2,1)S(1)} collective-permute-done((bf16[128,2048]{1,0:T(8,128)(2,1)S(1)}, bf16[128,2048]{1,0:T(8,128)(2,1)S(1)}, u32[]{:S(2)}, u32[]{:S(2)}) %collective-permute-start.18) | collective-permute-done | bytes 524320 | tf_op jit(solution)/shard_map/ppermute | solution.py:60
  244.9 10.5 %collective-permute-done.17 = bf16[128,2048]{1,0:T(8,128)(2,1)S(1)} collective-permute-done((bf16[128,2048]{1,0:T(8,128)(2,1)S(1)}, bf16[128,2048]{1,0:T(8,128)(2,1)S(1)}, u32[]{:S(2)}, u32[]{:S(2)}) %collective-permute-start.17) | collective-permute-done | bytes 524320 | tf_op jit(solution)/shard_map/ppermute | solution.py:60
  263.1 7.9 %fusion.110 = f32[1024,704]{0,1:T(8,128)} fusion(bf16[1024,2048]{1,0:T(8,128)(2,1)} %bitcast.432, bf16[2048,704]{1,0:T(8,128)(2,1)} %all-gather.10.cloned.1.call-done), kind=kOutput, calls=%fused_computation.381 | convolution fusion | flops 2952790016 | bytes 9961472 | tf_op jit(solution)/shard_map/dot_general | solution.py:28
  271.0 7.9 %fusion.111 = f32[1024,704]{0,1:T(8,128)} fusion(bf16[1024,2048]{1,0:T(8,128)(2,1)} %bitcast.433, bf16[2048,704]{1,0:T(8,128)(2,1)} %all-gather.12.cloned.1.call-done), kind=kOutput, calls=%fused_computation.382 | convolution fusion | flops 2952790016 | bytes 9961472 | tf_op jit(solution)/shard_map/dot_general | solution.py:28
  278.9 10.8 %multiply_convert_fusion = (bf16[1024,704]{0,1:T(8,128)(2,1)}, bf16[1024,704]{0,1:T(8,128)(2,1)S(1)}, bf16[1024,704]{0,1:T(8,128)(2,1)}) fusion(f32[1024,704]{0,1:T(8,128)} %fusion.110, f32[1024,704]{0,1:T(8,128)} %fusion.111, bf16[1024,2048]{1,0:T(8,128)(2,1)} %bitcast.428, bf16[704,2048]{1,0:T(8,128)(2,1)} %all-gather.14.cloned.1.call-done), kind=kOutput, calls=%fused_computation.24 | convolution fusion | flops 2964324352 | bytes 17170432 | tf_op jit(solution)/shard_map/dot_general | solution.py:36
  290.9 4.5 convolution_convert_fusion.1
  295.5 6.0 fusion.113
  301.5 3.6 convolution_add_fusion
  305.1 3.4 copy-done.9
  311.5 4.5 convolution_convert_fusion
  316.4 5.9 fusion.112
  335.2 6.3 collective-permute-done.39
  343.1 9.8 %collective-permute-done.38 = bf16[128,2048]{1,0:T(8,128)(2,1)S(1)} collective-permute-done((bf16[128,2048]{1,0:T(8,128)(2,1)S(1)}, bf16[128,2048]{1,0:T(8,128)(2,1)S(1)}, u32[]{:S(2)}, u32[]{:S(2)}) %collective-permute-start.38) | collective-permute-done | bytes 524320 | tf_op jit(solution)/shard_map/ppermute | solution.py:60
  353.5 10.6 %collective-permute-done.31 = bf16[128,2048]{1,0:T(8,128)(2,1)S(1)} collective-permute-done((bf16[128,2048]{1,0:T(8,128)(2,1)S(1)}, bf16[128,2048]{1,0:T(8,128)(2,1)S(1)}, u32[]{:S(2)}, u32[]{:S(2)}) %collective-permute-start.31) | collective-permute-done | bytes 524320 | tf_op jit(solution)/shard_map/ppermute | solution.py:60
  364.1 10.6 %collective-permute-done.30 = bf16[128,2048]{1,0:T(8,128)(2,1)S(1)} collective-permute-done((bf16[128,2048]{1,0:T(8,128)(2,1)S(1)}, bf16[128,2048]{1,0:T(8,128)(2,1)S(1)}, u32[]{:S(2)}, u32[]{:S(2)}) %collective-permute-start.30) | collective-permute-done | bytes 524320 | tf_op jit(solution)/shard_map/ppermute | solution.py:60
  374.7 3.1 fusion.98
  381.3 4.5 convolution_convert_fusion.2
  385.9 7.8 %collective-permute-done.42 = bf16[128,2048]{1,0:T(8,128)(2,1)S(1)} collective-permute-done((bf16[128,2048]{1,0:T(8,128)(2,1)}, bf16[128,2048]{1,0:T(8,128)(2,1)S(1)}, u32[]{:S(2)}, u32[]{:S(2)}) %collective-permute-start.42) | collective-permute-done | bytes 524320 | tf_op jit(solution)/shard_map/ppermute | solution.py:60
  393.7 10.4 %collective-permute-done.41 = bf16[128,2048]{1,0:T(8,128)(2,1)S(1)} collective-permute-done((bf16[128,2048]{1,0:T(8,128)(2,1)}, bf16[128,2048]{1,0:T(8,128)(2,1)S(1)}, u32[]{:S(2)}, u32[]{:S(2)}) %collective-permute-start.41) | collective-permute-done | bytes 524320 | tf_op jit(solution)/shard_map/ppermute | solution.py:60
  405.8 4.1 collective-permute-done.43
  413.7 5.4 collective-permute-start.53
  424.2 5.1 collective-permute-done.53
  434.4 3.5 convolution_convert_fusion.5.do_ref
  437.9 13.5 %attend_back.1 = bf16[1024,384]{1,0:T(8,128)(2,1)S(1)} custom-call(s32[1]{0:T(128)} %bitcast.index_ref, s32[1,1024]{1,0:T(1,128)S(1)} %bitcast.412, f32[1024,128]{1,0:T(8,128)S(1)} %get-tuple-element.170.cos_ref, f32[1024,128]{1,0:T(8,128)S(1)} %get-tuple-element.171.sin_ref, bf16[1024,256]{1,0:T(8,128)(2,1)S(1)} %get-tuple-element.30.q_ref, ...), custom_call_target="tpu_custom_call" | custom-call | flops 1789569664 | bytes 3145728 | tf_op jit(solution)/shard_map/attend_back/pallas_call | solution.py:264
  453.8 3.4 copy-done
  460.2 3.6 convolution_convert_fusion.3
  473.5 4.8 multiply_subtract_fusion
  492.0 4.6 multiply_subtract_fusion.2
  504.3 5.0 multiply_subtract_fusion.1
  509.3 6.0 fusion.96
  522.5 10.0 %collective-permute-done.47 = bf16[128,2048]{1,0:T(8,128)(2,1)S(1)} collective-permute-done((bf16[128,2048]{1,0:T(8,128)(2,1)}, bf16[128,2048]{1,0:T(8,128)(2,1)S(1)}, u32[]{:S(2)}, u32[]{:S(2)}) %collective-permute-start.47) | collective-permute-done | bytes 524320 | tf_op jit(solution)/shard_map/ppermute | solution.py:60
  532.5 9.1 %collective-permute-done.46 = bf16[128,2048]{1,0:T(8,128)(2,1)S(1)} collective-permute-done((bf16[128,2048]{1,0:T(8,128)(2,1)}, bf16[128,2048]{1,0:T(8,128)(2,1)S(1)}, u32[]{:S(2)}, u32[]{:S(2)}) %collective-permute-start.46) | collective-permute-done | bytes 524320 | tf_op jit(solution)/shard_map/ppermute | solution.py:60
  553.9 124.3 %reduce-scatter.19.cloned.1.call-done = f32[64,2]{1,0:T(8,128)} async-done(((f32[2048,2]{1,0:T(8,128)}), f32[64,2]{1,0:T(8,128)}) %reduce-scatter.19.cloned.1.call-update) | async-done | bytes 528
  679.2 3.4 collective-permute-start.49
  (458 shorter events, 208.6 us)
Async XLA Ops:
  7.2 127.0 %all-gather.16.cloned.1.call-start = ((), (), s32[]{:S(2)}) async-start(), calls=%async_computation.15 | async-start | bytes 1310720 | tf_op jit(solution)/shard_map/all_gather | solution.py:362
  12.6 12.2 %collective-permute-start.4 = (bf16[4,64,384]{2,1,0:T(8,128)(2,1)}, bf16[4,64,384]{2,1,0:T(8,128)(2,1)}, u32[]{:S(2)}, u32[]{:S(2)}) collective-permute-start(bf16[4,64,384]{2,1,0:T(8,128)(2,1)} %get-tuple-element.150), channel_id=1, source_target_pairs={{0,1},{1,0},{2,3},{3,2},{4,5},{5,4},{6,7},{7,6},{8,9},{9,8},{10,11... | collective-permute-start | bytes 589832 | tf_op jit(solution)/shard_map/ppermute | solution.py:55
  13.8 147.0 %all-gather.8.cloned.1.call-start = ((), (), s32[]{:S(2)}) async-start(), calls=%async_computation.6 | async-start | bytes 1966080 | tf_op jit(solution)/shard_map/all_gather | solution.py:359
  36.1 226.9 %all-gather.10.cloned.1.call-start = ((), (), s32[]{:S(2)}) async-start(), calls=%async_computation.7 | async-start | bytes 3932160 | tf_op jit(solution)/shard_map/all_gather | solution.py:382
  55.8 215.2 %all-gather.12.cloned.1.call-start = ((), (), s32[]{:S(2)}) async-start(), calls=%async_computation.8 | async-start | bytes 3932160 | tf_op jit(solution)/shard_map/all_gather | solution.py:382
  55.8 63.7 %collective-permute-start.2 = (bf16[128,2048]{1,0:T(8,128)(2,1)S(1)}, bf16[128,2048]{1,0:T(8,128)(2,1)}, u32[]{:S(2)}, u32[]{:S(2)}) collective-permute-start(bf16[128,2048]{1,0:T(8,128)(2,1)S(1)} %copy-done.2), channel_id=1, source_target_pairs={{0,6},{1,7},{2,4},{3,5},{4,2},{5,3},{6,0},{7,1},{8,14},{9,15},{10,... | collective-permute-start | bytes 1572872 | tf_op jit(solution)/shard_map/ppermute | solution.py:60
  57.4 65.5 %collective-permute-start.1 = (bf16[128,2048]{1,0:T(8,128)(2,1)S(1)}, bf16[128,2048]{1,0:T(8,128)(2,1)}, u32[]{:S(2)}, u32[]{:S(2)}) collective-permute-start(bf16[128,2048]{1,0:T(8,128)(2,1)S(1)} %copy-done.2), channel_id=1, source_target_pairs={{0,4},{1,5},{2,6},{3,7},{4,0},{5,1},{6,2},{7,3},{8,12},{9,13},{10,... | collective-permute-start | bytes 1572872 | tf_op jit(solution)/shard_map/ppermute | solution.py:60
  58.8 64.1 %collective-permute-start = (bf16[128,2048]{1,0:T(8,128)(2,1)S(1)}, bf16[128,2048]{1,0:T(8,128)(2,1)}, u32[]{:S(2)}, u32[]{:S(2)}) collective-permute-start(bf16[128,2048]{1,0:T(8,128)(2,1)S(1)} %copy-done.2), channel_id=1, source_target_pairs={{0,2},{1,3},{2,0},{3,1},{4,6},{5,7},{6,4},{7,5},{8,10},{9,11},{10,... | collective-permute-start | bytes 1572872 | tf_op jit(solution)/shard_map/ppermute | solution.py:60
  60.2 58.0 %collective-permute-start.24 = (bf16[4,64,704]{2,1,0:T(8,128)(2,1)}, bf16[4,64,704]{2,1,0:T(8,128)(2,1)}, u32[]{:S(2)}, u32[]{:S(2)}) collective-permute-start(bf16[4,64,704]{2,1,0:T(8,128)(2,1)} %get-tuple-element.129), channel_id=1, source_target_pairs={{0,1},{1,0},{2,3},{3,2},{4,5},{5,4},{6,7},{7,6},{8,9},{9,8},{10,11... | collective-permute-start | bytes 1081352 | tf_op jit(solution)/shard_map/ppermute | solution.py:55
  119.4 11.4 %collective-permute-start.26 = (bf16[2,64,704]{2,1,0:T(8,128)(2,1)S(1)}, bf16[2,64,704]{2,1,0:T(8,128)(2,1)S(1)}, u32[]{:S(2)}, u32[]{:S(2)}) collective-permute-start(bf16[2,64,704]{2,1,0:T(8,128)(2,1)S(1)} %get-tuple-element.127), channel_id=1, source_target_pairs={{0,4},{1,5},{2,6},{3,7},{4,0},{5,1},{6,2},{7,3},{8,12},{9,13},{10,... | collective-permute-start | bytes 540680 | tf_op jit(solution)/shard_map/ppermute | solution.py:60
  126.7 26.3 %collective-permute-start.3 = (bf16[4,128,2048]{2,1,0:T(8,128)(2,1)}, bf16[4,128,2048]{2,1,0:T(8,128)(2,1)}, u32[]{:S(2)}, u32[]{:S(2)}) collective-permute-start(bf16[4,128,2048]{2,1,0:T(8,128)(2,1)} %get-tuple-element.96), channel_id=1, source_target_pairs={{0,1},{1,0},{2,3},{3,2},{4,5},{5,4},{6,7},{7,6},{8,9},{9,8},{10,11... | collective-permute-start | bytes 6291464 | tf_op jit(solution)/shard_map/ppermute | solution.py:55
  135.5 12.0 %collective-permute-start.8 = (bf16[64,2048]{1,0:T(8,128)(2,1)S(1)}, bf16[64,2048]{1,0:T(8,128)(2,1)}, u32[]{:S(2)}, u32[]{:S(2)}) collective-permute-start(bf16[64,2048]{1,0:T(8,128)(2,1)S(1)} %get-tuple-element.105), channel_id=1, source_target_pairs={{0,0},{1,2},{2,4},{3,6},{4,1},{5,3},{6,5},{7,7},{8,8},{9,10},{10,1... | collective-permute-start | bytes 786440 | tf_op jit(solution)/shard_map/ppermute | solution.py:373
  138.8 140.2 %all-gather.14.cloned.1.call-start = ((), (), s32[]{:S(2)}) async-start(), calls=%async_computation.9 | async-start | bytes 3604480 | tf_op jit(solution)/shard_map/all_gather | solution.py:386
  184.0 16.1 %collective-permute-start.15 = (bf16[128,2048]{1,0:T(8,128)(2,1)}, bf16[128,2048]{1,0:T(8,128)(2,1)S(1)}, u32[]{:S(2)}, u32[]{:S(2)}) collective-permute-start(bf16[128,2048]{1,0:T(8,128)(2,1)} %get-tuple-element.93), channel_id=1, source_target_pairs={{0,6},{1,7},{2,4},{3,5},{4,2},{5,3},{6,0},{7,1},{8,14},{9,15},{10,... | collective-permute-start | bytes 1572872 | tf_op jit(solution)/shard_map/ppermute | solution.py:60
  186.8 24.4 %collective-permute-start.14 = (bf16[128,2048]{1,0:T(8,128)(2,1)}, bf16[128,2048]{1,0:T(8,128)(2,1)S(1)}, u32[]{:S(2)}, u32[]{:S(2)}) collective-permute-start(bf16[128,2048]{1,0:T(8,128)(2,1)} %get-tuple-element.94), channel_id=1, source_target_pairs={{0,4},{1,5},{2,6},{3,7},{4,0},{5,1},{6,2},{7,3},{8,12},{9,13},{10,... | collective-permute-start | bytes 1572872 | tf_op jit(solution)/shard_map/ppermute | solution.py:60
  186.8 24.9 %collective-permute-start.13 = (bf16[128,2048]{1,0:T(8,128)(2,1)}, bf16[128,2048]{1,0:T(8,128)(2,1)}, u32[]{:S(2)}, u32[]{:S(2)}) collective-permute-start(bf16[128,2048]{1,0:T(8,128)(2,1)} %get-tuple-element.92), channel_id=1, source_target_pairs={{0,2},{1,3},{2,0},{3,1},{4,6},{5,7},{6,4},{7,5},{8,10},{9,11},{10,... | collective-permute-start | bytes 1572872 | tf_op jit(solution)/shard_map/ppermute | solution.py:60
  187.5 35.0 %collective-permute-start.34 = (bf16[128,2048]{1,0:T(8,128)(2,1)}, bf16[128,2048]{1,0:T(8,128)(2,1)}, u32[]{:S(2)}, u32[]{:S(2)}) collective-permute-start(bf16[128,2048]{1,0:T(8,128)(2,1)} %param.28), channel_id=1, source_target_pairs={{0,6},{1,7},{2,4},{3,5},{4,2},{5,3},{6,0},{7,1},{8,14},{9,15},{10,... | collective-permute-start | bytes 1572872 | tf_op jit(solution)/shard_map/ppermute | solution.py:60
  190.3 43.5 %collective-permute-start.33 = (bf16[128,2048]{1,0:T(8,128)(2,1)}, bf16[128,2048]{1,0:T(8,128)(2,1)}, u32[]{:S(2)}, u32[]{:S(2)}) collective-permute-start(bf16[128,2048]{1,0:T(8,128)(2,1)} %param.28), channel_id=1, source_target_pairs={{0,4},{1,5},{2,6},{3,7},{4,0},{5,1},{6,2},{7,3},{8,12},{9,13},{10,... | collective-permute-start | bytes 1572872 | tf_op jit(solution)/shard_map/ppermute | solution.py:60
  191.2 272.6 %reduce-scatter.13.cloned.1.call-start = ((), (), s32[]{:S(2)}) async-start(), calls=%async_computation.12 | async-start | bytes 3604480 | tf_op jit(solution)/shard_map/reduce_scatter | solution.py:422
  200.1 34.0 %collective-permute-start.32 = (bf16[128,2048]{1,0:T(8,128)(2,1)}, bf16[128,2048]{1,0:T(8,128)(2,1)S(1)}, u32[]{:S(2)}, u32[]{:S(2)}) collective-permute-start(bf16[128,2048]{1,0:T(8,128)(2,1)} %param.28), channel_id=1, source_target_pairs={{0,2},{1,3},{2,0},{3,1},{4,6},{5,7},{6,4},{7,5},{8,10},{9,11},{10,... | collective-permute-start | bytes 1572872 | tf_op jit(solution)/shard_map/ppermute | solution.py:60
  214.4 30.4 %collective-permute-start.18 = (bf16[128,2048]{1,0:T(8,128)(2,1)S(1)}, bf16[128,2048]{1,0:T(8,128)(2,1)S(1)}, u32[]{:S(2)}, u32[]{:S(2)}) collective-permute-start(bf16[128,2048]{1,0:T(8,128)(2,1)S(1)} %multiply_convert_fusion.3), channel_id=1, source_target_pairs={{0,6},{1,7},{2,4},{3,5},{4,2},{5,3},{6,0},{7,1},{8,14},{9,15},{10,... | collective-permute-start | bytes 1572872 | tf_op jit(solution)/shard_map/ppermute | solution.py:60
  217.2 38.2 %collective-permute-start.17 = (bf16[128,2048]{1,0:T(8,128)(2,1)S(1)}, bf16[128,2048]{1,0:T(8,128)(2,1)S(1)}, u32[]{:S(2)}, u32[]{:S(2)}) collective-permute-start(bf16[128,2048]{1,0:T(8,128)(2,1)S(1)} %multiply_convert_fusion.3), channel_id=1, source_target_pairs={{0,4},{1,5},{2,6},{3,7},{4,0},{5,1},{6,2},{7,3},{8,12},{9,13},{10,... | collective-permute-start | bytes 1572872 | tf_op jit(solution)/shard_map/ppermute | solution.py:60
  222.5 33.3 %collective-permute-start.16 = (bf16[128,2048]{1,0:T(8,128)(2,1)S(1)}, bf16[128,2048]{1,0:T(8,128)(2,1)S(1)}, u32[]{:S(2)}, u32[]{:S(2)}) collective-permute-start(bf16[128,2048]{1,0:T(8,128)(2,1)S(1)} %multiply_convert_fusion.3), channel_id=1, source_target_pairs={{0,2},{1,3},{2,0},{3,1},{4,6},{5,7},{6,4},{7,5},{8,10},{9,11},{10,... | collective-permute-start | bytes 1572872 | tf_op jit(solution)/shard_map/ppermute | solution.py:60
  235.8 20.4 %collective-permute-start.35 = (bf16[4,128,2048]{2,1,0:T(8,128)(2,1)S(1)}, bf16[4,128,2048]{2,1,0:T(8,128)(2,1)S(1)}, u32[]{:S(2)}, u32[]{:S(2)}) collective-permute-start(bf16[4,128,2048]{2,1,0:T(8,128)(2,1)S(1)} %get-tuple-element.86), channel_id=1, source_target_pairs={{0,1},{1,0},{2,3},{3,2},{4,5},{5,4},{6,7},{7,6},{8,9},{9,8},{10,11... | collective-permute-start | bytes 6291464 | tf_op jit(solution)/shard_map/ppermute | solution.py:55
  295.4 170.8 %reduce-scatter.15.cloned.1.call-start = ((), (), s32[]{:S(2)}) async-start(), calls=%async_computation.13 | async-start | bytes 3604480 | tf_op jit(solution)/shard_map/reduce_scatter | solution.py:422
  310.1 12.8 %collective-permute-start.36 = (bf16[4,128,2048]{2,1,0:T(8,128)(2,1)}, bf16[4,128,2048]{2,1,0:T(8,128)(2,1)}, u32[]{:S(2)}, u32[]{:S(2)}) collective-permute-start(bf16[4,128,2048]{2,1,0:T(8,128)(2,1)} %fusion.8), channel_id=1, source_target_pairs={{0,1},{1,0},{2,3},{3,2},{4,5},{5,4},{6,7},{7,6},{8,9},{9,8},{10,11... | collective-permute-start | bytes 6291464 | tf_op jit(solution)/shard_map/ppermute | solution.py:55
  316.0 157.5 %reduce-scatter.17.cloned.1.call-start = ((), (), s32[]{:S(2)}) async-start(), calls=%async_computation.14 | async-start | bytes 3604480 | tf_op jit(solution)/shard_map/reduce_scatter | solution.py:430
  325.8 15.8 %collective-permute-start.39 = (bf16[128,2048]{1,0:T(8,128)(2,1)S(1)}, bf16[128,2048]{1,0:T(8,128)(2,1)S(1)}, u32[]{:S(2)}, u32[]{:S(2)}) collective-permute-start(bf16[128,2048]{1,0:T(8,128)(2,1)S(1)} %get-tuple-element.83), channel_id=1, source_target_pairs={{0,6},{1,7},{2,4},{3,5},{4,2},{5,3},{6,0},{7,1},{8,14},{9,15},{10,... | collective-permute-start | bytes 1572872 | tf_op jit(solution)/shard_map/ppermute | solution.py:60
  327.3 25.5 %collective-permute-start.38 = (bf16[128,2048]{1,0:T(8,128)(2,1)S(1)}, bf16[128,2048]{1,0:T(8,128)(2,1)S(1)}, u32[]{:S(2)}, u32[]{:S(2)}) collective-permute-start(bf16[128,2048]{1,0:T(8,128)(2,1)S(1)} %get-tuple-element.84), channel_id=1, source_target_pairs={{0,4},{1,5},{2,6},{3,7},{4,0},{5,1},{6,2},{7,3},{8,12},{9,13},{10,... | collective-permute-start | bytes 1572872 | tf_op jit(solution)/shard_map/ppermute | solution.py:60
  328.8 24.0 %collective-permute-start.37 = (bf16[128,2048]{1,0:T(8,128)(2,1)S(1)}, bf16[128,2048]{1,0:T(8,128)(2,1)S(1)}, u32[]{:S(2)}, u32[]{:S(2)}) collective-permute-start(bf16[128,2048]{1,0:T(8,128)(2,1)S(1)} %get-tuple-element.82), channel_id=1, source_target_pairs={{0,2},{1,3},{2,0},{3,1},{4,6},{5,7},{6,4},{7,5},{8,10},{9,11},{10,... | collective-permute-start | bytes 1572872 | tf_op jit(solution)/shard_map/ppermute | solution.py:60
  332.2 31.9 %collective-permute-start.31 = (bf16[128,2048]{1,0:T(8,128)(2,1)S(1)}, bf16[128,2048]{1,0:T(8,128)(2,1)S(1)}, u32[]{:S(2)}, u32[]{:S(2)}) collective-permute-start(bf16[128,2048]{1,0:T(8,128)(2,1)S(1)} %get-tuple-element.88), channel_id=1, source_target_pairs={{0,6},{1,7},{2,4},{3,5},{4,2},{5,3},{6,0},{7,1},{8,14},{9,15},{10,... | collective-permute-start | bytes 1572872 | tf_op jit(solution)/shard_map/ppermute | solution.py:60
  333.7 41.0 %collective-permute-start.30 = (bf16[128,2048]{1,0:T(8,128)(2,1)S(1)}, bf16[128,2048]{1,0:T(8,128)(2,1)S(1)}, u32[]{:S(2)}, u32[]{:S(2)}) collective-permute-start(bf16[128,2048]{1,0:T(8,128)(2,1)S(1)} %get-tuple-element.89), channel_id=1, source_target_pairs={{0,4},{1,5},{2,6},{3,7},{4,0},{5,1},{6,2},{7,3},{8,12},{9,13},{10,... | collective-permute-start | bytes 1572872 | tf_op jit(solution)/shard_map/ppermute | solution.py:60
  341.6 33.1 %collective-permute-start.29 = (bf16[128,2048]{1,0:T(8,128)(2,1)S(1)}, bf16[128,2048]{1,0:T(8,128)(2,1)S(1)}, u32[]{:S(2)}, u32[]{:S(2)}) collective-permute-start(bf16[128,2048]{1,0:T(8,128)(2,1)S(1)} %get-tuple-element.87), channel_id=1, source_target_pairs={{0,2},{1,3},{2,0},{3,1},{4,6},{5,7},{6,4},{7,5},{8,10},{9,11},{10,... | collective-permute-start | bytes 1572872 | tf_op jit(solution)/shard_map/ppermute | solution.py:60
  377.8 15.9 %collective-permute-start.42 = (bf16[128,2048]{1,0:T(8,128)(2,1)}, bf16[128,2048]{1,0:T(8,128)(2,1)S(1)}, u32[]{:S(2)}, u32[]{:S(2)}) collective-permute-start(bf16[128,2048]{1,0:T(8,128)(2,1)} %get-tuple-element.63), channel_id=1, source_target_pairs={{0,6},{1,7},{2,4},{3,5},{4,2},{5,3},{6,0},{7,1},{8,14},{9,15},{10,... | collective-permute-start | bytes 1572872 | tf_op jit(solution)/shard_map/ppermute | solution.py:60
  379.4 24.7 %collective-permute-start.41 = (bf16[128,2048]{1,0:T(8,128)(2,1)}, bf16[128,2048]{1,0:T(8,128)(2,1)S(1)}, u32[]{:S(2)}, u32[]{:S(2)}) collective-permute-start(bf16[128,2048]{1,0:T(8,128)(2,1)} %get-tuple-element.63), channel_id=1, source_target_pairs={{0,4},{1,5},{2,6},{3,7},{4,0},{5,1},{6,2},{7,3},{8,12},{9,13},{10,... | collective-permute-start | bytes 1572872 | tf_op jit(solution)/shard_map/ppermute | solution.py:60
  380.8 23.4 %collective-permute-start.40 = (bf16[128,2048]{1,0:T(8,128)(2,1)}, bf16[128,2048]{1,0:T(8,128)(2,1)}, u32[]{:S(2)}, u32[]{:S(2)}) collective-permute-start(bf16[128,2048]{1,0:T(8,128)(2,1)} %get-tuple-element.63), channel_id=1, source_target_pairs={{0,2},{1,3},{2,0},{3,1},{4,6},{5,7},{6,4},{7,5},{8,10},{9,11},{10,... | collective-permute-start | bytes 1572872 | tf_op jit(solution)/shard_map/ppermute | solution.py:60
  385.8 134.2 %reduce-scatter.11.cloned.1.call-start = ((), (), s32[]{:S(2)}) async-start(), calls=%async_computation.11 | async-start | bytes 1310720 | tf_op jit(solution)/shard_map/reduce_scatter | solution.py:459
  413.7 15.6 %collective-permute-start.53 = (bf16[64,2048]{1,0:T(8,128)(2,1)S(1)}, bf16[64,2048]{1,0:T(8,128)(2,1)S(1)}, u32[]{:S(2)}, u32[]{:S(2)}) collective-permute-start(bf16[64,2048]{1,0:T(8,128)(2,1)S(1)} %get-tuple-element.99), channel_id=1, source_target_pairs={{2,0},{4,1},{6,2},{0,3},{3,4},{5,5},{7,6},{1,7},{10,8},{12,9},{14,... | collective-permute-start | bytes 786440 | tf_op jit(solution)/shard_map/ppermute | solution.py:457
  419.1 13.6 %collective-permute-start.54 = (bf16[64,2048]{1,0:T(8,128)(2,1)S(1)}, bf16[64,2048]{1,0:T(8,128)(2,1)S(1)}, u32[]{:S(2)}, u32[]{:S(2)}) collective-permute-start(bf16[64,2048]{1,0:T(8,128)(2,1)S(1)} %get-tuple-element.98), channel_id=1, source_target_pairs={{4,0},{6,1},{0,2},{2,3},{5,4},{7,5},{1,6},{3,7},{12,8},{14,9},{8,1... | collective-permute-start | bytes 786440 | tf_op jit(solution)/shard_map/ppermute | solution.py:457
  419.2 14.2 %collective-permute-start.55 = (bf16[64,2048]{1,0:T(8,128)(2,1)S(1)}, bf16[64,2048]{1,0:T(8,128)(2,1)S(1)}, u32[]{:S(2)}, u32[]{:S(2)}) collective-permute-start(bf16[64,2048]{1,0:T(8,128)(2,1)S(1)} %get-tuple-element.97), channel_id=1, source_target_pairs={{6,0},{0,1},{2,2},{4,3},{7,4},{1,5},{3,6},{5,7},{14,8},{8,9},{10,1... | collective-permute-start | bytes 786440 | tf_op jit(solution)/shard_map/ppermute | solution.py:457
  434.2 111.8 %reduce-scatter.9.cloned.1.call-start = ((), (), s32[]{:S(2)}) async-start(), calls=%async_computation.10 | async-start | bytes 1966080 | tf_op jit(solution)/shard_map/reduce_scatter | solution.py:463
  458.9 50.4 %collective-permute-start.44 = (bf16[4,128,2048]{2,1,0:T(8,128)(2,1)}, bf16[4,128,2048]{2,1,0:T(8,128)(2,1)}, u32[]{:S(2)}, u32[]{:S(2)}) collective-permute-start(bf16[4,128,2048]{2,1,0:T(8,128)(2,1)} %fusion.9), channel_id=1, source_target_pairs={{0,1},{1,0},{2,3},{3,2},{4,5},{5,4},{6,7},{7,6},{8,9},{9,8},{10,11... | collective-permute-start | bytes 6291464 | tf_op jit(solution)/shard_map/ppermute | solution.py:55
  463.8 214.4 %reduce-scatter.19.cloned.1.call-start = ((), (), s32[]{:S(2)}) async-start(), calls=%async_computation.16 | async-start | bytes 1081344
  471.1 11.6 %collective-permute-start.57 = (bf16[2,64,704]{2,1,0:T(8,128)(2,1)S(1)}, bf16[2,64,704]{2,1,0:T(8,128)(2,1)S(1)}, u32[]{:S(2)}, u32[]{:S(2)}) collective-permute-start(bf16[2,64,704]{2,1,0:T(8,128)(2,1)S(1)} %get-tuple-element.113), channel_id=1, source_target_pairs={{0,2},{1,3},{2,0},{3,1},{4,6},{5,7},{6,4},{7,5},{8,10},{9,11},{10,... | collective-permute-start | bytes 540680 | tf_op jit(solution)/shard_map/ppermute | solution.py:60
  516.5 16.0 %collective-permute-start.47 = (bf16[128,2048]{1,0:T(8,128)(2,1)}, bf16[128,2048]{1,0:T(8,128)(2,1)S(1)}, u32[]{:S(2)}, u32[]{:S(2)}) collective-permute-start(bf16[128,2048]{1,0:T(8,128)(2,1)} %get-tuple-element.78), channel_id=1, source_target_pairs={{0,6},{1,7},{2,4},{3,5},{4,2},{5,3},{6,0},{7,1},{8,14},{9,15},{10,... | collective-permute-start | bytes 1572872 | tf_op jit(solution)/shard_map/ppermute | solution.py:60
  517.0 24.6 %collective-permute-start.46 = (bf16[128,2048]{1,0:T(8,128)(2,1)}, bf16[128,2048]{1,0:T(8,128)(2,1)S(1)}, u32[]{:S(2)}, u32[]{:S(2)}) collective-permute-start(bf16[128,2048]{1,0:T(8,128)(2,1)} %get-tuple-element.79), channel_id=1, source_target_pairs={{0,4},{1,5},{2,6},{3,7},{4,0},{5,1},{6,2},{7,3},{8,12},{9,13},{10,... | collective-permute-start | bytes 1572872 | tf_op jit(solution)/shard_map/ppermute | solution.py:60
  518.6 23.1 %collective-permute-start.45 = (bf16[128,2048]{1,0:T(8,128)(2,1)}, bf16[128,2048]{1,0:T(8,128)(2,1)S(1)}, u32[]{:S(2)}, u32[]{:S(2)}) collective-permute-start(bf16[128,2048]{1,0:T(8,128)(2,1)} %get-tuple-element.77), channel_id=1, source_target_pairs={{0,2},{1,3},{2,0},{3,1},{4,6},{5,7},{6,4},{7,5},{8,10},{9,11},{10,... | collective-permute-start | bytes 1572872 | tf_op jit(solution)/shard_map/ppermute | solution.py:60
  552.5 126.5 %collective-permute-start.48 = (bf16[4,64,384]{2,1,0:T(8,128)(2,1)S(1)}, bf16[4,64,384]{2,1,0:T(8,128)(2,1)S(1)}, u32[]{:S(2)}, u32[]{:S(2)}) collective-permute-start(bf16[4,64,384]{2,1,0:T(8,128)(2,1)S(1)} %get-tuple-element.144), channel_id=1, source_target_pairs={{0,1},{1,0},{2,3},{3,2},{4,5},{5,4},{6,7},{7,6},{8,9},{9,8},{10,11... | collective-permute-start | bytes 589832 | tf_op jit(solution)/shard_map/ppermute | solution.py:55
  (79 other events, 913.5 us)
Sparse Core Ops, SparseCore 0:
  13.9 30.3 all-gather.15
  46.4 36.5 all-gather.7
  85.2 62.3 all-gather.9
  149.6 62.1 all-gather.11
  213.8 57.8 all-gather.13
  295.6 53.4 reduce-scatter.12
  351.4 56.0 reduce-scatter.14
  409.7 56.0 reduce-scatter.16
  468.1 26.9 reduce-scatter.10
  497.4 33.9 reduce-scatter.8
  546.0 132.1 reduce-scatter.18

commit v2 on v1

v2 whole, which is shorter than its diff:
```python
import functools
import math

import jax
import jax.numpy as jnp
from jax import lax
from jax.experimental import pallas as pl
from jax.experimental.pallas import tpu as pltpu
from jax.sharding import PartitionSpec as P

HEADS = 32
KV_HEADS = 4
HEAD_DIM = 64
STEP = 3

NORM_EPS = 1e-05
ROPE_BASE = 10000.0
BETA = 0.5
ADAM_EPS = 1e-08
DECAY = 0.1
MASKED = -1e30
PAIR = 2 * HEAD_DIM
BF16 = jnp.bfloat16
F32 = jnp.float32


def matmul(left, right):
    return jnp.dot(left, right, preferred_element_type=F32)


def matmul_tn(left, right):
    return lax.dot_general(left, right, (((0,), (0,)), ((), ())), preferred_element_type=F32)


def matmul_nt(left, right):
    return lax.dot_general(left, right, (((1,), (1,)), ((), ())), preferred_element_type=F32)


def rms_scale(values):
    return lax.rsqrt(jnp.mean(values * values, -1, keepdims=True) + NORM_EPS)


def adam_step(master, first_moment, second_moment, gradient, rate):
    first_new = BETA * first_moment + (1.0 - BETA) * gradient
    second_new = BETA * second_moment + (1.0 - BETA) * gradient * gradient
    correction = 1.0 - BETA**STEP
    master_new = master - rate * (
        first_new / correction / (jnp.sqrt(second_new / correction) + ADAM_EPS) + DECAY * master
    )
    return (master_new, first_new, second_new)


def core_swap(value):
    members = lax.axis_size("fsdp")
    return lax.ppermute(value, "fsdp", [(i, i ^ 1) for i in range(members)])


def chip_send(value, step):
    members = lax.axis_size("fsdp")
    return lax.ppermute(value, "fsdp", [(i, i ^ (2 * step)) for i in range(members)])


def plane_send(value, step):
    planes = lax.axis_size("dp")
    return lax.ppermute(value, "dp", [(i, i ^ step) for i in range(planes)])


def gather(own, send, count):
    return [own] + [send(own, step) for step in range(1, count)]


def gather_line(own, send, count):
    got = {0: own}
    bit = count // 2
    while bit:
        for step in sorted(got):
            got[step + bit] = send(got[step], bit)
        bit //= 2
    return [got[step] for step in range(count)]


def gather_cores(own, send, count):
    blocks = []
    for block in send(own, count):
        blocks += [block, core_swap(block)]
    return blocks


def scatter_cores(mine, other, send):
    total = None
    for step in list(range(1, len(mine))) + [0]:
        part = mine[step] + core_swap(other[step]).astype(F32)
        if step:
            part = send(part.astype(BF16), step).astype(F32)
        total = part if total is None else total + part
    return total


def scatter_sum(parts, send):
    total = parts[0].astype(F32)
    for step in range(1, len(parts)):
        total = total + send(parts[step], step).astype(F32)
    return total


def exchange(mine, other, send):
    got = core_swap(other)
    pairs = [jnp.stack([mine[step], got[step]]) for step in range(mine.shape[0])]
    return pairs[:1] + [send(pairs[step], step) for step in range(1, len(pairs))]


def by_offset(blocks, index):
    count = blocks.shape[0]
    return jnp.stack(
        [lax.dynamic_index_in_dim(blocks, j ^ index, 0, keepdims=False) for j in range(count)]
    )


def lane_ids(shape):
    return lax.broadcasted_iota(jnp.int32, shape, len(shape) - 1)


def turn(values, cosine, sine):
    low_half = lane_ids(values.shape) % HEAD_DIM < HEAD_DIM // 2
    shifted = jnp.where(
        low_half,
        pltpu.roll(values, PAIR - HEAD_DIM // 2, 1),
        pltpu.roll(values, HEAD_DIM // 2, 1),
    )
    return values * cosine + shifted * sine


VMEM = pl.BlockSpec(memory_space=pltpu.VMEM)
SMEM = pl.BlockSpec(memory_space=pltpu.SMEM)
ANY = pl.BlockSpec(memory_space=pl.ANY)


def params(mib=56):
    return pltpu.CompilerParams(vmem_limit_bytes=mib * 2**20)


def shape_of(shape, dtype=BF16):
    return jax.ShapeDtypeStruct(shape, dtype)


def cost(flops, moved, exps=0):
    return pl.CostEstimate(flops=int(flops), bytes_accessed=int(moved), transcendentals=int(exps))


def pack_kernel(planes, chips, piece, place, gate, up, query, key, value, gu_mine, gu_other, qkv_mine, qkv_other):
    plane, chip, core = place[0], place[1], place[2]
    own_q = query.shape[1] // (2 * chips)
    sharing = 2 * chips // KV_HEADS

    def put(mine, other, core_to, index, block):
        @pl.when(core == core_to)
        def _():
            mine[index] = block

        @pl.when(core != core_to)
        def _():
            other[index] = block

    for to in range(2 * chips):
        head = slice(to // sharing * HEAD_DIM, (to // sharing + 1) * HEAD_DIM)
        block = jnp.concatenate(
            [query[:, to * own_q : (to + 1) * own_q], key[:, head], value[:, head]], 1
        )
        put(qkv_mine, qkv_other, to % 2, (to // 2) ^ chip, block.astype(BF16))
    for side, weight in enumerate((gate, up)):
        for to in range(2 * planes):
            starts = [((to // 2 * chips + c) * 2 + to % 2) * piece for c in range(chips)]
            block = jnp.concatenate([weight[:, s : s + piece] for s in starts], 1).astype(BF16)
            put(
                gu_mine.at[:, side],
                gu_other.at[:, side],
                to % 2,
                (to // 2) ^ plane,
                block,
            )


def pack(place, planes, chips, gate, up, query, key, value):
    rows, hidden = gate.shape
    gu = shape_of((planes, 2, rows, hidden // (2 * planes)))
    qkv = shape_of((chips, rows, query.shape[1] // (2 * chips) + PAIR))
    return pl.pallas_call(
        functools.partial(pack_kernel, planes, chips, hidden // (2 * planes * chips)),
        out_shape=(gu, gu, qkv, qkv),
        in_specs=[SMEM] + [VMEM] * 5,
        out_specs=(VMEM,) * 4,
        compiler_params=params(),
        cost_estimate=cost(0, rows * hidden * 12),
        name="pack",
    )(place, gate, up, query, key, value)


def gather_rows_kernel(members, place, *refs):
    blocks, out = refs[:-1], refs[-1]
    first, core = place[0], place[1]
    rows = blocks[0].shape[-2]
    for step, block in enumerate(blocks):
        for side in range(2):
            at = ((first ^ step) * 2 + (core ^ side)) * rows
            if len(block.shape) == 3:
                out[pl.ds(pl.multiple_of(at, 16), rows), :] = block[side]
            else:
                for part in range(2):
                    out[part, pl.ds(pl.multiple_of(at, 16), rows), :] = block[side, part]


def gather_rows(first, core, pairs):
    lead, (rows, width) = pairs[0].shape[1:-2], pairs[0].shape[-2:]
    return pl.pallas_call(
        functools.partial(gather_rows_kernel, 2 * len(pairs)),
        out_shape=shape_of(lead + (2 * len(pairs) * rows, width)),
        in_specs=[SMEM] + [VMEM] * len(pairs),
        out_specs=VMEM,
        compiler_params=params(),
        cost_estimate=cost(0, pairs[0].size * len(pairs) * 4),
        name="gather_rows",
    )(jnp.stack([first, core]), *pairs)


def spread_rows_kernel(place, whole, mine, other):
    first, core = place[0], place[1]
    count = mine.shape[0]
    rows = mine.shape[-2]
    for step in range(count):
        for side, out in enumerate((mine, other)):
            at = pl.ds(pl.multiple_of(((first ^ step) * 2 + (core ^ side)) * rows, 16), rows)
            if len(whole.shape) == 2:
                out[step] = whole[at, :].astype(BF16)
            else:
                for part in range(2):
                    out[step, part] = whole[part, at, :].astype(BF16)


def spread_rows(first, core, whole, count):
    rows = whole.shape[-2] // (2 * count)
    out = shape_of((count,) + whole.shape[:-2] + (rows, whole.shape[-1]))
    return pl.pallas_call(
        spread_rows_kernel,
        out_shape=(out, out),
        in_specs=[SMEM, VMEM],
        out_specs=(VMEM, VMEM),
        compiler_params=params(),
        cost_estimate=cost(0, whole.size * 6),
        name="spread_rows",
    )(jnp.stack([first, core]), whole)


def attend_kernel(members, pairs, planes, place, start_ref, cos_ref, sin_ref, gain_ref, *refs):
    tokens, refs = refs[:members], refs[members:]
    weights, refs = refs[:planes], refs[planes:]
    normed_ref, q_ref, kv_ref, o_ref = refs
    plane, index = place[0], place[1]
    rows = tokens[0].shape[0]
    length = rows * members
    even = lane_ids((rows, PAIR)) < HEAD_DIM
    depth = weights[0].shape[0]
    for j in range(members):
        values = tokens[j][...].astype(F32)
        normed = values * rms_scale(values) * gain_ref[...]
        normed_ref[j * rows : (j + 1) * rows, :] = normed.astype(BF16)
    block = min(2 * rows, 256)
    per = block // rows
    for first in range(0, length, block):
        qkv = None
        for step in range(planes):
            columns = pl.ds(pl.multiple_of((plane ^ step) * depth, 128), depth)
            term = matmul(normed_ref[first : first + block, columns], weights[step][...])
            qkv = term if qkv is None else qkv + term
        for part in range(per):
            j = first // rows + part
            here = pl.ds(pl.multiple_of((j ^ index) * rows, rows), rows)
            cosine = cos_ref[here, :]
            sine = sin_ref[here, :]
            piece = qkv[part * rows : (part + 1) * rows, :]
            for pair in range(pairs):
                lanes = slice(pair * PAIR, (pair + 1) * PAIR)
                turned = turn(piece[:, lanes], cosine, sine).astype(BF16).astype(F32)
                q_ref[here, lanes] = (turned * HEAD_DIM**-0.5).astype(BF16)
            both = piece[:, pairs * PAIR :]
            kv_ref[here, :] = jnp.where(even, turn(both, cosine, sine), both).astype(BF16)
    for first in range(0, length, block):
        reach = first + block
        both = kv_ref[:reach, :].astype(F32)
        left = lane_ids(both.shape) < HEAD_DIM
        keys_even = jnp.where(left, both, 0.0)
        values_odd = jnp.where(left, 0.0, both)
        keys = (keys_even.astype(BF16), pltpu.roll(keys_even, HEAD_DIM, 1).astype(BF16))
        values = (pltpu.roll(values_odd, HEAD_DIM, 1).astype(BF16), values_odd.astype(BF16))
        query_at = first + lax.broadcasted_iota(jnp.int32, (block, reach), 0)
        key_at = lax.broadcasted_iota(jnp.int32, (block, reach), 1)
        allowed = (key_at <= query_at) & (key_at >= start_ref[first:reach, :])
        for pair in range(pairs):
            lanes = slice(pair * PAIR, (pair + 1) * PAIR)
            query = q_ref[first:reach, lanes]
            mixed = jnp.zeros((block, PAIR), F32)
            for side in range(2):
                scores = jnp.where(allowed, matmul_nt(query, keys[side]), MASKED)
                raised = jnp.exp(scores - jnp.max(scores, -1, keepdims=True))
                probs = raised * (1.0 / jnp.sum(raised, -1, keepdims=True))
                mixed = mixed + matmul(probs.astype(BF16), values[side])
            mixed = mixed.astype(BF16)
            for part in range(per):
                j = first // rows + part
                there = pl.ds(pl.multiple_of((j ^ index) * rows, rows), rows)
                o_ref[there, lanes] = mixed[part * rows : (part + 1) * rows, :]


def attend(place, tokens, weights, gain, start, cosine, sine):
    members, planes = len(tokens), len(weights)
    rows, width = tokens[0].shape
    length = members * rows
    pairs = weights[0].shape[1] // PAIR - 1
    return pl.pallas_call(
        functools.partial(attend_kernel, members, pairs, planes),
        out_shape=(
            shape_of((length, width)),
            shape_of((length, pairs * PAIR)),
            shape_of((length, PAIR)),
            shape_of((length, pairs * PAIR)),
        ),
        in_specs=[SMEM] + [VMEM] * (4 + members + planes),
        out_specs=(VMEM,) * 4,
        compiler_params=params(),
        cost_estimate=cost(
            2 * length * width * (pairs + 1) * PAIR + 3 * length * length * pairs * PAIR,
            length * width * 4,
            length * length * pairs,
        ),
        name="attend",
    )(place, start, cosine, sine, gain, *tokens, *weights)


def attend_back_kernel(members, pairs, place, start_ref, cos_ref, sin_ref, q_ref, kv_ref, w_ref, *refs):
    grads, refs = refs[:members], refs[members:]
    out_ref, do_ref, dk_ref, dv_ref = refs
    length = q_ref.shape[0]
    rows = length // members
    index = place[1]
    block = min(2 * rows, 256)
    per = block // rows
    for j in range(0, members, 2):
        grad = jnp.concatenate([grads[j][...], grads[j + 1][...]], 0)
        do_ref[j * rows : (j + 2) * rows, :] = matmul_nt(grad, w_ref[...]).astype(BF16)
    dk_ref[...] = jnp.zeros_like(dk_ref)
    dv_ref[...] = jnp.zeros_like(dv_ref)
    for first in range(0, length, block):
        reach = first + block
        both = kv_ref[:reach, :].astype(F32)
        left = lane_ids(both.shape) < HEAD_DIM
        keys_even = jnp.where(left, both, 0.0)
        values_odd = jnp.where(left, 0.0, both)
        keys = (keys_even.astype(BF16), pltpu.roll(keys_even, HEAD_DIM, 1).astype(BF16))
        values = (pltpu.roll(values_odd, HEAD_DIM, 1).astype(BF16), values_odd.astype(BF16))
        key_at = lax.broadcasted_iota(jnp.int32, (reach, block), 0)
        query_at = first + lax.broadcasted_iota(jnp.int32, (reach, block), 1)
        allowed = (key_at <= query_at) & (key_at >= start_ref[:, first:reach])
        half = lane_ids((block, PAIR)) < HEAD_DIM
        theres = [
            pl.ds(pl.multiple_of(((first // rows + part) ^ index) * rows, rows), rows)
            for part in range(per)
        ]
        for pair in range(pairs):
            lanes = slice(pair * PAIR, (pair + 1) * PAIR)
            query = q_ref[first:reach, lanes]
            grad = jnp.concatenate([do_ref[there, lanes] for there in theres], 0)
            dq = jnp.zeros((block, PAIR), F32)
            for side in range(2):
                keep = half if side == 0 else ~half
                query_side = jnp.where(keep, query.astype(F32), 0.0).astype(BF16)
                grad_side = jnp.where(keep, grad.astype(F32), 0.0).astype(BF16)
                scores = jnp.where(allowed, matmul_nt(keys[side], query), MASKED)
                raised = jnp.exp(scores - jnp.max(scores, 0, keepdims=True))
                probs = raised * (1.0 / jnp.sum(raised, 0, keepdims=True))
                dp = matmul_nt(values[side], grad)
                centre = jnp.sum(probs * dp, 0, keepdims=True)
                ds = (probs * (dp - centre)).astype(BF16)
                dv_ref[:reach, :] += matmul(probs.astype(BF16), grad_side)
                dk_ref[:reach, :] += matmul(ds, query_side)
                dq = dq + matmul_tn(ds, keys[side])
            dq = dq * HEAD_DIM**-0.5
            for part in range(per):
                piece = dq[part * rows : (part + 1) * rows, :]
                here = slice(first + part * rows, first + (part + 1) * rows)
                out_ref[theres[part], lanes] = turn(
                    piece, cos_ref[here, :], -sin_ref[here, :]
                ).astype(BF16)
    left = lane_ids((rows, PAIR)) < HEAD_DIM
    for j in range(members):
        here = slice(j * rows, (j + 1) * rows)
        there = pl.ds(pl.multiple_of((j ^ index) * rows, rows), rows)
        dk = dk_ref[here, :]
        dv = dv_ref[here, :]
        dk = turn(dk + pltpu.roll(dk, HEAD_DIM, 1), cos_ref[here, :], -sin_ref[here, :])
        dv = dv + pltpu.roll(dv, HEAD_DIM, 1)
        out_ref[there, pairs * PAIR :] = jnp.where(left, dk, dv).astype(BF16)


def attend_back(place, queries, keys_values, w_output, grads, start, cosine, sine):
    length, width = queries.shape
    pairs = width // PAIR
    members = len(grads)
    model = grads[0].shape[1]
    return pl.pallas_call(
        functools.partial(attend_back_kernel, members, pairs),
        out_shape=shape_of((length, width + PAIR)),
        in_specs=[SMEM] + [VMEM] * (6 + members),
        out_specs=VMEM,
        scratch_shapes=[
            pltpu.VMEM((length, width), BF16),
            pltpu.VMEM((length, PAIR), F32),
            pltpu.VMEM((length, PAIR), F32),
        ],
        compiler_params=params(),
        cost_estimate=cost(
            2 * length * width * model + 7 * length * length * width,
            length * model * 2,
            length * length * pairs,
        ),
        name="attend_back",
    )(place, start, cosine, sine, queries, keys_values, w_output, *grads)


def project_kernel(count, left_ref, weight_ref, *outs):
    rows = left_ref.shape[0] // (2 * count)
    for step in range(count):
        whole = matmul(left_ref[2 * step * rows : 2 * (step + 1) * rows, :], weight_ref[...])
        outs[step][...] = whole[:rows, :]
        outs[count + step][...] = whole[rows:, :].astype(BF16)


def project(left, weight, count):
    rows, width = left.shape[0] // (2 * count), weight.shape[1]
    outs = pl.pallas_call(
        functools.partial(project_kernel, count),
        out_shape=(shape_of((rows, width), F32),) * count + (shape_of((rows, width)),) * count,
        in_specs=[VMEM, VMEM],
        out_specs=(VMEM,) * (2 * count),
        compiler_params=params(),
        cost_estimate=cost(2 * left.size * width, left.shape[0] * width * 3),
        name="project",
    )(left, weight)
    return outs[:count], outs[count:]


def project_back_kernel(planes, count, place, left_ref, *refs):
    weights, outs = refs[:planes], refs[planes:]
    rows = left_ref.shape[0] // (2 * count)
    depth = weights[0].shape[0]
    for step in range(count):
        left = left_ref[2 * step * rows : 2 * (step + 1) * rows, :]
        for far in range(planes):
            columns = pl.ds(pl.multiple_of((place[0] ^ far) * depth, 128), depth)
            whole = matmul_nt(left, weights[far][...])
            outs[step][:, columns] = whole[:rows, :]
            outs[count + step][:, columns] = whole[rows:, :].astype(BF16)


def project_back(place, left, weights, count):
    rows, planes = left.shape[0] // (2 * count), len(weights)
    width = weights[0].shape[0] * planes
    outs = pl.pallas_call(
        functools.partial(project_back_kernel, planes, count),
        out_shape=(shape_of((rows, width), F32),) * count + (shape_of((rows, width)),) * count,
        in_specs=[SMEM] + [VMEM] * (1 + planes),
        out_specs=(VMEM,) * (2 * count),
        compiler_params=params(),
        cost_estimate=cost(2 * left.size * width, left.shape[0] * width * 3),
        name="project_back",
    )(place, left, *weights)
    return outs[:count], outs[count:]


def qkv_grad_kernel(place, normed_ref, grad_ref, *outs):
    depth = outs[0].shape[0]
    for far, out in enumerate(outs):
        columns = pl.ds(pl.multiple_of((place[0] ^ far) * depth, 128), depth)
        out[...] = matmul_tn(normed_ref[:, columns], grad_ref[...]).astype(BF16)


def qkv_grad(place, normed, grad, planes):
    depth, width = normed.shape[1] // planes, grad.shape[1]
    return pl.pallas_call(
        qkv_grad_kernel,
        out_shape=(shape_of((depth, width)),) * planes,
        in_specs=[SMEM, VMEM, VMEM],
        out_specs=(VMEM,) * planes,
        compiler_params=params(),
        cost_estimate=cost(2 * normed.size * width, normed.size * 2),
        name="qkv_grad",
    )(place, normed, grad)


def rows_grad_kernel(count, left_ref, *refs):
    grads, out = refs[:-1], refs[-1]
    left = left_ref[...]
    width = out.shape[1]
    block = 512
    for first in range(0, width, block):
        columns = slice(first, first + block)
        right = jnp.concatenate([grad[:, columns] for grad in grads], 0)
        out[:, columns] = matmul_tn(left, right).astype(BF16)


def rows_grad(left, grads):
    return pl.pallas_call(
        functools.partial(rows_grad_kernel, len(grads)),
        out_shape=shape_of((left.shape[1], grads[0].shape[1])),
        in_specs=[VMEM] * (1 + len(grads)),
        out_specs=VMEM,
        compiler_params=params(),
        cost_estimate=cost(2 * left.size * grads[0].shape[1], left.size * 2),
        name="rows_grad",
    )(left, *grads)


def weight_copies(planes, chips, gu_ref, gu, sem):
    rows = gu.shape[1] // (planes * chips)
    return [
        pltpu.make_async_copy(
            gu_ref.at[chip, side, pl.ds(plane * rows, rows), :],
            gu.at[side, pl.ds((plane * chips + chip) * rows, rows), :],
            sem.at[side],
        )
        for side in range(2)
        for chip in range(chips)
        for plane in range(planes)
    ]


def feed_kernel(planes, chips, x_mine, x_other, g_mine, g_other, gu_ref, down_ref, *refs):
    (hidden_ref, gate_ref, up_ref, out_mine, out_other, dx_mine, dx_other, gu, down, sem) = refs
    rows = x_mine.shape[0]
    copies = weight_copies(planes, chips, gu_ref, gu, sem)
    down_copy = pltpu.make_async_copy(down_ref, down, sem.at[2])
    half = len(copies) // 2
    for copy in copies:
        copy.start()
    down_copy.start()
    x = jnp.concatenate([x_mine[...], x_other[...]], 0)
    grad = jnp.concatenate([g_mine[...], g_other[...]], 0)
    for copy in copies[:half]:
        copy.wait()
    gate = matmul(x, gu[0])
    for copy in copies[half:]:
        copy.wait()
    up = matmul(x, gu[1])
    down_copy.wait()
    dhidden = matmul_nt(grad, down[...])
    sigmoid = 1.0 / (1.0 + jnp.exp(-gate))
    hidden = (gate * sigmoid * up).astype(BF16)
    dgate = (dhidden * up * sigmoid * (1.0 + gate * (1.0 - sigmoid))).astype(BF16)
    dup = (dhidden * gate * sigmoid).astype(BF16)
    hidden_ref[...] = hidden
    gate_ref[...] = dgate
    up_ref[...] = dup
    block = 512
    for first in range(0, x.shape[1], block):
        columns = slice(first, first + block)
        dx = matmul_nt(dgate, gu[0, columns, :]) + matmul_nt(dup, gu[1, columns, :])
        dx_mine[:, columns] = dx[:rows, :]
        dx_other[:, columns] = dx[rows:, :].astype(BF16)
    for first in range(0, x.shape[1], block):
        columns = slice(first, first + block)
        out = matmul(hidden, down[:, columns])
        out_mine[:, columns] = out[:rows, :]
        out_other[:, columns] = out[rows:, :].astype(BF16)


def feed(planes, chips, x, grad, w_gate_up, w_down):
    rows, width = x[0].shape
    units = w_down.shape[0]
    part = shape_of((2 * rows, units))
    return pl.pallas_call(
        functools.partial(feed_kernel, planes, chips),
        out_shape=(part,) * 3 + (shape_of((rows, width), F32), shape_of((rows, width))) * 2,
        in_specs=[VMEM] * 4 + [ANY] * 2,
        out_specs=(VMEM,) * 7,
        scratch_shapes=[
            pltpu.VMEM((2, width, units), BF16),
            pltpu.VMEM((units, width), BF16),
            pltpu.SemaphoreType.DMA((3,)),
        ],
        compiler_params=params(),
        cost_estimate=cost(24 * rows * width * units, 6 * width * units, 2 * rows * units),
        name="feed",
    )(*x, *grad, w_gate_up, w_down)


def feed_grad_kernel(planes, chips, count, *refs):
    x, refs = refs[:count], refs[count:]
    gates, refs = refs[: count // 2], refs[count // 2 :]
    ups, refs = refs[: count // 2], refs[count // 2 :]
    out, held, sem = refs
    width = held.shape[1]
    block = 256
    rows = width // (planes * chips)
    copies = []
    dgate = jnp.concatenate([gate[...] for gate in gates], 0)
    dup = jnp.concatenate([up[...] for up in ups], 0)
    for first in range(0, width, block):
        columns = slice(first, first + block)
        left = jnp.concatenate([part[:, columns] for part in x], 0)
        held[0, columns, :] = matmul_tn(left, dgate).astype(BF16)
        held[1, columns, :] = matmul_tn(left, dup).astype(BF16)
        for at in range(first // rows, (first + block) // rows):
            for side in range(2):
                copy = pltpu.make_async_copy(
                    held.at[side, pl.ds(at * rows, rows), :],
                    out.at[at % chips, side, pl.ds(at // chips * rows, rows), :],
                    sem,
                )
                copy.start()
                copies.append(copy)
    for copy in copies:
        copy.wait()


def feed_grad(planes, chips, x, gates, ups):
    width, units = x[0].shape[1], gates[0].shape[1]
    tokens = x[0].shape[0] * len(x)
    return pl.pallas_call(
        functools.partial(feed_grad_kernel, planes, chips, len(x)),
        out_shape=shape_of((chips, 2, width // chips, units)),
        in_specs=[VMEM] * (len(x) + len(gates) + len(ups)),
        out_specs=ANY,
        scratch_shapes=[pltpu.VMEM((2, width, units), BF16), pltpu.SemaphoreType.DMA],
        compiler_params=params(),
        cost_estimate=cost(4 * tokens * width * units, 4 * width * units),
        name="feed_grad",
    )(*x, *gates, *ups)


def feed_adam_kernel(planes, chips, piece, place, *refs):
    blocks, refs = refs[:planes], refs[planes:]
    ins, outs = refs[:6], refs[6:12]
    held = refs[12]
    plane, core = place[0], place[2]
    for step in range(planes):
        for side in range(2):
            held[plane ^ step, core ^ side] = blocks[step][side].astype(F32)
    for part in range(2):
        w, m, u = ins[3 * part : 3 * part + 3]
        new = outs[3 * part : 3 * part + 3]
        for to in range(2 * planes):
            grad_block = held[to // 2, to % 2, part]
            for c in range(chips):
                at = ((to // 2 * chips + c) * 2 + to % 2) * piece
                columns = slice(at, at + piece)
                grad = grad_block[:, c * piece : (c + 1) * piece]
                updated = adam_step(w[:, columns], m[:, columns], u[:, columns], grad, 0.02)
                for out, value in zip(new, updated):
                    out[:, columns] = value


def feed_adam(place, planes, chips, blocks, arrays):
    rows, hidden = arrays[0].shape
    piece = hidden // (2 * planes * chips)
    tile = min(rows, 16)
    whole = pl.BlockSpec((tile, hidden), lambda i: (i, 0))
    block = pl.BlockSpec((2, 2, tile, piece * chips), lambda i: (0, 0, i, 0))
    return pl.pallas_call(
        functools.partial(feed_adam_kernel, planes, chips, piece),
        grid=(rows // tile,),
        out_shape=(shape_of((rows, hidden), F32),) * 6,
        in_specs=[SMEM] + [block] * planes + [whole] * 6,
        out_specs=(whole,) * 6,
        scratch_shapes=[pltpu.VMEM((planes, 2, 2, tile, piece * chips), F32)],
        compiler_params=params(),
        cost_estimate=cost(40 * rows * hidden, 52 * rows * hidden),
        name="feed_adam",
    )(place, *blocks, *arrays)


def segment_starts(lengths_row, length):
    count = lengths_row.shape[0]
    ahead = jnp.arange(count)[:, None] < jnp.arange(count)[None, :]
    starts = jnp.sum(jnp.where(ahead, lengths_row[:, None], 0), 0, dtype=jnp.int32)
    ends = starts + lengths_row
    places = jnp.arange(length, dtype=jnp.int32)
    within = (places[:, None] >= starts[None, :]) & (places[:, None] < ends[None, :])
    return jnp.sum(jnp.where(within, starts[None, :], 0), 1, dtype=jnp.int32)


def rope_tables(positions):
    half = HEAD_DIM // 2
    freqs = jnp.exp(jnp.arange(half, dtype=F32) * (-2.0 * math.log(ROPE_BASE) / HEAD_DIM))
    angles = positions.astype(F32)[:, None] * freqs[None, :]
    cosine = jnp.cos(angles)
    sine = jnp.sin(angles)
    return (
        jnp.concatenate([cosine] * 4, 1),
        jnp.concatenate([-sine, sine, -sine, sine], 1),
    )


def local(
    tokens,
    out_grad,
    seq_lengths,
    query_weight,
    query_first,
    query_second,
    key_weight,
    key_first,
    key_second,
    value_weight,
    value_first,
    value_second,
    output_weight,
    output_first,
    output_second,
    gate_weight,
    gate_first,
    gate_second,
    up_weight,
    up_first,
    up_second,
    down_weight,
    down_first,
    down_second,
    norm_gains,
    gains_first,
    gains_second,
):
    planes = lax.axis_size("dp")
    members = lax.axis_size("fsdp")
    chips = members // 2
    plane = lax.axis_index("dp")
    index = lax.axis_index("fsdp")
    chip = index // 2
    core = index % 2
    place = jnp.stack([plane, chip, core]).astype(jnp.int32)
    spot = jnp.stack([plane, index]).astype(jnp.int32)
    count, width = tokens.shape
    length = count * members
    slice_rows = query_weight.shape[0]
    own_q = query_weight.shape[1] // members
    sharing = members // KV_HEADS
    same_core = [list(range(c, members, 2)) for c in range(2)]

    def chip_all(own, size):
        return gather(own, chip_send, size)

    def plane_all(own, size):
        return gather_line(own, plane_send, size)

    gu_mine, gu_other, qkv_mine, qkv_other = pack(
        place, planes, chips, gate_weight, up_weight, query_weight, key_weight, value_weight
    )
    tokens_all = gather_cores(tokens, chip_all, chips)
    qkv_rows = gather_rows(chip, core, exchange(qkv_mine, qkv_other, chip_send))
    gate_up_rows = gather_rows(plane, core, exchange(gu_mine, gu_other, plane_send))
    w_down = lax.all_gather(
        down_weight.astype(BF16), "fsdp", axis=0, tiled=True, axis_index_groups=same_core
    )
    gate_up_rows, w_down = lax.optimization_barrier((gate_up_rows, w_down))
    w_gate_up = lax.all_gather(
        gate_up_rows, "fsdp", axis=0, tiled=False, axis_index_groups=same_core
    )
    w_qkv = plane_all(qkv_rows, planes)

    gains = norm_gains.astype(BF16).astype(F32)
    gains = by_offset(jnp.stack(gather(gains, plane_send, planes)), plane)
    gains = jnp.stack(gather_cores(gains, chip_all, chips))
    gains = jnp.transpose(by_offset(gains, index), (2, 1, 0, 3)).reshape(2, width)

    start = segment_starts(seq_lengths[0], length)
    cosine, sine = rope_tables(jnp.arange(length, dtype=jnp.int32) - start)

    hop = members // planes
    out_rows = jnp.stack(plane_all(output_weight.astype(BF16), planes))
    own_plane = index // hop

    def out_route(turn_no):
        return [(i, ((turn_no + i) % planes) * hop + i // planes) for i in range(members)]

    w_output = jnp.zeros((planes, slice_rows, width), BF16)
    for turn_no in range(planes):
        sent = lax.dynamic_index_in_dim(
            out_rows, ((turn_no + index) % planes) ^ plane, 0, keepdims=False
        )
        got = lax.ppermute(sent, "fsdp", out_route(turn_no))
        spare = (own_plane + planes - turn_no) % planes
        w_output = lax.dynamic_update_index_in_dim(w_output, got, spare, 0)
    w_output = w_output.reshape(planes * slice_rows, width)
    out_grad_all = gather_cores(out_grad, plane_all, planes)

    normed, queries, keys_values, attended = attend(
        spot, tokens_all, w_qkv, gains[:1], start[:, None], cosine, sine
    )
    own_tokens = tokens.astype(F32)
    resid = own_tokens + scatter_cores(*project(attended, w_output, chips), chip_send)
    scale_two = rms_scale(resid)
    own_normed_two = (resid * scale_two * gains[1]).astype(BF16)

    normed_two = gather_cores(own_normed_two, plane_all, planes)
    fed = [
        feed(
            planes,
            chips,
            normed_two[2 * step : 2 * step + 2],
            out_grad_all[2 * step : 2 * step + 2],
            w_gate_up,
            w_down,
        )
        for step in range(planes)
    ]
    hidden, grad_gate, grad_up, out_mine, out_other, dx_mine, dx_other = zip(*fed)
    grad_normed_two = scatter_cores(dx_mine, dx_other, plane_send)
    weighted_two = grad_normed_two * gains[1]
    grad_gain_two = jnp.sum(grad_normed_two * resid * scale_two, 0)
    grad_resid = (
        out_grad.astype(F32)
        + scale_two * weighted_two
        - resid
        * (scale_two * scale_two * scale_two)
        * jnp.mean(weighted_two * resid, -1, keepdims=True)
    )
    grad_attn_out = gather_cores(grad_resid.astype(BF16), chip_all, chips)

    grad_gate_up = feed_grad(planes, chips, normed_two, grad_gate, grad_up)
    grad_gate_up = lax.psum_scatter(
        grad_gate_up, "fsdp", scatter_dimension=0, tiled=False, axis_index_groups=same_core
    )
    grad_down = rows_grad(jnp.concatenate(hidden), out_grad_all)
    grad_down, grad_gate_up = lax.optimization_barrier((grad_down, grad_gate_up))
    grad_down_weight = lax.psum_scatter(
        grad_down, "fsdp", scatter_dimension=0, tiled=True, axis_index_groups=same_core
    ).astype(F32)
    grad_gate_up = exchange(*spread_rows(plane, core, grad_gate_up, planes), plane_send)

    grad_qkv = attend_back(
        spot, queries, keys_values, w_output, grad_attn_out, start[None, :], cosine, sine
    )
    grad_normed = scatter_cores(*project_back(spot, grad_qkv, w_qkv, chips), chip_send)
    scale_one = rms_scale(own_tokens)
    weighted_one = grad_normed * gains[0]
    grad_gain_one = jnp.sum(grad_normed * own_tokens * scale_one, 0)
    grad_tokens = (
        grad_resid
        + scale_one * weighted_one
        - own_tokens
        * (scale_one * scale_one * scale_one)
        * jnp.mean(weighted_one * own_tokens, -1, keepdims=True)
    )
    out_mine, _ = lax.optimization_barrier((out_mine, grad_attn_out[0]))
    result = resid + scatter_cores(out_mine, out_other, plane_send)

    grad_output = rows_grad(attended, grad_attn_out).reshape(planes, slice_rows, width)
    out_parts = jnp.zeros((planes, slice_rows, width), BF16)
    for turn_no in range(planes):
        spare = (own_plane + planes - turn_no) % planes
        sent = lax.dynamic_index_in_dim(grad_output, spare, 0, keepdims=False)
        got = lax.ppermute(sent, "fsdp", [(b, a) for a, b in out_route(turn_no)])
        out_parts = lax.dynamic_update_index_in_dim(
            out_parts, got, ((turn_no + index) % planes) ^ plane, 0
        )
    grad_output_weight = scatter_sum([out_parts[step] for step in range(planes)], plane_send)

    grad_w_qkv = scatter_sum(qkv_grad(spot, normed, grad_qkv, planes), plane_send)
    got = exchange(*spread_rows(chip, core, grad_w_qkv, chips), chip_send)
    got = by_offset(jnp.concatenate(got), index).astype(F32)
    got = jnp.transpose(got, (1, 0, 2))
    grad_query_weight = got[:, :, :own_q].reshape(slice_rows, -1)
    grad_kv = got[:, :, own_q:].reshape(slice_rows, KV_HEADS, sharing, PAIR).sum(2)
    grad_key_weight = grad_kv[:, :, :HEAD_DIM].reshape(slice_rows, -1)
    grad_value_weight = grad_kv[:, :, HEAD_DIM:].reshape(slice_rows, -1)

    gain_grads = jnp.stack([grad_gain_one, grad_gain_two]).reshape(2, planes, members, -1)
    gain_grads = by_offset(jnp.transpose(gain_grads, (2, 1, 0, 3)), index)
    gain_grads = gain_grads.reshape((chips, 2) + gain_grads.shape[1:])
    gain_grads = gain_grads[:, 0] + core_swap(gain_grads[:, 1])
    gain_grads = gain_grads[0] + sum(chip_send(gain_grads[s], s) for s in range(1, chips))
    gain_grads = by_offset(gain_grads, plane)
    gain_grads = gain_grads[0] + sum(plane_send(gain_grads[s], s) for s in range(1, planes))

    updated = (
        adam_step(query_weight, query_first, query_second, grad_query_weight, 0.02)
        + adam_step(key_weight, key_first, key_second, grad_key_weight, 0.02)
        + adam_step(value_weight, value_first, value_second, grad_value_weight, 0.02)
        + adam_step(output_weight, output_first, output_second, grad_output_weight, 0.1)
        + tuple(
            feed_adam(
                place,
                planes,
                chips,
                grad_gate_up,
                (gate_weight, gate_first, gate_second, up_weight, up_first, up_second),
            )
        )
        + adam_step(down_weight, down_first, down_second, grad_down_weight, 0.02)
        + adam_step(norm_gains, gains_first, gains_second, gain_grads, 0.2)
    )
    return (result.astype(BF16), grad_tokens) + updated


def solution(mesh):
    rows = P(("dp", "fsdp"), None)
    columns = P(None, ("dp", "fsdp"))
    in_specs = (rows, rows, P("dp", None)) + (rows,) * 21 + (columns,) * 3
    out_specs = (rows, rows) + (rows,) * 21 + (columns,) * 3
    return jax.shard_map(local, mesh=mesh, in_specs=in_specs, out_specs=out_specs, check_vma=False)
```

time: 708 us -> 681 us (0.962)
  Pallas kernels: 21.4 us -> 142 us
  matrix products: 72.7 us -> 0 us
  starting transfers between devices: 81.6 us -> 154 us
  blocking collectives: 54.6 us -> 0 us
  local copies, waits for them, and re-layouts: 85.8 us -> 40.3 us
  other arithmetic: 76.5 us -> 53.5 us
  waiting for transfers between devices: 290 us -> 268 us
    ppermute x0 -> x36, waiting for transfers between devices: none -> 183 us  [plane_send(): return lax.ppermute(value, 'dp', [(i, i ^ step) for i in range(planes)])]
    unnamed x12 -> x5, waiting for transfers between devices: 124 us -> 0.09 us
    pallas_call x2 -> x18, Pallas kernels: 21.4 us -> 142 us  [the longest x4 44.2 us: feed(): pl.pallas_call(functools.partial(feed_kernel, planes, chips), out_shape=(...]
    ppermute x0 -> x36, starting transfers between devices: none -> 91.6 us  [plane_send(): return lax.ppermute(value, 'dp', [(i, i ^ step) for i in range(planes)])]
    dot_general x15 -> x0, matrix products: 72.7 us -> none  [the longest x5 28.1 us: matmul(): return jnp.dot(left, right, preferred_element_type=F32)]
    ppermute x42 -> x24, waiting for transfers between devices: 142 us -> 73.1 us  [chip_send(): lax.ppermute(value, 'fsdp', [(i, i ^ 2 * step) for i in range(members)])]
    all_gather x1 -> x0, blocking collectives: 54.6 us -> none  [local(): lax.all_gather(norm_gains.astype(BF16), both, axis=1, tiled=True)]
    unnamed x198 -> x184, local copies, waits for them, and re-layouts: 38.5 us -> 9.94 us
  transfers between devices with their start and end apart: 75 -> 113, of which waited for: 37 -> 31; matrix products, arithmetic and copies ran while one was open for 28% -> 12% of each run, Pallas kernels for 3% -> 21%
where the time goes in v2:
time: 681 us; the launch traced here: 673 us
  waiting for transfers between devices  268 us (39%)
  starting transfers between devices  154 us (23%)
  Pallas kernels  142 us (21%)
  other arithmetic  53.5 us (8%)
  local copies, waits for them, and re-layouts  40.3 us (6%)
  between operations  15.5 us (2%)
    ppermute x36, waiting for transfers between devices, plane_send(): return lax.ppermute(value, 'dp', [(i, i ^ step) for i in range(planes)])  183 us
    ppermute x36, starting transfers between devices, plane_send(): return lax.ppermute(value, 'dp', [(i, i ^ step) for i in range(planes)])  91.6 us
    ppermute x24, waiting for transfers between devices, chip_send(): lax.ppermute(value, 'fsdp', [(i, i ^ 2 * step) for i in range(members)])  73.1 us
    pallas_call x4, Pallas kernels, feed(): pl.pallas_call(functools.partial(feed_kernel, planes, chips), out_shape=(...  44.2 us
    ppermute x24, starting transfers between devices, chip_send(): lax.ppermute(value, 'fsdp', [(i, i ^ 2 * step) for i in range(members)])  25.4 us
    pallas_call x1, Pallas kernels, attend_back(): pl.pallas_call(functools.partial(attend_back_kernel, members, pairs), out...  18.1 us
    ppermute x4, starting transfers between devices, local(): got = lax.ppermute(sent, 'fsdp', out_route(turn_no))  17.5 us
    pallas_call x1, Pallas kernels, attend(): pl.pallas_call(functools.partial(attend_kernel, members, pairs, planes),...  15.3 us
  transfers between devices with their start and end apart: 113, of which 31 were waited for; matrix products, arithmetic and copies ran while one was open for 12% of the time, Pallas kernels for 21%

profile of v2, /device:TPU:0, one launch (start us, length us, event | category | flops | bytes accessed | tf_op | source)
XLA Modules:
  0.0 672.6 jit_solution(7187720637169882047)
XLA Ops:
  8.3 4.1 collective-permute-start.25
  27.1 5.9 pack.1
  45.9 3.9 collective-permute-start.43
  50.6 12.0 %collective-permute-done.41.refs_1_ = bf16[2,2,64,704]{3,2,1,0:T(8,128)(2,1)S(1)} collective-permute-done((bf16[2,2,64,704]{3,2,1,0:T(8,128)(2,1)S(1)}, bf16[2,2,64,704]{3,2,1,0:T(8,128)(2,1)S(1)}, u32[]{:S(2)}, u32[]{:S(2)}) %collective-permute-start.41) | collective-permute-done | bytes 360480 | tf_op jit(solution)/shard_map/ppermute | solution.py:65
  62.6 12.4 %collective-permute-done.42.refs_2_ = bf16[2,2,64,704]{3,2,1,0:T(8,128)(2,1)S(1)} collective-permute-done((bf16[2,2,64,704]{3,2,1,0:T(8,128)(2,1)S(1)}, bf16[2,2,64,704]{3,2,1,0:T(8,128)(2,1)S(1)}, u32[]{:S(2)}, u32[]{:S(2)}) %collective-permute-start.42) | collective-permute-done | bytes 360480 | tf_op jit(solution)/shard_map/ppermute | solution.py:65
  83.2 7.7 %collective-permute-start.26 = (bf16[64,2048]{1,0:T(8,128)(2,1)S(1)}, bf16[64,2048]{1,0:T(8,128)(2,1)S(1)}, u32[]{:S(2)}, u32[]{:S(2)}) collective-permute-start(bf16[64,2048]{1,0:T(8,128)(2,1)S(1)} %collective-permute-done.25), channel_id=1, source_target_pairs={{0,8},{8,0},{16,24},{24,16},{1,9},{9,1},{17,25},{25,17},{2,10},{10... | collective-permute-start | bytes 786440 | tf_op jit(solution)/shard_map/ppermute | solution.py:65
  91.5 5.4 collective-permute-done.26
  103.4 15.1 %collective-permute-done.19.refs_2_ = bf16[2,64,384]{2,1,0:T(8,128)(2,1)S(1)} collective-permute-done((bf16[2,64,384]{2,1,0:T(8,128)(2,1)S(1)}, bf16[2,64,384]{2,1,0:T(8,128)(2,1)S(1)}, u32[]{:S(2)}, u32[]{:S(2)}) %collective-permute-start.19) | collective-permute-done | bytes 98336 | tf_op jit(solution)/shard_map/ppermute | solution.py:60
  124.1 9.5 %collective-permute-done.28 = bf16[64,2048]{1,0:T(8,128)(2,1)S(1)} collective-permute-done((bf16[64,2048]{1,0:T(8,128)(2,1)S(1)}, bf16[64,2048]{1,0:T(8,128)(2,1)S(1)}, u32[]{:S(2)}, u32[]{:S(2)}) %collective-permute-start.28) | collective-permute-done | bytes 262176 | tf_op jit(solution)/shard_map/ppermute | solution.py:787
  133.6 11.3 %collective-permute-start.29 = (bf16[64,2048]{1,0:T(8,128)(2,1)S(1)}, bf16[64,2048]{1,0:T(8,128)(2,1)S(1)}, u32[]{:S(2)}, u32[]{:S(2)}) collective-permute-start(bf16[64,2048]{1,0:T(8,128)(2,1)S(1)} %get-tuple-element.210), channel_id=1, source_target_pairs={{0,4},{1,6},{2,0},{3,2},{4,5},{5,7},{6,1},{7,3},{8,12},{9,14},{10,... | collective-permute-start | bytes 786440 | tf_op jit(solution)/shard_map/ppermute | solution.py:787
  152.6 13.5 %collective-permute-done.22.refs_10_.refs_2_ = bf16[512,384]{1,0:T(8,128)(2,1)S(1)} collective-permute-done((bf16[512,384]{1,0:T(8,128)(2,1)S(1)}, bf16[512,384]{1,0:T(8,128)(2,1)S(1)}, u32[]{:S(2)}, u32[]{:S(2)}) %collective-permute-start.22) | collective-permute-done | bytes 393248 | tf_op jit(solution)/shard_map/ppermute | solution.py:65
  168.1 9.9 %collective-permute-done.21.refs_9_.refs_1_ = bf16[512,384]{1,0:T(8,128)(2,1)S(1)} collective-permute-done((bf16[512,384]{1,0:T(8,128)(2,1)S(1)}, bf16[512,384]{1,0:T(8,128)(2,1)S(1)}, u32[]{:S(2)}, u32[]{:S(2)}) %collective-permute-start.21) | collective-permute-done | bytes 393248 | tf_op jit(solution)/shard_map/ppermute | solution.py:65
  178.0 7.6 %collective-permute-done.23.refs_11_.refs_3_ = bf16[512,384]{1,0:T(8,128)(2,1)S(1)} collective-permute-done((bf16[512,384]{1,0:T(8,128)(2,1)S(1)}, bf16[512,384]{1,0:T(8,128)(2,1)S(1)}, u32[]{:S(2)}, u32[]{:S(2)}) %collective-permute-start.23) | collective-permute-done | bytes 393248 | tf_op jit(solution)/shard_map/ppermute | solution.py:65
  186.4 15.3 %attend.1 = (bf16[1024,2048]{1,0:T(8,128)(2,1)}, bf16[1024,256]{1,0:T(8,128)(2,1)}, bf16[1024,128]{1,0:T(8,128)(2,1)}, bf16[1024,256]{1,0:T(8,128)(2,1)}) custom-call(s32[2]{0:T(128)} %pad_add_fusion.place, s32[1024,1]{1,0:T(8,128)} %copy.108.start_ref, f32[1024,128]{1,0:T(8,128)} %get-tuple-element.280.cos_ref, f32[1024,128]{1,0:T(8,128)} %get-tuple-element.281.sin_ref, ...), custom_call_target="tpu_custom_call" | custom-call | flops 2415919104 | bytes 8388608 | tf_op jit(solution)/shard_map/attend/pallas_call | solution.py:318
  201.7 4.8 project.1
  220.5 5.2 collective-permute-done.32
  225.7 11.5 %collective-permute-done.34 = bf16[128,2048]{1,0:T(8,128)(2,1)} collective-permute-done((bf16[128,2048]{1,0:T(8,128)(2,1)}, bf16[128,2048]{1,0:T(8,128)(2,1)}, u32[]{:S(2)}, u32[]{:S(2)}) %collective-permute-start.34) | collective-permute-done | bytes 524320 | tf_op jit(solution)/shard_map/ppermute | solution.py:60
  245.0 21.7 %collective-permute-done.44.x_mine.refs_2_ = bf16[128,2048]{1,0:T(8,128)(2,1)} collective-permute-done((bf16[128,2048]{1,0:T(8,128)(2,1)}, bf16[128,2048]{1,0:T(8,128)(2,1)}, u32[]{:S(2)}, u32[]{:S(2)}) %collective-permute-start.44) | collective-permute-done | bytes 524320 | tf_op jit(solution)/shard_map/ppermute | solution.py:65
  269.8 8.5 %copy.111 = bf16[8,512,704]{2,1,0:T(8,128)(2,1)} copy(bf16[8,512,704]{1,2,0:T(8,128)(2,1)} %all-gather.6.cloned.1.call-done) | data formatting | bytes 11534336 | tf_op jit(solution)/shard_map/all_gather | solution.py:762
  278.9 8.8 %collective-permute-done.52.x_mine.refs_6_ = bf16[128,2048]{1,0:T(8,128)(2,1)} collective-permute-done((bf16[128,2048]{1,0:T(8,128)(2,1)}, bf16[128,2048]{1,0:T(8,128)(2,1)}, u32[]{:S(2)}, u32[]{:S(2)}) %collective-permute-start.52) | collective-permute-done | bytes 524320 | tf_op jit(solution)/shard_map/ppermute | solution.py:65
  287.8 11.0 %feed.5 = (bf16[256,704]{1,0:T(8,128)(2,1)}, bf16[256,704]{1,0:T(8,128)(2,1)}, bf16[256,704]{1,0:T(8,128)(2,1)}, f32[128,2048]{1,0:T(8,128)}, bf16[128,2048]{1,0...) custom-call(bf16[128,2048]{1,0:T(8,128)(2,1)} %collective-permute-done.44.x_mine.refs_2_, ...), custom_call_target="tpu_custom_call" | custom-call | flops 4429185024 | bytes 8650752 | tf_op jit(solution)/shard_map/feed/pallas_call | solution.py:578
  299.5 11.0 %feed.6 = (bf16[256,704]{1,0:T(8,128)(2,1)}, bf16[256,704]{1,0:T(8,128)(2,1)}, bf16[256,704]{1,0:T(8,128)(2,1)}, f32[128,2048]{1,0:T(8,128)}, bf16[128,2048]{1,0...) custom-call(bf16[128,2048]{1,0:T(8,128)(2,1)} %collective-permute-done.48.x_mine.refs_4_, ...), custom_call_target="tpu_custom_call" | custom-call | flops 4429185024 | bytes 8650752 | tf_op jit(solution)/shard_map/feed/pallas_call | solution.py:578
  312.1 11.2 %feed.7 = (bf16[256,704]{1,0:T(8,128)(2,1)}, bf16[256,704]{1,0:T(8,128)(2,1)}, bf16[256,704]{1,0:T(8,128)(2,1)}, f32[128,2048]{1,0:T(8,128)}, bf16[128,2048]{1,0...) custom-call(bf16[128,2048]{1,0:T(8,128)(2,1)} %collective-permute-done.52.x_mine.refs_6_, ...), custom_call_target="tpu_custom_call" | custom-call | flops 4429185024 | bytes 8650752 | tf_op jit(solution)/shard_map/feed/pallas_call | solution.py:578
  325.4 11.0 %feed.4 = (bf16[256,704]{1,0:T(8,128)(2,1)}, bf16[256,704]{1,0:T(8,128)(2,1)}, bf16[256,704]{1,0:T(8,128)(2,1)}, f32[128,2048]{1,0:T(8,128)}, bf16[128,2048]{1,0...) custom-call(bf16[128,2048]{1,0:T(8,128)(2,1)} %multiply_convert_fusion.x_mine.refs_0_, ...), custom_call_target="tpu_custom_call" | custom-call | flops 4429185024 | bytes 8650752 | tf_op jit(solution)/shard_map/feed/pallas_call | solution.py:578
  343.7 10.9 %feed_grad.1 = bf16[4,2,512,704]{3,2,1,0:T(8,128)(2,1)} custom-call(bf16[128,2048]{1,0:T(8,128)(2,1)} %multiply_convert_fusion.x_mine.refs_0_, bf16[128,2048]{1,0:T(8,128)(2,1)} %copy-done.67, bf16[128,2048]{1,0:T(8,128)(2,1)} %collective-permute-done.44.x_mine.refs_2_, bf16[128,2048]{1,0:T(8,128)(2,1)} %collective-permute-done.45.x_other.refs_3_, ...), custom_call_target="tpu_custom_call" | custom-call | flops 5905580032 | bytes 5767168 | tf_op jit(solution)/shard_map/feed_grad/pallas_call | solution.py:626
  354.6 8.4 %copy.116 = bf16[4,2,512,704]{2,3,1,0:T(8,128)(2,1)} copy(bf16[4,2,512,704]{3,2,1,0:T(8,128)(2,1)} %feed_grad.1) | data formatting | bytes 11534336 | tf_op jit(solution)/shard_map/feed_grad/pallas_call | solution.py:626
  364.3 13.6 %collective-permute-done.59 = bf16[128,2048]{1,0:T(8,128)(2,1)} collective-permute-done((bf16[128,2048]{1,0:T(8,128)(2,1)}, bf16[128,2048]{1,0:T(8,128)(2,1)}, u32[]{:S(2)}, u32[]{:S(2)}) %collective-permute-start.59) | collective-permute-done | bytes 524320 | tf_op jit(solution)/shard_map/ppermute | solution.py:65
  387.8 11.5 %collective-permute-start.64 = (bf16[128,2048]{1,0:T(8,128)(2,1)}, bf16[128,2048]{1,0:T(8,128)(2,1)}, u32[]{:S(2)}, u32[]{:S(2)}) collective-permute-start(bf16[128,2048]{1,0:T(8,128)(2,1)} %add_convert_fusion.6), channel_id=1, source_target_pairs={{0,8},{8,0},{16,24},{24,16},{1,9},{9,1},{17,25},{25,17},{2,10},{10... | collective-permute-start | bytes 1572872 | tf_op jit(solution)/shard_map/ppermute | solution.py:65
  401.2 7.5 %collective-permute-done.71.refs_2_ = bf16[128,2048]{1,0:T(8,128)(2,1)} collective-permute-done((bf16[128,2048]{1,0:T(8,128)(2,1)}, bf16[128,2048]{1,0:T(8,128)(2,1)}, u32[]{:S(2)}, u32[]{:S(2)}) %collective-permute-start.71) | collective-permute-done | bytes 524320 | tf_op jit(solution)/shard_map/ppermute | solution.py:60
  413.4 7.5 %rows_grad.3 = bf16[704,2048]{1,0:T(8,128)(2,1)} custom-call(bf16[1024,704]{1,0:T(8,128)(2,1)} %pad_maximum_fusion.left_ref, bf16[128,2048]{1,0:T(8,128)(2,1)} %refs_0_.3, bf16[128,2048]{1,0:T(8,128)(2,1)} %copy-done.61, bf16[128,2048]{1,0:T(8,128)(2,1)} %collective-permute-done.46.g_mine.refs_2_, bf16[128,2048]{1,0:T(8,128)(2,1)} %copy-done.59, ...), custom_call_target="tpu_custom_call" | custom-call | flops 2952790016 | bytes 1441792 | tf_op jit(solution)/shard_map/rows_grad/pallas_call | solution.py:510
  421.0 5.2 collective-permute-done.75.refs_6_
  426.7 11.0 %collective-permute-done.66 = bf16[128,2048]{1,0:T(8,128)(2,1)} collective-permute-done((bf16[128,2048]{1,0:T(8,128)(2,1)}, bf16[128,2048]{1,0:T(8,128)(2,1)}, u32[]{:S(2)}, u32[]{:S(2)}) %collective-permute-start.66) | collective-permute-done | bytes 524320 | tf_op jit(solution)/shard_map/ppermute | solution.py:65
  442.7 4.6 rows_grad.2
  449.8 18.1 %attend_back.1.left_ref.grad_ref = bf16[1024,384]{1,0:T(8,128)(2,1)} custom-call(s32[2]{0:T(128)} %pad_add_fusion.place, s32[1,1024]{1,0:T(1,128)} %bitcast.169, f32[1024,128]{1,0:T(8,128)} %get-tuple-element.280.cos_ref, f32[1024,128]{1,0:T(8,128)} %get-tuple-element.281.sin_ref, bf16[1024,256]{1,0:T(8,128)(2,1)} %get-tuple-element.135.q_ref, ...), custom_call_target="tpu_custom_call" | custom-call | flops 2952790016 | bytes 4194304 | tf_op jit(solution)/shard_map/attend_back/pallas_call | solution.py:408
  467.9 6.2 project_back.1
  480.1 5.5 qkv_grad.1
  489.4 9.6 %collective-permute-start.84 = (bf16[512,384]{1,0:T(8,128)(2,1)S(1)}, bf16[512,384]{1,0:T(8,128)(2,1)S(1)}, u32[]{:S(2)}, u32[]{:S(2)}) collective-permute-start(bf16[512,384]{1,0:T(8,128)(2,1)S(1)} %copy-done.76), channel_id=1, source_target_pairs={{0,8},{8,0},{16,24},{24,16},{1,9},{9,1},{17,25},{25,17},{2,10},{10... | collective-permute-start | bytes 1179656 | tf_op jit(solution)/shard_map/ppermute | solution.py:65
  503.5 12.4 %collective-permute-done.84 = bf16[512,384]{1,0:T(8,128)(2,1)S(1)} collective-permute-done((bf16[512,384]{1,0:T(8,128)(2,1)S(1)}, bf16[512,384]{1,0:T(8,128)(2,1)S(1)}, u32[]{:S(2)}, u32[]{:S(2)}) %collective-permute-start.84) | collective-permute-done | bytes 393248 | tf_op jit(solution)/shard_map/ppermute | solution.py:65
  515.9 13.0 %collective-permute-done.85 = bf16[512,384]{1,0:T(8,128)(2,1)S(1)} collective-permute-done((bf16[512,384]{1,0:T(8,128)(2,1)S(1)}, bf16[512,384]{1,0:T(8,128)(2,1)S(1)}, u32[]{:S(2)}, u32[]{:S(2)}) %collective-permute-start.85) | collective-permute-done | bytes 393248 | tf_op jit(solution)/shard_map/ppermute | solution.py:65
  528.9 7.9 %collective-permute-start.95 = (bf16[64,2048]{1,0:T(8,128)(2,1)S(1)}, bf16[64,2048]{1,0:T(8,128)(2,1)S(1)}, u32[]{:S(2)}, u32[]{:S(2)}) collective-permute-start(bf16[64,2048]{1,0:T(8,128)(2,1)S(1)} %get-tuple-element.202), channel_id=1, source_target_pairs={{0,8},{8,0},{16,24},{24,16},{1,9},{9,1},{17,25},{25,17},{2,10},{10... | collective-permute-start | bytes 786440 | tf_op jit(solution)/shard_map/ppermute | solution.py:65
  547.4 13.6 %collective-permute-done.96 = bf16[64,2048]{1,0:T(8,128)(2,1)S(1)} collective-permute-done((bf16[64,2048]{1,0:T(8,128)(2,1)S(1)}, bf16[64,2048]{1,0:T(8,128)(2,1)S(1)}, u32[]{:S(2)}, u32[]{:S(2)}) %collective-permute-start.96) | collective-permute-done | bytes 262176 | tf_op jit(solution)/shard_map/ppermute | solution.py:65
  566.1 10.1 %collective-permute-done.88 = bf16[2,64,384]{2,1,0:T(8,128)(2,1)S(1)} collective-permute-done((bf16[2,64,384]{2,1,0:T(8,128)(2,1)S(1)}, bf16[2,64,384]{2,1,0:T(8,128)(2,1)S(1)}, u32[]{:S(2)}, u32[]{:S(2)}) %collective-permute-start.88) | collective-permute-done | bytes 98336 | tf_op jit(solution)/shard_map/ppermute | solution.py:60
  576.4 9.7 %collective-permute-done.89 = bf16[2,64,384]{2,1,0:T(8,128)(2,1)S(1)} collective-permute-done((bf16[2,64,384]{2,1,0:T(8,128)(2,1)S(1)}, bf16[2,64,384]{2,1,0:T(8,128)(2,1)S(1)}, u32[]{:S(2)}, u32[]{:S(2)}) %collective-permute-start.89) | collective-permute-done | bytes 98336 | tf_op jit(solution)/shard_map/ppermute | solution.py:60
  586.8 4.8 collective-permute-done.90
  623.0 6.6 collective-permute-done.101.refs_3_
  629.6 20.9 %collective-permute-done.100.refs_2_ = bf16[2,2,64,704]{3,2,1,0:T(8,128)(2,1)S(1)} collective-permute-done((bf16[2,2,64,704]{3,2,1,0:T(8,128)(2,1)S(1)}, bf16[2,2,64,704]{3,2,1,0:T(8,128)(2,1)S(1)}, u32[]{:S(2)}, u32[]{:S(2)}) %collective-permute-start.100) | collective-permute-done | bytes 360480 | tf_op jit(solution)/shard_map/ppermute | solution.py:65
  652.0 9.5 %feed_adam.1 = (f32[64,5632]{1,0:T(8,128)}, f32[64,5632]{1,0:T(8,128)}, f32[64,5632]{1,0:T(8,128)}, f32[64,5632]{1,0:T(8,128)}, f32[64,5632]{1,0:T(8,128)}, /*index=5*/f32[64,5632]{1,0:T(8,128)}) custom-call(s32[3]{0:T(128)} %pad_add_fusion.2.place, bf16[2,2,64,704]{3,2,1,0:T(8,128)(2,1)} %pad_maximum_fusion.8.refs_0_, bf16[2,2,64,704]{3,2,1,0:T(8,128)(2,1)} %copy-done.33, ...), custom_call_target="tpu_custom_call" | custom-call | flops 14417920 | bytes 18743296 | tf_op jit(solution)/shard_map/feed_adam/pallas_call | solution.py:666
  661.6 4.3 multiply_subtract_fusion
  (504 shorter events, 186.5 us)
Async XLA Ops:
  7.2 72.0 %all-gather.4.cloned.1.call-start = ((), (), s32[]{:S(2)}) async-start(), calls=%async_computation.2 | async-start | bytes 3604480 | tf_op jit(solution)/shard_map/all_gather | solution.py:758
  8.3 74.9 %collective-permute-start.25 = (bf16[64,2048]{1,0:T(8,128)(2,1)S(1)}, bf16[64,2048]{1,0:T(8,128)(2,1)S(1)}, u32[]{:S(2)}, u32[]{:S(2)}) collective-permute-start(bf16[64,2048]{1,0:T(8,128)(2,1)S(1)} %convert_element_type.189), channel_id=1, source_target_pairs={{0,16},{8,24},{16,0},{24,8},{1,17},{9,25},{17,1},{25,9},{2,18},{10... | collective-permute-start | bytes 786440 | tf_op jit(solution)/shard_map/ppermute | solution.py:65
  12.4 79.1 %collective-permute-start.24 = (bf16[64,2048]{1,0:T(8,128)(2,1)S(1)}, bf16[64,2048]{1,0:T(8,128)(2,1)S(1)}, u32[]{:S(2)}, u32[]{:S(2)}) collective-permute-start(bf16[64,2048]{1,0:T(8,128)(2,1)S(1)} %convert_element_type.189), channel_id=1, source_target_pairs={{0,8},{8,0},{16,24},{24,16},{1,9},{9,1},{17,25},{25,17},{2,10},{10... | collective-permute-start | bytes 786440 | tf_op jit(solution)/shard_map/ppermute | solution.py:65
  21.4 248.4 %all-gather.6.cloned.1.call-start = ((), (), s32[]{:S(2)}) async-start(), calls=%async_computation.4 | async-start | bytes 7208960 | tf_op jit(solution)/shard_map/all_gather | solution.py:762
  45.3 29.8 %collective-permute-start.42 = (bf16[2,2,64,704]{3,2,1,0:T(8,128)(2,1)S(1)}, bf16[2,2,64,704]{3,2,1,0:T(8,128)(2,1)S(1)}, u32[]{:S(2)}, u32[]{:S(2)}) collective-permute-start(bf16[2,2,64,704]{3,2,1,0:T(8,128)(2,1)S(1)} %pad_maximum_fusion.6), channel_id=1, source_target_pairs={{0,16},{8,24},{16,0},{24,8},{1,17},{9,25},{17,1},{25,9},{2,18},{10... | collective-permute-start | bytes 1081352 | tf_op jit(solution)/shard_map/ppermute | solution.py:65
  45.9 29.7 %collective-permute-start.43 = (bf16[2,2,64,704]{3,2,1,0:T(8,128)(2,1)S(1)}, bf16[2,2,64,704]{3,2,1,0:T(8,128)(2,1)S(1)}, u32[]{:S(2)}, u32[]{:S(2)}) collective-permute-start(bf16[2,2,64,704]{3,2,1,0:T(8,128)(2,1)S(1)} %pad_maximum_fusion.7), channel_id=1, source_target_pairs={{0,24},{8,16},{16,8},{24,0},{1,25},{9,17},{17,9},{25,1},{2,26},{10... | collective-permute-start | bytes 1081352 | tf_op jit(solution)/shard_map/ppermute | solution.py:65
  62.6 28.2 %collective-permute-start.17 = (bf16[4,64,384]{2,1,0:T(8,128)(2,1)S(1)}, bf16[4,64,384]{2,1,0:T(8,128)(2,1)S(1)}, u32[]{:S(2)}, u32[]{:S(2)}) collective-permute-start(bf16[4,64,384]{2,1,0:T(8,128)(2,1)S(1)} %copy-done.77), channel_id=1, source_target_pairs={{0,1},{1,0},{2,3},{3,2},{4,5},{5,4},{6,7},{7,6},{8,9},{9,8},{10,11... | collective-permute-start | bytes 589832 | tf_op jit(solution)/shard_map/ppermute | solution.py:55
  75.1 69.8 %collective-permute-start.11 = (bf16[128,2048]{1,0:T(8,128)(2,1)S(1)}, bf16[128,2048]{1,0:T(8,128)(2,1)}, u32[]{:S(2)}, u32[]{:S(2)}) collective-permute-start(bf16[128,2048]{1,0:T(8,128)(2,1)S(1)} %copy-done.2), channel_id=1, source_target_pairs={{0,2},{1,3},{2,0},{3,1},{4,6},{5,7},{6,4},{7,5},{8,10},{9,11},{10,... | collective-permute-start | bytes 1572872 | tf_op jit(solution)/shard_map/ppermute | solution.py:60
  81.7 510.0 %reduce-scatter.7.cloned.1.call-start = ((), (), s32[]{:S(2)}) async-start(), calls=%async_computation.5 | async-start | bytes 7208960
  103.4 44.3 %collective-permute-start.13 = (bf16[128,2048]{1,0:T(8,128)(2,1)S(1)}, bf16[128,2048]{1,0:T(8,128)(2,1)S(1)}, u32[]{:S(2)}, u32[]{:S(2)}) collective-permute-start(bf16[128,2048]{1,0:T(8,128)(2,1)S(1)} %copy-done.2), channel_id=1, source_target_pairs={{0,4},{1,5},{2,6},{3,7},{4,0},{5,1},{6,2},{7,3},{8,12},{9,13},{10,... | collective-permute-start | bytes 1572872 | tf_op jit(solution)/shard_map/ppermute | solution.py:60
  118.5 32.2 %collective-permute-start.15 = (bf16[128,2048]{1,0:T(8,128)(2,1)S(1)}, bf16[128,2048]{1,0:T(8,128)(2,1)S(1)}, u32[]{:S(2)}, u32[]{:S(2)}) collective-permute-start(bf16[128,2048]{1,0:T(8,128)(2,1)S(1)} %copy-done.2), channel_id=1, source_target_pairs={{0,6},{1,7},{2,4},{3,5},{4,2},{5,3},{6,0},{7,1},{8,14},{9,15},{10,... | collective-permute-start | bytes 1572872 | tf_op jit(solution)/shard_map/ppermute | solution.py:60
  118.5 32.3 %collective-permute-start.10 = (bf16[128,2048]{1,0:T(8,128)(2,1)S(1)}, bf16[128,2048]{1,0:T(8,128)(2,1)S(1)}, u32[]{:S(2)}, u32[]{:S(2)}) collective-permute-start(bf16[128,2048]{1,0:T(8,128)(2,1)S(1)} %copy-done.2), channel_id=1, source_target_pairs={{0,1},{1,0},{2,3},{3,2},{4,5},{5,4},{6,7},{7,6},{8,9},{9,8},{10,11... | collective-permute-start | bytes 1572872 | tf_op jit(solution)/shard_map/ppermute | solution.py:55
  150.7 27.3 %collective-permute-start.12 = (bf16[128,2048]{1,0:T(8,128)(2,1)}, bf16[128,2048]{1,0:T(8,128)(2,1)S(1)}, u32[]{:S(2)}, u32[]{:S(2)}) collective-permute-start(bf16[128,2048]{1,0:T(8,128)(2,1)} %collective-permute-done.11.refs_2_), channel_id=1, source_target_pairs={{0,1},{1,0},{2,3},{3,2},{4,5},{5,4},{6,7},{7,6},{8,9},{9,8},{10,11... | collective-permute-start | bytes 1572872 | tf_op jit(solution)/shard_map/ppermute | solution.py:55
  150.8 27.2 %collective-permute-start.14 = (bf16[128,2048]{1,0:T(8,128)(2,1)S(1)}, bf16[128,2048]{1,0:T(8,128)(2,1)S(1)}, u32[]{:S(2)}, u32[]{:S(2)}) collective-permute-start(bf16[128,2048]{1,0:T(8,128)(2,1)S(1)} %collective-permute-done.13.refs_4_), channel_id=1, source_target_pairs={{0,1},{1,0},{2,3},{3,2},{4,5},{5,4},{6,7},{7,6},{8,9},{9,8},{10,11... | collective-permute-start | bytes 1572872 | tf_op jit(solution)/shard_map/ppermute | solution.py:55
  151.2 26.8 %collective-permute-start.16 = (bf16[128,2048]{1,0:T(8,128)(2,1)S(1)}, bf16[128,2048]{1,0:T(8,128)(2,1)S(1)}, u32[]{:S(2)}, u32[]{:S(2)}) collective-permute-start(bf16[128,2048]{1,0:T(8,128)(2,1)S(1)} %collective-permute-done.15.refs_6_), channel_id=1, source_target_pairs={{0,1},{1,0},{2,3},{3,2},{4,5},{5,4},{6,7},{7,6},{8,9},{9,8},{10,11... | collective-permute-start | bytes 1572872 | tf_op jit(solution)/shard_map/ppermute | solution.py:55
  216.1 28.5 %collective-permute-start.46 = (bf16[128,2048]{1,0:T(8,128)(2,1)}, bf16[128,2048]{1,0:T(8,128)(2,1)}, u32[]{:S(2)}, u32[]{:S(2)}) collective-permute-start(bf16[128,2048]{1,0:T(8,128)(2,1)} %refs_0_.3), channel_id=1, source_target_pairs={{0,8},{8,0},{16,24},{24,16},{1,9},{9,1},{17,25},{25,17},{2,10},{10... | collective-permute-start | bytes 1572872 | tf_op jit(solution)/shard_map/ppermute | solution.py:65
  217.1 27.5 %collective-permute-start.50 = (bf16[128,2048]{1,0:T(8,128)(2,1)}, bf16[128,2048]{1,0:T(8,128)(2,1)}, u32[]{:S(2)}, u32[]{:S(2)}) collective-permute-start(bf16[128,2048]{1,0:T(8,128)(2,1)} %refs_0_.3), channel_id=1, source_target_pairs={{0,16},{8,24},{16,0},{24,8},{1,17},{9,25},{17,1},{25,9},{2,18},{10... | collective-permute-start | bytes 1572872 | tf_op jit(solution)/shard_map/ppermute | solution.py:65
  240.3 26.4 %collective-permute-start.44 = (bf16[128,2048]{1,0:T(8,128)(2,1)}, bf16[128,2048]{1,0:T(8,128)(2,1)}, u32[]{:S(2)}, u32[]{:S(2)}) collective-permute-start(bf16[128,2048]{1,0:T(8,128)(2,1)} %multiply_convert_fusion.x_mine.refs_0_), channel_id=1, source_target_pairs={{0,8},{8,0},{16,24},{24,16},{1,9},{9,1},{17,25},{25,17},{2,10},{10... | collective-permute-start | bytes 1572872 | tf_op jit(solution)/shard_map/ppermute | solution.py:65
  244.6 33.7 %collective-permute-start.54 = (bf16[128,2048]{1,0:T(8,128)(2,1)}, bf16[128,2048]{1,0:T(8,128)(2,1)S(1)}, u32[]{:S(2)}, u32[]{:S(2)}) collective-permute-start(bf16[128,2048]{1,0:T(8,128)(2,1)} %collective-permute-done.50.g_mine.refs_4_), channel_id=1, source_target_pairs={{0,8},{8,0},{16,24},{24,16},{1,9},{9,1},{17,25},{25,17},{2,10},{10... | collective-permute-start | bytes 1572872 | tf_op jit(solution)/shard_map/ppermute | solution.py:65
  269.3 29.5 %collective-permute-start.51 = (bf16[128,2048]{1,0:T(8,128)(2,1)}, bf16[128,2048]{1,0:T(8,128)(2,1)}, u32[]{:S(2)}, u32[]{:S(2)}) collective-permute-start(bf16[128,2048]{1,0:T(8,128)(2,1)} %collective-permute-done.50.g_mine.refs_4_), channel_id=1, source_target_pairs={{0,1},{1,0},{2,3},{3,2},{4,5},{5,4},{6,7},{7,6},{8,9},{9,8},{10,11... | collective-permute-start | bytes 1572872 | tf_op jit(solution)/shard_map/ppermute | solution.py:55
  269.3 30.0 %collective-permute-start.49 = (bf16[128,2048]{1,0:T(8,128)(2,1)}, bf16[128,2048]{1,0:T(8,128)(2,1)}, u32[]{:S(2)}, u32[]{:S(2)}) collective-permute-start(bf16[128,2048]{1,0:T(8,128)(2,1)} %collective-permute-done.48.x_mine.refs_4_), channel_id=1, source_target_pairs={{0,1},{1,0},{2,3},{3,2},{4,5},{5,4},{6,7},{7,6},{8,9},{9,8},{10,11... | collective-permute-start | bytes 1572872 | tf_op jit(solution)/shard_map/ppermute | solution.py:55
  278.4 45.5 %collective-permute-start.39 = (bf16[128,2048]{1,0:T(8,128)(2,1)}, bf16[128,2048]{1,0:T(8,128)(2,1)S(1)}, u32[]{:S(2)}, u32[]{:S(2)}) collective-permute-start(bf16[128,2048]{1,0:T(8,128)(2,1)} %refs_0_.3), channel_id=1, source_target_pairs={{0,1},{1,0},{2,3},{3,2},{4,5},{5,4},{6,7},{7,6},{8,9},{9,8},{10,11... | collective-permute-start | bytes 1572872 | tf_op jit(solution)/shard_map/ppermute | solution.py:55
  278.6 31.9 %collective-permute-start.55 = (bf16[128,2048]{1,0:T(8,128)(2,1)S(1)}, bf16[128,2048]{1,0:T(8,128)(2,1)S(1)}, u32[]{:S(2)}, u32[]{:S(2)}) collective-permute-start(bf16[128,2048]{1,0:T(8,128)(2,1)S(1)} %collective-permute-done.54.g_mine.refs_6_), channel_id=1, source_target_pairs={{0,1},{1,0},{2,3},{3,2},{4,5},{5,4},{6,7},{7,6},{8,9},{9,8},{10,11... | collective-permute-start | bytes 1572872 | tf_op jit(solution)/shard_map/ppermute | solution.py:55
  299.4 37.2 %collective-permute-start.56 = (bf16[128,2048]{1,0:T(8,128)(2,1)}, bf16[128,2048]{1,0:T(8,128)(2,1)S(1)}, u32[]{:S(2)}, u32[]{:S(2)}) collective-permute-start(bf16[128,2048]{1,0:T(8,128)(2,1)} %get-tuple-element.120), channel_id=1, source_target_pairs={{0,1},{1,0},{2,3},{3,2},{4,5},{5,4},{6,7},{7,6},{8,9},{9,8},{10,11... | collective-permute-start | bytes 1572872 | tf_op jit(solution)/shard_map/ppermute | solution.py:55
  310.5 27.6 %collective-permute-start.58 = (bf16[128,2048]{1,0:T(8,128)(2,1)}, bf16[128,2048]{1,0:T(8,128)(2,1)S(1)}, u32[]{:S(2)}, u32[]{:S(2)}) collective-permute-start(bf16[128,2048]{1,0:T(8,128)(2,1)} %get-tuple-element.122), channel_id=1, source_target_pairs={{0,1},{1,0},{2,3},{3,2},{4,5},{5,4},{6,7},{7,6},{8,9},{9,8},{10,11... | collective-permute-start | bytes 1572872 | tf_op jit(solution)/shard_map/ppermute | solution.py:55
  336.4 27.3 %collective-permute-start.62 = (bf16[128,2048]{1,0:T(8,128)(2,1)}, bf16[128,2048]{1,0:T(8,128)(2,1)}, u32[]{:S(2)}, u32[]{:S(2)}) collective-permute-start(bf16[128,2048]{1,0:T(8,128)(2,1)} %get-tuple-element.126), channel_id=1, source_target_pairs={{0,1},{1,0},{2,3},{3,2},{4,5},{5,4},{6,7},{7,6},{8,9},{9,8},{10,11... | collective-permute-start | bytes 1572872 | tf_op jit(solution)/shard_map/ppermute | solution.py:55
  337.5 26.8 %collective-permute-start.57 = (bf16[128,2048]{1,0:T(8,128)(2,1)}, bf16[128,2048]{1,0:T(8,128)(2,1)}, u32[]{:S(2)}, u32[]{:S(2)}) collective-permute-start(bf16[128,2048]{1,0:T(8,128)(2,1)} %add_convert_fusion.9), channel_id=1, source_target_pairs={{0,8},{8,0},{16,24},{24,16},{1,9},{9,1},{17,25},{25,17},{2,10},{10... | collective-permute-start | bytes 1572872 | tf_op jit(solution)/shard_map/ppermute | solution.py:65
  339.1 38.9 %collective-permute-start.59 = (bf16[128,2048]{1,0:T(8,128)(2,1)}, bf16[128,2048]{1,0:T(8,128)(2,1)}, u32[]{:S(2)}, u32[]{:S(2)}) collective-permute-start(bf16[128,2048]{1,0:T(8,128)(2,1)} %add_convert_fusion.8), channel_id=1, source_target_pairs={{0,16},{8,24},{16,0},{24,8},{1,17},{9,25},{17,1},{25,9},{2,18},{10... | collective-permute-start | bytes 1572872 | tf_op jit(solution)/shard_map/ppermute | solution.py:65
  343.3 34.6 %collective-permute-start.61 = (bf16[128,2048]{1,0:T(8,128)(2,1)}, bf16[128,2048]{1,0:T(8,128)(2,1)}, u32[]{:S(2)}, u32[]{:S(2)}) collective-permute-start(bf16[128,2048]{1,0:T(8,128)(2,1)} %add_convert_fusion.7), channel_id=1, source_target_pairs={{0,24},{8,16},{16,8},{24,0},{1,25},{9,17},{17,9},{25,1},{2,26},{10... | collective-permute-start | bytes 1572872 | tf_op jit(solution)/shard_map/ppermute | solution.py:65
  363.0 298.6 %reduce-scatter.5.cloned.1.call-start = ((), (), s32[]{:S(2)}) async-start(), calls=%async_computation.3 | async-start | bytes 3604480 | tf_op jit(solution)/shard_map/reduce_scatter | solution.py:832
  383.8 37.1 %collective-permute-start.73 = (bf16[128,2048]{1,0:T(8,128)(2,1)}, bf16[128,2048]{1,0:T(8,128)(2,1)}, u32[]{:S(2)}, u32[]{:S(2)}) collective-permute-start(bf16[128,2048]{1,0:T(8,128)(2,1)} %get-tuple-element.197.refs_0_), channel_id=1, source_target_pairs={{0,4},{1,5},{2,6},{3,7},{4,0},{5,1},{6,2},{7,3},{8,12},{9,13},{10,... | collective-permute-start | bytes 1572872 | tf_op jit(solution)/shard_map/ppermute | solution.py:60
  385.3 40.8 %collective-permute-start.75 = (bf16[128,2048]{1,0:T(8,128)(2,1)}, bf16[128,2048]{1,0:T(8,128)(2,1)}, u32[]{:S(2)}, u32[]{:S(2)}) collective-permute-start(bf16[128,2048]{1,0:T(8,128)(2,1)} %get-tuple-element.197.refs_0_), channel_id=1, source_target_pairs={{0,6},{1,7},{2,4},{3,5},{4,2},{5,3},{6,0},{7,1},{8,14},{9,15},{10,... | collective-permute-start | bytes 1572872 | tf_op jit(solution)/shard_map/ppermute | solution.py:60
  387.8 38.4 %collective-permute-start.64 = (bf16[128,2048]{1,0:T(8,128)(2,1)}, bf16[128,2048]{1,0:T(8,128)(2,1)}, u32[]{:S(2)}, u32[]{:S(2)}) collective-permute-start(bf16[128,2048]{1,0:T(8,128)(2,1)} %add_convert_fusion.6), channel_id=1, source_target_pairs={{0,8},{8,0},{16,24},{24,16},{1,9},{9,1},{17,25},{25,17},{2,10},{10... | collective-permute-start | bytes 1572872 | tf_op jit(solution)/shard_map/ppermute | solution.py:65
  400.2 37.5 %collective-permute-start.66 = (bf16[128,2048]{1,0:T(8,128)(2,1)}, bf16[128,2048]{1,0:T(8,128)(2,1)}, u32[]{:S(2)}, u32[]{:S(2)}) collective-permute-start(bf16[128,2048]{1,0:T(8,128)(2,1)} %add_convert_fusion.5), channel_id=1, source_target_pairs={{0,16},{8,24},{16,0},{24,8},{1,17},{9,25},{17,1},{25,9},{2,18},{10... | collective-permute-start | bytes 1572872 | tf_op jit(solution)/shard_map/ppermute | solution.py:65
  408.7 29.0 %collective-permute-start.68 = (bf16[128,2048]{1,0:T(8,128)(2,1)}, bf16[128,2048]{1,0:T(8,128)(2,1)}, u32[]{:S(2)}, u32[]{:S(2)}) collective-permute-start(bf16[128,2048]{1,0:T(8,128)(2,1)} %add_convert_fusion.4), channel_id=1, source_target_pairs={{0,24},{8,16},{16,8},{24,0},{1,25},{9,17},{17,9},{25,1},{2,26},{10... | collective-permute-start | bytes 1572872 | tf_op jit(solution)/shard_map/ppermute | solution.py:65
  448.6 37.0 %collective-permute-start.91 = (bf16[64,2048]{1,0:T(8,128)(2,1)S(1)}, bf16[64,2048]{1,0:T(8,128)(2,1)S(1)}, u32[]{:S(2)}, u32[]{:S(2)}) collective-permute-start(bf16[64,2048]{1,0:T(8,128)(2,1)S(1)} %get-tuple-element.208), channel_id=1, source_target_pairs={{0,0},{2,1},{4,2},{6,3},{1,4},{3,5},{5,6},{7,7},{8,8},{10,9},{12,1... | collective-permute-start | bytes 786440 | tf_op jit(solution)/shard_map/ppermute | solution.py:859
  474.1 66.7 %collective-permute-start.77 = (bf16[128,2048]{1,0:T(8,128)(2,1)}, bf16[128,2048]{1,0:T(8,128)(2,1)S(1)}, u32[]{:S(2)}, u32[]{:S(2)}) collective-permute-start(bf16[128,2048]{1,0:T(8,128)(2,1)} %get-tuple-element.138), channel_id=1, source_target_pairs={{0,1},{1,0},{2,3},{3,2},{4,5},{5,4},{6,7},{7,6},{8,9},{9,8},{10,11... | collective-permute-start | bytes 1572872 | tf_op jit(solution)/shard_map/ppermute | solution.py:55
  476.0 66.3 %collective-permute-start.79 = (bf16[128,2048]{1,0:T(8,128)(2,1)}, bf16[128,2048]{1,0:T(8,128)(2,1)S(1)}, u32[]{:S(2)}, u32[]{:S(2)}) collective-permute-start(bf16[128,2048]{1,0:T(8,128)(2,1)} %get-tuple-element.140), channel_id=1, source_target_pairs={{0,1},{1,0},{2,3},{3,2},{4,5},{5,4},{6,7},{7,6},{8,9},{9,8},{10,11... | collective-permute-start | bytes 1572872 | tf_op jit(solution)/shard_map/ppermute | solution.py:55
  489.4 26.5 %collective-permute-start.84 = (bf16[512,384]{1,0:T(8,128)(2,1)S(1)}, bf16[512,384]{1,0:T(8,128)(2,1)S(1)}, u32[]{:S(2)}, u32[]{:S(2)}) collective-permute-start(bf16[512,384]{1,0:T(8,128)(2,1)S(1)} %copy-done.76), channel_id=1, source_target_pairs={{0,8},{8,0},{16,24},{24,16},{1,9},{9,1},{17,25},{25,17},{2,10},{10... | collective-permute-start | bytes 1179656 | tf_op jit(solution)/shard_map/ppermute | solution.py:65
  499.0 29.8 %collective-permute-start.85 = (bf16[512,384]{1,0:T(8,128)(2,1)S(1)}, bf16[512,384]{1,0:T(8,128)(2,1)S(1)}, u32[]{:S(2)}, u32[]{:S(2)}) collective-permute-start(bf16[512,384]{1,0:T(8,128)(2,1)S(1)} %copy-done.75), channel_id=1, source_target_pairs={{0,16},{8,24},{16,0},{24,8},{1,17},{9,25},{17,1},{25,9},{2,18},{10... | collective-permute-start | bytes 1179656 | tf_op jit(solution)/shard_map/ppermute | solution.py:65
  501.5 27.4 %collective-permute-start.86 = (bf16[512,384]{1,0:T(8,128)(2,1)S(1)}, bf16[512,384]{1,0:T(8,128)(2,1)S(1)}, u32[]{:S(2)}, u32[]{:S(2)}) collective-permute-start(bf16[512,384]{1,0:T(8,128)(2,1)S(1)} %copy-done.74), channel_id=1, source_target_pairs={{0,24},{8,16},{16,8},{24,0},{1,25},{9,17},{17,9},{25,1},{2,26},{10... | collective-permute-start | bytes 1179656 | tf_op jit(solution)/shard_map/ppermute | solution.py:65
  515.9 29.1 %collective-permute-start.81 = (bf16[128,2048]{1,0:T(8,128)(2,1)}, bf16[128,2048]{1,0:T(8,128)(2,1)S(1)}, u32[]{:S(2)}, u32[]{:S(2)}) collective-permute-start(bf16[128,2048]{1,0:T(8,128)(2,1)} %get-tuple-element.142), channel_id=1, source_target_pairs={{0,1},{1,0},{2,3},{3,2},{4,5},{5,4},{6,7},{7,6},{8,9},{9,8},{10,11... | collective-permute-start | bytes 1572872 | tf_op jit(solution)/shard_map/ppermute | solution.py:55
  528.9 70.7 %collective-permute-start.83 = (bf16[128,2048]{1,0:T(8,128)(2,1)}, bf16[128,2048]{1,0:T(8,128)(2,1)}, u32[]{:S(2)}, u32[]{:S(2)}) collective-permute-start(bf16[128,2048]{1,0:T(8,128)(2,1)} %get-tuple-element.144), channel_id=1, source_target_pairs={{0,1},{1,0},{2,3},{3,2},{4,5},{5,4},{6,7},{7,6},{8,9},{9,8},{10,11... | collective-permute-start | bytes 1572872 | tf_op jit(solution)/shard_map/ppermute | solution.py:55
  546.0 53.6 %collective-permute-start.78 = (bf16[128,2048]{1,0:T(8,128)(2,1)}, bf16[128,2048]{1,0:T(8,128)(2,1)}, u32[]{:S(2)}, u32[]{:S(2)}) collective-permute-start(bf16[128,2048]{1,0:T(8,128)(2,1)} %add_convert_fusion.2), channel_id=1, source_target_pairs={{0,2},{1,3},{2,0},{3,1},{4,6},{5,7},{6,4},{7,5},{8,10},{9,11},{10,... | collective-permute-start | bytes 1572872 | tf_op jit(solution)/shard_map/ppermute | solution.py:60
  560.9 38.7 %collective-permute-start.80 = (bf16[128,2048]{1,0:T(8,128)(2,1)}, bf16[128,2048]{1,0:T(8,128)(2,1)}, u32[]{:S(2)}, u32[]{:S(2)}) collective-permute-start(bf16[128,2048]{1,0:T(8,128)(2,1)} %add_convert_fusion.1), channel_id=1, source_target_pairs={{0,4},{1,5},{2,6},{3,7},{4,0},{5,1},{6,2},{7,3},{8,12},{9,13},{10,... | collective-permute-start | bytes 1572872 | tf_op jit(solution)/shard_map/ppermute | solution.py:60
  560.9 38.7 %collective-permute-start.82 = (bf16[128,2048]{1,0:T(8,128)(2,1)}, bf16[128,2048]{1,0:T(8,128)(2,1)}, u32[]{:S(2)}, u32[]{:S(2)}) collective-permute-start(bf16[128,2048]{1,0:T(8,128)(2,1)} %add_convert_fusion), channel_id=1, source_target_pairs={{0,6},{1,7},{2,4},{3,5},{4,2},{5,3},{6,0},{7,1},{8,14},{9,15},{10,... | collective-permute-start | bytes 1572872 | tf_op jit(solution)/shard_map/ppermute | solution.py:60
  617.9 32.6 %collective-permute-start.100 = (bf16[2,2,64,704]{3,2,1,0:T(8,128)(2,1)S(1)}, bf16[2,2,64,704]{3,2,1,0:T(8,128)(2,1)S(1)}, u32[]{:S(2)}, u32[]{:S(2)}) collective-permute-start(bf16[2,2,64,704]{3,2,1,0:T(8,128)(2,1)S(1)} %pad_maximum_fusion.10), channel_id=1, source_target_pairs={{0,16},{8,24},{16,0},{24,8},{1,17},{9,25},{17,1},{25,9},{2,18},{10... | collective-permute-start | bytes 1081352 | tf_op jit(solution)/shard_map/ppermute | solution.py:65
  618.0 32.5 %collective-permute-start.99 = (bf16[2,2,64,704]{3,2,1,0:T(8,128)(2,1)S(1)}, bf16[2,2,64,704]{3,2,1,0:T(8,128)(2,1)S(1)}, u32[]{:S(2)}, u32[]{:S(2)}) collective-permute-start(bf16[2,2,64,704]{3,2,1,0:T(8,128)(2,1)S(1)} %pad_maximum_fusion.9), channel_id=1, source_target_pairs={{0,8},{8,0},{16,24},{24,16},{1,9},{9,1},{17,25},{25,17},{2,10},{10... | collective-permute-start | bytes 1081352 | tf_op jit(solution)/shard_map/ppermute | solution.py:65
  (145 other events, 1765.3 us)
Sparse Core Ops, SparseCore 0:
  21.5 40.1 all-gather.3
  81.9 104.1 all-gather.5
  363.1 85.4 reduce-scatter.6
  594.5 40.3 reduce-scatter.4

commit v3 on v2

--- a/solution.py
+++ b/solution.py
@@ -69,43 +69,42 @@
     return [own] + [send(own, step) for step in range(1, count)]
 
 
-def gather_line(own, send, count):
-    got = {0: own}
-    bit = count // 2
-    while bit:
-        for step in sorted(got):
-            got[step + bit] = send(got[step], bit)
-        bit //= 2
-    return [got[step] for step in range(count)]
-
-
-def gather_cores(own, send, count):
-    blocks = []
-    for block in send(own, count):
-        blocks += [block, core_swap(block)]
-    return blocks
-
-
-def scatter_cores(mine, other, send):
-    total = None
-    for step in list(range(1, len(mine))) + [0]:
-        part = mine[step] + core_swap(other[step]).astype(F32)
-        if step:
-            part = send(part.astype(BF16), step).astype(F32)
-        total = part if total is None else total + part
-    return total
+def ones(step):
+    return step.bit_count()
+
+
+def gather_stage(got, send, count, stage):
+    more = {j: send(got[j & (j - 1)], j & -j) for j in range(count) if ones(j) == stage}
+    return {**got, **more}
+
+
+def scatter_stage(parts, send, stage):
+    parts = dict(parts)
+    for j in sorted(parts, reverse=True):
+        if ones(j) == stage:
+            got = send(parts.pop(j).astype(BF16), j & -j)
+            parts[j & (j - 1)] = parts[j & (j - 1)].astype(F32) + got.astype(F32)
+    return parts
+
+
+def gather_terms(parts, send):
+    return [parts[0]] + [send(parts[step], step) for step in range(1, len(parts))]
 
 
 def scatter_sum(parts, send):
-    total = parts[0].astype(F32)
-    for step in range(1, len(parts)):
-        total = total + send(parts[step], step).astype(F32)
-    return total
-
-
-def exchange(mine, other, send):
+    return sum(part.astype(F32) for part in gather_terms(parts, send))
+
+
+def together(*values):
+    return lax.optimization_barrier(values)
+
+
+def swap_pairs(mine, other):
     got = core_swap(other)
-    pairs = [jnp.stack([mine[step], got[step]]) for step in range(mine.shape[0])]
+    return [jnp.stack([mine[step], got[step]]) for step in range(mine.shape[0])]
+
+
+def exchange(pairs, send):
     return pairs[:1] + [send(pairs[step], step) for step in range(1, len(pairs))]
 
 
@@ -147,10 +146,26 @@
     return pl.CostEstimate(flops=int(flops), bytes_accessed=int(moved), transcendentals=int(exps))
 
 
-def pack_kernel(planes, chips, piece, place, gate, up, query, key, value, gu_mine, gu_other, qkv_mine, qkv_other):
+def whole_lanes(width):
+    return -(-width // 128) * 128
+
+
+def head_order(planes, members):
+    chips = members // 2
+    if HEADS == planes * members and planes == chips:
+        return [
+            [f // 2 * members + 2 * ((f // 2) ^ step) + f % 2 for step in range(chips)]
+            for f in range(members)
+        ]
+    share = HEADS // members
+    return [list(range(f * share, (f + 1) * share)) for f in range(members)]
+
+
+def pack_kernel(planes, chips, piece, place, gains, gate, up, query, key, value, *outs):
+    gu_mine, gu_other, qkv_mine, qkv_other = outs
     plane, chip, core = place[0], place[1], place[2]
-    own_q = query.shape[1] // (2 * chips)
     sharing = 2 * chips // KV_HEADS
+    heads = head_order(planes, 2 * chips)
 
     def put(mine, other, core_to, index, block):
         @pl.when(core == core_to)
@@ -161,38 +176,42 @@
         def _():
             other[index] = block
 
+    def rounded(block, row):
+        return (block.astype(BF16).astype(F32) * gains[:, row : row + 1]).astype(BF16)
+
     for to in range(2 * chips):
         head = slice(to // sharing * HEAD_DIM, (to // sharing + 1) * HEAD_DIM)
-        block = jnp.concatenate(
-            [query[:, to * own_q : (to + 1) * own_q], key[:, head], value[:, head]], 1
-        )
-        put(qkv_mine, qkv_other, to % 2, (to // 2) ^ chip, block.astype(BF16))
+        columns = [query[:, h * HEAD_DIM : (h + 1) * HEAD_DIM] for h in heads[to]]
+        block = jnp.concatenate(columns + [key[:, head], value[:, head]], 1)
+        put(qkv_mine, qkv_other, to % 2, (to // 2) ^ chip, rounded(block, 0))
     for side, weight in enumerate((gate, up)):
         for to in range(2 * planes):
             starts = [((to // 2 * chips + c) * 2 + to % 2) * piece for c in range(chips)]
-            block = jnp.concatenate([weight[:, s : s + piece] for s in starts], 1).astype(BF16)
-            put(
-                gu_mine.at[:, side],
-                gu_other.at[:, side],
-                to % 2,
-                (to // 2) ^ plane,
-                block,
-            )
-
-
-def pack(place, planes, chips, gate, up, query, key, value):
+            columns = [weight[:, s : s + piece] for s in starts]
+            spare = gu_mine.shape[-1] - chips * piece
+            if spare:
+                columns.append(jnp.zeros((weight.shape[0], spare), F32))
+            block = rounded(jnp.concatenate(columns, 1), 1)
+            put(gu_mine.at[:, side], gu_other.at[:, side], to % 2, (to // 2) ^ plane, block)
+
+
+def whole_lanes(width):
+    return -(-width // 128) * 128
+
+
+def pack(place, planes, chips, gains, gate, up, query, key, value):
     rows, hidden = gate.shape
-    gu = shape_of((planes, 2, rows, hidden // (2 * planes)))
+    gu = shape_of((planes, 2, rows, whole_lanes(hidden // (2 * planes))))
     qkv = shape_of((chips, rows, query.shape[1] // (2 * chips) + PAIR))
     return pl.pallas_call(
         functools.partial(pack_kernel, planes, chips, hidden // (2 * planes * chips)),
         out_shape=(gu, gu, qkv, qkv),
-        in_specs=[SMEM] + [VMEM] * 5,
+        in_specs=[SMEM] + [VMEM] * 6,
         out_specs=(VMEM,) * 4,
         compiler_params=params(),
         cost_estimate=cost(0, rows * hidden * 12),
         name="pack",
-    )(place, gate, up, query, key, value)
+    )(place, gains, gate, up, query, key, value)
 
 
 def gather_rows_kernel(members, place, *refs):
@@ -222,47 +241,48 @@
     )(jnp.stack([first, core]), *pairs)
 
 
-def spread_rows_kernel(place, whole, mine, other):
+def spread_rows_kernel(place, *refs):
+    terms, (mine, other) = refs[:-2], refs[-2:]
     first, core = place[0], place[1]
     count = mine.shape[0]
     rows = mine.shape[-2]
     for step in range(count):
         for side, out in enumerate((mine, other)):
             at = pl.ds(pl.multiple_of(((first ^ step) * 2 + (core ^ side)) * rows, 16), rows)
-            if len(whole.shape) == 2:
-                out[step] = whole[at, :].astype(BF16)
+            if len(mine.shape) == 3:
+                out[step] = sum(t[at, :].astype(F32) for t in terms).astype(BF16)
             else:
                 for part in range(2):
-                    out[step, part] = whole[part, at, :].astype(BF16)
-
-
-def spread_rows(first, core, whole, count):
+                    out[step, part] = sum(t[part, at, :].astype(F32) for t in terms).astype(BF16)
+
+
+def spread_rows(first, core, terms, count):
+    whole = terms[0]
     rows = whole.shape[-2] // (2 * count)
     out = shape_of((count,) + whole.shape[:-2] + (rows, whole.shape[-1]))
     return pl.pallas_call(
         spread_rows_kernel,
         out_shape=(out, out),
-        in_specs=[SMEM, VMEM],
+        in_specs=[SMEM] + [VMEM] * len(terms),
         out_specs=(VMEM, VMEM),
         compiler_params=params(),
         cost_estimate=cost(0, whole.size * 6),
         name="spread_rows",
-    )(jnp.stack([first, core]), whole)
-
-
-def attend_kernel(members, pairs, planes, place, start_ref, cos_ref, sin_ref, gain_ref, *refs):
-    tokens, refs = refs[:members], refs[members:]
+    )(jnp.stack([first, core]), *terms)
+
+
+def attend_kernel(members, pairs, planes, place, start_ref, cos_ref, sin_ref, *refs):
+    tokens, refs = refs[:2], refs[2:]
     weights, refs = refs[:planes], refs[planes:]
     normed_ref, q_ref, kv_ref, o_ref = refs
     plane, index = place[0], place[1]
-    rows = tokens[0].shape[0]
+    rows = tokens[0].shape[1]
     length = rows * members
     even = lane_ids((rows, PAIR)) < HEAD_DIM
     depth = weights[0].shape[0]
     for j in range(members):
-        values = tokens[j][...].astype(F32)
-        normed = values * rms_scale(values) * gain_ref[...]
-        normed_ref[j * rows : (j + 1) * rows, :] = normed.astype(BF16)
+        values = tokens[j % 2][j // 2].astype(F32)
+        normed_ref[j * rows : (j + 1) * rows, :] = (values * rms_scale(values)).astype(BF16)
     block = min(2 * rows, 256)
     per = block // rows
     for first in range(0, length, block):
@@ -310,9 +330,9 @@
                 o_ref[there, lanes] = mixed[part * rows : (part + 1) * rows, :]
 
 
-def attend(place, tokens, weights, gain, start, cosine, sine):
-    members, planes = len(tokens), len(weights)
-    rows, width = tokens[0].shape
+def attend(place, mine, other, weights, start, cosine, sine):
+    members, planes = 2 * mine.shape[0], len(weights)
+    rows, width = mine.shape[1:]
     length = members * rows
     pairs = weights[0].shape[1] // PAIR - 1
     return pl.pallas_call(
@@ -323,7 +343,7 @@
             shape_of((length, PAIR)),
             shape_of((length, pairs * PAIR)),
         ),
-        in_specs=[SMEM] + [VMEM] * (4 + members + planes),
+        in_specs=[SMEM] + [VMEM] * (5 + planes),
         out_specs=(VMEM,) * 4,
         compiler_params=params(),
         cost_estimate=cost(
@@ -332,7 +352,7 @@
             length * length * pairs,
         ),
         name="attend",
-    )(place, start, cosine, sine, gain, *tokens, *weights)
+    )(place, start, cosine, sine, mine, other, *weights)
 
 
 def attend_back_kernel(members, pairs, place, start_ref, cos_ref, sin_ref, q_ref, kv_ref, w_ref, *refs):
@@ -518,37 +538,53 @@
     )(left, *grads)
 
 
-def weight_copies(planes, chips, gu_ref, gu, sem):
+def weight_copies(place, planes, sides, gu, sem):
+    chips = len(sides)
     rows = gu.shape[1] // (planes * chips)
-    return [
-        pltpu.make_async_copy(
-            gu_ref.at[chip, side, pl.ds(plane * rows, rows), :],
-            gu.at[side, pl.ds((plane * chips + chip) * rows, rows), :],
-            sem.at[side],
-        )
-        for side in range(2)
-        for chip in range(chips)
-        for plane in range(planes)
-    ]
-
-
-def feed_kernel(planes, chips, x_mine, x_other, g_mine, g_other, gu_ref, down_ref, *refs):
-    (hidden_ref, gate_ref, up_ref, out_mine, out_other, dx_mine, dx_other, gu, down, sem) = refs
-    rows = x_mine.shape[0]
-    copies = weight_copies(planes, chips, gu_ref, gu, sem)
+    copies = []
+    for side in range(2):
+        for step, pair in enumerate(sides):
+            for plane in range(planes):
+                to = (plane * chips + (place[1] ^ step)) * rows
+                copies.append(
+                    pltpu.make_async_copy(
+                        pair[side].at[pl.ds(plane * rows, rows), :],
+                        gu.at[side, pl.ds(pl.multiple_of(to, 16), rows), :],
+                        sem.at[side],
+                    )
+                )
+    return copies
+
+
+def feed_kernel(planes, layout, count, place, *refs):
+    x, refs = refs[:count], refs[count:]
+    grads, refs = refs[:count], refs[count:]
+    blocks, refs = refs[: len(layout)], refs[len(layout) :]
+    chips = 1 + max(step for step, _ in layout)
+    sides = [[None, None] for _ in range(chips)]
+    for (step, side), ref in zip(layout, blocks):
+        for part in (0, 1) if side is None else (side,):
+            sides[step][part] = ref.at[part] if side is None else ref
+    down_ref, hidden_ref, gate_ref, up_ref = refs[:4]
+    outs, refs = refs[4 : 4 + count], refs[4 + count :]
+    dxs, refs = refs[:count], refs[count:]
+    gu, down, sem = refs
+    rows = x[0].shape[0]
+    units = down.shape[0]
+    copies = weight_copies(place, planes, sides, gu, sem)
     down_copy = pltpu.make_async_copy(down_ref, down, sem.at[2])
     half = len(copies) // 2
     for copy in copies:
         copy.start()
     down_copy.start()
-    x = jnp.concatenate([x_mine[...], x_other[...]], 0)
-    grad = jnp.concatenate([g_mine[...], g_other[...]], 0)
+    x = jnp.concatenate([part[...] for part in x], 0)
+    grad = jnp.concatenate([part[...] for part in grads], 0)
     for copy in copies[:half]:
         copy.wait()
-    gate = matmul(x, gu[0])
+    gate = matmul(x, gu[0, :, :units])
     for copy in copies[half:]:
         copy.wait()
-    up = matmul(x, gu[1])
+    up = matmul(x, gu[1, :, :units])
     down_copy.wait()
     dhidden = matmul_nt(grad, down[...])
     sigmoid = 1.0 / (1.0 + jnp.exp(-gate))
@@ -561,57 +597,67 @@
     block = 512
     for first in range(0, x.shape[1], block):
         columns = slice(first, first + block)
-        dx = matmul_nt(dgate, gu[0, columns, :]) + matmul_nt(dup, gu[1, columns, :])
-        dx_mine[:, columns] = dx[:rows, :]
-        dx_other[:, columns] = dx[rows:, :].astype(BF16)
+        dx = matmul_nt(dgate, gu[0, columns, :units]) + matmul_nt(dup, gu[1, columns, :units])
+        for j in range(count):
+            dxs[j][:, columns] = dx[j * rows : (j + 1) * rows, :].astype(dxs[j].dtype)
     for first in range(0, x.shape[1], block):
         columns = slice(first, first + block)
         out = matmul(hidden, down[:, columns])
-        out_mine[:, columns] = out[:rows, :]
-        out_other[:, columns] = out[rows:, :].astype(BF16)
-
-
-def feed(planes, chips, x, grad, w_gate_up, w_down):
+        for j in range(count):
+            outs[j][:, columns] = out[j * rows : (j + 1) * rows, :].astype(outs[j].dtype)
+
+
+def feed(place, planes, x, grad, w_gate_up, w_down):
+    layout, blocks = zip(*w_gate_up)
     rows, width = x[0].shape
     units = w_down.shape[0]
-    part = shape_of((2 * rows, units))
-    return pl.pallas_call(
-        functools.partial(feed_kernel, planes, chips),
-        out_shape=(part,) * 3 + (shape_of((rows, width), F32), shape_of((rows, width))) * 2,
-        in_specs=[VMEM] * 4 + [ANY] * 2,
-        out_specs=(VMEM,) * 7,
+    count = len(x)
+    part = shape_of((count * rows, units))
+    terms = (shape_of((rows, width), F32), shape_of((rows, width))) * (count // 2)
+    got = pl.pallas_call(
+        functools.partial(feed_kernel, planes, layout, count),
+        out_shape=(part,) * 3 + terms * 2,
+        in_specs=[SMEM] + [VMEM] * (2 * count) + [ANY] * (len(blocks) + 1),
+        out_specs=(VMEM,) * (3 + 2 * count),
         scratch_shapes=[
-            pltpu.VMEM((2, width, units), BF16),
+            pltpu.VMEM((2, width, blocks[0].shape[-1]), BF16),
             pltpu.VMEM((units, width), BF16),
             pltpu.SemaphoreType.DMA((3,)),
         ],
         compiler_params=params(),
-        cost_estimate=cost(24 * rows * width * units, 6 * width * units, 2 * rows * units),
+        cost_estimate=cost(12 * count * rows * width * units, 6 * width * units, rows * units),
         name="feed",
-    )(*x, *grad, w_gate_up, w_down)
-
-
-def feed_grad_kernel(planes, chips, count, *refs):
+    )(place, *x, *grad, *blocks, w_down)
+    return got[:3], got[3 : 3 + count], got[3 + count :]
+
+
+def feed_grad_kernel(planes, chips, count, place, *refs):
     x, refs = refs[:count], refs[count:]
     gates, refs = refs[: count // 2], refs[count // 2 :]
     ups, refs = refs[: count // 2], refs[count // 2 :]
-    out, held, sem = refs
+    outs, (held, sem) = refs[:-2], refs[-2:]
     width = held.shape[1]
+    units = gates[0].shape[1]
     block = 256
     rows = width // (planes * chips)
     copies = []
     dgate = jnp.concatenate([gate[...] for gate in gates], 0)
     dup = jnp.concatenate([up[...] for up in ups], 0)
-    for first in range(0, width, block):
-        columns = slice(first, first + block)
-        left = jnp.concatenate([part[:, columns] for part in x], 0)
-        held[0, columns, :] = matmul_tn(left, dgate).astype(BF16)
-        held[1, columns, :] = matmul_tn(left, dup).astype(BF16)
-        for at in range(first // rows, (first + block) // rows):
+    if held.shape[2] > units:
+        held[:, :, units:] = jnp.zeros((2, width, held.shape[2] - units), BF16)
+    for plane in range(planes):
+        for first in range(plane * chips * rows, (plane + 1) * chips * rows, block):
+            columns = slice(first, first + block)
+            left = jnp.concatenate([part[:, columns] for part in x], 0)
+            held[0, columns, :units] = matmul_tn(left, dgate).astype(BF16)
+            held[1, columns, :units] = matmul_tn(left, dup).astype(BF16)
+        for step in range(chips):
+            at = (plane * chips + (place[1] ^ step)) * rows
             for side in range(2):
+                to = outs[0].at[side] if step == 0 else outs[2 * step - 1 + side]
                 copy = pltpu.make_async_copy(
-                    held.at[side, pl.ds(at * rows, rows), :],
-                    out.at[at % chips, side, pl.ds(at // chips * rows, rows), :],
+                    held.at[side, pl.ds(pl.multiple_of(at, 16), rows), :],
+                    to.at[pl.ds(plane * rows, rows), :],
                     sem,
                 )
                 copy.start()
@@ -620,60 +666,73 @@
         copy.wait()
 
 
-def feed_grad(planes, chips, x, gates, ups):
+def feed_grad(place, planes, chips, x, gates, ups, lanes):
     width, units = x[0].shape[1], gates[0].shape[1]
     tokens = x[0].shape[0] * len(x)
+    own = shape_of((2, width // chips, lanes))
+    part = shape_of((width // chips, lanes))
+    outs = (own,) + (part,) * (2 * chips - 2)
     return pl.pallas_call(
         functools.partial(feed_grad_kernel, planes, chips, len(x)),
-        out_shape=shape_of((chips, 2, width // chips, units)),
-        in_specs=[VMEM] * (len(x) + len(gates) + len(ups)),
-        out_specs=ANY,
-        scratch_shapes=[pltpu.VMEM((2, width, units), BF16), pltpu.SemaphoreType.DMA],
+        out_shape=outs,
+        in_specs=[SMEM] + [VMEM] * (len(x) + len(gates) + len(ups)),
+        out_specs=(ANY,) * len(outs),
+        scratch_shapes=[pltpu.VMEM((2, width, lanes), BF16), pltpu.SemaphoreType.DMA],
         compiler_params=params(),
         cost_estimate=cost(4 * tokens * width * units, 4 * width * units),
         name="feed_grad",
-    )(*x, *gates, *ups)
-
-
-def feed_adam_kernel(planes, chips, piece, place, *refs):
+    )(place, *x, *gates, *ups)
+
+
+def feed_adam_kernel(planes, chips, piece, place, gains, *refs):
     blocks, refs = refs[:planes], refs[planes:]
     ins, outs = refs[:6], refs[6:12]
-    held = refs[12]
+    gain_grad, held = refs[12], refs[13]
     plane, core = place[0], place[2]
     for step in range(planes):
         for side in range(2):
             held[plane ^ step, core ^ side] = blocks[step][side].astype(F32)
+    gain = gains[:, 1:2]
+    total = jnp.zeros(gain.shape, F32)
     for part in range(2):
         w, m, u = ins[3 * part : 3 * part + 3]
-        new = outs[3 * part : 3 * part + 3]
-        for to in range(2 * planes):
-            grad_block = held[to // 2, to % 2, part]
-            for c in range(chips):
-                at = ((to // 2 * chips + c) * 2 + to % 2) * piece
-                columns = slice(at, at + piece)
-                grad = grad_block[:, c * piece : (c + 1) * piece]
-                updated = adam_step(w[:, columns], m[:, columns], u[:, columns], grad, 0.02)
-                for out, value in zip(new, updated):
-                    out[:, columns] = value
-
-
-def feed_adam(place, planes, chips, blocks, arrays):
+        grad = jnp.concatenate(
+            [
+                held[far, c, part, :, at * piece : (at + 1) * piece]
+                for far in range(planes)
+                for at in range(chips)
+                for c in range(2)
+            ],
+            1,
+        )
+        weight = w[...]
+        total = total + jnp.sum(weight.astype(BF16).astype(F32) * grad, -1, keepdims=True)
+        updated = adam_step(weight, m[...], u[...], grad * gain, 0.02)
+        for out, value in zip(outs[3 * part : 3 * part + 3], updated):
+            out[...] = value
+    gain_grad[...] = jnp.broadcast_to(total, gain_grad.shape)
+
+
+def feed_adam(place, planes, chips, gains, blocks, arrays):
     rows, hidden = arrays[0].shape
     piece = hidden // (2 * planes * chips)
     tile = min(rows, 16)
     whole = pl.BlockSpec((tile, hidden), lambda i: (i, 0))
-    block = pl.BlockSpec((2, 2, tile, piece * chips), lambda i: (0, 0, i, 0))
-    return pl.pallas_call(
+    lanes = blocks[0].shape[-1]
+    block = pl.BlockSpec((2, 2, tile, lanes), lambda i: (0, 0, i, 0))
+    two = pl.BlockSpec((tile, 2), lambda i: (i, 0))
+    *new, gain_grad = pl.pallas_call(
         functools.partial(feed_adam_kernel, planes, chips, piece),
         grid=(rows // tile,),
-        out_shape=(shape_of((rows, hidden), F32),) * 6,
-        in_specs=[SMEM] + [block] * planes + [whole] * 6,
-        out_specs=(whole,) * 6,
-        scratch_shapes=[pltpu.VMEM((planes, 2, 2, tile, piece * chips), F32)],
+        out_shape=(shape_of((rows, hidden), F32),) * 6 + (shape_of((rows, 128), F32),),
+        in_specs=[SMEM, two] + [block] * planes + [whole] * 6,
+        out_specs=(whole,) * 6 + (pl.BlockSpec((tile, 128), lambda i: (i, 0)),),
+        scratch_shapes=[pltpu.VMEM((planes, 2, 2, tile, lanes), F32)],
         compiler_params=params(),
         cost_estimate=cost(40 * rows * hidden, 52 * rows * hidden),
         name="feed_adam",
-    )(place, *blocks, *arrays)
+    )(place, gains, *blocks, *arrays)
+    return tuple(new), gain_grad[:, 0]
 
 
 def segment_starts(lengths_row, length):
@@ -743,160 +802,327 @@
     sharing = members // KV_HEADS
     same_core = [list(range(c, members, 2)) for c in range(2)]
 
-    def chip_all(own, size):
-        return gather(own, chip_send, size)
-
-    def plane_all(own, size):
-        return gather_line(own, plane_send, size)
-
+    stages = planes.bit_length() - 1
+    chip_stages = chips.bit_length() - 1
+    everyone = range(planes)
+    heads = head_order(planes, members)
+    head_rows = HEADS == planes * members and planes == chips
+
+    def both_cores(blocks):
+        return [b for block in blocks for b in (block, core_swap(block))]
+
+    def over_cores(terms):
+        return terms[0] + core_swap(terms[1]).astype(F32)
+
+    gains = norm_gains.astype(BF16).astype(F32)
+    gain_columns = gains.T
     gu_mine, gu_other, qkv_mine, qkv_other = pack(
-        place, planes, chips, gate_weight, up_weight, query_weight, key_weight, value_weight
-    )
-    tokens_all = gather_cores(tokens, chip_all, chips)
-    qkv_rows = gather_rows(chip, core, exchange(qkv_mine, qkv_other, chip_send))
-    gate_up_rows = gather_rows(plane, core, exchange(gu_mine, gu_other, plane_send))
+        place,
+        planes,
+        chips,
+        gain_columns,
+        gate_weight,
+        up_weight,
+        query_weight,
+        key_weight,
+        value_weight,
+    )
     w_down = lax.all_gather(
         down_weight.astype(BF16), "fsdp", axis=0, tiled=True, axis_index_groups=same_core
     )
-    gate_up_rows, w_down = lax.optimization_barrier((gate_up_rows, w_down))
-    w_gate_up = lax.all_gather(
-        gate_up_rows, "fsdp", axis=0, tiled=False, axis_index_groups=same_core
-    )
-    w_qkv = plane_all(qkv_rows, planes)
-
-    gains = norm_gains.astype(BF16).astype(F32)
-    gains = by_offset(jnp.stack(gather(gains, plane_send, planes)), plane)
-    gains = jnp.stack(gather_cores(gains, chip_all, chips))
-    gains = jnp.transpose(by_offset(gains, index), (2, 1, 0, 3)).reshape(2, width)
-
+    gu_mine, gu_other, qkv_mine, qkv_other, output_rows = together(
+        gu_mine, gu_other, qkv_mine, qkv_other, output_weight
+    )
+
+    qkv_pairs = swap_pairs(qkv_mine, qkv_other)
+    gu_pairs = swap_pairs(gu_mine, gu_other)
+    out_rows = gather_stage({0: output_rows.astype(BF16)}, plane_send, planes, 1)
+    qkv_pairs, gu_pairs, out_rows = together(qkv_pairs, gu_pairs, out_rows)
+
+    qkv_got = exchange(qkv_pairs, chip_send)
+    gu_near = plane_send(gu_pairs[1], 1)
+    for stage in range(2, stages + 1):
+        out_rows = gather_stage(out_rows, plane_send, planes, stage)
+    out_rows = jnp.stack([out_rows[far] for far in everyone])
+    qkv_got, gu_pairs, gu_near, tokens, out_rows = together(
+        qkv_got, gu_pairs, gu_near, tokens, out_rows
+    )
+
+    gu_got = [gu_pairs[0], gu_near] + [
+        plane_send(gu_pairs[step], step) for step in range(2, planes)
+    ]
+    out_got = []
+    token_blocks = [tokens]
+    for step in range(chips):
+        if head_rows:
+            rows = lax.dynamic_index_in_dim(out_rows, (chip ^ step) ^ plane, 0, keepdims=False)
+            if step:
+                both = chip_send(jnp.concatenate([tokens, rows]), step)
+                token_blocks.append(both[:count])
+                rows = both[count:]
+            out_got.append(rows)
+        elif step:
+            token_blocks.append(chip_send(tokens, step))
     start = segment_starts(seq_lengths[0], length)
     cosine, sine = rope_tables(jnp.arange(length, dtype=jnp.int32) - start)
-
+    gu_got, qkv_got, token_blocks, out_got, cosine, sine, w_down = together(
+        gu_got, qkv_got, token_blocks, out_got, cosine, sine, w_down
+    )
+
+    tokens_mine = jnp.stack(token_blocks)
+    tokens_other = core_swap(tokens_mine)
+    gu_rows = gather_rows(plane, core, gu_got)
+    qkv_rows = gather_rows(chip, core, qkv_got)
+    steps = [step for step in range(chips) if ones(step) <= 1]
+    w_gate_up = [gu_rows] + [chip_send(gu_rows, step) for step in steps[1:]]
+    w_qkv = {0: qkv_rows}
+    for stage in range(1, stages + 1):
+        w_qkv = gather_stage(w_qkv, plane_send, planes, stage)
+    w_qkv = [w_qkv[far] for far in everyone]
+    w_gate_up, w_qkv, out_grad, tokens_mine, tokens_other, out_rows = together(
+        w_gate_up, w_qkv, out_grad, tokens_mine, tokens_other, out_rows
+    )
+
+    gate_up = {step: (block[0], block[1]) for step, block in zip(steps, w_gate_up)}
+    for stage in range(2, chip_stages + 1):
+        for step in range(1, chips):
+            if ones(step) == stage:
+                top = 1 << (step.bit_length() - 1)
+                gate_up[step] = (
+                    chip_send(gate_up[step & (step - 1)][0], step & -step),
+                    chip_send(gate_up[step ^ top][1], top),
+                )
+    more = [step for step in range(chips) if ones(step) > 1]
+    layout = [(step, None) for step in steps] + [(step, side) for step in more for side in range(2)]
+    w_gate_up = w_gate_up + [gate_up[step][side] for step in more for side in range(2)]
+    normed, queries, keys_values, attended = attend(
+        spot, tokens_mine, tokens_other, w_qkv, start[:, None], cosine, sine
+    )
+    out_grad_blocks = gather_stage({0: out_grad}, plane_send, planes, 1)
     hop = members // planes
-    out_rows = jnp.stack(plane_all(output_weight.astype(BF16), planes))
     own_plane = index // hop
 
     def out_route(turn_no):
         return [(i, ((turn_no + i) % planes) * hop + i // planes) for i in range(members)]
 
-    w_output = jnp.zeros((planes, slice_rows, width), BF16)
-    for turn_no in range(planes):
-        sent = lax.dynamic_index_in_dim(
-            out_rows, ((turn_no + index) % planes) ^ plane, 0, keepdims=False
-        )
-        got = lax.ppermute(sent, "fsdp", out_route(turn_no))
-        spare = (own_plane + planes - turn_no) % planes
-        w_output = lax.dynamic_update_index_in_dim(w_output, got, spare, 0)
-    w_output = w_output.reshape(planes * slice_rows, width)
-    out_grad_all = gather_cores(out_grad, plane_all, planes)
-
-    normed, queries, keys_values, attended = attend(
-        spot, tokens_all, w_qkv, gains[:1], start[:, None], cosine, sine
-    )
+    if head_rows:
+        w_output = jnp.concatenate(out_got)
+    else:
+        w_output = jnp.zeros((planes, slice_rows, width), BF16)
+        for turn_no in range(planes):
+            sent = lax.dynamic_index_in_dim(
+                out_rows, ((turn_no + index) % planes) ^ plane, 0, keepdims=False
+            )
+            got = lax.ppermute(sent, "fsdp", out_route(turn_no))
+            spare = (own_plane + planes - turn_no) % planes
+            w_output = lax.dynamic_update_index_in_dim(w_output, got, spare, 0)
+        w_output = w_output.reshape(planes * slice_rows, width)
+    w_gate_up, attended, out_grad_blocks, w_output = together(
+        w_gate_up, attended, out_grad_blocks, w_output
+    )
+
+    w_gate_up = list(zip(layout, w_gate_up))
+    for stage in range(2, stages + 1):
+        out_grad_blocks = gather_stage(out_grad_blocks, plane_send, planes, stage)
     own_tokens = tokens.astype(F32)
-    resid = own_tokens + scatter_cores(*project(attended, w_output, chips), chip_send)
+    mixed = [over_cores(terms) for terms in zip(*project(attended, w_output, chips))]
+    mixed = mixed[:1] + [
+        chip_send(mixed[step].astype(BF16), step).astype(F32) for step in range(1, chips)
+    ]
+    resid = own_tokens + sum(mixed[1:], mixed[0])
+    resid, out_grad_blocks = together(resid, out_grad_blocks)
+
     scale_two = rms_scale(resid)
-    own_normed_two = (resid * scale_two * gains[1]).astype(BF16)
-
-    normed_two = gather_cores(own_normed_two, plane_all, planes)
-    fed = [
-        feed(
-            planes,
-            chips,
-            normed_two[2 * step : 2 * step + 2],
-            out_grad_all[2 * step : 2 * step + 2],
-            w_gate_up,
-            w_down,
-        )
-        for step in range(planes)
-    ]
-    hidden, grad_gate, grad_up, out_mine, out_other, dx_mine, dx_other = zip(*fed)
-    grad_normed_two = scatter_cores(dx_mine, dx_other, plane_send)
-    weighted_two = grad_normed_two * gains[1]
-    grad_gain_two = jnp.sum(grad_normed_two * resid * scale_two, 0)
+    own_normed_two = (resid * scale_two).astype(BF16)
+    normed_blocks = gather_stage({0: own_normed_two}, plane_send, planes, 1)
+    out_grad_all = both_cores([out_grad_blocks[far] for far in everyone])
+    normed_blocks, out_grad_all = together(normed_blocks, out_grad_all)
+
+    for stage in range(2, stages + 1):
+        normed_blocks = gather_stage(normed_blocks, plane_send, planes, stage)
+    normed_two = both_cores([normed_blocks[far] for far in everyone])
+    normed_two, out_grad_all = together(normed_two, out_grad_all)
+
+    order = sorted(everyone, key=lambda j: (-ones(j), -j))
+    x = {far: normed_two[2 * far : 2 * far + 2] for far in everyone}
+    fed = {}
+    sums = ({}, {})
+    last = []
+    moved_here = {}
+    for turn_no, far in enumerate(order):
+        span = slice(2 * far, 2 * far + 2)
+        fed[far] = feed(place, planes, x[far], out_grad_all[span], w_gate_up, w_down)
+        pair, moved = None, None
+        if turn_no >= 1:
+            pair = tuple(over_cores(fed[order[turn_no - 1]][side]) for side in (2, 1))
+        if turn_no >= 2:
+            near = order[turn_no - 2]
+            if ones(near) > 1:
+                moved = plane_send(sums[0][near].astype(BF16), near & -near)
+            else:
+                last.append(plane_send(sums[0][near].astype(BF16), near))
+        later = {j: x[j] for j in order[turn_no + 1 :]}
+        fed[far], later, pair, moved = together(fed[far], later, pair, moved)
+        x.update(later)
+        for side in (0, 1):
+            if pair is not None:
+                sums[side][order[turn_no - 1]] = pair[side]
+        if moved is not None:
+            moved_here.setdefault(near & (near - 1), []).append(moved)
+        for target in list(moved_here):
+            if target in sums[0]:
+                for part in moved_here.pop(target):
+                    sums[0][target] = sums[0][target] + part.astype(F32)
+    last.append(plane_send(sums[0][order[-2]].astype(BF16), order[-2]))
+    sums[1][0] = over_cores(fed[0][1])
+    grad_normed_two = over_cores(fed[0][2])
+    hidden, grad_gate, grad_up = zip(*[fed[far][0] for far in everyone])
+    lanes = w_gate_up[0][1].shape[-1]
+    grads = feed_grad(place, planes, chips, normed_two, grad_gate, grad_up, lanes)
+    grad_normed_two, last, grads, result = together(grad_normed_two, last, grads, sums[1])
+    grad_normed_two = sum([part.astype(F32) for part in last], grad_normed_two)
+
     grad_resid = (
         out_grad.astype(F32)
-        + scale_two * weighted_two
+        + scale_two * grad_normed_two
         - resid
         * (scale_two * scale_two * scale_two)
-        * jnp.mean(weighted_two * resid, -1, keepdims=True)
-    )
-    grad_attn_out = gather_cores(grad_resid.astype(BF16), chip_all, chips)
-
-    grad_gate_up = feed_grad(planes, chips, normed_two, grad_gate, grad_up)
-    grad_gate_up = lax.psum_scatter(
-        grad_gate_up, "fsdp", scatter_dimension=0, tiled=False, axis_index_groups=same_core
-    )
+        * jnp.mean(grad_normed_two * resid, -1, keepdims=True)
+    )
+    own_grad = grad_resid.astype(BF16)
+    own_grad, result, hidden = together(own_grad, result, hidden)
+
+    grad_blocks = gather(own_grad, chip_send, chips)
+    for stage in range(stages, 1, -1):
+        result = scatter_stage(result, plane_send, stage)
     grad_down = rows_grad(jnp.concatenate(hidden), out_grad_all)
-    grad_down, grad_gate_up = lax.optimization_barrier((grad_down, grad_gate_up))
+    grad_blocks, result, grad_down = together(grad_blocks, result, grad_down)
+
+    grad_attn_out = both_cores(grad_blocks)
+    grad_output = rows_grad(attended, grad_attn_out).reshape(planes, slice_rows, width)
+    grad_output, grad_attn_out, grads, result = together(
+        grad_output, grad_attn_out, grads, result
+    )
+
+    result = scatter_stage(result, plane_send, 1)[0]
+    grad_gate_up = {step: grads[2 * step - 1 : 2 * step + 1] for step in range(1, chips)}
+
+    def plus(one, two):
+        return (one.astype(F32) + two.astype(F32)).astype(BF16)
+
+    for stage in range(chip_stages, 1, -1):
+        for step in range(chips - 1, 0, -1):
+            if ones(step) == stage:
+                top = 1 << (step.bit_length() - 1)
+                low = step & (step - 1)
+                gate, up = grad_gate_up.pop(step)
+                gate, up = chip_send(gate, step & -step), chip_send(up, top)
+                grad_gate_up[low] = (plus(grad_gate_up[low][0], gate), grad_gate_up[low][1])
+                low = step ^ top
+                grad_gate_up[low] = (grad_gate_up[low][0], plus(grad_gate_up[low][1], up))
+    grad_gate_up = {step: jnp.stack(pair) for step, pair in grad_gate_up.items()}
+    grad_qkv = attend_back(
+        spot, queries, keys_values, w_output, grad_attn_out, start[None, :], cosine, sine
+    )
+    grad_qkv, result, grad_gate_up = together(grad_qkv, result, grad_gate_up)
+    result = (resid + result).astype(BF16)
+
+    grad_w_qkv = qkv_grad(spot, normed, grad_qkv, planes)
+    grad_qkv, grad_w_qkv, grad_gate_up = together(grad_qkv, grad_w_qkv, grad_gate_up)
+
+    grad_gate_up = [grads[0]] + [chip_send(part, step) for step, part in grad_gate_up.items()]
+    grad_w_qkv = dict(enumerate(grad_w_qkv))
+    for stage in range(stages, 0, -1):
+        grad_w_qkv = scatter_stage(grad_w_qkv, plane_send, stage)
+    mixed = [over_cores(terms) for terms in zip(*project_back(spot, grad_qkv, w_qkv, chips))]
+    mixed, grad_w_qkv, grad_gate_up, grad_down, grad_output = together(
+        mixed, grad_w_qkv[0], grad_gate_up, grad_down, grad_output
+    )
+
     grad_down_weight = lax.psum_scatter(
         grad_down, "fsdp", scatter_dimension=0, tiled=True, axis_index_groups=same_core
     ).astype(F32)
-    grad_gate_up = exchange(*spread_rows(plane, core, grad_gate_up, planes), plane_send)
-
-    grad_qkv = attend_back(
-        spot, queries, keys_values, w_output, grad_attn_out, start[None, :], cosine, sine
-    )
-    grad_normed = scatter_cores(*project_back(spot, grad_qkv, w_qkv, chips), chip_send)
+    gu_pairs = swap_pairs(*spread_rows(plane, core, grad_gate_up, planes))
+    qkv_pairs = swap_pairs(*spread_rows(chip, core, [grad_w_qkv], chips))
+    mixed = dict(enumerate(mixed))
+    for stage in range(chip_stages, 1, -1):
+        mixed = scatter_stage(mixed, chip_send, stage)
+    if head_rows:
+        parts = [grad_output[0]] + [chip_send(grad_output[step], step) for step in range(1, chips)]
+        parts = jnp.stack(parts)
+        out_parts = [
+            lax.dynamic_index_in_dim(parts, (plane ^ far) ^ chip, 0, keepdims=False)
+            for far in everyone
+        ]
+    else:
+        parts = jnp.zeros((planes, slice_rows, width), BF16)
+        for turn_no in range(planes):
+            spare = (own_plane + planes - turn_no) % planes
+            sent = lax.dynamic_index_in_dim(grad_output, spare, 0, keepdims=False)
+            part = lax.ppermute(sent, "fsdp", [(b, a) for a, b in out_route(turn_no)])
+            parts = lax.dynamic_update_index_in_dim(
+                parts, part, ((turn_no + index) % planes) ^ plane, 0
+            )
+        out_parts = [parts[far] for far in everyone]
+    gu_pairs, qkv_pairs, mixed, out_parts = together(gu_pairs, qkv_pairs, mixed, out_parts)
+
+    grad_gate_up = exchange(gu_pairs, plane_send)
+    got = exchange(qkv_pairs, chip_send)
+    got = by_offset(jnp.concatenate(got), index).astype(F32)
+    got = jnp.transpose(got, (1, 0, 2))
+    grad_query = got[:, :, :own_q].reshape(slice_rows, HEADS, HEAD_DIM)
+    kept = [head for device_heads in heads for head in device_heads]
+    grad_query = jnp.stack([grad_query[:, kept.index(head)] for head in range(HEADS)], 1)
+    grad_query = grad_query.reshape(slice_rows, -1)
+    grad_kv = got[:, :, own_q:].reshape(slice_rows, KV_HEADS, sharing, PAIR).sum(2)
+    grad_key = grad_kv[:, :, :HEAD_DIM].reshape(slice_rows, -1)
+    grad_value = grad_kv[:, :, HEAD_DIM:].reshape(slice_rows, -1)
+
+    gain_one = gain_columns[:, :1]
+    grad_gain_one = sum(
+        jnp.sum(weight.astype(BF16).astype(F32) * gradient, 1)
+        for weight, gradient in (
+            (query_weight, grad_query),
+            (key_weight, grad_key),
+            (value_weight, grad_value),
+        )
+    )
+    attention_new = (
+        adam_step(query_weight, query_first, query_second, grad_query * gain_one, 0.02)
+        + adam_step(key_weight, key_first, key_second, grad_key * gain_one, 0.02)
+        + adam_step(value_weight, value_first, value_second, grad_value * gain_one, 0.02)
+    )
+    grad_gate_up, attention_new, grad_gain_one, out_parts, mixed, grad_down_weight = together(
+        grad_gate_up, attention_new, grad_gain_one, out_parts, mixed, grad_down_weight
+    )
+
+    grad_normed = scatter_stage(mixed, chip_send, 1)[0]
+    grad_output_weight = scatter_sum(out_parts, plane_send)
     scale_one = rms_scale(own_tokens)
-    weighted_one = grad_normed * gains[0]
-    grad_gain_one = jnp.sum(grad_normed * own_tokens * scale_one, 0)
     grad_tokens = (
         grad_resid
-        + scale_one * weighted_one
+        + scale_one * grad_normed
         - own_tokens
         * (scale_one * scale_one * scale_one)
-        * jnp.mean(weighted_one * own_tokens, -1, keepdims=True)
-    )
-    out_mine, _ = lax.optimization_barrier((out_mine, grad_attn_out[0]))
-    result = resid + scatter_cores(out_mine, out_other, plane_send)
-
-    grad_output = rows_grad(attended, grad_attn_out).reshape(planes, slice_rows, width)
-    out_parts = jnp.zeros((planes, slice_rows, width), BF16)
-    for turn_no in range(planes):
-        spare = (own_plane + planes - turn_no) % planes
-        sent = lax.dynamic_index_in_dim(grad_output, spare, 0, keepdims=False)
-        got = lax.ppermute(sent, "fsdp", [(b, a) for a, b in out_route(turn_no)])
-        out_parts = lax.dynamic_update_index_in_dim(
-            out_parts, got, ((turn_no + index) % planes) ^ plane, 0
-        )
-    grad_output_weight = scatter_sum([out_parts[step] for step in range(planes)], plane_send)
-
-    grad_w_qkv = scatter_sum(qkv_grad(spot, normed, grad_qkv, planes), plane_send)
-    got = exchange(*spread_rows(chip, core, grad_w_qkv, chips), chip_send)
-    got = by_offset(jnp.concatenate(got), index).astype(F32)
-    got = jnp.transpose(got, (1, 0, 2))
-    grad_query_weight = got[:, :, :own_q].reshape(slice_rows, -1)
-    grad_kv = got[:, :, own_q:].reshape(slice_rows, KV_HEADS, sharing, PAIR).sum(2)
-    grad_key_weight = grad_kv[:, :, :HEAD_DIM].reshape(slice_rows, -1)
-    grad_value_weight = grad_kv[:, :, HEAD_DIM:].reshape(slice_rows, -1)
-
-    gain_grads = jnp.stack([grad_gain_one, grad_gain_two]).reshape(2, planes, members, -1)
-    gain_grads = by_offset(jnp.transpose(gain_grads, (2, 1, 0, 3)), index)
-    gain_grads = gain_grads.reshape((chips, 2) + gain_grads.shape[1:])
-    gain_grads = gain_grads[:, 0] + core_swap(gain_grads[:, 1])
-    gain_grads = gain_grads[0] + sum(chip_send(gain_grads[s], s) for s in range(1, chips))
-    gain_grads = by_offset(gain_grads, plane)
-    gain_grads = gain_grads[0] + sum(plane_send(gain_grads[s], s) for s in range(1, planes))
-
+        * jnp.mean(grad_normed * own_tokens, -1, keepdims=True)
+    )
+    fed_weights, grad_gain_two = feed_adam(
+        place,
+        planes,
+        chips,
+        gain_columns,
+        grad_gate_up,
+        (gate_weight, gate_first, gate_second, up_weight, up_first, up_second),
+    )
+    gain_grads = jnp.stack([grad_gain_one, grad_gain_two])
     updated = (
-        adam_step(query_weight, query_first, query_second, grad_query_weight, 0.02)
-        + adam_step(key_weight, key_first, key_second, grad_key_weight, 0.02)
-        + adam_step(value_weight, value_first, value_second, grad_value_weight, 0.02)
+        attention_new
         + adam_step(output_weight, output_first, output_second, grad_output_weight, 0.1)
-        + tuple(
-            feed_adam(
-                place,
-                planes,
-                chips,
-                grad_gate_up,
-                (gate_weight, gate_first, gate_second, up_weight, up_first, up_second),
-            )
-        )
+        + fed_weights
         + adam_step(down_weight, down_first, down_second, grad_down_weight, 0.02)
         + adam_step(norm_gains, gains_first, gains_second, gain_grads, 0.2)
     )
-    return (result.astype(BF16), grad_tokens) + updated
+    return (result, grad_tokens) + updated
 
 
 def solution(mesh):

time: 681 us -> 556 us (0.82)
  starting transfers between devices: 154 us -> 77.8 us
  waiting for transfers between devices: 268 us -> 232 us
  local copies, waits for them, and re-layouts: 40.3 us -> 28.3 us
    ppermute x36 -> x30, waiting for transfers between devices: 183 us -> 122 us  [plane_send(): return lax.ppermute(value, 'dp', [(i, i ^ step) for i in range(planes)])]
    ppermute x36 -> x30, starting transfers between devices: 91.6 us -> 37.2 us  [plane_send(): return lax.ppermute(value, 'dp', [(i, i ^ step) for i in range(planes)])]
    ppermute x8 -> x0, starting transfers between devices: 26.3 us -> none  [the longest x4 17.5 us: local(): got = lax.ppermute(sent, 'fsdp', out_route(turn_no))]
    ppermute x24 -> x29, waiting for transfers between devices: 73.1 us -> 98.3 us  [chip_send(): lax.ppermute(value, 'fsdp', [(i, i ^ 2 * step) for i in range(members)])]
    convert_element_type x16 -> x10, other arithmetic: 19.5 us -> 6.79 us  [the longest x1 2.59 us: local(): own_grad = grad_resid.astype(BF16)]
    add x3 -> x18, other arithmetic: 1.07 us -> 12.9 us  [the longest x4 6.57 us: scatter_stage(): parts[j & j - 1] = parts[j & j - 1].astype(F32) + got.astype(F32)]
    ppermute x8 -> x0, waiting for transfers between devices: 9.52 us -> none  [the longest x4 9.51 us: local(): got = lax.ppermute(sent, 'fsdp', out_route(turn_no))]
    all_gather x1 -> x0, local copies, waits for them, and re-layouts: 8.49 us -> none  [local(): lax.all_gather(gate_up_rows, 'fsdp', axis=0, tiled=False, axis_index_grou...]
  transfers between devices with their start and end apart: 113 -> 94, of which waited for: 31 -> 42; matrix products, arithmetic and copies ran while one was open for 12% -> 11% of each run, Pallas kernels for 21% -> 21%
where the time goes in v3:
time: 556 us; the launch traced here: 552 us
  waiting for transfers between devices  232 us (42%)
  Pallas kernels  144 us (26%)
  starting transfers between devices  77.8 us (14%)
  other arithmetic  54.8 us (10%)
  local copies, waits for them, and re-layouts  28.3 us (5%)
  between operations  15.8 us (3%)
    ppermute x30, waiting for transfers between devices, plane_send(): return lax.ppermute(value, 'dp', [(i, i ^ step) for i in range(planes)])  122 us
    ppermute x29, waiting for transfers between devices, chip_send(): lax.ppermute(value, 'fsdp', [(i, i ^ 2 * step) for i in range(members)])  98.3 us
    pallas_call x4, Pallas kernels, feed(): pl.pallas_call(functools.partial(feed_kernel, planes, layout, count), out...  44.7 us
    ppermute x30, starting transfers between devices, plane_send(): return lax.ppermute(value, 'dp', [(i, i ^ step) for i in range(planes)])  37.2 us
    ppermute x29, starting transfers between devices, chip_send(): lax.ppermute(value, 'fsdp', [(i, i ^ 2 * step) for i in range(members)])  33.6 us
    pallas_call x1, Pallas kernels, attend_back(): pl.pallas_call(functools.partial(attend_back_kernel, members, pairs), out...  18.1 us
    pallas_call x1, Pallas kernels, attend(): pl.pallas_call(functools.partial(attend_kernel, members, pairs, planes),...  14.9 us
    pallas_call x2, Pallas kernels, rows_grad(): pl.pallas_call(functools.partial(rows_grad_kernel, len(grads)), out_shape...  11.9 us
  transfers between devices with their start and end apart: 94, of which 42 were waited for; matrix products, arithmetic and copies ran while one was open for 11% of the time, Pallas kernels for 21%

profile of v3, /device:TPU:0, one launch (start us, length us, event | category | flops | bytes accessed | tf_op | source)
XLA Modules:
  0.0 552.1 jit_solution(9147698034593502417)
XLA Ops:
  11.0 6.5 %pack.1 = (bf16[4,2,64,768]{3,2,1,0:T(8,128)(2,1)}, bf16[4,2,64,768]{3,2,1,0:T(8,128)(2,1)}, bf16[4,64,384]{2,1,0:T(8,128)(2,1)}, bf16[4,64,384]{2,1,0:T(8,128)(2,1)}) custom-call(s32[3]{0:T(128)} %pad_add_fusion.place, f32[64,2]{1,0:T(8,128)} %bitcast.72, f32[64,5632]{1,0:T(8,128)} %refs_4_.1, f32[64,5632]{1,0:T(8,128)} %refs_7_.1, f32[64,2048]{1,0:T(8,128)} %query.1, ...), custom_call_target="tpu_custom_call" | custom-call | bytes 4325376 | tf_op jit(solution)/shard_map/pack/pallas_call | solution.py:206
  17.6 3.1 collective-permute-start.2
  20.7 2.6 collective-permute-start.3
  27.7 4.8 collective-permute-done.2
  32.5 2.5 collective-permute-done.3
  40.6 3.6 collective-permute-done.8
  54.1 2.3 collective-permute-start.10
  61.2 14.8 %collective-permute-done.11 = bf16[192,2048]{1,0:T(8,128)(2,1)S(1)} collective-permute-done((bf16[192,2048]{1,0:T(8,128)(2,1)S(1)}, bf16[192,2048]{1,0:T(8,128)(2,1)S(1)}, u32[]{:S(2)}, u32[]{:S(2)}) %collective-permute-start.11) | collective-permute-done | bytes 786464 | tf_op jit(solution)/shard_map/ppermute | solution.py:60
  77.0 15.5 %collective-permute-done.13 = bf16[192,2048]{1,0:T(8,128)(2,1)S(1)} collective-permute-done((bf16[192,2048]{1,0:T(8,128)(2,1)S(1)}, bf16[192,2048]{1,0:T(8,128)(2,1)S(1)}, u32[]{:S(2)}, u32[]{:S(2)}) %collective-permute-start.13) | collective-permute-done | bytes 786464 | tf_op jit(solution)/shard_map/ppermute | solution.py:60
  97.2 2.6 gather_rows.2.refs_4_
  106.2 18.4 %collective-permute-done.17.refs_4_.refs_2_ = bf16[512,384]{1,0:T(8,128)(2,1)S(1)} collective-permute-done((bf16[512,384]{1,0:T(8,128)(2,1)}, bf16[512,384]{1,0:T(8,128)(2,1)S(1)}, u32[]{:S(2)}, u32[]{:S(2)}) %collective-permute-start.17) | collective-permute-done | bytes 393248 | tf_op jit(solution)/shard_map/ppermute | solution.py:65
  124.7 10.0 %collective-permute-done.18.refs_5_.refs_3_ = bf16[512,384]{1,0:T(8,128)(2,1)S(1)} collective-permute-done((bf16[512,384]{1,0:T(8,128)(2,1)S(1)}, bf16[512,384]{1,0:T(8,128)(2,1)S(1)}, u32[]{:S(2)}, u32[]{:S(2)}) %collective-permute-start.18) | collective-permute-done | bytes 393248 | tf_op jit(solution)/shard_map/ppermute | solution.py:65
  145.7 14.9 %attend.1 = (bf16[1024,2048]{1,0:T(8,128)(2,1)}, bf16[1024,256]{1,0:T(8,128)(2,1)}, bf16[1024,128]{1,0:T(8,128)(2,1)}, bf16[1024,256]{1,0:T(8,128)(2,1)}) custom-call(s32[2]{0:T(128)} %pad_add_fusion.2.place, s32[1024,1]{1,0:T(8,128)} %copy.72.start_ref, f32[1024,128]{1,0:T(8,128)} %get-tuple-element.397.cos_ref, f32[1024,128]{1,0:T(8,128)} %get-tuple-element.398.sin_ref, ...), custom_call_target="tpu_custom_call" | custom-call | flops 2415919104 | bytes 8388608 | tf_op jit(solution)/shard_map/attend/pallas_call | solution.py:338
  162.1 4.6 collective-permute-done.23.refs_2_.refs_4_
  166.7 4.4 project.1
  178.6 10.9 %collective-permute-done.26 = bf16[128,2048]{1,0:T(8,128)(2,1)S(1)} collective-permute-done((bf16[128,2048]{1,0:T(8,128)(2,1)S(1)}, bf16[128,2048]{1,0:T(8,128)(2,1)S(1)}, u32[]{:S(2)}, u32[]{:S(2)}) %collective-permute-start.26) | collective-permute-done | bytes 524320 | tf_op jit(solution)/shard_map/ppermute | solution.py:60
  189.5 11.3 %collective-permute-done.28 = bf16[128,2048]{1,0:T(8,128)(2,1)S(1)} collective-permute-done((bf16[128,2048]{1,0:T(8,128)(2,1)S(1)}, bf16[128,2048]{1,0:T(8,128)(2,1)S(1)}, u32[]{:S(2)}, u32[]{:S(2)}) %collective-permute-start.28) | collective-permute-done | bytes 524320 | tf_op jit(solution)/shard_map/ppermute | solution.py:60
  203.4 20.6 %collective-permute-done.32.refs_0_.refs_2_ = bf16[128,2048]{1,0:T(8,128)(2,1)S(1)} collective-permute-done((bf16[128,2048]{1,0:T(8,128)(2,1)S(1)}, bf16[128,2048]{1,0:T(8,128)(2,1)S(1)}, u32[]{:S(2)}, u32[]{:S(2)}) %collective-permute-start.32) | collective-permute-done | bytes 524320 | tf_op jit(solution)/shard_map/ppermute | solution.py:65
  226.9 13.0 %collective-permute-done.41.refs_0_.refs_6_ = bf16[128,2048]{1,0:T(8,128)(2,1)S(1)} collective-permute-done((bf16[128,2048]{1,0:T(8,128)(2,1)S(1)}, bf16[128,2048]{1,0:T(8,128)(2,1)S(1)}, u32[]{:S(2)}, u32[]{:S(2)}) %collective-permute-start.41) | collective-permute-done | bytes 524320 | tf_op jit(solution)/shard_map/ppermute | solution.py:65
  241.9 11.3 %feed.4 = (bf16[256,704]{1,0:T(8,128)(2,1)}, bf16[256,704]{1,0:T(8,128)(2,1)}, bf16[256,704]{1,0:T(8,128)(2,1)}, f32[128,2048]{1,0:T(8,128)}, bf16[128,2048]{1,0...) custom-call(s32[3]{0:T(128)} %pad_add_fusion.place, bf16[128,2048]{1,0:T(8,128)(2,1)} %copy-done.77, ...), custom_call_target="tpu_custom_call" | custom-call | flops 4429185024 | bytes 8650752 | tf_op jit(solution)/shard_map/feed/pallas_call | solution.py:617
  253.9 11.0 %feed.5 = (bf16[256,704]{1,0:T(8,128)(2,1)}, bf16[256,704]{1,0:T(8,128)(2,1)}, bf16[256,704]{1,0:T(8,128)(2,1)}, f32[128,2048]{1,0:T(8,128)}, bf16[128,2048]{1,0...) custom-call(s32[3]{0:T(128)} %pad_add_fusion.place, bf16[128,2048]{1,0:T(8,128)(2,1)} %copy-done.76, ...), custom_call_target="tpu_custom_call" | custom-call | flops 4429185024 | bytes 8650752 | tf_op jit(solution)/shard_map/feed/pallas_call | solution.py:617
  267.8 11.4 %feed.6 = (bf16[256,704]{1,0:T(8,128)(2,1)}, bf16[256,704]{1,0:T(8,128)(2,1)}, bf16[256,704]{1,0:T(8,128)(2,1)}, f32[128,2048]{1,0:T(8,128)}, bf16[128,2048]{1,0...) custom-call(s32[3]{0:T(128)} %pad_add_fusion.place, bf16[128,2048]{1,0:T(8,128)(2,1)} %copy-done.75, ...), custom_call_target="tpu_custom_call" | custom-call | flops 4429185024 | bytes 8650752 | tf_op jit(solution)/shard_map/feed/pallas_call | solution.py:617
  282.1 2.6 collective-permute-start.51
  284.7 11.0 %feed.7 = (bf16[256,704]{1,0:T(8,128)(2,1)}, bf16[256,704]{1,0:T(8,128)(2,1)}, bf16[256,704]{1,0:T(8,128)(2,1)}, f32[128,2048]{1,0:T(8,128)}, bf16[128,2048]{1,0...) custom-call(s32[3]{0:T(128)} %pad_add_fusion.place, bf16[128,2048]{1,0:T(8,128)(2,1)} %copy-done.37, ...), custom_call_target="tpu_custom_call" | custom-call | flops 4429185024 | bytes 8650752 | tf_op jit(solution)/shard_map/feed/pallas_call | solution.py:617
  298.6 11.1 %feed_grad.1 = (bf16[2,512,768]{2,1,0:T(8,128)(2,1)}, bf16[512,768]{1,0:T(8,128)(2,1)}, bf16[512,768]{1,0:T(8,128)(2,1)}, bf16[512,768]{1,0:T(8,128)(2,1)}, bf16...) custom-call(s32[3]{0:T(128)} %pad_add_fusion.place, bf16[128,2048]{1,0:T(8,128)(2,1)} %copy-done.37, ...), custom_call_target="tpu_custom_call" | custom-call | flops 5905580032 | bytes 5767168 | tf_op jit(solution)/shard_map/feed_grad/pallas_call | solution.py:675
  311.0 8.5 %collective-permute-done.52 = bf16[128,2048]{1,0:T(8,128)(2,1)S(1)} collective-permute-done((bf16[128,2048]{1,0:T(8,128)(2,1)S(1)}, bf16[128,2048]{1,0:T(8,128)(2,1)S(1)}, u32[]{:S(2)}, u32[]{:S(2)}) %collective-permute-start.52) | collective-permute-done | bytes 524320 | tf_op jit(solution)/shard_map/ppermute | solution.py:65
  320.1 2.6 fusion.21
  327.6 7.3 %rows_grad.2 = bf16[704,2048]{1,0:T(8,128)(2,1)} custom-call(bf16[1024,704]{1,0:T(8,128)(2,1)} %pad_maximum_fusion.1.left_ref, bf16[128,2048]{1,0:T(8,128)(2,1)} %refs_0_, bf16[128,2048]{1,0:T(8,128)(2,1)} %copy-done.71, bf16[128,2048]{1,0:T(8,128)(2,1)} %copy-done.69, bf16[128,2048]{1,0:T(8,128)(2,1)} %copy-done.72, ...), custom_call_target="tpu_custom_call" | custom-call | flops 2952790016 | bytes 1441792 | tf_op jit(solution)/shard_map/rows_grad/pallas_call | solution.py:530
  339.1 8.3 %collective-permute-done.55.refs_4_ = bf16[128,2048]{1,0:T(8,128)(2,1)} collective-permute-done((bf16[128,2048]{1,0:T(8,128)(2,1)S(1)}, bf16[128,2048]{1,0:T(8,128)(2,1)}, u32[]{:S(2)}, u32[]{:S(2)}) %collective-permute-start.55) | collective-permute-done | bytes 524320 | tf_op jit(solution)/shard_map/ppermute | solution.py:60
  353.9 4.6 rows_grad.3
  358.5 2.4 collective-permute-start.62
  363.7 18.1 %attend_back.1.grad_ref.left_ref = bf16[1024,384]{1,0:T(8,128)(2,1)} custom-call(s32[2]{0:T(128)} %pad_add_fusion.2.place, s32[1,1024]{1,0:T(1,128)} %bitcast.79, f32[1024,128]{1,0:T(8,128)} %get-tuple-element.397.cos_ref, f32[1024,128]{1,0:T(8,128)} %get-tuple-element.398.sin_ref, bf16[1024,256]{1,0:T(8,128)(2,1)} %get-tuple-element.425.q_ref, ...), custom_call_target="tpu_custom_call" | custom-call | flops 2952790016 | bytes 4194304 | tf_op jit(solution)/shard_map/attend_back/pallas_call | solution.py:428
  381.9 3.1 collective-permute-done.62
  390.2 5.5 %qkv_grad.1 = (bf16[512,384]{1,0:T(8,128)(2,1)}, bf16[512,384]{1,0:T(8,128)(2,1)}, bf16[512,384]{1,0:T(8,128)(2,1)}, bf16[512,384]{1,0:T(8,128)(2,1)}) custom-call(s32[2]{0:T(128)} %pad_add_fusion.2.place, bf16[1024,2048]{1,0:T(8,128)(2,1)} %get-tuple-element.595.normed_ref, bf16[1024,384]{1,0:T(8,128)(2,1)} %attend_back.1.grad_ref.left_ref), custom_call_target="tpu_custom_call" | custom-call | flops 1610612736 | bytes 4194304 | tf_op jit(solution)/shard_map/qkv_grad/pallas_call | solution.py:507
  397.8 6.2 %project_back.1 = (f32[128,2048]{1,0:T(8,128)}, f32[128,2048]{1,0:T(8,128)}, f32[128,2048]{1,0:T(8,128)}, f32[128,2048]{1,0:T(8,128)}, bf16[128,2048]{1,0:T(8,12...) custom-call(s32[2]{0:T(128)} %pad_add_fusion.2.place, ...), custom_call_target="tpu_custom_call" | custom-call | flops 1610612736 | bytes 6291456 | tf_op jit(solution)/shard_map/project_back/pallas_call | solution.py:486
  405.5 2.5 collective-permute-done.70
  414.9 17.4 %collective-permute-done.71 = bf16[512,384]{1,0:T(8,128)(2,1)S(1)} collective-permute-done((bf16[512,384]{1,0:T(8,128)(2,1)S(1)}, bf16[512,384]{1,0:T(8,128)(2,1)S(1)}, u32[]{:S(2)}, u32[]{:S(2)}) %collective-permute-start.71) | collective-permute-done | bytes 393248 | tf_op jit(solution)/shard_map/ppermute | solution.py:65
  433.3 11.9 %collective-permute-done.73.refs_1_ = bf16[2,512,768]{2,1,0:T(8,128)(2,1)S(1)} collective-permute-done((bf16[2,512,768]{2,1,0:T(8,128)(2,1)}, bf16[2,512,768]{2,1,0:T(8,128)(2,1)S(1)}, u32[]{:S(2)}, u32[]{:S(2)}) %collective-permute-start.73) | collective-permute-done | bytes 1572896 | tf_op jit(solution)/shard_map/ppermute | solution.py:60
  453.4 4.0 spread_rows.2
  465.0 12.7 %collective-permute-done.77 = bf16[128,2048]{1,0:T(8,128)(2,1)} collective-permute-done((bf16[128,2048]{1,0:T(8,128)(2,1)}, bf16[128,2048]{1,0:T(8,128)(2,1)}, u32[]{:S(2)}, u32[]{:S(2)}) %collective-permute-start.77) | collective-permute-done | bytes 524320 | tf_op jit(solution)/shard_map/ppermute | solution.py:60
  495.8 3.4 stack.208
  499.6 3.2 multiply_subtract_fusion.3
  503.9 3.9 reduce-scatter.2.cloned.1.call-done
  509.3 6.0 %collective-permute-done.82.refs_2_ = bf16[2,2,64,768]{3,2,1,0:T(8,128)(2,1)} collective-permute-done((bf16[2,2,64,768]{3,2,1,0:T(8,128)(2,1)}, bf16[2,2,64,768]{3,2,1,0:T(8,128)(2,1)}, u32[]{:S(2)}, u32[]{:S(2)}) %collective-permute-start.82) | collective-permute-done | bytes 393248 | tf_op jit(solution)/shard_map/ppermute | solution.py:65
  515.2 5.4 collective-permute-start.89
  520.7 2.4 collective-permute-start.91
  525.2 4.2 multiply_subtract_fusion
  529.5 10.0 %feed_adam.1 = (f32[64,5632]{1,0:T(8,128)}, f32[64,5632]{1,0:T(8,128)}, f32[64,5632]{1,0:T(8,128)}, f32[64,5632]{1,0:T(8,128)}, f32[64,5632]{1,0:T(8,128)}, /*index=5*/f32[64,5632]{1,0:T(8,128)}, f32[64,128]{1,0:T(8,128)}) custom-call(s32[3]{0:T(128)} %pad_add_fusion.place, f32[64,2]{1,0:T(8,128)} %bitcast.73, ...), custom_call_target="tpu_custom_call" | custom-call | flops 14417920 | bytes 18743296 | tf_op jit(solution)/shard_map/feed_adam/pallas_call | solution.py:724
  (470 shorter events, 158.1 us)
Async XLA Ops:
  7.2 86.8 %all-gather.2.cloned.1.call-start = ((), (), s32[]{:S(2)}) async-start(), calls=%async_computation.1 | async-start | bytes 3604480 | tf_op jit(solution)/shard_map/all_gather | solution.py:830
  9.6 498.3 %reduce-scatter.2.cloned.1.call-start = ((), (), s32[]{:S(2)}) async-start(), calls=%async_computation.2 | async-start | bytes 3604480 | tf_op jit(solution)/shard_map/reduce_scatter | solution.py:1042
  50.5 25.5 %collective-permute-start.11 = (bf16[192,2048]{1,0:T(8,128)(2,1)S(1)}, bf16[192,2048]{1,0:T(8,128)(2,1)S(1)}, u32[]{:S(2)}, u32[]{:S(2)}) collective-permute-start(bf16[192,2048]{1,0:T(8,128)(2,1)S(1)} %get-tuple-element.763), channel_id=1, source_target_pairs={{0,2},{1,3},{2,0},{3,1},{4,6},{5,7},{6,4},{7,5},{8,10},{9,11},{10,... | collective-permute-start | bytes 2359304 | tf_op jit(solution)/shard_map/ppermute | solution.py:60
  52.0 23.9 %collective-permute-start.12 = (bf16[192,2048]{1,0:T(8,128)(2,1)S(1)}, bf16[192,2048]{1,0:T(8,128)(2,1)S(1)}, u32[]{:S(2)}, u32[]{:S(2)}) collective-permute-start(bf16[192,2048]{1,0:T(8,128)(2,1)S(1)} %get-tuple-element.762), channel_id=1, source_target_pairs={{0,4},{1,5},{2,6},{3,7},{4,0},{5,1},{6,2},{7,3},{8,12},{9,13},{10,... | collective-permute-start | bytes 2359304 | tf_op jit(solution)/shard_map/ppermute | solution.py:60
  53.5 38.9 %collective-permute-start.13 = (bf16[192,2048]{1,0:T(8,128)(2,1)S(1)}, bf16[192,2048]{1,0:T(8,128)(2,1)S(1)}, u32[]{:S(2)}, u32[]{:S(2)}) collective-permute-start(bf16[192,2048]{1,0:T(8,128)(2,1)S(1)} %get-tuple-element.761), channel_id=1, source_target_pairs={{0,6},{1,7},{2,4},{3,5},{4,2},{5,3},{6,0},{7,1},{8,14},{9,15},{10,... | collective-permute-start | bytes 2359304 | tf_op jit(solution)/shard_map/ppermute | solution.py:60
  54.1 39.9 %collective-permute-start.10 = (bf16[2,2,64,768]{3,2,1,0:T(8,128)(2,1)S(1)}, bf16[2,2,64,768]{3,2,1,0:T(8,128)(2,1)S(1)}, u32[]{:S(2)}, u32[]{:S(2)}) collective-permute-start(bf16[2,2,64,768]{3,2,1,0:T(8,128)(2,1)S(1)} %get-tuple-element.376), channel_id=1, source_target_pairs={{0,24},{8,16},{16,8},{24,0},{1,25},{9,17},{17,9},{25,1},{2,26},{10... | collective-permute-start | bytes 1179656 | tf_op jit(solution)/shard_map/ppermute | solution.py:65
  56.5 37.5 %collective-permute-start.9 = (bf16[2,2,64,768]{3,2,1,0:T(8,128)(2,1)S(1)}, bf16[2,2,64,768]{3,2,1,0:T(8,128)(2,1)S(1)}, u32[]{:S(2)}, u32[]{:S(2)}) collective-permute-start(bf16[2,2,64,768]{3,2,1,0:T(8,128)(2,1)S(1)} %get-tuple-element.375), channel_id=1, source_target_pairs={{0,16},{8,24},{16,0},{24,8},{1,17},{9,25},{17,1},{25,9},{2,18},{10... | collective-permute-start | bytes 1179656 | tf_op jit(solution)/shard_map/ppermute | solution.py:65
  96.4 40.5 %collective-permute-start.19 = (bf16[4,128,2048]{2,1,0:T(8,128)(2,1)S(1)}, bf16[4,128,2048]{2,1,0:T(8,128)(2,1)}, u32[]{:S(2)}, u32[]{:S(2)}) collective-permute-start(bf16[4,128,2048]{2,1,0:T(8,128)(2,1)S(1)} %pad_maximum_fusion.refs_0_), channel_id=1, source_target_pairs={{0,1},{1,0},{2,3},{3,2},{4,5},{5,4},{6,7},{7,6},{8,9},{9,8},{10,11... | collective-permute-start | bytes 6291464 | tf_op jit(solution)/shard_map/ppermute | solution.py:55
  99.8 36.9 %collective-permute-start.14 = (bf16[2,512,768]{2,1,0:T(8,128)(2,1)}, bf16[2,512,768]{2,1,0:T(8,128)(2,1)S(1)}, u32[]{:S(2)}, u32[]{:S(2)}) collective-permute-start(bf16[2,512,768]{2,1,0:T(8,128)(2,1)} %gather_rows.2.refs_4_), channel_id=1, source_target_pairs={{0,2},{1,3},{2,0},{3,1},{4,6},{5,7},{6,4},{7,5},{8,10},{9,11},{10,... | collective-permute-start | bytes 4718600 | tf_op jit(solution)/shard_map/ppermute | solution.py:60
  100.3 36.6 %collective-permute-start.15 = (bf16[2,512,768]{2,1,0:T(8,128)(2,1)}, bf16[2,512,768]{2,1,0:T(8,128)(2,1)S(1)}, u32[]{:S(2)}, u32[]{:S(2)}) collective-permute-start(bf16[2,512,768]{2,1,0:T(8,128)(2,1)} %gather_rows.2.refs_4_), channel_id=1, source_target_pairs={{0,4},{1,5},{2,6},{3,7},{4,0},{5,1},{6,2},{7,3},{8,12},{9,13},{10,... | collective-permute-start | bytes 4718600 | tf_op jit(solution)/shard_map/ppermute | solution.py:60
  104.2 20.5 %collective-permute-start.17 = (bf16[512,384]{1,0:T(8,128)(2,1)}, bf16[512,384]{1,0:T(8,128)(2,1)S(1)}, u32[]{:S(2)}, u32[]{:S(2)}) collective-permute-start(bf16[512,384]{1,0:T(8,128)(2,1)} %gather_rows.3.refs_2_.refs_0_), channel_id=1, source_target_pairs={{0,16},{8,24},{16,0},{24,8},{1,17},{9,25},{17,1},{25,9},{2,18},{10... | collective-permute-start | bytes 1179656 | tf_op jit(solution)/shard_map/ppermute | solution.py:65
  104.9 19.7 %collective-permute-start.16 = (bf16[512,384]{1,0:T(8,128)(2,1)}, bf16[512,384]{1,0:T(8,128)(2,1)S(1)}, u32[]{:S(2)}, u32[]{:S(2)}) collective-permute-start(bf16[512,384]{1,0:T(8,128)(2,1)} %gather_rows.3.refs_2_.refs_0_), channel_id=1, source_target_pairs={{0,8},{8,0},{16,24},{24,16},{1,9},{9,1},{17,25},{25,17},{2,10},{10... | collective-permute-start | bytes 1179656 | tf_op jit(solution)/shard_map/ppermute | solution.py:65
  137.0 29.7 %collective-permute-start.20 = (bf16[512,768]{1,0:T(8,128)(2,1)S(1)}, bf16[512,768]{1,0:T(8,128)(2,1)}, u32[]{:S(2)}, u32[]{:S(2)}) collective-permute-start(bf16[512,768]{1,0:T(8,128)(2,1)S(1)} %slice_bitcast_fusion.1), channel_id=1, source_target_pairs={{0,2},{1,3},{2,0},{3,1},{4,6},{5,7},{6,4},{7,5},{8,10},{9,11},{10,... | collective-permute-start | bytes 2359304 | tf_op jit(solution)/shard_map/ppermute | solution.py:60
  138.6 28.1 %collective-permute-start.21 = (bf16[512,768]{1,0:T(8,128)(2,1)S(1)}, bf16[512,768]{1,0:T(8,128)(2,1)}, u32[]{:S(2)}, u32[]{:S(2)}) collective-permute-start(bf16[512,768]{1,0:T(8,128)(2,1)S(1)} %slice_bitcast_fusion), channel_id=1, source_target_pairs={{0,4},{1,5},{2,6},{3,7},{4,0},{5,1},{6,2},{7,3},{8,12},{9,13},{10,... | collective-permute-start | bytes 2359304 | tf_op jit(solution)/shard_map/ppermute | solution.py:60
  139.5 22.6 %collective-permute-start.22 = (bf16[128,2048]{1,0:T(8,128)(2,1)}, bf16[128,2048]{1,0:T(8,128)(2,1)S(1)}, u32[]{:S(2)}, u32[]{:S(2)}) collective-permute-start(bf16[128,2048]{1,0:T(8,128)(2,1)} %refs_0_), channel_id=1, source_target_pairs={{0,8},{8,0},{16,24},{24,16},{1,9},{9,1},{17,25},{25,17},{2,10},{10... | collective-permute-start | bytes 1572872 | tf_op jit(solution)/shard_map/ppermute | solution.py:65
  141.7 25.0 %collective-permute-start.23 = (bf16[128,2048]{1,0:T(8,128)(2,1)}, bf16[128,2048]{1,0:T(8,128)(2,1)}, u32[]{:S(2)}, u32[]{:S(2)}) collective-permute-start(bf16[128,2048]{1,0:T(8,128)(2,1)} %refs_0_), channel_id=1, source_target_pairs={{0,16},{8,24},{16,0},{24,8},{1,17},{9,25},{17,1},{25,9},{2,18},{10... | collective-permute-start | bytes 1572872 | tf_op jit(solution)/shard_map/ppermute | solution.py:65
  175.8 25.0 %collective-permute-start.28 = (bf16[128,2048]{1,0:T(8,128)(2,1)S(1)}, bf16[128,2048]{1,0:T(8,128)(2,1)S(1)}, u32[]{:S(2)}, u32[]{:S(2)}) collective-permute-start(bf16[128,2048]{1,0:T(8,128)(2,1)S(1)} %add_convert_fusion.5), channel_id=1, source_target_pairs={{0,4},{1,5},{2,6},{3,7},{4,0},{5,1},{6,2},{7,3},{8,12},{9,13},{10,... | collective-permute-start | bytes 1572872 | tf_op jit(solution)/shard_map/ppermute | solution.py:60
  176.4 24.3 %collective-permute-start.30 = (bf16[128,2048]{1,0:T(8,128)(2,1)S(1)}, bf16[128,2048]{1,0:T(8,128)(2,1)S(1)}, u32[]{:S(2)}, u32[]{:S(2)}) collective-permute-start(bf16[128,2048]{1,0:T(8,128)(2,1)S(1)} %add_convert_fusion.4), channel_id=1, source_target_pairs={{0,6},{1,7},{2,4},{3,5},{4,2},{5,3},{6,0},{7,1},{8,14},{9,15},{10,... | collective-permute-start | bytes 1572872 | tf_op jit(solution)/shard_map/ppermute | solution.py:60
  178.6 22.6 %collective-permute-start.31 = (bf16[128,2048]{1,0:T(8,128)(2,1)}, bf16[128,2048]{1,0:T(8,128)(2,1)S(1)}, u32[]{:S(2)}, u32[]{:S(2)}) collective-permute-start(bf16[128,2048]{1,0:T(8,128)(2,1)} %collective-permute-done.23.refs_2_.refs_4_), channel_id=1, source_target_pairs={{0,8},{8,0},{16,24},{24,16},{1,9},{9,1},{17,25},{25,17},{2,10},{10... | collective-permute-start | bytes 1572872 | tf_op jit(solution)/shard_map/ppermute | solution.py:65
  201.6 22.4 %collective-permute-start.32 = (bf16[128,2048]{1,0:T(8,128)(2,1)S(1)}, bf16[128,2048]{1,0:T(8,128)(2,1)S(1)}, u32[]{:S(2)}, u32[]{:S(2)}) collective-permute-start(bf16[128,2048]{1,0:T(8,128)(2,1)S(1)} %multiply_convert_fusion.refs_0_), channel_id=1, source_target_pairs={{0,8},{8,0},{16,24},{24,16},{1,9},{9,1},{17,25},{25,17},{2,10},{10... | collective-permute-start | bytes 1572872 | tf_op jit(solution)/shard_map/ppermute | solution.py:65
  201.6 24.5 %collective-permute-start.33 = (bf16[128,2048]{1,0:T(8,128)(2,1)S(1)}, bf16[128,2048]{1,0:T(8,128)(2,1)S(1)}, u32[]{:S(2)}, u32[]{:S(2)}) collective-permute-start(bf16[128,2048]{1,0:T(8,128)(2,1)S(1)} %multiply_convert_fusion.refs_0_), channel_id=1, source_target_pairs={{0,16},{8,24},{16,0},{24,8},{1,17},{9,25},{17,1},{25,9},{2,18},{10... | collective-permute-start | bytes 1572872 | tf_op jit(solution)/shard_map/ppermute | solution.py:65
  202.8 23.3 %collective-permute-start.34 = (bf16[128,2048]{1,0:T(8,128)(2,1)}, bf16[128,2048]{1,0:T(8,128)(2,1)S(1)}, u32[]{:S(2)}, u32[]{:S(2)}) collective-permute-start(bf16[128,2048]{1,0:T(8,128)(2,1)} %refs_0_), channel_id=1, source_target_pairs={{0,1},{1,0},{2,3},{3,2},{4,5},{5,4},{6,7},{7,6},{8,9},{9,8},{10,11... | collective-permute-start | bytes 1572872 | tf_op jit(solution)/shard_map/ppermute | solution.py:55
  202.9 23.3 %collective-permute-start.35 = (bf16[128,2048]{1,0:T(8,128)(2,1)S(1)}, bf16[128,2048]{1,0:T(8,128)(2,1)S(1)}, u32[]{:S(2)}, u32[]{:S(2)}) collective-permute-start(bf16[128,2048]{1,0:T(8,128)(2,1)S(1)} %collective-permute-done.22.refs_2_), channel_id=1, source_target_pairs={{0,1},{1,0},{2,3},{3,2},{4,5},{5,4},{6,7},{7,6},{8,9},{9,8},{10,11... | collective-permute-start | bytes 1572872 | tf_op jit(solution)/shard_map/ppermute | solution.py:55
  203.4 22.8 %collective-permute-start.36 = (bf16[128,2048]{1,0:T(8,128)(2,1)}, bf16[128,2048]{1,0:T(8,128)(2,1)S(1)}, u32[]{:S(2)}, u32[]{:S(2)}) collective-permute-start(bf16[128,2048]{1,0:T(8,128)(2,1)} %collective-permute-done.23.refs_2_.refs_4_), channel_id=1, source_target_pairs={{0,1},{1,0},{2,3},{3,2},{4,5},{5,4},{6,7},{7,6},{8,9},{9,8},{10,11... | collective-permute-start | bytes 1572872 | tf_op jit(solution)/shard_map/ppermute | solution.py:55
  281.6 15.1 %collective-permute-start.48 = (bf16[128,2048]{1,0:T(8,128)(2,1)S(1)}, bf16[128,2048]{1,0:T(8,128)(2,1)S(1)}, u32[]{:S(2)}, u32[]{:S(2)}) collective-permute-start(bf16[128,2048]{1,0:T(8,128)(2,1)S(1)} %copy-done.82), channel_id=1, source_target_pairs={{0,1},{1,0},{2,3},{3,2},{4,5},{5,4},{6,7},{7,6},{8,9},{9,8},{10,11... | collective-permute-start | bytes 1572872 | tf_op jit(solution)/shard_map/ppermute | solution.py:55
  282.1 28.9 %collective-permute-start.51 = (bf16[128,2048]{1,0:T(8,128)(2,1)S(1)}, bf16[128,2048]{1,0:T(8,128)(2,1)S(1)}, u32[]{:S(2)}, u32[]{:S(2)}) collective-permute-start(bf16[128,2048]{1,0:T(8,128)(2,1)S(1)} %add_convert_fusion.3), channel_id=1, source_target_pairs={{0,16},{8,24},{16,0},{24,8},{1,17},{9,25},{17,1},{25,9},{2,18},{10... | collective-permute-start | bytes 1572872 | tf_op jit(solution)/shard_map/ppermute | solution.py:65
  298.3 21.2 %collective-permute-start.52 = (bf16[128,2048]{1,0:T(8,128)(2,1)S(1)}, bf16[128,2048]{1,0:T(8,128)(2,1)S(1)}, u32[]{:S(2)}, u32[]{:S(2)}) collective-permute-start(bf16[128,2048]{1,0:T(8,128)(2,1)S(1)} %convert_add_fusion.13), channel_id=1, source_target_pairs={{0,8},{8,0},{16,24},{24,16},{1,9},{9,1},{17,25},{25,17},{2,10},{10... | collective-permute-start | bytes 1572872 | tf_op jit(solution)/shard_map/ppermute | solution.py:65
  322.7 16.4 %collective-permute-start.54 = (bf16[128,2048]{1,0:T(8,128)(2,1)S(1)}, bf16[128,2048]{1,0:T(8,128)(2,1)}, u32[]{:S(2)}, u32[]{:S(2)}) collective-permute-start(bf16[128,2048]{1,0:T(8,128)(2,1)S(1)} %get-tuple-element.576.refs_0_), channel_id=1, source_target_pairs={{0,2},{1,3},{2,0},{3,1},{4,6},{5,7},{6,4},{7,5},{8,10},{9,11},{10,... | collective-permute-start | bytes 1572872 | tf_op jit(solution)/shard_map/ppermute | solution.py:60
  323.6 23.8 %collective-permute-start.55 = (bf16[128,2048]{1,0:T(8,128)(2,1)S(1)}, bf16[128,2048]{1,0:T(8,128)(2,1)}, u32[]{:S(2)}, u32[]{:S(2)}) collective-permute-start(bf16[128,2048]{1,0:T(8,128)(2,1)S(1)} %get-tuple-element.576.refs_0_), channel_id=1, source_target_pairs={{0,4},{1,5},{2,6},{3,7},{4,0},{5,1},{6,2},{7,3},{8,12},{9,13},{10,... | collective-permute-start | bytes 1572872 | tf_op jit(solution)/shard_map/ppermute | solution.py:60
  325.0 23.7 %collective-permute-start.56 = (bf16[128,2048]{1,0:T(8,128)(2,1)S(1)}, bf16[128,2048]{1,0:T(8,128)(2,1)}, u32[]{:S(2)}, u32[]{:S(2)}) collective-permute-start(bf16[128,2048]{1,0:T(8,128)(2,1)S(1)} %get-tuple-element.576.refs_0_), channel_id=1, source_target_pairs={{0,6},{1,7},{2,4},{3,5},{4,2},{5,3},{6,0},{7,1},{8,14},{9,15},{10,... | collective-permute-start | bytes 1572872 | tf_op jit(solution)/shard_map/ppermute | solution.py:60
  358.5 26.4 %collective-permute-start.62 = (bf16[128,2048]{1,0:T(8,128)(2,1)}, bf16[128,2048]{1,0:T(8,128)(2,1)}, u32[]{:S(2)}, u32[]{:S(2)}) collective-permute-start(bf16[128,2048]{1,0:T(8,128)(2,1)} %convert_add_fusion.8), channel_id=1, source_target_pairs={{0,16},{8,24},{16,0},{24,8},{1,17},{9,25},{17,1},{25,9},{2,18},{10... | collective-permute-start | bytes 1572872 | tf_op jit(solution)/shard_map/ppermute | solution.py:65
  360.9 24.0 %collective-permute-start.63 = (bf16[128,2048]{1,0:T(8,128)(2,1)}, bf16[128,2048]{1,0:T(8,128)(2,1)}, u32[]{:S(2)}, u32[]{:S(2)}) collective-permute-start(bf16[128,2048]{1,0:T(8,128)(2,1)} %convert_add_fusion.12), channel_id=1, source_target_pairs={{0,8},{8,0},{16,24},{24,16},{1,9},{9,1},{17,25},{25,17},{2,10},{10... | collective-permute-start | bytes 1572872 | tf_op jit(solution)/shard_map/ppermute | solution.py:65
  361.3 25.0 %collective-permute-start.65 = (bf16[512,768]{1,0:T(8,128)(2,1)}, bf16[512,768]{1,0:T(8,128)(2,1)S(1)}, u32[]{:S(2)}, u32[]{:S(2)}) collective-permute-start(bf16[512,768]{1,0:T(8,128)(2,1)} %get-tuple-element.591), channel_id=1, source_target_pairs={{0,2},{1,3},{2,0},{3,1},{4,6},{5,7},{6,4},{7,5},{8,10},{9,11},{10,... | collective-permute-start | bytes 2359304 | tf_op jit(solution)/shard_map/ppermute | solution.py:60
  362.5 25.1 %collective-permute-start.64 = (bf16[512,768]{1,0:T(8,128)(2,1)}, bf16[512,768]{1,0:T(8,128)(2,1)S(1)}, u32[]{:S(2)}, u32[]{:S(2)}) collective-permute-start(bf16[512,768]{1,0:T(8,128)(2,1)} %get-tuple-element.589), channel_id=1, source_target_pairs={{0,4},{1,5},{2,6},{3,7},{4,0},{5,1},{6,2},{7,3},{8,12},{9,13},{10,... | collective-permute-start | bytes 2359304 | tf_op jit(solution)/shard_map/ppermute | solution.py:60
  397.3 17.6 %collective-permute-start.72 = (bf16[512,384]{1,0:T(8,128)(2,1)}, bf16[512,384]{1,0:T(8,128)(2,1)S(1)}, u32[]{:S(2)}, u32[]{:S(2)}) collective-permute-start(bf16[512,384]{1,0:T(8,128)(2,1)} %get-tuple-element.614), channel_id=1, source_target_pairs={{0,8},{8,0},{16,24},{24,16},{1,9},{9,1},{17,25},{25,17},{2,10},{10... | collective-permute-start | bytes 1179656 | tf_op jit(solution)/shard_map/ppermute | solution.py:65
  408.1 37.1 %collective-permute-start.73 = (bf16[2,512,768]{2,1,0:T(8,128)(2,1)}, bf16[2,512,768]{2,1,0:T(8,128)(2,1)S(1)}, u32[]{:S(2)}, u32[]{:S(2)}) collective-permute-start(bf16[2,512,768]{2,1,0:T(8,128)(2,1)} %pad_maximum_fusion.2), channel_id=1, source_target_pairs={{0,2},{1,3},{2,0},{3,1},{4,6},{5,7},{6,4},{7,5},{8,10},{9,11},{10,... | collective-permute-start | bytes 4718600 | tf_op jit(solution)/shard_map/ppermute | solution.py:60
  409.4 36.6 %collective-permute-start.74 = (bf16[2,512,768]{2,1,0:T(8,128)(2,1)S(1)}, bf16[2,512,768]{2,1,0:T(8,128)(2,1)S(1)}, u32[]{:S(2)}, u32[]{:S(2)}) collective-permute-start(bf16[2,512,768]{2,1,0:T(8,128)(2,1)S(1)} %pad_maximum_fusion.3), channel_id=1, source_target_pairs={{0,4},{1,5},{2,6},{3,7},{4,0},{5,1},{6,2},{7,3},{8,12},{9,13},{10,... | collective-permute-start | bytes 4718600 | tf_op jit(solution)/shard_map/ppermute | solution.py:60
  412.0 20.3 %collective-permute-start.71 = (bf16[512,384]{1,0:T(8,128)(2,1)S(1)}, bf16[512,384]{1,0:T(8,128)(2,1)S(1)}, u32[]{:S(2)}, u32[]{:S(2)}) collective-permute-start(bf16[512,384]{1,0:T(8,128)(2,1)S(1)} %add_convert_fusion.7), channel_id=1, source_target_pairs={{0,16},{8,24},{16,0},{24,8},{1,17},{9,25},{17,1},{25,9},{2,18},{10... | collective-permute-start | bytes 1179656 | tf_op jit(solution)/shard_map/ppermute | solution.py:65
  450.5 27.2 %collective-permute-start.77 = (bf16[128,2048]{1,0:T(8,128)(2,1)}, bf16[128,2048]{1,0:T(8,128)(2,1)}, u32[]{:S(2)}, u32[]{:S(2)}) collective-permute-start(bf16[128,2048]{1,0:T(8,128)(2,1)} %convert_add_fusion.3), channel_id=1, source_target_pairs={{0,2},{1,3},{2,0},{3,1},{4,6},{5,7},{6,4},{7,5},{8,10},{9,11},{10,... | collective-permute-start | bytes 1572872 | tf_op jit(solution)/shard_map/ppermute | solution.py:60
  460.4 19.3 %collective-permute-start.75 = (bf16[4,2,64,768]{3,2,1,0:T(8,128)(2,1)}, bf16[4,2,64,768]{3,2,1,0:T(8,128)(2,1)S(1)}, u32[]{:S(2)}, u32[]{:S(2)}) collective-permute-start(bf16[4,2,64,768]{3,2,1,0:T(8,128)(2,1)} %get-tuple-element.624), channel_id=1, source_target_pairs={{0,1},{1,0},{2,3},{3,2},{4,5},{5,4},{6,7},{7,6},{8,9},{9,8},{10,11... | collective-permute-start | bytes 2359304 | tf_op jit(solution)/shard_map/ppermute | solution.py:55
  486.4 22.9 %collective-permute-start.81 = (bf16[2,2,64,768]{3,2,1,0:T(8,128)(2,1)}, bf16[2,2,64,768]{3,2,1,0:T(8,128)(2,1)}, u32[]{:S(2)}, u32[]{:S(2)}) collective-permute-start(bf16[2,2,64,768]{3,2,1,0:T(8,128)(2,1)} %pad_maximum_fusion.17), channel_id=1, source_target_pairs={{0,8},{8,0},{16,24},{24,16},{1,9},{9,1},{17,25},{25,17},{2,10},{10... | collective-permute-start | bytes 1179656 | tf_op jit(solution)/shard_map/ppermute | solution.py:65
  488.1 27.1 %collective-permute-start.82 = (bf16[2,2,64,768]{3,2,1,0:T(8,128)(2,1)}, bf16[2,2,64,768]{3,2,1,0:T(8,128)(2,1)}, u32[]{:S(2)}, u32[]{:S(2)}) collective-permute-start(bf16[2,2,64,768]{3,2,1,0:T(8,128)(2,1)} %pad_maximum_fusion.18), channel_id=1, source_target_pairs={{0,16},{8,24},{16,0},{24,8},{1,17},{9,25},{17,1},{25,9},{2,18},{10... | collective-permute-start | bytes 1179656 | tf_op jit(solution)/shard_map/ppermute | solution.py:65
  489.9 25.3 %collective-permute-start.83 = (bf16[2,2,64,768]{3,2,1,0:T(8,128)(2,1)}, bf16[2,2,64,768]{3,2,1,0:T(8,128)(2,1)}, u32[]{:S(2)}, u32[]{:S(2)}) collective-permute-start(bf16[2,2,64,768]{3,2,1,0:T(8,128)(2,1)} %pad_maximum_fusion.19), channel_id=1, source_target_pairs={{0,24},{8,16},{16,8},{24,0},{1,25},{9,17},{17,9},{25,1},{2,26},{10... | collective-permute-start | bytes 1179656 | tf_op jit(solution)/shard_map/ppermute | solution.py:65
  515.2 25.7 %collective-permute-start.89 = (bf16[64,2048]{1,0:T(8,128)(2,1)}, bf16[64,2048]{1,0:T(8,128)(2,1)S(1)}, u32[]{:S(2)}, u32[]{:S(2)}) collective-permute-start(bf16[64,2048]{1,0:T(8,128)(2,1)} %get-tuple-element.662), channel_id=1, source_target_pairs={{0,8},{8,0},{16,24},{24,16},{1,9},{9,1},{17,25},{25,17},{2,10},{10... | collective-permute-start | bytes 786440 | tf_op jit(solution)/shard_map/ppermute | solution.py:65
  520.7 20.3 %collective-permute-start.90 = (bf16[64,2048]{1,0:T(8,128)(2,1)}, bf16[64,2048]{1,0:T(8,128)(2,1)S(1)}, u32[]{:S(2)}, u32[]{:S(2)}) collective-permute-start(bf16[64,2048]{1,0:T(8,128)(2,1)} %get-tuple-element.663), channel_id=1, source_target_pairs={{0,16},{8,24},{16,0},{24,8},{1,17},{9,25},{17,1},{25,9},{2,18},{10... | collective-permute-start | bytes 786440 | tf_op jit(solution)/shard_map/ppermute | solution.py:65
  520.7 20.3 %collective-permute-start.91 = (bf16[64,2048]{1,0:T(8,128)(2,1)}, bf16[64,2048]{1,0:T(8,128)(2,1)S(1)}, u32[]{:S(2)}, u32[]{:S(2)}) collective-permute-start(bf16[64,2048]{1,0:T(8,128)(2,1)} %get-tuple-element.664), channel_id=1, source_target_pairs={{0,24},{8,16},{16,8},{24,0},{1,25},{9,17},{17,9},{25,1},{2,26},{10... | collective-permute-start | bytes 786440 | tf_op jit(solution)/shard_map/ppermute | solution.py:65
  523.0 19.5 %collective-permute-start.87 = (bf16[128,2048]{1,0:T(8,128)(2,1)}, bf16[128,2048]{1,0:T(8,128)(2,1)S(1)}, u32[]{:S(2)}, u32[]{:S(2)}) collective-permute-start(bf16[128,2048]{1,0:T(8,128)(2,1)} %convert_add_fusion.2), channel_id=1, source_target_pairs={{0,4},{1,5},{2,6},{3,7},{4,0},{5,1},{6,2},{7,3},{8,12},{9,13},{10,... | collective-permute-start | bytes 1572872 | tf_op jit(solution)/shard_map/ppermute | solution.py:60
  524.4 18.1 %collective-permute-start.88 = (bf16[128,2048]{1,0:T(8,128)(2,1)}, bf16[128,2048]{1,0:T(8,128)(2,1)S(1)}, u32[]{:S(2)}, u32[]{:S(2)}) collective-permute-start(bf16[128,2048]{1,0:T(8,128)(2,1)} %convert_add_fusion.5), channel_id=1, source_target_pairs={{0,2},{1,3},{2,0},{3,1},{4,6},{5,7},{6,4},{7,5},{8,10},{9,11},{10,... | collective-permute-start | bytes 1572872 | tf_op jit(solution)/shard_map/ppermute | solution.py:60
  (140 other events, 1462.6 us)
Sparse Core Ops, SparseCore 0:
  10.5 53.9 all-gather.1
  459.6 48.2 reduce-scatter.1

commit v4 on v3

--- a/solution.py
+++ b/solution.py
@@ -631,10 +631,10 @@
     return got[:3], got[3 : 3 + count], got[3 + count :]
 
 
-def feed_grad_kernel(planes, chips, count, place, *refs):
+def feed_grad_kernel(planes, chips, count, batches, place, *refs):
     x, refs = refs[:count], refs[count:]
-    gates, refs = refs[: count // 2], refs[count // 2 :]
-    ups, refs = refs[: count // 2], refs[count // 2 :]
+    gates, refs = refs[:batches], refs[batches:]
+    ups, refs = refs[:batches], refs[batches:]
     outs, (held, sem) = refs[:-2], refs[-2:]
     width = held.shape[1]
     units = gates[0].shape[1]
@@ -673,7 +673,7 @@
     part = shape_of((width // chips, lanes))
     outs = (own,) + (part,) * (2 * chips - 2)
     return pl.pallas_call(
-        functools.partial(feed_grad_kernel, planes, chips, len(x)),
+        functools.partial(feed_grad_kernel, planes, chips, len(x), len(gates)),
         out_shape=outs,
         in_specs=[SMEM] + [VMEM] * (len(x) + len(gates) + len(ups)),
         out_specs=(ANY,) * len(outs),
@@ -731,6 +731,72 @@
         compiler_params=params(),
         cost_estimate=cost(40 * rows * hidden, 52 * rows * hidden),
         name="feed_adam",
+    )(place, gains, *blocks, *arrays)
+    return tuple(new), gain_grad[:, 0]
+
+
+def attention_adam_kernel(heads, place, gains, *refs):
+    members = len(heads)
+    blocks, refs = refs[: members // 2], refs[members // 2 :]
+    ins, refs = refs[:9], refs[9:]
+    outs, gain_grad, held = refs[:9], refs[9], refs[10]
+    chip, core = place[1], place[2]
+    own_q = len(heads[0]) * HEAD_DIM
+    sharing = members // KV_HEADS
+    for step in range(members // 2):
+        for side in range(2):
+            held[(chip ^ step) * 2 + (core ^ side)] = blocks[step][side].astype(F32)
+    kept = {head: (f, at) for f, own in enumerate(heads) for at, head in enumerate(own)}
+
+    def shared(first):
+        return jnp.concatenate(
+            [
+                sum(
+                    held[group * sharing + one, :, first : first + HEAD_DIM]
+                    for one in range(sharing)
+                )
+                for group in range(KV_HEADS)
+            ],
+            1,
+        )
+
+    query = jnp.concatenate(
+        [
+            held[kept[head][0], :, kept[head][1] * HEAD_DIM : (kept[head][1] + 1) * HEAD_DIM]
+            for head in range(HEADS)
+        ],
+        1,
+    )
+    gain = gains[:, 0:1]
+    total = jnp.zeros(gain.shape, F32)
+    for part, grad in enumerate((query, shared(own_q), shared(own_q + HEAD_DIM))):
+        w, m, u = ins[3 * part : 3 * part + 3]
+        weight = w[...]
+        total = total + jnp.sum(weight.astype(BF16).astype(F32) * grad, -1, keepdims=True)
+        updated = adam_step(weight, m[...], u[...], grad * gain, 0.02)
+        for out, value in zip(outs[3 * part : 3 * part + 3], updated):
+            out[...] = value
+    gain_grad[...] = jnp.broadcast_to(total, gain_grad.shape)
+
+
+def attention_adam(place, heads, gains, blocks, arrays):
+    rows = arrays[0].shape[0]
+    tile = min(rows, 16)
+    lanes = blocks[0].shape[-1]
+    wholes = [pl.BlockSpec((tile, array.shape[1]), lambda i: (i, 0)) for array in arrays]
+    block = pl.BlockSpec((2, tile, lanes), lambda i: (0, i, 0))
+    two = pl.BlockSpec((tile, 2), lambda i: (i, 0))
+    *new, gain_grad = pl.pallas_call(
+        functools.partial(attention_adam_kernel, heads),
+        grid=(rows // tile,),
+        out_shape=tuple(shape_of(array.shape, F32) for array in arrays)
+        + (shape_of((rows, 128), F32),),
+        in_specs=[SMEM, two] + [block] * len(blocks) + wholes,
+        out_specs=tuple(wholes) + (pl.BlockSpec((tile, 128), lambda i: (i, 0)),),
+        scratch_shapes=[pltpu.VMEM((len(heads), tile, lanes), F32)],
+        compiler_params=params(),
+        cost_estimate=cost(40 * arrays[0].size, 28 * arrays[0].size),
+        name="attention_adam",
     )(place, gains, *blocks, *arrays)
     return tuple(new), gain_grad[:, 0]
 
@@ -830,20 +896,17 @@
     w_down = lax.all_gather(
         down_weight.astype(BF16), "fsdp", axis=0, tiled=True, axis_index_groups=same_core
     )
-    gu_mine, gu_other, qkv_mine, qkv_other, output_rows = together(
-        gu_mine, gu_other, qkv_mine, qkv_other, output_weight
+    start = segment_starts(seq_lengths[0], length)
+    starts = (start[:, None], start[None, :])
+    gu_mine, gu_other, qkv_mine, qkv_other, starts, place, spot, output_rows = together(
+        gu_mine, gu_other, qkv_mine, qkv_other, starts, place, spot, output_weight.astype(BF16)
     )
 
     qkv_pairs = swap_pairs(qkv_mine, qkv_other)
     gu_pairs = swap_pairs(gu_mine, gu_other)
-    out_rows = gather_stage({0: output_rows.astype(BF16)}, plane_send, planes, 1)
-    qkv_pairs, gu_pairs, out_rows = together(qkv_pairs, gu_pairs, out_rows)
-
     qkv_got = exchange(qkv_pairs, chip_send)
     gu_near = plane_send(gu_pairs[1], 1)
-    for stage in range(2, stages + 1):
-        out_rows = gather_stage(out_rows, plane_send, planes, stage)
-    out_rows = jnp.stack([out_rows[far] for far in everyone])
+    out_rows = gather_stage({0: output_rows}, plane_send, planes, 1)
     qkv_got, gu_pairs, gu_near, tokens, out_rows = together(
         qkv_got, gu_pairs, gu_near, tokens, out_rows
     )
@@ -851,22 +914,10 @@
     gu_got = [gu_pairs[0], gu_near] + [
         plane_send(gu_pairs[step], step) for step in range(2, planes)
     ]
-    out_got = []
-    token_blocks = [tokens]
-    for step in range(chips):
-        if head_rows:
-            rows = lax.dynamic_index_in_dim(out_rows, (chip ^ step) ^ plane, 0, keepdims=False)
-            if step:
-                both = chip_send(jnp.concatenate([tokens, rows]), step)
-                token_blocks.append(both[:count])
-                rows = both[count:]
-            out_got.append(rows)
-        elif step:
-            token_blocks.append(chip_send(tokens, step))
-    start = segment_starts(seq_lengths[0], length)
+    token_blocks = gather(tokens, chip_send, chips)
     cosine, sine = rope_tables(jnp.arange(length, dtype=jnp.int32) - start)
-    gu_got, qkv_got, token_blocks, out_got, cosine, sine, w_down = together(
-        gu_got, qkv_got, token_blocks, out_got, cosine, sine, w_down
+    gu_got, qkv_got, token_blocks, cosine, sine, w_down, out_rows = together(
+        gu_got, qkv_got, token_blocks, cosine, sine, w_down, out_rows
     )
 
     tokens_mine = jnp.stack(token_blocks)
@@ -875,10 +926,14 @@
     qkv_rows = gather_rows(chip, core, qkv_got)
     steps = [step for step in range(chips) if ones(step) <= 1]
     w_gate_up = [gu_rows] + [chip_send(gu_rows, step) for step in steps[1:]]
-    w_qkv = {0: qkv_rows}
-    for stage in range(1, stages + 1):
+    w_qkv = gather_stage({0: qkv_rows}, plane_send, planes, 1)
+    w_qkv, out_rows = together(w_qkv, out_rows)
+    for stage in range(2, stages + 1):
         w_qkv = gather_stage(w_qkv, plane_send, planes, stage)
     w_qkv = [w_qkv[far] for far in everyone]
+    for stage in range(2, stages + 1):
+        out_rows = gather_stage(out_rows, plane_send, planes, stage)
+    out_rows = jnp.stack([out_rows[far] for far in everyone])
     w_gate_up, w_qkv, out_grad, tokens_mine, tokens_other, out_rows = together(
         w_gate_up, w_qkv, out_grad, tokens_mine, tokens_other, out_rows
     )
@@ -896,9 +951,8 @@
     layout = [(step, None) for step in steps] + [(step, side) for step in more for side in range(2)]
     w_gate_up = w_gate_up + [gate_up[step][side] for step in more for side in range(2)]
     normed, queries, keys_values, attended = attend(
-        spot, tokens_mine, tokens_other, w_qkv, start[:, None], cosine, sine
-    )
-    out_grad_blocks = gather_stage({0: out_grad}, plane_send, planes, 1)
+        spot, tokens_mine, tokens_other, w_qkv, starts[0], cosine, sine
+    )
     hop = members // planes
     own_plane = index // hop
 
@@ -906,7 +960,11 @@
         return [(i, ((turn_no + i) % planes) * hop + i // planes) for i in range(members)]
 
     if head_rows:
-        w_output = jnp.concatenate(out_got)
+        out_got = [
+            lax.dynamic_index_in_dim(out_rows, (chip ^ step) ^ plane, 0, keepdims=False)
+            for step in range(chips)
+        ]
+        w_output = [out_got[0]] + [chip_send(out_got[step], step) for step in range(1, chips)]
     else:
         w_output = jnp.zeros((planes, slice_rows, width), BF16)
         for turn_no in range(planes):
@@ -916,14 +974,12 @@
             got = lax.ppermute(sent, "fsdp", out_route(turn_no))
             spare = (own_plane + planes - turn_no) % planes
             w_output = lax.dynamic_update_index_in_dim(w_output, got, spare, 0)
-        w_output = w_output.reshape(planes * slice_rows, width)
-    w_gate_up, attended, out_grad_blocks, w_output = together(
-        w_gate_up, attended, out_grad_blocks, w_output
-    )
+        w_output = [w_output.reshape(planes * slice_rows, width)]
+    w_gate_up, attended, w_output, out_grad = together(w_gate_up, attended, w_output, out_grad)
 
     w_gate_up = list(zip(layout, w_gate_up))
-    for stage in range(2, stages + 1):
-        out_grad_blocks = gather_stage(out_grad_blocks, plane_send, planes, stage)
+    w_output = jnp.concatenate(w_output)
+    out_grad_blocks = gather_stage({0: out_grad}, plane_send, planes, 1)
     own_tokens = tokens.astype(F32)
     mixed = [over_cores(terms) for terms in zip(*project(attended, w_output, chips))]
     mixed = mixed[:1] + [
@@ -935,51 +991,55 @@
     scale_two = rms_scale(resid)
     own_normed_two = (resid * scale_two).astype(BF16)
     normed_blocks = gather_stage({0: own_normed_two}, plane_send, planes, 1)
-    out_grad_all = both_cores([out_grad_blocks[far] for far in everyone])
-    normed_blocks, out_grad_all = together(normed_blocks, out_grad_all)
-
-    for stage in range(2, stages + 1):
-        normed_blocks = gather_stage(normed_blocks, plane_send, planes, stage)
-    normed_two = both_cores([normed_blocks[far] for far in everyone])
-    normed_two, out_grad_all = together(normed_two, out_grad_all)
-
-    order = sorted(everyone, key=lambda j: (-ones(j), -j))
-    x = {far: normed_two[2 * far : 2 * far + 2] for far in everyone}
-    fed = {}
-    sums = ({}, {})
+    out_grad_pairs = {far: [block, core_swap(block)] for far, block in out_grad_blocks.items()}
+    normed_blocks, out_grad_pairs, out_grad_blocks = together(
+        normed_blocks, out_grad_pairs, out_grad_blocks
+    )
+
+    x = {far: [block, core_swap(block)] for far, block in normed_blocks.items()}
+    x, out_grad_pairs = together(x, out_grad_pairs)
+    fed = []
+    fed_order = []
+    sums = {}
+    result = {}
     last = []
-    moved_here = {}
-    for turn_no, far in enumerate(order):
-        span = slice(2 * far, 2 * far + 2)
-        fed[far] = feed(place, planes, x[far], out_grad_all[span], w_gate_up, w_down)
-        pair, moved = None, None
-        if turn_no >= 1:
-            pair = tuple(over_cores(fed[order[turn_no - 1]][side]) for side in (2, 1))
-        if turn_no >= 2:
-            near = order[turn_no - 2]
-            if ones(near) > 1:
-                moved = plane_send(sums[0][near].astype(BF16), near & -near)
-            else:
-                last.append(plane_send(sums[0][near].astype(BF16), near))
-        later = {j: x[j] for j in order[turn_no + 1 :]}
-        fed[far], later, pair, moved = together(fed[far], later, pair, moved)
-        x.update(later)
-        for side in (0, 1):
-            if pair is not None:
-                sums[side][order[turn_no - 1]] = pair[side]
-        if moved is not None:
-            moved_here.setdefault(near & (near - 1), []).append(moved)
-        for target in list(moved_here):
-            if target in sums[0]:
-                for part in moved_here.pop(target):
-                    sums[0][target] = sums[0][target] + part.astype(F32)
-    last.append(plane_send(sums[0][order[-2]].astype(BF16), order[-2]))
-    sums[1][0] = over_cores(fed[0][1])
-    grad_normed_two = over_cores(fed[0][2])
-    hidden, grad_gate, grad_up = zip(*[fed[far][0] for far in everyone])
+    sent = []
+    for stage in range(1, stages + 1):
+        batch = [far for far in reversed(everyone) if ones(far) == stage]
+        if stage == stages:
+            batch.append(0)
+        fed_order += batch
+        parts, outs, dxs = feed(
+            place,
+            planes,
+            [part for far in batch for part in x[far]],
+            [part for far in batch for part in out_grad_pairs[far]],
+            w_gate_up,
+            w_down,
+        )
+        last += [plane_send(sums[far].astype(BF16), far) for far in sent]
+        more = gather_stage(normed_blocks, plane_send, planes, stage + 1)
+        more_grad = gather_stage(out_grad_blocks, plane_send, planes, stage + 1)
+        parts, outs, dxs, last, normed_blocks, out_grad_blocks = together(
+            parts, outs, dxs, last, more, more_grad
+        )
+        fed.append(parts)
+        for blocks, pairs in ((normed_blocks, x), (out_grad_blocks, out_grad_pairs)):
+            for far, block in blocks.items():
+                if far not in pairs:
+                    pairs[far] = [block, core_swap(block)]
+        for at, far in enumerate(batch):
+            sums[far] = over_cores(dxs[2 * at : 2 * at + 2])
+            result[far] = over_cores(outs[2 * at : 2 * at + 2])
+        x, sums, out_grad_pairs = together(x, sums, out_grad_pairs)
+        sent = [far for far in batch if far]
+    last += [plane_send(sums[far].astype(BF16), far) for far in sent]
+    hidden, grad_gate, grad_up = zip(*fed)
     lanes = w_gate_up[0][1].shape[-1]
-    grads = feed_grad(place, planes, chips, normed_two, grad_gate, grad_up, lanes)
-    grad_normed_two, last, grads, result = together(grad_normed_two, last, grads, sums[1])
+    fed_x = [part for far in fed_order for part in x[far]]
+    fed_grad = [part for far in fed_order for part in out_grad_pairs[far]]
+    grads = feed_grad(place, planes, chips, fed_x, grad_gate, grad_up, lanes)
+    grad_normed_two, last, grads, result = together(sums[0], last, grads, result)
     grad_normed_two = sum([part.astype(F32) for part in last], grad_normed_two)
 
     grad_resid = (
@@ -995,14 +1055,11 @@
     grad_blocks = gather(own_grad, chip_send, chips)
     for stage in range(stages, 1, -1):
         result = scatter_stage(result, plane_send, stage)
-    grad_down = rows_grad(jnp.concatenate(hidden), out_grad_all)
+    grad_down = rows_grad(jnp.concatenate(hidden), fed_grad)
     grad_blocks, result, grad_down = together(grad_blocks, result, grad_down)
 
     grad_attn_out = both_cores(grad_blocks)
-    grad_output = rows_grad(attended, grad_attn_out).reshape(planes, slice_rows, width)
-    grad_output, grad_attn_out, grads, result = together(
-        grad_output, grad_attn_out, grads, result
-    )
+    grad_attn_out, grads, result = together(grad_attn_out, grads, result)
 
     result = scatter_stage(result, plane_send, 1)[0]
     grad_gate_up = {step: grads[2 * step - 1 : 2 * step + 1] for step in range(1, chips)}
@@ -1022,28 +1079,45 @@
                 grad_gate_up[low] = (grad_gate_up[low][0], plus(grad_gate_up[low][1], up))
     grad_gate_up = {step: jnp.stack(pair) for step, pair in grad_gate_up.items()}
     grad_qkv = attend_back(
-        spot, queries, keys_values, w_output, grad_attn_out, start[None, :], cosine, sine
-    )
-    grad_qkv, result, grad_gate_up = together(grad_qkv, result, grad_gate_up)
+        spot, queries, keys_values, w_output, grad_attn_out, starts[1], cosine, sine
+    )
+    grad_qkv, result, grad_gate_up, grad_attn_out = together(
+        grad_qkv, result, grad_gate_up, grad_attn_out
+    )
     result = (resid + result).astype(BF16)
 
-    grad_w_qkv = qkv_grad(spot, normed, grad_qkv, planes)
-    grad_qkv, grad_w_qkv, grad_gate_up = together(grad_qkv, grad_w_qkv, grad_gate_up)
-
     grad_gate_up = [grads[0]] + [chip_send(part, step) for step, part in grad_gate_up.items()]
-    grad_w_qkv = dict(enumerate(grad_w_qkv))
+    grad_w_qkv = dict(enumerate(qkv_grad(spot, normed, grad_qkv, planes)))
     for stage in range(stages, 0, -1):
         grad_w_qkv = scatter_stage(grad_w_qkv, plane_send, stage)
-    mixed = [over_cores(terms) for terms in zip(*project_back(spot, grad_qkv, w_qkv, chips))]
-    mixed, grad_w_qkv, grad_gate_up, grad_down, grad_output = together(
-        mixed, grad_w_qkv[0], grad_gate_up, grad_down, grad_output
+    mixed = project_back(spot, grad_qkv, w_qkv, chips)
+    grad_output = rows_grad(attended, grad_attn_out).reshape(planes, slice_rows, width)
+    grad_gate_up, grad_w_qkv, mixed, grad_output = together(
+        grad_gate_up, grad_w_qkv[0], mixed, grad_output
+    )
+
+    gu_pairs = swap_pairs(*spread_rows(plane, core, grad_gate_up, planes))
+    qkv_pairs = swap_pairs(*spread_rows(chip, core, [grad_w_qkv], chips))
+    mixed = [(mine, core_swap(other)) for mine, other in zip(*mixed)]
+    gu_pairs, qkv_pairs, mixed, grad_output, grad_down = together(
+        gu_pairs, qkv_pairs, mixed, grad_output, grad_down
     )
 
     grad_down_weight = lax.psum_scatter(
         grad_down, "fsdp", scatter_dimension=0, tiled=True, axis_index_groups=same_core
     ).astype(F32)
-    gu_pairs = swap_pairs(*spread_rows(plane, core, grad_gate_up, planes))
-    qkv_pairs = swap_pairs(*spread_rows(chip, core, [grad_w_qkv], chips))
+    got = exchange(qkv_pairs, chip_send)
+    mixed = [mine + other.astype(F32) for mine, other in mixed]
+    far_pairs = gu_pairs[planes // 2 + 1 :]
+    near_got = exchange(gu_pairs[: planes // 2 + 1], plane_send)
+    far_pairs, near_got, got, mixed, grad_output = together(
+        far_pairs, near_got, got, mixed, grad_output
+    )
+
+    far_got = [
+        plane_send(pair, planes // 2 + 1 + step) for step, pair in enumerate(far_pairs)
+    ]
+    grad_gate_up = near_got + far_got
     mixed = dict(enumerate(mixed))
     for stage in range(chip_stages, 1, -1):
         mixed = scatter_stage(mixed, chip_send, stage)
@@ -1064,36 +1138,25 @@
                 parts, part, ((turn_no + index) % planes) ^ plane, 0
             )
         out_parts = [parts[far] for far in everyone]
-    gu_pairs, qkv_pairs, mixed, out_parts = together(gu_pairs, qkv_pairs, mixed, out_parts)
-
-    grad_gate_up = exchange(gu_pairs, plane_send)
-    got = exchange(qkv_pairs, chip_send)
-    got = by_offset(jnp.concatenate(got), index).astype(F32)
-    got = jnp.transpose(got, (1, 0, 2))
-    grad_query = got[:, :, :own_q].reshape(slice_rows, HEADS, HEAD_DIM)
-    kept = [head for device_heads in heads for head in device_heads]
-    grad_query = jnp.stack([grad_query[:, kept.index(head)] for head in range(HEADS)], 1)
-    grad_query = grad_query.reshape(slice_rows, -1)
-    grad_kv = got[:, :, own_q:].reshape(slice_rows, KV_HEADS, sharing, PAIR).sum(2)
-    grad_key = grad_kv[:, :, :HEAD_DIM].reshape(slice_rows, -1)
-    grad_value = grad_kv[:, :, HEAD_DIM:].reshape(slice_rows, -1)
-
-    gain_one = gain_columns[:, :1]
-    grad_gain_one = sum(
-        jnp.sum(weight.astype(BF16).astype(F32) * gradient, 1)
-        for weight, gradient in (
-            (query_weight, grad_query),
-            (key_weight, grad_key),
-            (value_weight, grad_value),
-        )
-    )
-    attention_new = (
-        adam_step(query_weight, query_first, query_second, grad_query * gain_one, 0.02)
-        + adam_step(key_weight, key_first, key_second, grad_key * gain_one, 0.02)
-        + adam_step(value_weight, value_first, value_second, grad_value * gain_one, 0.02)
-    )
-    grad_gate_up, attention_new, grad_gain_one, out_parts, mixed, grad_down_weight = together(
-        grad_gate_up, attention_new, grad_gain_one, out_parts, mixed, grad_down_weight
+    attention_new, grad_gain_one = attention_adam(
+        place,
+        heads,
+        gain_columns,
+        got,
+        (
+            query_weight,
+            query_first,
+            query_second,
+            key_weight,
+            key_first,
+            key_second,
+            value_weight,
+            value_first,
+            value_second,
+        ),
+    )
+    grad_gate_up, grad_gain_one, out_parts, mixed, grad_down_weight = together(
+        grad_gate_up, grad_gain_one, out_parts, mixed, grad_down_weight
     )
 
     grad_normed = scatter_stage(mixed, chip_send, 1)[0]

time: 556 us -> 526 us (0.946)
  waiting for transfers between devices: 232 us -> 194 us
  starting transfers between devices: 77.8 us -> 97.7 us
  local copies, waits for them, and re-layouts: 28.3 us -> 22.3 us
    ppermute x29 -> x32, waiting for transfers between devices: 98.3 us -> 64.9 us  [chip_send(): lax.ppermute(value, 'fsdp', [(i, i ^ 2 * step) for i in range(members)])]
    ppermute x30, starting transfers between devices: 37.2 us -> 53 us  [plane_send(): return lax.ppermute(value, 'dp', [(i, i ^ step) for i in range(planes)])]
    pallas_call x4 -> x2, Pallas kernels: 44.7 us -> 37.2 us  [feed(): pl.pallas_call(functools.partial(feed_kernel, planes, layout, count), out...]
    add x1 -> x4, other arithmetic: 0.01 us -> 5.83 us  [local(): mixed = [mine + other.astype(F32) for mine, other in mixed]]
    pallas_call x1 -> x2, Pallas kernels: 11.1 us -> 15.4 us  [the longest x1 11.1 us: feed_grad(): pl.pallas_call(functools.partial(feed_grad_kernel, planes, chips, len(x),...]
    ppermute x29 -> x32, starting transfers between devices: 33.6 us -> 37 us  [chip_send(): lax.ppermute(value, 'fsdp', [(i, i ^ 2 * step) for i in range(members)])]
    unnamed x192 -> x177, local copies, waits for them, and re-layouts: 8.9 us -> 11.9 us
  transfers between devices with their start and end apart: 94 -> 97, of which waited for: 42 -> 34; matrix products, arithmetic and copies ran while one was open for 11% -> 10% of each run, Pallas kernels for 21% -> 25%
where the time goes in v4:
time: 526 us; the launch traced here: 522 us
  waiting for transfers between devices  194 us (37%)
  Pallas kernels  140 us (27%)
  starting transfers between devices  97.7 us (19%)
  other arithmetic  51.3 us (10%)
  local copies, waits for them, and re-layouts  22.3 us (4%)
  between operations  15.5 us (3%)
    ppermute x30, waiting for transfers between devices, plane_send(): return lax.ppermute(value, 'dp', [(i, i ^ step) for i in range(planes)])  122 us
    ppermute x32, waiting for transfers between devices, chip_send(): lax.ppermute(value, 'fsdp', [(i, i ^ 2 * step) for i in range(members)])  64.9 us
    ppermute x30, starting transfers between devices, plane_send(): return lax.ppermute(value, 'dp', [(i, i ^ step) for i in range(planes)])  53 us
    pallas_call x2, Pallas kernels, feed(): pl.pallas_call(functools.partial(feed_kernel, planes, layout, count), out...  37.2 us
    ppermute x32, starting transfers between devices, chip_send(): lax.ppermute(value, 'fsdp', [(i, i ^ 2 * step) for i in range(members)])  37 us
    pallas_call x1, Pallas kernels, attend_back(): pl.pallas_call(functools.partial(attend_back_kernel, members, pairs), out...  18.4 us
    pallas_call x1, Pallas kernels, attend(): pl.pallas_call(functools.partial(attend_kernel, members, pairs, planes),...  14.9 us
    pallas_call x2, Pallas kernels, rows_grad(): pl.pallas_call(functools.partial(rows_grad_kernel, len(grads)), out_shape...  12.1 us
  transfers between devices with their start and end apart: 97, of which 34 were waited for; matrix products, arithmetic and copies ran while one was open for 10% of the time, Pallas kernels for 25%

profile of v4, /device:TPU:0, one launch (start us, length us, event | category | flops | bytes accessed | tf_op | source)
XLA Modules:
  0.0 521.6 jit_solution(7258567712862641155)
XLA Ops:
  7.3 2.4 convert_element_type.207
  11.2 6.1 %pack.1 = (bf16[4,2,64,768]{3,2,1,0:T(8,128)(2,1)}, bf16[4,2,64,768]{3,2,1,0:T(8,128)(2,1)}, bf16[4,64,384]{2,1,0:T(8,128)(2,1)}, bf16[4,64,384]{2,1,0:T(8,128)(2,1)}) custom-call(s32[3]{0:T(128)} %pad_add_fusion.place, f32[64,2]{1,0:T(8,128)} %bitcast.65, f32[64,5632]{1,0:T(8,128)} %refs_4_.3, f32[64,5632]{1,0:T(8,128)} %refs_7_.3, f32[64,2048]{1,0:T(8,128)} %refs_4_.2, ...), custom_call_target="tpu_custom_call" | custom-call | bytes 4325376 | tf_op jit(solution)/shard_map/pack/pallas_call | solution.py:206
  18.0 4.1 collective-permute-start.7
  30.9 3.3 collective-permute-done.7
  34.2 2.5 collective-permute-start.3
  36.8 2.9 collective-permute-done.3.refs_3_
  39.7 3.1 collective-permute-done.5.refs_1_
  42.8 2.6 collective-permute-start.12
  47.8 2.5 collective-permute-start.9
  54.1 20.3 %collective-permute-done.8.refs_2_ = bf16[2,2,64,768]{3,2,1,0:T(8,128)(2,1)S(1)} collective-permute-done((bf16[2,2,64,768]{3,2,1,0:T(8,128)(2,1)S(1)}, bf16[2,2,64,768]{3,2,1,0:T(8,128)(2,1)S(1)}, u32[]{:S(2)}, u32[]{:S(2)}) %collective-permute-start.8) | collective-permute-done | bytes 393248 | tf_op jit(solution)/shard_map/ppermute | solution.py:65
  74.4 4.9 collective-permute-done.11
  80.4 2.7 gather_rows.2.refs_8_
  87.5 5.6 %collective-permute-start.16 = (bf16[512,384]{1,0:T(8,128)(2,1)}, bf16[512,384]{1,0:T(8,128)(2,1)S(1)}, u32[]{:S(2)}, u32[]{:S(2)}) collective-permute-start(bf16[512,384]{1,0:T(8,128)(2,1)} %gather_rows.3.refs_2_.refs_0_), channel_id=1, source_target_pairs={{0,16},{8,24},{16,0},{24,8},{1,17},{9,25},{17,1},{25,9},{2,18},{10... | collective-permute-start | bytes 1179656 | tf_op jit(solution)/shard_map/ppermute | solution.py:65
  93.1 17.7 %collective-permute-done.16.refs_4_.refs_2_ = bf16[512,384]{1,0:T(8,128)(2,1)S(1)} collective-permute-done((bf16[512,384]{1,0:T(8,128)(2,1)}, bf16[512,384]{1,0:T(8,128)(2,1)S(1)}, u32[]{:S(2)}, u32[]{:S(2)}) %collective-permute-start.16) | collective-permute-done | bytes 393248 | tf_op jit(solution)/shard_map/ppermute | solution.py:65
  112.9 7.2 %collective-permute-done.19 = bf16[64,2048]{1,0:T(8,128)(2,1)S(1)} collective-permute-done((bf16[64,2048]{1,0:T(8,128)(2,1)S(1)}, bf16[64,2048]{1,0:T(8,128)(2,1)S(1)}, u32[]{:S(2)}, u32[]{:S(2)}) %collective-permute-start.19) | collective-permute-done | bytes 262176 | tf_op jit(solution)/shard_map/ppermute | solution.py:65
  120.3 6.5 %collective-permute-done.17.refs_5_.refs_3_ = bf16[512,384]{1,0:T(8,128)(2,1)S(1)} collective-permute-done((bf16[512,384]{1,0:T(8,128)(2,1)S(1)}, bf16[512,384]{1,0:T(8,128)(2,1)S(1)}, u32[]{:S(2)}, u32[]{:S(2)}) %collective-permute-start.17) | collective-permute-done | bytes 393248 | tf_op jit(solution)/shard_map/ppermute | solution.py:65
  136.5 14.9 %attend.1 = (bf16[1024,2048]{1,0:T(8,128)(2,1)}, bf16[1024,256]{1,0:T(8,128)(2,1)}, bf16[1024,128]{1,0:T(8,128)(2,1)}, bf16[1024,256]{1,0:T(8,128)(2,1)}) custom-call(s32[2]{0:T(128)} %pad_add_fusion.1.place, s32[1024,1]{1,0:T(8,128)} %copy.60.start_ref, f32[1024,128]{1,0:T(8,128)} %get-tuple-element.423.cos_ref, f32[1024,128]{1,0:T(8,128)} %get-tuple-element.424.sin_ref, ...), custom_call_target="tpu_custom_call" | custom-call | flops 2415919104 | bytes 8388608 | tf_op jit(solution)/shard_map/attend/pallas_call | solution.py:338
  151.4 4.7 collective-permute-done.24
  156.0 3.3 collective-permute-done.23
  160.4 4.4 project.1
  174.8 8.3 %collective-permute-done.27 = bf16[128,2048]{1,0:T(8,128)(2,1)S(1)} collective-permute-done((bf16[128,2048]{1,0:T(8,128)(2,1)S(1)}, bf16[128,2048]{1,0:T(8,128)(2,1)S(1)}, u32[]{:S(2)}, u32[]{:S(2)}) %collective-permute-start.27) | collective-permute-done | bytes 524320 | tf_op jit(solution)/shard_map/ppermute | solution.py:60
  183.2 11.6 %collective-permute-done.29 = bf16[128,2048]{1,0:T(8,128)(2,1)S(1)} collective-permute-done((bf16[128,2048]{1,0:T(8,128)(2,1)S(1)}, bf16[128,2048]{1,0:T(8,128)(2,1)S(1)}, u32[]{:S(2)}, u32[]{:S(2)}) %collective-permute-start.29) | collective-permute-done | bytes 524320 | tf_op jit(solution)/shard_map/ppermute | solution.py:60
  195.3 2.3 collective-permute-done.33.refs_4_.refs_0_
  201.0 21.8 %collective-permute-done.35.refs_0_ = bf16[128,2048]{1,0:T(8,128)(2,1)S(1)} collective-permute-done((bf16[128,2048]{1,0:T(8,128)(2,1)S(1)}, bf16[128,2048]{1,0:T(8,128)(2,1)S(1)}, u32[]{:S(2)}, u32[]{:S(2)}) %collective-permute-start.35) | collective-permute-done | bytes 524320 | tf_op jit(solution)/shard_map/ppermute | solution.py:65
  227.2 18.7 %feed.2 = (bf16[512,704]{1,0:T(8,128)(2,1)}, bf16[512,704]{1,0:T(8,128)(2,1)}, bf16[512,704]{1,0:T(8,128)(2,1)}, f32[128,2048]{1,0:T(8,128)}, bf16[128,2048]{1,0...) custom-call(s32[3]{0:T(128)} %pad_add_fusion.place, ...), custom_call_target="tpu_custom_call" | custom-call | flops 8858370048 | bytes 8650752 | tf_op jit(solution)/shard_map/feed/pallas_call | solution.py:617
  245.9 3.0 collective-permute-done.43.refs_4_
  257.4 18.5 %feed.3 = (bf16[512,704]{1,0:T(8,128)(2,1)}, bf16[512,704]{1,0:T(8,128)(2,1)}, bf16[512,704]{1,0:T(8,128)(2,1)}, f32[128,2048]{1,0:T(8,128)}, bf16[128,2048]{1,0...) custom-call(s32[3]{0:T(128)} %pad_add_fusion.place, ...), custom_call_target="tpu_custom_call" | custom-call | flops 8858370048 | bytes 8650752 | tf_op jit(solution)/shard_map/feed/pallas_call | solution.py:617
  275.9 4.8 collective-permute-done.48
  287.2 11.1 %feed_grad.1 = (bf16[2,512,768]{2,1,0:T(8,128)(2,1)}, bf16[512,768]{1,0:T(8,128)(2,1)}, bf16[512,768]{1,0:T(8,128)(2,1)}, bf16[512,768]{1,0:T(8,128)(2,1)}, bf16...) custom-call(s32[3]{0:T(128)} %pad_add_fusion.place, bf16[128,2048]{1,0:T(8,128)(2,1)} %copy-done.71, ...), custom_call_target="tpu_custom_call" | custom-call | flops 5905580032 | bytes 5767168 | tf_op jit(solution)/shard_map/feed_grad/pallas_call | solution.py:675
  303.9 9.4 %collective-permute-start.60 = (bf16[128,2048]{1,0:T(8,128)(2,1)}, bf16[128,2048]{1,0:T(8,128)(2,1)}, u32[]{:S(2)}, u32[]{:S(2)}) collective-permute-start(bf16[128,2048]{1,0:T(8,128)(2,1)} %convert_add_fusion.10), channel_id=1, source_target_pairs={{0,8},{8,0},{16,24},{24,16},{1,9},{9,1},{17,25},{25,17},{2,10},{10... | collective-permute-start | bytes 1572872 | tf_op jit(solution)/shard_map/ppermute | solution.py:65
  318.3 7.6 %rows_grad.2 = bf16[704,2048]{1,0:T(8,128)(2,1)} custom-call(bf16[1024,704]{1,0:T(8,128)(2,1)} %pad_maximum_fusion.1.left_ref, bf16[128,2048]{1,0:T(8,128)(2,1)} %copy-done.65, bf16[128,2048]{1,0:T(8,128)(2,1)} %copy-done.69, bf16[128,2048]{1,0:T(8,128)(2,1)} %copy-done.66, bf16[128,2048]{1,0:T(8,128)(2,1)} %copy-done.68, bf16[128,2048]{1,0:T(8,128)(2,1)} %copy-done.70, ...), custom_call_target="tpu_custom_call" | custom-call | flops 2952790016 | bytes 1441792 | tf_op jit(solution)/shard_map/rows_grad/pallas_call | solution.py:530
  329.3 9.3 %collective-permute-done.58.refs_4_ = bf16[128,2048]{1,0:T(8,128)(2,1)} collective-permute-done((bf16[128,2048]{1,0:T(8,128)(2,1)S(1)}, bf16[128,2048]{1,0:T(8,128)(2,1)}, u32[]{:S(2)}, u32[]{:S(2)}) %collective-permute-start.58) | collective-permute-done | bytes 524320 | tf_op jit(solution)/shard_map/ppermute | solution.py:60
  348.3 18.4 %attend_back.1.grad_ref.left_ref = bf16[1024,384]{1,0:T(8,128)(2,1)} custom-call(s32[2]{0:T(128)} %pad_add_fusion.1.place, s32[1,1024]{1,0:T(1,128)} %bitcast.78, f32[1024,128]{1,0:T(8,128)} %get-tuple-element.423.cos_ref, f32[1024,128]{1,0:T(8,128)} %get-tuple-element.424.sin_ref, bf16[1024,256]{1,0:T(8,128)(2,1)} %get-tuple-element.450.q_ref, ...), custom_call_target="tpu_custom_call" | custom-call | flops 2952790016 | bytes 4194304 | tf_op jit(solution)/shard_map/attend_back/pallas_call | solution.py:428
  366.7 2.9 collective-permute-done.65
  375.5 5.5 %qkv_grad.1 = (bf16[512,384]{1,0:T(8,128)(2,1)}, bf16[512,384]{1,0:T(8,128)(2,1)}, bf16[512,384]{1,0:T(8,128)(2,1)}, bf16[512,384]{1,0:T(8,128)(2,1)}) custom-call(s32[2]{0:T(128)} %pad_add_fusion.1.place, bf16[1024,2048]{1,0:T(8,128)(2,1)} %get-tuple-element.625.normed_ref, bf16[1024,384]{1,0:T(8,128)(2,1)} %attend_back.1.grad_ref.left_ref), custom_call_target="tpu_custom_call" | custom-call | flops 1610612736 | bytes 4194304 | tf_op jit(solution)/shard_map/qkv_grad/pallas_call | solution.py:507
  383.1 10.2 %collective-permute-done.71 = bf16[512,384]{1,0:T(8,128)(2,1)S(1)} collective-permute-done((bf16[512,384]{1,0:T(8,128)(2,1)}, bf16[512,384]{1,0:T(8,128)(2,1)S(1)}, u32[]{:S(2)}, u32[]{:S(2)}) %collective-permute-start.71) | collective-permute-done | bytes 393248 | tf_op jit(solution)/shard_map/ppermute | solution.py:65
  395.0 4.6 rows_grad.3
  399.6 6.2 %project_back.1 = (f32[128,2048]{1,0:T(8,128)}, f32[128,2048]{1,0:T(8,128)}, f32[128,2048]{1,0:T(8,128)}, f32[128,2048]{1,0:T(8,128)}, bf16[128,2048]{1,0:T(8,12...) custom-call(s32[2]{0:T(128)} %pad_add_fusion.1.place, ...), custom_call_target="tpu_custom_call" | custom-call | flops 1610612736 | bytes 6291456 | tf_op jit(solution)/shard_map/project_back/pallas_call | solution.py:486
  405.8 6.1 %collective-permute-done.72 = bf16[512,384]{1,0:T(8,128)(2,1)} collective-permute-done((bf16[512,384]{1,0:T(8,128)(2,1)S(1)}, bf16[512,384]{1,0:T(8,128)(2,1)}, u32[]{:S(2)}, u32[]{:S(2)}) %collective-permute-start.72) | collective-permute-done | bytes 393248 | tf_op jit(solution)/shard_map/ppermute | solution.py:65
  415.9 4.1 spread_rows.2
  434.6 2.6 collective-permute-start.81
  443.4 9.8 %collective-permute-done.80.refs_1_ = bf16[2,2,64,768]{3,2,1,0:T(8,128)(2,1)S(1)} collective-permute-done((bf16[2,2,64,768]{3,2,1,0:T(8,128)(2,1)}, bf16[2,2,64,768]{3,2,1,0:T(8,128)(2,1)S(1)}, u32[]{:S(2)}, u32[]{:S(2)}) %collective-permute-start.80) | collective-permute-done | bytes 393248 | tf_op jit(solution)/shard_map/ppermute | solution.py:65
  461.9 4.3 attention_adam.1
  467.1 4.2 collective-permute-done.87
  471.3 5.7 %collective-permute-done.86 = bf16[64,2048]{1,0:T(8,128)(2,1)S(1)} collective-permute-done((bf16[64,2048]{1,0:T(8,128)(2,1)S(1)}, bf16[64,2048]{1,0:T(8,128)(2,1)S(1)}, u32[]{:S(2)}, u32[]{:S(2)}) %collective-permute-start.86) | collective-permute-done | bytes 262176 | tf_op jit(solution)/shard_map/ppermute | solution.py:60
  478.1 8.0 %collective-permute-done.89 = bf16[128,2048]{1,0:T(8,128)(2,1)S(1)} collective-permute-done((bf16[128,2048]{1,0:T(8,128)(2,1)S(1)}, bf16[128,2048]{1,0:T(8,128)(2,1)S(1)}, u32[]{:S(2)}, u32[]{:S(2)}) %collective-permute-start.89) | collective-permute-done | bytes 524320 | tf_op jit(solution)/shard_map/ppermute | solution.py:60
  494.6 4.6 multiply_subtract_fusion
  499.3 9.7 %feed_adam.1 = (f32[64,5632]{1,0:T(8,128)}, f32[64,5632]{1,0:T(8,128)}, f32[64,5632]{1,0:T(8,128)}, f32[64,5632]{1,0:T(8,128)}, f32[64,5632]{1,0:T(8,128)}, /*index=5*/f32[64,5632]{1,0:T(8,128)}, f32[64,128]{1,0:T(8,128)}) custom-call(s32[3]{0:T(128)} %pad_add_fusion.place, f32[64,2]{1,0:T(8,128)} %bitcast.67, ...), custom_call_target="tpu_custom_call" | custom-call | flops 14417920 | bytes 18743296 | tf_op jit(solution)/shard_map/feed_adam/pallas_call | solution.py:724
  (433 shorter events, 151.3 us)
Async XLA Ops:
  7.2 72.1 %all-gather.2.cloned.1.call-start = ((), (), s32[]{:S(2)}) async-start(), calls=%async_computation.1 | async-start | bytes 3604480 | tf_op jit(solution)/shard_map/all_gather | solution.py:896
  9.7 477.4 %reduce-scatter.2.cloned.1.call-start = ((), (), s32[]{:S(2)}) async-start(), calls=%async_computation.2 | async-start | bytes 3604480 | tf_op jit(solution)/shard_map/reduce_scatter | solution.py:1106
  42.8 31.5 %collective-permute-start.12 = (bf16[128,2048]{1,0:T(8,128)(2,1)S(1)}, bf16[128,2048]{1,0:T(8,128)(2,1)S(1)}, u32[]{:S(2)}, u32[]{:S(2)}) collective-permute-start(bf16[128,2048]{1,0:T(8,128)(2,1)S(1)} %copy-done), channel_id=1, source_target_pairs={{0,6},{1,7},{2,4},{3,5},{4,2},{5,3},{6,0},{7,1},{8,14},{9,15},{10,... | collective-permute-start | bytes 1572872 | tf_op jit(solution)/shard_map/ppermute | solution.py:60
  45.4 33.9 %collective-permute-start.11 = (bf16[128,2048]{1,0:T(8,128)(2,1)S(1)}, bf16[128,2048]{1,0:T(8,128)(2,1)S(1)}, u32[]{:S(2)}, u32[]{:S(2)}) collective-permute-start(bf16[128,2048]{1,0:T(8,128)(2,1)S(1)} %copy-done), channel_id=1, source_target_pairs={{0,4},{1,5},{2,6},{3,7},{4,0},{5,1},{6,2},{7,3},{8,12},{9,13},{10,... | collective-permute-start | bytes 1572872 | tf_op jit(solution)/shard_map/ppermute | solution.py:60
  45.9 33.4 %collective-permute-start.10 = (bf16[128,2048]{1,0:T(8,128)(2,1)S(1)}, bf16[128,2048]{1,0:T(8,128)(2,1)S(1)}, u32[]{:S(2)}, u32[]{:S(2)}) collective-permute-start(bf16[128,2048]{1,0:T(8,128)(2,1)S(1)} %copy-done), channel_id=1, source_target_pairs={{0,2},{1,3},{2,0},{3,1},{4,6},{5,7},{6,4},{7,5},{8,10},{9,11},{10,... | collective-permute-start | bytes 1572872 | tf_op jit(solution)/shard_map/ppermute | solution.py:60
  46.4 28.0 %collective-permute-start.8 = (bf16[2,2,64,768]{3,2,1,0:T(8,128)(2,1)S(1)}, bf16[2,2,64,768]{3,2,1,0:T(8,128)(2,1)S(1)}, u32[]{:S(2)}, u32[]{:S(2)}) collective-permute-start(bf16[2,2,64,768]{3,2,1,0:T(8,128)(2,1)S(1)} %get-tuple-element.388), channel_id=1, source_target_pairs={{0,16},{8,24},{16,0},{24,8},{1,17},{9,25},{17,1},{25,9},{2,18},{10... | collective-permute-start | bytes 1179656 | tf_op jit(solution)/shard_map/ppermute | solution.py:65
  47.8 26.5 %collective-permute-start.9 = (bf16[2,2,64,768]{3,2,1,0:T(8,128)(2,1)S(1)}, bf16[2,2,64,768]{3,2,1,0:T(8,128)(2,1)S(1)}, u32[]{:S(2)}, u32[]{:S(2)}) collective-permute-start(bf16[2,2,64,768]{3,2,1,0:T(8,128)(2,1)S(1)} %pad_maximum_fusion.11), channel_id=1, source_target_pairs={{0,24},{8,16},{16,8},{24,0},{1,25},{9,17},{17,9},{25,1},{2,26},{10... | collective-permute-start | bytes 1179656 | tf_op jit(solution)/shard_map/ppermute | solution.py:65
  79.6 48.9 %collective-permute-start.18 = (bf16[4,128,2048]{2,1,0:T(8,128)(2,1)S(1)}, bf16[4,128,2048]{2,1,0:T(8,128)(2,1)}, u32[]{:S(2)}, u32[]{:S(2)}) collective-permute-start(bf16[4,128,2048]{2,1,0:T(8,128)(2,1)S(1)} %pad_maximum_fusion.refs_0_), channel_id=1, source_target_pairs={{0,1},{1,0},{2,3},{3,2},{4,5},{5,4},{6,7},{7,6},{8,9},{9,8},{10,11... | collective-permute-start | bytes 6291464 | tf_op jit(solution)/shard_map/ppermute | solution.py:55
  83.1 43.7 %collective-permute-start.14 = (bf16[2,512,768]{2,1,0:T(8,128)(2,1)}, bf16[2,512,768]{2,1,0:T(8,128)(2,1)S(1)}, u32[]{:S(2)}, u32[]{:S(2)}) collective-permute-start(bf16[2,512,768]{2,1,0:T(8,128)(2,1)} %gather_rows.2.refs_8_), channel_id=1, source_target_pairs={{0,4},{1,5},{2,6},{3,7},{4,0},{5,1},{6,2},{7,3},{8,12},{9,13},{10,... | collective-permute-start | bytes 4718600 | tf_op jit(solution)/shard_map/ppermute | solution.py:60
  84.5 42.3 %collective-permute-start.13 = (bf16[2,512,768]{2,1,0:T(8,128)(2,1)}, bf16[2,512,768]{2,1,0:T(8,128)(2,1)S(1)}, u32[]{:S(2)}, u32[]{:S(2)}) collective-permute-start(bf16[2,512,768]{2,1,0:T(8,128)(2,1)} %gather_rows.2.refs_8_), channel_id=1, source_target_pairs={{0,2},{1,3},{2,0},{3,1},{4,6},{5,7},{6,4},{7,5},{8,10},{9,11},{10,... | collective-permute-start | bytes 4718600 | tf_op jit(solution)/shard_map/ppermute | solution.py:60
  87.5 23.3 %collective-permute-start.16 = (bf16[512,384]{1,0:T(8,128)(2,1)}, bf16[512,384]{1,0:T(8,128)(2,1)S(1)}, u32[]{:S(2)}, u32[]{:S(2)}) collective-permute-start(bf16[512,384]{1,0:T(8,128)(2,1)} %gather_rows.3.refs_2_.refs_0_), channel_id=1, source_target_pairs={{0,16},{8,24},{16,0},{24,8},{1,17},{9,25},{17,1},{25,9},{2,18},{10... | collective-permute-start | bytes 1179656 | tf_op jit(solution)/shard_map/ppermute | solution.py:65
  129.8 29.6 %collective-permute-start.20 = (bf16[512,768]{1,0:T(8,128)(2,1)S(1)}, bf16[512,768]{1,0:T(8,128)(2,1)}, u32[]{:S(2)}, u32[]{:S(2)}) collective-permute-start(bf16[512,768]{1,0:T(8,128)(2,1)S(1)} %slice_bitcast_fusion.1), channel_id=1, source_target_pairs={{0,2},{1,3},{2,0},{3,1},{4,6},{5,7},{6,4},{7,5},{8,10},{9,11},{10,... | collective-permute-start | bytes 2359304 | tf_op jit(solution)/shard_map/ppermute | solution.py:60
  130.5 28.8 %collective-permute-start.21 = (bf16[512,768]{1,0:T(8,128)(2,1)S(1)}, bf16[512,768]{1,0:T(8,128)(2,1)}, u32[]{:S(2)}, u32[]{:S(2)}) collective-permute-start(bf16[512,768]{1,0:T(8,128)(2,1)S(1)} %slice_bitcast_fusion), channel_id=1, source_target_pairs={{0,4},{1,5},{2,6},{3,7},{4,0},{5,1},{6,2},{7,3},{8,12},{9,13},{10,... | collective-permute-start | bytes 2359304 | tf_op jit(solution)/shard_map/ppermute | solution.py:60
  131.9 24.1 %collective-permute-start.24 = (bf16[64,2048]{1,0:T(8,128)(2,1)}, bf16[64,2048]{1,0:T(8,128)(2,1)S(1)}, u32[]{:S(2)}, u32[]{:S(2)}) collective-permute-start(bf16[64,2048]{1,0:T(8,128)(2,1)} %get-tuple-element.747), channel_id=1, source_target_pairs={{0,6},{1,7},{2,4},{3,5},{4,2},{5,3},{6,0},{7,1},{8,14},{9,15},{10,... | collective-permute-start | bytes 786440 | tf_op jit(solution)/shard_map/ppermute | solution.py:60
  134.2 25.1 %collective-permute-start.23 = (bf16[64,2048]{1,0:T(8,128)(2,1)}, bf16[64,2048]{1,0:T(8,128)(2,1)S(1)}, u32[]{:S(2)}, u32[]{:S(2)}) collective-permute-start(bf16[64,2048]{1,0:T(8,128)(2,1)} %get-tuple-element.748), channel_id=1, source_target_pairs={{0,4},{1,5},{2,6},{3,7},{4,0},{5,1},{6,2},{7,3},{8,12},{9,13},{10,... | collective-permute-start | bytes 786440 | tf_op jit(solution)/shard_map/ppermute | solution.py:60
  134.9 24.4 %collective-permute-start.22 = (bf16[64,2048]{1,0:T(8,128)(2,1)}, bf16[64,2048]{1,0:T(8,128)(2,1)S(1)}, u32[]{:S(2)}, u32[]{:S(2)}) collective-permute-start(bf16[64,2048]{1,0:T(8,128)(2,1)} %get-tuple-element.749), channel_id=1, source_target_pairs={{0,2},{1,3},{2,0},{3,1},{4,6},{5,7},{6,4},{7,5},{8,10},{9,11},{10,... | collective-permute-start | bytes 786440 | tf_op jit(solution)/shard_map/ppermute | solution.py:60
  169.8 25.0 %collective-permute-start.29 = (bf16[128,2048]{1,0:T(8,128)(2,1)S(1)}, bf16[128,2048]{1,0:T(8,128)(2,1)S(1)}, u32[]{:S(2)}, u32[]{:S(2)}) collective-permute-start(bf16[128,2048]{1,0:T(8,128)(2,1)S(1)} %add_convert_fusion.4), channel_id=1, source_target_pairs={{0,4},{1,5},{2,6},{3,7},{4,0},{5,1},{6,2},{7,3},{8,12},{9,13},{10,... | collective-permute-start | bytes 1572872 | tf_op jit(solution)/shard_map/ppermute | solution.py:60
  170.7 24.1 %collective-permute-start.31 = (bf16[128,2048]{1,0:T(8,128)(2,1)S(1)}, bf16[128,2048]{1,0:T(8,128)(2,1)S(1)}, u32[]{:S(2)}, u32[]{:S(2)}) collective-permute-start(bf16[128,2048]{1,0:T(8,128)(2,1)S(1)} %add_convert_fusion.3), channel_id=1, source_target_pairs={{0,6},{1,7},{2,4},{3,5},{4,2},{5,3},{6,0},{7,1},{8,14},{9,15},{10,... | collective-permute-start | bytes 1572872 | tf_op jit(solution)/shard_map/ppermute | solution.py:60
  172.3 25.3 %collective-permute-start.33 = (bf16[128,2048]{1,0:T(8,128)(2,1)S(1)}, bf16[128,2048]{1,0:T(8,128)(2,1)S(1)}, u32[]{:S(2)}, u32[]{:S(2)}) collective-permute-start(bf16[128,2048]{1,0:T(8,128)(2,1)S(1)} %copy-done.30), channel_id=1, source_target_pairs={{0,16},{8,24},{16,0},{24,8},{1,17},{9,25},{17,1},{25,9},{2,18},{10... | collective-permute-start | bytes 1572872 | tf_op jit(solution)/shard_map/ppermute | solution.py:65
  174.1 23.5 %collective-permute-start.32 = (bf16[128,2048]{1,0:T(8,128)(2,1)S(1)}, bf16[128,2048]{1,0:T(8,128)(2,1)S(1)}, u32[]{:S(2)}, u32[]{:S(2)}) collective-permute-start(bf16[128,2048]{1,0:T(8,128)(2,1)S(1)} %copy-done.30), channel_id=1, source_target_pairs={{0,8},{8,0},{16,24},{24,16},{1,9},{9,1},{17,25},{25,17},{2,10},{10... | collective-permute-start | bytes 1572872 | tf_op jit(solution)/shard_map/ppermute | solution.py:65
  197.9 24.9 %collective-permute-start.35 = (bf16[128,2048]{1,0:T(8,128)(2,1)S(1)}, bf16[128,2048]{1,0:T(8,128)(2,1)S(1)}, u32[]{:S(2)}, u32[]{:S(2)}) collective-permute-start(bf16[128,2048]{1,0:T(8,128)(2,1)S(1)} %multiply_convert_fusion.refs_2_.refs_6_), channel_id=1, source_target_pairs={{0,16},{8,24},{16,0},{24,8},{1,17},{9,25},{17,1},{25,9},{2,18},{10... | collective-permute-start | bytes 1572872 | tf_op jit(solution)/shard_map/ppermute | solution.py:65
  199.3 23.5 %collective-permute-start.34 = (bf16[128,2048]{1,0:T(8,128)(2,1)S(1)}, bf16[128,2048]{1,0:T(8,128)(2,1)S(1)}, u32[]{:S(2)}, u32[]{:S(2)}) collective-permute-start(bf16[128,2048]{1,0:T(8,128)(2,1)S(1)} %multiply_convert_fusion.refs_2_.refs_6_), channel_id=1, source_target_pairs={{0,8},{8,0},{16,24},{24,16},{1,9},{9,1},{17,25},{25,17},{2,10},{10... | collective-permute-start | bytes 1572872 | tf_op jit(solution)/shard_map/ppermute | solution.py:65
  200.5 22.3 %collective-permute-start.36 = (bf16[128,2048]{1,0:T(8,128)(2,1)S(1)}, bf16[128,2048]{1,0:T(8,128)(2,1)S(1)}, u32[]{:S(2)}, u32[]{:S(2)}) collective-permute-start(bf16[128,2048]{1,0:T(8,128)(2,1)S(1)} %copy-done.30), channel_id=1, source_target_pairs={{0,1},{1,0},{2,3},{3,2},{4,5},{5,4},{6,7},{7,6},{8,9},{9,8},{10,11... | collective-permute-start | bytes 1572872 | tf_op jit(solution)/shard_map/ppermute | solution.py:55
  200.5 22.3 %collective-permute-start.37 = (bf16[128,2048]{1,0:T(8,128)(2,1)S(1)}, bf16[128,2048]{1,0:T(8,128)(2,1)S(1)}, u32[]{:S(2)}, u32[]{:S(2)}) collective-permute-start(bf16[128,2048]{1,0:T(8,128)(2,1)S(1)} %collective-permute-done.32.refs_6_.refs_2_), channel_id=1, source_target_pairs={{0,1},{1,0},{2,3},{3,2},{4,5},{5,4},{6,7},{7,6},{8,9},{9,8},{10,11... | collective-permute-start | bytes 1572872 | tf_op jit(solution)/shard_map/ppermute | solution.py:55
  201.0 21.8 %collective-permute-start.38 = (bf16[128,2048]{1,0:T(8,128)(2,1)S(1)}, bf16[128,2048]{1,0:T(8,128)(2,1)S(1)}, u32[]{:S(2)}, u32[]{:S(2)}) collective-permute-start(bf16[128,2048]{1,0:T(8,128)(2,1)S(1)} %collective-permute-done.33.refs_4_.refs_0_), channel_id=1, source_target_pairs={{0,1},{1,0},{2,3},{3,2},{4,5},{5,4},{6,7},{7,6},{8,9},{9,8},{10,11... | collective-permute-start | bytes 1572872 | tf_op jit(solution)/shard_map/ppermute | solution.py:55
  223.5 25.5 %collective-permute-start.42 = (bf16[128,2048]{1,0:T(8,128)(2,1)S(1)}, bf16[128,2048]{1,0:T(8,128)(2,1)}, u32[]{:S(2)}, u32[]{:S(2)}) collective-permute-start(bf16[128,2048]{1,0:T(8,128)(2,1)S(1)} %collective-permute-done.35.refs_0_), channel_id=1, source_target_pairs={{0,8},{8,0},{16,24},{24,16},{1,9},{9,1},{17,25},{25,17},{2,10},{10... | collective-permute-start | bytes 1572872 | tf_op jit(solution)/shard_map/ppermute | solution.py:65
  223.5 25.5 %collective-permute-start.43 = (bf16[128,2048]{1,0:T(8,128)(2,1)S(1)}, bf16[128,2048]{1,0:T(8,128)(2,1)S(1)}, u32[]{:S(2)}, u32[]{:S(2)}) collective-permute-start(bf16[128,2048]{1,0:T(8,128)(2,1)S(1)} %collective-permute-done.33.refs_4_.refs_0_), channel_id=1, source_target_pairs={{0,8},{8,0},{16,24},{24,16},{1,9},{9,1},{17,25},{25,17},{2,10},{10... | collective-permute-start | bytes 1572872 | tf_op jit(solution)/shard_map/ppermute | solution.py:65
  249.5 32.8 %collective-permute-start.54 = (bf16[128,2048]{1,0:T(8,128)(2,1)}, bf16[128,2048]{1,0:T(8,128)(2,1)S(1)}, u32[]{:S(2)}, u32[]{:S(2)}) collective-permute-start(bf16[128,2048]{1,0:T(8,128)(2,1)} %get-tuple-element.560), channel_id=1, source_target_pairs={{0,1},{1,0},{2,3},{3,2},{4,5},{5,4},{6,7},{7,6},{8,9},{9,8},{10,11... | collective-permute-start | bytes 1572872 | tf_op jit(solution)/shard_map/ppermute | solution.py:55
  249.6 31.1 %collective-permute-start.55 = (bf16[128,2048]{1,0:T(8,128)(2,1)}, bf16[128,2048]{1,0:T(8,128)(2,1)S(1)}, u32[]{:S(2)}, u32[]{:S(2)}) collective-permute-start(bf16[128,2048]{1,0:T(8,128)(2,1)} %get-tuple-element.562), channel_id=1, source_target_pairs={{0,1},{1,0},{2,3},{3,2},{4,5},{5,4},{6,7},{7,6},{8,9},{9,8},{10,11... | collective-permute-start | bytes 1572872 | tf_op jit(solution)/shard_map/ppermute | solution.py:55
  254.9 25.8 %collective-permute-start.48 = (bf16[128,2048]{1,0:T(8,128)(2,1)S(1)}, bf16[128,2048]{1,0:T(8,128)(2,1)S(1)}, u32[]{:S(2)}, u32[]{:S(2)}) collective-permute-start(bf16[128,2048]{1,0:T(8,128)(2,1)S(1)} %convert_add_fusion.16), channel_id=1, source_target_pairs={{0,16},{8,24},{16,0},{24,8},{1,17},{9,25},{17,1},{25,9},{2,18},{10... | collective-permute-start | bytes 1572872 | tf_op jit(solution)/shard_map/ppermute | solution.py:65
  255.6 25.1 %collective-permute-start.49 = (bf16[128,2048]{1,0:T(8,128)(2,1)S(1)}, bf16[128,2048]{1,0:T(8,128)(2,1)S(1)}, u32[]{:S(2)}, u32[]{:S(2)}) collective-permute-start(bf16[128,2048]{1,0:T(8,128)(2,1)S(1)} %convert_add_fusion.17), channel_id=1, source_target_pairs={{0,8},{8,0},{16,24},{24,16},{1,9},{9,1},{17,25},{25,17},{2,10},{10... | collective-permute-start | bytes 1572872 | tf_op jit(solution)/shard_map/ppermute | solution.py:65
  303.9 21.9 %collective-permute-start.60 = (bf16[128,2048]{1,0:T(8,128)(2,1)}, bf16[128,2048]{1,0:T(8,128)(2,1)}, u32[]{:S(2)}, u32[]{:S(2)}) collective-permute-start(bf16[128,2048]{1,0:T(8,128)(2,1)} %convert_add_fusion.10), channel_id=1, source_target_pairs={{0,8},{8,0},{16,24},{24,16},{1,9},{9,1},{17,25},{25,17},{2,10},{10... | collective-permute-start | bytes 1572872 | tf_op jit(solution)/shard_map/ppermute | solution.py:65
  314.8 23.7 %collective-permute-start.58 = (bf16[128,2048]{1,0:T(8,128)(2,1)S(1)}, bf16[128,2048]{1,0:T(8,128)(2,1)}, u32[]{:S(2)}, u32[]{:S(2)}) collective-permute-start(bf16[128,2048]{1,0:T(8,128)(2,1)S(1)} %get-tuple-element.639.refs_0_), channel_id=1, source_target_pairs={{0,4},{1,5},{2,6},{3,7},{4,0},{5,1},{6,2},{7,3},{8,12},{9,13},{10,... | collective-permute-start | bytes 1572872 | tf_op jit(solution)/shard_map/ppermute | solution.py:60
  316.1 22.5 %collective-permute-start.57 = (bf16[128,2048]{1,0:T(8,128)(2,1)S(1)}, bf16[128,2048]{1,0:T(8,128)(2,1)}, u32[]{:S(2)}, u32[]{:S(2)}) collective-permute-start(bf16[128,2048]{1,0:T(8,128)(2,1)S(1)} %get-tuple-element.639.refs_0_), channel_id=1, source_target_pairs={{0,2},{1,3},{2,0},{3,1},{4,6},{5,7},{6,4},{7,5},{8,10},{9,11},{10,... | collective-permute-start | bytes 1572872 | tf_op jit(solution)/shard_map/ppermute | solution.py:60
  343.8 25.8 %collective-permute-start.65 = (bf16[128,2048]{1,0:T(8,128)(2,1)S(1)}, bf16[128,2048]{1,0:T(8,128)(2,1)S(1)}, u32[]{:S(2)}, u32[]{:S(2)}) collective-permute-start(bf16[128,2048]{1,0:T(8,128)(2,1)S(1)} %convert_add_fusion.8), channel_id=1, source_target_pairs={{0,16},{8,24},{16,0},{24,8},{1,17},{9,25},{17,1},{25,9},{2,18},{10... | collective-permute-start | bytes 1572872 | tf_op jit(solution)/shard_map/ppermute | solution.py:65
  344.6 25.0 %collective-permute-start.66 = (bf16[128,2048]{1,0:T(8,128)(2,1)S(1)}, bf16[128,2048]{1,0:T(8,128)(2,1)S(1)}, u32[]{:S(2)}, u32[]{:S(2)}) collective-permute-start(bf16[128,2048]{1,0:T(8,128)(2,1)S(1)} %copy-done.34), channel_id=1, source_target_pairs={{0,8},{8,0},{16,24},{24,16},{1,9},{9,1},{17,25},{25,17},{2,10},{10... | collective-permute-start | bytes 1572872 | tf_op jit(solution)/shard_map/ppermute | solution.py:65
  346.3 24.4 %collective-permute-start.67 = (bf16[512,768]{1,0:T(8,128)(2,1)}, bf16[512,768]{1,0:T(8,128)(2,1)S(1)}, u32[]{:S(2)}, u32[]{:S(2)}) collective-permute-start(bf16[512,768]{1,0:T(8,128)(2,1)} %get-tuple-element.617), channel_id=1, source_target_pairs={{0,4},{1,5},{2,6},{3,7},{4,0},{5,1},{6,2},{7,3},{8,12},{9,13},{10,... | collective-permute-start | bytes 2359304 | tf_op jit(solution)/shard_map/ppermute | solution.py:60
  347.2 24.8 %collective-permute-start.68 = (bf16[512,768]{1,0:T(8,128)(2,1)}, bf16[512,768]{1,0:T(8,128)(2,1)S(1)}, u32[]{:S(2)}, u32[]{:S(2)}) collective-permute-start(bf16[512,768]{1,0:T(8,128)(2,1)} %get-tuple-element.619), channel_id=1, source_target_pairs={{0,2},{1,3},{2,0},{3,1},{4,6},{5,7},{6,4},{7,5},{8,10},{9,11},{10,... | collective-permute-start | bytes 2359304 | tf_op jit(solution)/shard_map/ppermute | solution.py:60
  373.4 40.8 %collective-permute-start.69 = (bf16[2,512,768]{2,1,0:T(8,128)(2,1)S(1)}, bf16[2,512,768]{2,1,0:T(8,128)(2,1)S(1)}, u32[]{:S(2)}, u32[]{:S(2)}) collective-permute-start(bf16[2,512,768]{2,1,0:T(8,128)(2,1)S(1)} %pad_maximum_fusion.2), channel_id=1, source_target_pairs={{0,2},{1,3},{2,0},{3,1},{4,6},{5,7},{6,4},{7,5},{8,10},{9,11},{10,... | collective-permute-start | bytes 4718600 | tf_op jit(solution)/shard_map/ppermute | solution.py:60
  374.6 39.6 %collective-permute-start.70 = (bf16[2,512,768]{2,1,0:T(8,128)(2,1)S(1)}, bf16[2,512,768]{2,1,0:T(8,128)(2,1)S(1)}, u32[]{:S(2)}, u32[]{:S(2)}) collective-permute-start(bf16[2,512,768]{2,1,0:T(8,128)(2,1)S(1)} %pad_maximum_fusion.3), channel_id=1, source_target_pairs={{0,4},{1,5},{2,6},{3,7},{4,0},{5,1},{6,2},{7,3},{8,12},{9,13},{10,... | collective-permute-start | bytes 4718600 | tf_op jit(solution)/shard_map/ppermute | solution.py:60
  381.3 24.5 %collective-permute-start.73 = (bf16[512,384]{1,0:T(8,128)(2,1)}, bf16[512,384]{1,0:T(8,128)(2,1)}, u32[]{:S(2)}, u32[]{:S(2)}) collective-permute-start(bf16[512,384]{1,0:T(8,128)(2,1)} %get-tuple-element.630), channel_id=1, source_target_pairs={{0,8},{8,0},{16,24},{24,16},{1,9},{9,1},{17,25},{25,17},{2,10},{10... | collective-permute-start | bytes 1179656 | tf_op jit(solution)/shard_map/ppermute | solution.py:65
  434.6 19.6 %collective-permute-start.81 = (bf16[2,2,64,768]{3,2,1,0:T(8,128)(2,1)S(1)}, bf16[2,2,64,768]{3,2,1,0:T(8,128)(2,1)S(1)}, u32[]{:S(2)}, u32[]{:S(2)}) collective-permute-start(bf16[2,2,64,768]{3,2,1,0:T(8,128)(2,1)S(1)} %pad_maximum_fusion.14), channel_id=1, source_target_pairs={{0,16},{8,24},{16,0},{24,8},{1,17},{9,25},{17,1},{25,9},{2,18},{10... | collective-permute-start | bytes 1179656 | tf_op jit(solution)/shard_map/ppermute | solution.py:65
  456.8 20.3 %collective-permute-start.86 = (bf16[64,2048]{1,0:T(8,128)(2,1)S(1)}, bf16[64,2048]{1,0:T(8,128)(2,1)S(1)}, u32[]{:S(2)}, u32[]{:S(2)}) collective-permute-start(bf16[64,2048]{1,0:T(8,128)(2,1)S(1)} %get-tuple-element.746), channel_id=1, source_target_pairs={{0,2},{1,3},{2,0},{3,1},{4,6},{5,7},{6,4},{7,5},{8,10},{9,11},{10,... | collective-permute-start | bytes 786440 | tf_op jit(solution)/shard_map/ppermute | solution.py:60
  459.0 29.5 %collective-permute-start.85 = (bf16[2,2,64,768]{3,2,1,0:T(8,128)(2,1)}, bf16[2,2,64,768]{3,2,1,0:T(8,128)(2,1)}, u32[]{:S(2)}, u32[]{:S(2)}) collective-permute-start(bf16[2,2,64,768]{3,2,1,0:T(8,128)(2,1)} %pad_maximum_fusion.15), channel_id=1, source_target_pairs={{0,24},{8,16},{16,8},{24,0},{1,25},{9,17},{17,9},{25,1},{2,26},{10... | collective-permute-start | bytes 1179656 | tf_op jit(solution)/shard_map/ppermute | solution.py:65
  461.0 25.1 %collective-permute-start.89 = (bf16[128,2048]{1,0:T(8,128)(2,1)S(1)}, bf16[128,2048]{1,0:T(8,128)(2,1)S(1)}, u32[]{:S(2)}, u32[]{:S(2)}) collective-permute-start(bf16[128,2048]{1,0:T(8,128)(2,1)S(1)} %convert_add_fusion.3), channel_id=1, source_target_pairs={{0,2},{1,3},{2,0},{3,1},{4,6},{5,7},{6,4},{7,5},{8,10},{9,11},{10,... | collective-permute-start | bytes 1572872 | tf_op jit(solution)/shard_map/ppermute | solution.py:60
  488.4 22.0 %collective-permute-start.92 = (bf16[64,2048]{1,0:T(8,128)(2,1)}, bf16[64,2048]{1,0:T(8,128)(2,1)S(1)}, u32[]{:S(2)}, u32[]{:S(2)}) collective-permute-start(bf16[64,2048]{1,0:T(8,128)(2,1)} %get-tuple-element.710), channel_id=1, source_target_pairs={{0,8},{8,0},{16,24},{24,16},{1,9},{9,1},{17,25},{25,17},{2,10},{10... | collective-permute-start | bytes 786440 | tf_op jit(solution)/shard_map/ppermute | solution.py:65
  489.0 21.5 %collective-permute-start.93 = (bf16[64,2048]{1,0:T(8,128)(2,1)}, bf16[64,2048]{1,0:T(8,128)(2,1)S(1)}, u32[]{:S(2)}, u32[]{:S(2)}) collective-permute-start(bf16[64,2048]{1,0:T(8,128)(2,1)} %get-tuple-element.711), channel_id=1, source_target_pairs={{0,16},{8,24},{16,0},{24,8},{1,17},{9,25},{17,1},{25,9},{2,18},{10... | collective-permute-start | bytes 786440 | tf_op jit(solution)/shard_map/ppermute | solution.py:65
  490.9 19.6 %collective-permute-start.94 = (bf16[64,2048]{1,0:T(8,128)(2,1)}, bf16[64,2048]{1,0:T(8,128)(2,1)S(1)}, u32[]{:S(2)}, u32[]{:S(2)}) collective-permute-start(bf16[64,2048]{1,0:T(8,128)(2,1)} %get-tuple-element.712), channel_id=1, source_target_pairs={{0,24},{8,16},{16,8},{24,0},{1,25},{9,17},{17,9},{25,1},{2,26},{10... | collective-permute-start | bytes 786440 | tf_op jit(solution)/shard_map/ppermute | solution.py:65
  (136 other events, 1368.8 us)
Sparse Core Ops, SparseCore 0:
  10.5 67.6 all-gather.1
  431.2 48.1 reduce-scatter.1

commit v5 on v4

--- a/solution.py
+++ b/solution.py
@@ -143,7 +143,9 @@
 
 
 def cost(flops, moved, exps=0):
-    return pl.CostEstimate(flops=int(flops), bytes_accessed=int(moved), transcendentals=int(exps))
+    return pl.CostEstimate(
+        flops=3 * int(flops), bytes_accessed=3 * int(moved), transcendentals=3 * int(exps)
+    )
 
 
 def whole_lanes(width):
@@ -1092,35 +1094,25 @@
         grad_w_qkv = scatter_stage(grad_w_qkv, plane_send, stage)
     mixed = project_back(spot, grad_qkv, w_qkv, chips)
     grad_output = rows_grad(attended, grad_attn_out).reshape(planes, slice_rows, width)
-    grad_gate_up, grad_w_qkv, mixed, grad_output = together(
-        grad_gate_up, grad_w_qkv[0], mixed, grad_output
-    )
-
-    gu_pairs = swap_pairs(*spread_rows(plane, core, grad_gate_up, planes))
-    qkv_pairs = swap_pairs(*spread_rows(chip, core, [grad_w_qkv], chips))
-    mixed = [(mine, core_swap(other)) for mine, other in zip(*mixed)]
-    gu_pairs, qkv_pairs, mixed, grad_output, grad_down = together(
-        gu_pairs, qkv_pairs, mixed, grad_output, grad_down
+    grad_gate_up, grad_w_qkv, mixed, grad_output, grad_down = together(
+        grad_gate_up, grad_w_qkv[0], mixed, grad_output, grad_down
     )
 
     grad_down_weight = lax.psum_scatter(
         grad_down, "fsdp", scatter_dimension=0, tiled=True, axis_index_groups=same_core
     ).astype(F32)
+
+    qkv_pairs = swap_pairs(*spread_rows(chip, core, [grad_w_qkv], chips))
+    gu_mine, gu_other = spread_rows(plane, core, grad_gate_up, planes)
+    gu_other = core_swap(gu_other)
     got = exchange(qkv_pairs, chip_send)
-    mixed = [mine + other.astype(F32) for mine, other in mixed]
+    gu_mine, gu_other, got, mixed, grad_output = together(
+        gu_mine, gu_other, got, mixed, grad_output
+    )
+
+    gu_pairs = [jnp.stack([gu_mine[step], gu_other[step]]) for step in everyone]
     far_pairs = gu_pairs[planes // 2 + 1 :]
     near_got = exchange(gu_pairs[: planes // 2 + 1], plane_send)
-    far_pairs, near_got, got, mixed, grad_output = together(
-        far_pairs, near_got, got, mixed, grad_output
-    )
-
-    far_got = [
-        plane_send(pair, planes // 2 + 1 + step) for step, pair in enumerate(far_pairs)
-    ]
-    grad_gate_up = near_got + far_got
-    mixed = dict(enumerate(mixed))
-    for stage in range(chip_stages, 1, -1):
-        mixed = scatter_stage(mixed, chip_send, stage)
     if head_rows:
         parts = [grad_output[0]] + [chip_send(grad_output[step], step) for step in range(1, chips)]
         parts = jnp.stack(parts)
@@ -1155,12 +1147,25 @@
             value_second,
         ),
     )
-    grad_gate_up, grad_gain_one, out_parts, mixed, grad_down_weight = together(
-        grad_gate_up, grad_gain_one, out_parts, mixed, grad_down_weight
-    )
+    far_pairs, near_got, out_parts, mixed, grad_gain_one = together(
+        far_pairs, near_got, out_parts, mixed, grad_gain_one
+    )
+
+    far_got = [
+        plane_send(pair, planes // 2 + 1 + step) for step, pair in enumerate(far_pairs)
+    ]
+    grad_gate_up = near_got + far_got
+    out_parts = dict(enumerate(out_parts))
+    for stage in range(stages, 1, -1):
+        out_parts = scatter_stage(out_parts, plane_send, stage)
+    mixed = {step: over_cores(terms) for step, terms in enumerate(zip(*mixed))}
+    for stage in range(chip_stages, 1, -1):
+        mixed = scatter_stage(mixed, chip_send, stage)
+    down_new = adam_step(down_weight, down_first, down_second, grad_down_weight, 0.02)
+    grad_gate_up, out_parts, mixed, down_new = together(grad_gate_up, out_parts, mixed, down_new)
 
     grad_normed = scatter_stage(mixed, chip_send, 1)[0]
-    grad_output_weight = scatter_sum(out_parts, plane_send)
+    grad_output_weight = scatter_stage(out_parts, plane_send, 1)[0]
     scale_one = rms_scale(own_tokens)
     grad_tokens = (
         grad_resid
@@ -1182,7 +1187,7 @@
         attention_new
         + adam_step(output_weight, output_first, output_second, grad_output_weight, 0.1)
         + fed_weights
-        + adam_step(down_weight, down_first, down_second, grad_down_weight, 0.02)
+        + tuple(down_new)
         + adam_step(norm_gains, gains_first, gains_second, gain_grads, 0.2)
     )
     return (result, grad_tokens) + updated

time: 526 us -> 513 us (0.975)
  waiting for transfers between devices: 194 us -> 184 us
  starting transfers between devices: 97.7 us -> 107 us
  other arithmetic: 51.3 us -> 44.5 us
    ppermute x30, waiting for transfers between devices: 122 us -> 112 us  [plane_send(): return lax.ppermute(value, 'dp', [(i, i ^ step) for i in range(planes)])]
    ppermute x30, starting transfers between devices: 53 us -> 61.6 us  [plane_send(): return lax.ppermute(value, 'dp', [(i, i ^ step) for i in range(planes)])]
    add x4 -> x0, other arithmetic: 5.83 us -> none  [local(): mixed = [mine + other.astype(F32) for mine, other in mixed]]
    unnamed x177 -> x183, local copies, waits for them, and re-layouts: 11.9 us -> 10 us
  transfers between devices with their start and end apart: 97 -> 97, of which waited for: 34 -> 37; matrix products, arithmetic and copies ran while one was open for 10% -> 8% of each run, Pallas kernels for 25% -> 27%
where the time goes in v5:
time: 513 us; the launch traced here: 509 us
  waiting for transfers between devices  184 us (36%)
  Pallas kernels  141 us (27%)
  starting transfers between devices  107 us (21%)
  other arithmetic  44.5 us (9%)
  local copies, waits for them, and re-layouts  17.1 us (3%)
  between operations  15.5 us (3%)
    ppermute x30, waiting for transfers between devices, plane_send(): return lax.ppermute(value, 'dp', [(i, i ^ step) for i in range(planes)])  112 us
    ppermute x32, waiting for transfers between devices, chip_send(): lax.ppermute(value, 'fsdp', [(i, i ^ 2 * step) for i in range(members)])  66.1 us
    ppermute x30, starting transfers between devices, plane_send(): return lax.ppermute(value, 'dp', [(i, i ^ step) for i in range(planes)])  61.6 us
    ppermute x32, starting transfers between devices, chip_send(): lax.ppermute(value, 'fsdp', [(i, i ^ 2 * step) for i in range(members)])  38.1 us
    pallas_call x2, Pallas kernels, feed(): pl.pallas_call(functools.partial(feed_kernel, planes, layout, count), out...  37.2 us
    pallas_call x1, Pallas kernels, attend_back(): pl.pallas_call(functools.partial(attend_back_kernel, members, pairs), out...  18.4 us
    pallas_call x1, Pallas kernels, attend(): pl.pallas_call(functools.partial(attend_kernel, members, pairs, planes),...  14.9 us
    pallas_call x2, Pallas kernels, rows_grad(): pl.pallas_call(functools.partial(rows_grad_kernel, len(grads)), out_shape...  12.1 us
  transfers between devices with their start and end apart: 97, of which 37 were waited for; matrix products, arithmetic and copies ran while one was open for 8% of the time, Pallas kernels for 27%

profile of v5, /device:TPU:0, one launch (start us, length us, event | category | flops | bytes accessed | tf_op | source)
XLA Modules:
  0.0 509.0 jit_solution(10663904147596125942)
XLA Ops:
  11.1 6.1 %pack.1 = (bf16[4,2,64,768]{3,2,1,0:T(8,128)(2,1)}, bf16[4,2,64,768]{3,2,1,0:T(8,128)(2,1)}, bf16[4,64,384]{2,1,0:T(8,128)(2,1)}, bf16[4,64,384]{2,1,0:T(8,128)(2,1)}) custom-call(s32[3]{0:T(128)} %pad_add_fusion.place, f32[64,2]{1,0:T(8,128)} %bitcast.65, f32[64,5632]{1,0:T(8,128)} %refs_4_.3, f32[64,5632]{1,0:T(8,128)} %refs_7_.3, f32[64,2048]{1,0:T(8,128)} %refs_4_.2, ...), custom_call_target="tpu_custom_call" | custom-call | bytes 12976128 | tf_op jit(solution)/shard_map/pack/pallas_call | solution.py:208
  18.0 4.1 collective-permute-start.7
  30.8 3.3 collective-permute-done.7
  34.1 2.5 collective-permute-start.3
  36.7 2.9 collective-permute-done.3.refs_3_
  39.6 3.1 collective-permute-done.5.refs_1_
  42.7 2.6 collective-permute-start.12
  47.8 2.5 collective-permute-start.9
  54.0 20.3 %collective-permute-done.8.refs_2_ = bf16[2,2,64,768]{3,2,1,0:T(8,128)(2,1)S(1)} collective-permute-done((bf16[2,2,64,768]{3,2,1,0:T(8,128)(2,1)S(1)}, bf16[2,2,64,768]{3,2,1,0:T(8,128)(2,1)S(1)}, u32[]{:S(2)}, u32[]{:S(2)}) %collective-permute-start.8) | collective-permute-done | bytes 393248 | tf_op jit(solution)/shard_map/ppermute | solution.py:65
  74.3 4.9 collective-permute-done.11
  81.4 2.8 gather_rows.2.refs_8_
  88.6 5.6 %collective-permute-start.16 = (bf16[512,384]{1,0:T(8,128)(2,1)}, bf16[512,384]{1,0:T(8,128)(2,1)}, u32[]{:S(2)}, u32[]{:S(2)}) collective-permute-start(bf16[512,384]{1,0:T(8,128)(2,1)} %gather_rows.3.refs_2_.refs_0_), channel_id=1, source_target_pairs={{0,16},{8,24},{16,0},{24,8},{1,17},{9,25},{17,1},{25,9},{2,18},{10... | collective-permute-start | bytes 1179656 | tf_op jit(solution)/shard_map/ppermute | solution.py:65
  94.2 18.0 %collective-permute-done.16.refs_4_.refs_2_ = bf16[512,384]{1,0:T(8,128)(2,1)} collective-permute-done((bf16[512,384]{1,0:T(8,128)(2,1)}, bf16[512,384]{1,0:T(8,128)(2,1)}, u32[]{:S(2)}, u32[]{:S(2)}) %collective-permute-start.16) | collective-permute-done | bytes 393248 | tf_op jit(solution)/shard_map/ppermute | solution.py:65
  115.2 6.2 %collective-permute-done.19 = bf16[64,2048]{1,0:T(8,128)(2,1)S(1)} collective-permute-done((bf16[64,2048]{1,0:T(8,128)(2,1)S(1)}, bf16[64,2048]{1,0:T(8,128)(2,1)S(1)}, u32[]{:S(2)}, u32[]{:S(2)}) %collective-permute-start.19) | collective-permute-done | bytes 262176 | tf_op jit(solution)/shard_map/ppermute | solution.py:65
  121.5 6.8 %collective-permute-done.17.refs_5_.refs_3_ = bf16[512,384]{1,0:T(8,128)(2,1)} collective-permute-done((bf16[512,384]{1,0:T(8,128)(2,1)}, bf16[512,384]{1,0:T(8,128)(2,1)}, u32[]{:S(2)}, u32[]{:S(2)}) %collective-permute-start.17) | collective-permute-done | bytes 393248 | tf_op jit(solution)/shard_map/ppermute | solution.py:65
  131.3 2.5 collective-permute-start.24
  134.9 14.9 %attend.1 = (bf16[1024,2048]{1,0:T(8,128)(2,1)}, bf16[1024,256]{1,0:T(8,128)(2,1)}, bf16[1024,128]{1,0:T(8,128)(2,1)}, bf16[1024,256]{1,0:T(8,128)(2,1)}) custom-call(s32[2]{0:T(128)} %pad_add_fusion.1.place, s32[1024,1]{1,0:T(8,128)} %copy.60.start_ref, f32[1024,128]{1,0:T(8,128)} %get-tuple-element.425.cos_ref, f32[1024,128]{1,0:T(8,128)} %get-tuple-element.426.sin_ref, ...), custom_call_target="tpu_custom_call" | custom-call | flops 7247757312 | bytes 25165824 | tf_op jit(solution)/shard_map/attend/pallas_call | solution.py:340
  149.8 6.5 %collective-permute-done.24 = bf16[64,2048]{1,0:T(8,128)(2,1)S(1)} collective-permute-done((bf16[64,2048]{1,0:T(8,128)(2,1)S(1)}, bf16[64,2048]{1,0:T(8,128)(2,1)S(1)}, u32[]{:S(2)}, u32[]{:S(2)}) %collective-permute-start.24) | collective-permute-done | bytes 262176 | tf_op jit(solution)/shard_map/ppermute | solution.py:60
  156.3 3.4 collective-permute-done.23
  160.9 4.4 project.1
  175.6 8.1 %collective-permute-done.27 = bf16[128,2048]{1,0:T(8,128)(2,1)S(1)} collective-permute-done((bf16[128,2048]{1,0:T(8,128)(2,1)S(1)}, bf16[128,2048]{1,0:T(8,128)(2,1)S(1)}, u32[]{:S(2)}, u32[]{:S(2)}) %collective-permute-start.27) | collective-permute-done | bytes 524320 | tf_op jit(solution)/shard_map/ppermute | solution.py:60
  183.7 11.9 %collective-permute-done.29 = bf16[128,2048]{1,0:T(8,128)(2,1)S(1)} collective-permute-done((bf16[128,2048]{1,0:T(8,128)(2,1)S(1)}, bf16[128,2048]{1,0:T(8,128)(2,1)S(1)}, u32[]{:S(2)}, u32[]{:S(2)}) %collective-permute-start.29) | collective-permute-done | bytes 524320 | tf_op jit(solution)/shard_map/ppermute | solution.py:60
  201.8 21.7 %collective-permute-done.35.refs_0_ = bf16[128,2048]{1,0:T(8,128)(2,1)S(1)} collective-permute-done((bf16[128,2048]{1,0:T(8,128)(2,1)S(1)}, bf16[128,2048]{1,0:T(8,128)(2,1)S(1)}, u32[]{:S(2)}, u32[]{:S(2)}) %collective-permute-start.35) | collective-permute-done | bytes 524320 | tf_op jit(solution)/shard_map/ppermute | solution.py:65
  228.7 18.7 %feed.2 = (bf16[512,704]{1,0:T(8,128)(2,1)}, bf16[512,704]{1,0:T(8,128)(2,1)}, bf16[512,704]{1,0:T(8,128)(2,1)}, f32[128,2048]{1,0:T(8,128)}, bf16[128,2048]{1,0...) custom-call(s32[3]{0:T(128)} %pad_add_fusion.place, ...), custom_call_target="tpu_custom_call" | custom-call | flops 26575110144 | bytes 25952256 | tf_op jit(solution)/shard_map/feed/pallas_call | solution.py:619
  258.0 18.5 %feed.3 = (bf16[512,704]{1,0:T(8,128)(2,1)}, bf16[512,704]{1,0:T(8,128)(2,1)}, bf16[512,704]{1,0:T(8,128)(2,1)}, f32[128,2048]{1,0:T(8,128)}, bf16[128,2048]{1,0...) custom-call(s32[3]{0:T(128)} %pad_add_fusion.place, ...), custom_call_target="tpu_custom_call" | custom-call | flops 26575110144 | bytes 25952256 | tf_op jit(solution)/shard_map/feed/pallas_call | solution.py:619
  276.6 4.9 collective-permute-done.48
  287.0 11.1 %feed_grad.1 = (bf16[2,512,768]{2,1,0:T(8,128)(2,1)}, bf16[512,768]{1,0:T(8,128)(2,1)}, bf16[512,768]{1,0:T(8,128)(2,1)}, bf16[512,768]{1,0:T(8,128)(2,1)}, bf16...) custom-call(s32[3]{0:T(128)} %pad_add_fusion.place, bf16[128,2048]{1,0:T(8,128)(2,1)} %copy-done.76, ...), custom_call_target="tpu_custom_call" | custom-call | flops 17716740096 | bytes 17301504 | tf_op jit(solution)/shard_map/feed_grad/pallas_call | solution.py:677
  307.3 9.3 %collective-permute-start.60 = (bf16[128,2048]{1,0:T(8,128)(2,1)}, bf16[128,2048]{1,0:T(8,128)(2,1)}, u32[]{:S(2)}, u32[]{:S(2)}) collective-permute-start(bf16[128,2048]{1,0:T(8,128)(2,1)} %convert_add_fusion.8), channel_id=1, source_target_pairs={{0,8},{8,0},{16,24},{24,16},{1,9},{9,1},{17,25},{25,17},{2,10},{10... | collective-permute-start | bytes 1572872 | tf_op jit(solution)/shard_map/ppermute | solution.py:65
  318.0 7.6 %rows_grad.2 = bf16[704,2048]{1,0:T(8,128)(2,1)} custom-call(bf16[1024,704]{1,0:T(8,128)(2,1)} %pad_maximum_fusion.1.left_ref, bf16[128,2048]{1,0:T(8,128)(2,1)} %copy-done.66, bf16[128,2048]{1,0:T(8,128)(2,1)} %copy-done.73, bf16[128,2048]{1,0:T(8,128)(2,1)} %copy-done.67, bf16[128,2048]{1,0:T(8,128)(2,1)} %copy-done.71, bf16[128,2048]{1,0:T(8,128)(2,1)} %copy-done.75, ...), custom_call_target="tpu_custom_call" | custom-call | flops 8858370048 | bytes 4325376 | tf_op jit(solution)/shard_map/rows_grad/pallas_call | solution.py:532
  334.9 9.4 %collective-permute-start.65 = (bf16[128,2048]{1,0:T(8,128)(2,1)S(1)}, bf16[128,2048]{1,0:T(8,128)(2,1)S(1)}, u32[]{:S(2)}, u32[]{:S(2)}) collective-permute-start(bf16[128,2048]{1,0:T(8,128)(2,1)S(1)} %convert_add_fusion.6), channel_id=1, source_target_pairs={{0,16},{8,24},{16,0},{24,8},{1,17},{9,25},{17,1},{25,9},{2,18},{10... | collective-permute-start | bytes 1572872 | tf_op jit(solution)/shard_map/ppermute | solution.py:65
  346.4 18.4 %attend_back.1.grad_ref.left_ref = bf16[1024,384]{1,0:T(8,128)(2,1)} custom-call(s32[2]{0:T(128)} %pad_add_fusion.1.place, s32[1,1024]{1,0:T(1,128)} %bitcast.78, f32[1024,128]{1,0:T(8,128)} %get-tuple-element.425.cos_ref, f32[1024,128]{1,0:T(8,128)} %get-tuple-element.426.sin_ref, bf16[1024,256]{1,0:T(8,128)(2,1)} %get-tuple-element.452.q_ref, ...), custom_call_target="tpu_custom_call" | custom-call | flops 8858370048 | bytes 12582912 | tf_op jit(solution)/shard_map/attend_back/pallas_call | solution.py:430
  364.9 2.9 collective-permute-done.65
  375.0 5.5 %qkv_grad.1 = (bf16[512,384]{1,0:T(8,128)(2,1)}, bf16[512,384]{1,0:T(8,128)(2,1)}, bf16[512,384]{1,0:T(8,128)(2,1)}, bf16[512,384]{1,0:T(8,128)(2,1)}) custom-call(s32[2]{0:T(128)} %pad_add_fusion.1.place, bf16[1024,2048]{1,0:T(8,128)(2,1)} %get-tuple-element.627.normed_ref, bf16[1024,384]{1,0:T(8,128)(2,1)} %attend_back.1.grad_ref.left_ref), custom_call_target="tpu_custom_call" | custom-call | flops 4831838208 | bytes 12582912 | tf_op jit(solution)/shard_map/qkv_grad/pallas_call | solution.py:509
  382.5 4.6 rows_grad.3
  387.1 5.7 %collective-permute-done.71 = bf16[512,384]{1,0:T(8,128)(2,1)S(1)} collective-permute-done((bf16[512,384]{1,0:T(8,128)(2,1)}, bf16[512,384]{1,0:T(8,128)(2,1)S(1)}, u32[]{:S(2)}, u32[]{:S(2)}) %collective-permute-start.71) | collective-permute-done | bytes 393248 | tf_op jit(solution)/shard_map/ppermute | solution.py:65
  395.0 6.2 %project_back.1 = (f32[128,2048]{1,0:T(8,128)}, f32[128,2048]{1,0:T(8,128)}, f32[128,2048]{1,0:T(8,128)}, f32[128,2048]{1,0:T(8,128)}, bf16[128,2048]{1,0:T(8,12...) custom-call(s32[2]{0:T(128)} %pad_add_fusion.1.place, ...), custom_call_target="tpu_custom_call" | custom-call | flops 4831838208 | bytes 18874368 | tf_op jit(solution)/shard_map/project_back/pallas_call | solution.py:488
  401.2 5.3 %collective-permute-done.73 = bf16[512,384]{1,0:T(8,128)(2,1)S(1)} collective-permute-done((bf16[512,384]{1,0:T(8,128)(2,1)}, bf16[512,384]{1,0:T(8,128)(2,1)S(1)}, u32[]{:S(2)}, u32[]{:S(2)}) %collective-permute-start.73) | collective-permute-done | bytes 393248 | tf_op jit(solution)/shard_map/ppermute | solution.py:65
  406.5 3.6 collective-permute-done.72
  413.1 4.0 spread_rows.2
  422.0 3.4 collective-permute-done.76.refs_1_
  426.6 3.3 collective-permute-done.78.refs_3_
  436.7 4.5 attention_adam.1
  445.1 4.0 collective-permute-done.82
  451.9 2.6 collective-permute-start.84
  460.8 14.1 %collective-permute-done.90 = bf16[128,2048]{1,0:T(8,128)(2,1)S(1)} collective-permute-done((bf16[128,2048]{1,0:T(8,128)(2,1)S(1)}, bf16[128,2048]{1,0:T(8,128)(2,1)S(1)}, u32[]{:S(2)}, u32[]{:S(2)}) %collective-permute-start.90) | collective-permute-done | bytes 524320 | tf_op jit(solution)/shard_map/ppermute | solution.py:60
  475.9 4.8 multiply_subtract_fusion
  480.8 2.5 collective-permute-start.93
  486.8 9.6 %feed_adam.1 = (f32[64,5632]{1,0:T(8,128)}, f32[64,5632]{1,0:T(8,128)}, f32[64,5632]{1,0:T(8,128)}, f32[64,5632]{1,0:T(8,128)}, f32[64,5632]{1,0:T(8,128)}, /*index=5*/f32[64,5632]{1,0:T(8,128)}, f32[64,128]{1,0:T(8,128)}) custom-call(s32[3]{0:T(128)} %pad_add_fusion.place, f32[64,2]{1,0:T(8,128)} %bitcast.67, ...), custom_call_target="tpu_custom_call" | custom-call | flops 43253760 | bytes 56229888 | tf_op jit(solution)/shard_map/feed_adam/pallas_call | solution.py:726
  (438 shorter events, 144.0 us)
Async XLA Ops:
  7.2 72.0 %all-gather.2.cloned.1.call-start = ((), (), s32[]{:S(2)}) async-start(), calls=%async_computation.1 | async-start | bytes 3604480 | tf_op jit(solution)/shard_map/all_gather | solution.py:898
  9.7 466.2 %reduce-scatter.2.cloned.1.call-start = ((), (), s32[]{:S(2)}) async-start(), calls=%async_computation.2 | async-start | bytes 3604480 | tf_op jit(solution)/shard_map/reduce_scatter | solution.py:1101
  42.7 31.6 %collective-permute-start.12 = (bf16[128,2048]{1,0:T(8,128)(2,1)S(1)}, bf16[128,2048]{1,0:T(8,128)(2,1)S(1)}, u32[]{:S(2)}, u32[]{:S(2)}) collective-permute-start(bf16[128,2048]{1,0:T(8,128)(2,1)S(1)} %copy-done), channel_id=1, source_target_pairs={{0,6},{1,7},{2,4},{3,5},{4,2},{5,3},{6,0},{7,1},{8,14},{9,15},{10,... | collective-permute-start | bytes 1572872 | tf_op jit(solution)/shard_map/ppermute | solution.py:60
  45.3 33.9 %collective-permute-start.11 = (bf16[128,2048]{1,0:T(8,128)(2,1)S(1)}, bf16[128,2048]{1,0:T(8,128)(2,1)S(1)}, u32[]{:S(2)}, u32[]{:S(2)}) collective-permute-start(bf16[128,2048]{1,0:T(8,128)(2,1)S(1)} %copy-done), channel_id=1, source_target_pairs={{0,4},{1,5},{2,6},{3,7},{4,0},{5,1},{6,2},{7,3},{8,12},{9,13},{10,... | collective-permute-start | bytes 1572872 | tf_op jit(solution)/shard_map/ppermute | solution.py:60
  45.8 33.4 %collective-permute-start.10 = (bf16[128,2048]{1,0:T(8,128)(2,1)S(1)}, bf16[128,2048]{1,0:T(8,128)(2,1)S(1)}, u32[]{:S(2)}, u32[]{:S(2)}) collective-permute-start(bf16[128,2048]{1,0:T(8,128)(2,1)S(1)} %copy-done), channel_id=1, source_target_pairs={{0,2},{1,3},{2,0},{3,1},{4,6},{5,7},{6,4},{7,5},{8,10},{9,11},{10,... | collective-permute-start | bytes 1572872 | tf_op jit(solution)/shard_map/ppermute | solution.py:60
  46.3 28.0 %collective-permute-start.8 = (bf16[2,2,64,768]{3,2,1,0:T(8,128)(2,1)S(1)}, bf16[2,2,64,768]{3,2,1,0:T(8,128)(2,1)S(1)}, u32[]{:S(2)}, u32[]{:S(2)}) collective-permute-start(bf16[2,2,64,768]{3,2,1,0:T(8,128)(2,1)S(1)} %get-tuple-element.390), channel_id=1, source_target_pairs={{0,16},{8,24},{16,0},{24,8},{1,17},{9,25},{17,1},{25,9},{2,18},{10... | collective-permute-start | bytes 1179656 | tf_op jit(solution)/shard_map/ppermute | solution.py:65
  47.8 26.5 %collective-permute-start.9 = (bf16[2,2,64,768]{3,2,1,0:T(8,128)(2,1)S(1)}, bf16[2,2,64,768]{3,2,1,0:T(8,128)(2,1)S(1)}, u32[]{:S(2)}, u32[]{:S(2)}) collective-permute-start(bf16[2,2,64,768]{3,2,1,0:T(8,128)(2,1)S(1)} %pad_maximum_fusion.11), channel_id=1, source_target_pairs={{0,24},{8,16},{16,8},{24,0},{1,25},{9,17},{17,9},{25,1},{2,26},{10... | collective-permute-start | bytes 1179656 | tf_op jit(solution)/shard_map/ppermute | solution.py:65
  80.8 47.5 %collective-permute-start.18 = (bf16[4,128,2048]{2,1,0:T(8,128)(2,1)}, bf16[4,128,2048]{2,1,0:T(8,128)(2,1)}, u32[]{:S(2)}, u32[]{:S(2)}) collective-permute-start(bf16[4,128,2048]{2,1,0:T(8,128)(2,1)} %pad_maximum_fusion.refs_0_), channel_id=1, source_target_pairs={{0,1},{1,0},{2,3},{3,2},{4,5},{5,4},{6,7},{7,6},{8,9},{9,8},{10,11... | collective-permute-start | bytes 6291464 | tf_op jit(solution)/shard_map/ppermute | solution.py:55
  84.2 44.1 %collective-permute-start.14 = (bf16[2,512,768]{2,1,0:T(8,128)(2,1)}, bf16[2,512,768]{2,1,0:T(8,128)(2,1)S(1)}, u32[]{:S(2)}, u32[]{:S(2)}) collective-permute-start(bf16[2,512,768]{2,1,0:T(8,128)(2,1)} %gather_rows.2.refs_8_), channel_id=1, source_target_pairs={{0,4},{1,5},{2,6},{3,7},{4,0},{5,1},{6,2},{7,3},{8,12},{9,13},{10,... | collective-permute-start | bytes 4718600 | tf_op jit(solution)/shard_map/ppermute | solution.py:60
  85.6 42.7 %collective-permute-start.13 = (bf16[2,512,768]{2,1,0:T(8,128)(2,1)}, bf16[2,512,768]{2,1,0:T(8,128)(2,1)}, u32[]{:S(2)}, u32[]{:S(2)}) collective-permute-start(bf16[2,512,768]{2,1,0:T(8,128)(2,1)} %gather_rows.2.refs_8_), channel_id=1, source_target_pairs={{0,2},{1,3},{2,0},{3,1},{4,6},{5,7},{6,4},{7,5},{8,10},{9,11},{10,... | collective-permute-start | bytes 4718600 | tf_op jit(solution)/shard_map/ppermute | solution.py:60
  88.6 23.5 %collective-permute-start.16 = (bf16[512,384]{1,0:T(8,128)(2,1)}, bf16[512,384]{1,0:T(8,128)(2,1)}, u32[]{:S(2)}, u32[]{:S(2)}) collective-permute-start(bf16[512,384]{1,0:T(8,128)(2,1)} %gather_rows.3.refs_2_.refs_0_), channel_id=1, source_target_pairs={{0,16},{8,24},{16,0},{24,8},{1,17},{9,25},{17,1},{25,9},{2,18},{10... | collective-permute-start | bytes 1179656 | tf_op jit(solution)/shard_map/ppermute | solution.py:65
  94.2 18.0 %collective-permute-start.15 = (bf16[512,384]{1,0:T(8,128)(2,1)}, bf16[512,384]{1,0:T(8,128)(2,1)}, u32[]{:S(2)}, u32[]{:S(2)}) collective-permute-start(bf16[512,384]{1,0:T(8,128)(2,1)} %gather_rows.3.refs_2_.refs_0_), channel_id=1, source_target_pairs={{0,8},{8,0},{16,24},{24,16},{1,9},{9,1},{17,25},{25,17},{2,10},{10... | collective-permute-start | bytes 1179656 | tf_op jit(solution)/shard_map/ppermute | solution.py:65
  130.2 29.5 %collective-permute-start.20 = (bf16[512,768]{1,0:T(8,128)(2,1)S(1)}, bf16[512,768]{1,0:T(8,128)(2,1)S(1)}, u32[]{:S(2)}, u32[]{:S(2)}) collective-permute-start(bf16[512,768]{1,0:T(8,128)(2,1)S(1)} %slice_bitcast_fusion.1), channel_id=1, source_target_pairs={{0,2},{1,3},{2,0},{3,1},{4,6},{5,7},{6,4},{7,5},{8,10},{9,11},{10,... | collective-permute-start | bytes 2359304 | tf_op jit(solution)/shard_map/ppermute | solution.py:60
  130.8 28.9 %collective-permute-start.21 = (bf16[512,768]{1,0:T(8,128)(2,1)S(1)}, bf16[512,768]{1,0:T(8,128)(2,1)S(1)}, u32[]{:S(2)}, u32[]{:S(2)}) collective-permute-start(bf16[512,768]{1,0:T(8,128)(2,1)S(1)} %slice_bitcast_fusion), channel_id=1, source_target_pairs={{0,4},{1,5},{2,6},{3,7},{4,0},{5,1},{6,2},{7,3},{8,12},{9,13},{10,... | collective-permute-start | bytes 2359304 | tf_op jit(solution)/shard_map/ppermute | solution.py:60
  131.3 24.9 %collective-permute-start.24 = (bf16[64,2048]{1,0:T(8,128)(2,1)S(1)}, bf16[64,2048]{1,0:T(8,128)(2,1)S(1)}, u32[]{:S(2)}, u32[]{:S(2)}) collective-permute-start(bf16[64,2048]{1,0:T(8,128)(2,1)S(1)} %get-tuple-element.751), channel_id=1, source_target_pairs={{0,6},{1,7},{2,4},{3,5},{4,2},{5,3},{6,0},{7,1},{8,14},{9,15},{10,... | collective-permute-start | bytes 786440 | tf_op jit(solution)/shard_map/ppermute | solution.py:60
  133.8 25.8 %collective-permute-start.23 = (bf16[64,2048]{1,0:T(8,128)(2,1)S(1)}, bf16[64,2048]{1,0:T(8,128)(2,1)S(1)}, u32[]{:S(2)}, u32[]{:S(2)}) collective-permute-start(bf16[64,2048]{1,0:T(8,128)(2,1)S(1)} %get-tuple-element.752), channel_id=1, source_target_pairs={{0,4},{1,5},{2,6},{3,7},{4,0},{5,1},{6,2},{7,3},{8,12},{9,13},{10,... | collective-permute-start | bytes 786440 | tf_op jit(solution)/shard_map/ppermute | solution.py:60
  134.4 25.3 %collective-permute-start.22 = (bf16[64,2048]{1,0:T(8,128)(2,1)S(1)}, bf16[64,2048]{1,0:T(8,128)(2,1)S(1)}, u32[]{:S(2)}, u32[]{:S(2)}) collective-permute-start(bf16[64,2048]{1,0:T(8,128)(2,1)S(1)} %get-tuple-element.753), channel_id=1, source_target_pairs={{0,2},{1,3},{2,0},{3,1},{4,6},{5,7},{6,4},{7,5},{8,10},{9,11},{10,... | collective-permute-start | bytes 786440 | tf_op jit(solution)/shard_map/ppermute | solution.py:60
  170.6 25.0 %collective-permute-start.29 = (bf16[128,2048]{1,0:T(8,128)(2,1)S(1)}, bf16[128,2048]{1,0:T(8,128)(2,1)S(1)}, u32[]{:S(2)}, u32[]{:S(2)}) collective-permute-start(bf16[128,2048]{1,0:T(8,128)(2,1)S(1)} %add_convert_fusion.5), channel_id=1, source_target_pairs={{0,4},{1,5},{2,6},{3,7},{4,0},{5,1},{6,2},{7,3},{8,12},{9,13},{10,... | collective-permute-start | bytes 1572872 | tf_op jit(solution)/shard_map/ppermute | solution.py:60
  171.3 24.3 %collective-permute-start.31 = (bf16[128,2048]{1,0:T(8,128)(2,1)S(1)}, bf16[128,2048]{1,0:T(8,128)(2,1)S(1)}, u32[]{:S(2)}, u32[]{:S(2)}) collective-permute-start(bf16[128,2048]{1,0:T(8,128)(2,1)S(1)} %add_convert_fusion.4), channel_id=1, source_target_pairs={{0,6},{1,7},{2,4},{3,5},{4,2},{5,3},{6,0},{7,1},{8,14},{9,15},{10,... | collective-permute-start | bytes 1572872 | tf_op jit(solution)/shard_map/ppermute | solution.py:60
  172.8 25.4 %collective-permute-start.33 = (bf16[128,2048]{1,0:T(8,128)(2,1)S(1)}, bf16[128,2048]{1,0:T(8,128)(2,1)S(1)}, u32[]{:S(2)}, u32[]{:S(2)}) collective-permute-start(bf16[128,2048]{1,0:T(8,128)(2,1)S(1)} %copy-done.28), channel_id=1, source_target_pairs={{0,16},{8,24},{16,0},{24,8},{1,17},{9,25},{17,1},{25,9},{2,18},{10... | collective-permute-start | bytes 1572872 | tf_op jit(solution)/shard_map/ppermute | solution.py:65
  174.9 23.3 %collective-permute-start.32 = (bf16[128,2048]{1,0:T(8,128)(2,1)S(1)}, bf16[128,2048]{1,0:T(8,128)(2,1)S(1)}, u32[]{:S(2)}, u32[]{:S(2)}) collective-permute-start(bf16[128,2048]{1,0:T(8,128)(2,1)S(1)} %copy-done.28), channel_id=1, source_target_pairs={{0,8},{8,0},{16,24},{24,16},{1,9},{9,1},{17,25},{25,17},{2,10},{10... | collective-permute-start | bytes 1572872 | tf_op jit(solution)/shard_map/ppermute | solution.py:65
  198.5 25.0 %collective-permute-start.35 = (bf16[128,2048]{1,0:T(8,128)(2,1)S(1)}, bf16[128,2048]{1,0:T(8,128)(2,1)S(1)}, u32[]{:S(2)}, u32[]{:S(2)}) collective-permute-start(bf16[128,2048]{1,0:T(8,128)(2,1)S(1)} %multiply_convert_fusion.refs_2_.refs_6_), channel_id=1, source_target_pairs={{0,16},{8,24},{16,0},{24,8},{1,17},{9,25},{17,1},{25,9},{2,18},{10... | collective-permute-start | bytes 1572872 | tf_op jit(solution)/shard_map/ppermute | solution.py:65
  199.8 23.8 %collective-permute-start.34 = (bf16[128,2048]{1,0:T(8,128)(2,1)S(1)}, bf16[128,2048]{1,0:T(8,128)(2,1)S(1)}, u32[]{:S(2)}, u32[]{:S(2)}) collective-permute-start(bf16[128,2048]{1,0:T(8,128)(2,1)S(1)} %multiply_convert_fusion.refs_2_.refs_6_), channel_id=1, source_target_pairs={{0,8},{8,0},{16,24},{24,16},{1,9},{9,1},{17,25},{25,17},{2,10},{10... | collective-permute-start | bytes 1572872 | tf_op jit(solution)/shard_map/ppermute | solution.py:65
  201.3 22.3 %collective-permute-start.36 = (bf16[128,2048]{1,0:T(8,128)(2,1)S(1)}, bf16[128,2048]{1,0:T(8,128)(2,1)S(1)}, u32[]{:S(2)}, u32[]{:S(2)}) collective-permute-start(bf16[128,2048]{1,0:T(8,128)(2,1)S(1)} %copy-done.28), channel_id=1, source_target_pairs={{0,1},{1,0},{2,3},{3,2},{4,5},{5,4},{6,7},{7,6},{8,9},{9,8},{10,11... | collective-permute-start | bytes 1572872 | tf_op jit(solution)/shard_map/ppermute | solution.py:55
  201.3 22.3 %collective-permute-start.37 = (bf16[128,2048]{1,0:T(8,128)(2,1)S(1)}, bf16[128,2048]{1,0:T(8,128)(2,1)S(1)}, u32[]{:S(2)}, u32[]{:S(2)}) collective-permute-start(bf16[128,2048]{1,0:T(8,128)(2,1)S(1)} %collective-permute-done.32.refs_6_.refs_2_), channel_id=1, source_target_pairs={{0,1},{1,0},{2,3},{3,2},{4,5},{5,4},{6,7},{7,6},{8,9},{9,8},{10,11... | collective-permute-start | bytes 1572872 | tf_op jit(solution)/shard_map/ppermute | solution.py:55
  201.8 21.8 %collective-permute-start.38 = (bf16[128,2048]{1,0:T(8,128)(2,1)S(1)}, bf16[128,2048]{1,0:T(8,128)(2,1)S(1)}, u32[]{:S(2)}, u32[]{:S(2)}) collective-permute-start(bf16[128,2048]{1,0:T(8,128)(2,1)S(1)} %collective-permute-done.33.refs_4_.refs_0_), channel_id=1, source_target_pairs={{0,1},{1,0},{2,3},{3,2},{4,5},{5,4},{6,7},{7,6},{8,9},{9,8},{10,11... | collective-permute-start | bytes 1572872 | tf_op jit(solution)/shard_map/ppermute | solution.py:55
  224.2 25.5 %collective-permute-start.42 = (bf16[128,2048]{1,0:T(8,128)(2,1)S(1)}, bf16[128,2048]{1,0:T(8,128)(2,1)S(1)}, u32[]{:S(2)}, u32[]{:S(2)}) collective-permute-start(bf16[128,2048]{1,0:T(8,128)(2,1)S(1)} %collective-permute-done.35.refs_0_), channel_id=1, source_target_pairs={{0,8},{8,0},{16,24},{24,16},{1,9},{9,1},{17,25},{25,17},{2,10},{10... | collective-permute-start | bytes 1572872 | tf_op jit(solution)/shard_map/ppermute | solution.py:65
  224.2 25.5 %collective-permute-start.43 = (bf16[128,2048]{1,0:T(8,128)(2,1)S(1)}, bf16[128,2048]{1,0:T(8,128)(2,1)S(1)}, u32[]{:S(2)}, u32[]{:S(2)}) collective-permute-start(bf16[128,2048]{1,0:T(8,128)(2,1)S(1)} %collective-permute-done.33.refs_4_.refs_0_), channel_id=1, source_target_pairs={{0,8},{8,0},{16,24},{24,16},{1,9},{9,1},{17,25},{25,17},{2,10},{10... | collective-permute-start | bytes 1572872 | tf_op jit(solution)/shard_map/ppermute | solution.py:65
  250.6 31.7 %collective-permute-start.54 = (bf16[128,2048]{1,0:T(8,128)(2,1)}, bf16[128,2048]{1,0:T(8,128)(2,1)S(1)}, u32[]{:S(2)}, u32[]{:S(2)}) collective-permute-start(bf16[128,2048]{1,0:T(8,128)(2,1)} %get-tuple-element.562), channel_id=1, source_target_pairs={{0,1},{1,0},{2,3},{3,2},{4,5},{5,4},{6,7},{7,6},{8,9},{9,8},{10,11... | collective-permute-start | bytes 1572872 | tf_op jit(solution)/shard_map/ppermute | solution.py:55
  251.1 30.5 %collective-permute-start.55 = (bf16[128,2048]{1,0:T(8,128)(2,1)}, bf16[128,2048]{1,0:T(8,128)(2,1)S(1)}, u32[]{:S(2)}, u32[]{:S(2)}) collective-permute-start(bf16[128,2048]{1,0:T(8,128)(2,1)} %get-tuple-element.564), channel_id=1, source_target_pairs={{0,1},{1,0},{2,3},{3,2},{4,5},{5,4},{6,7},{7,6},{8,9},{9,8},{10,11... | collective-permute-start | bytes 1572872 | tf_op jit(solution)/shard_map/ppermute | solution.py:55
  255.7 25.8 %collective-permute-start.48 = (bf16[128,2048]{1,0:T(8,128)(2,1)S(1)}, bf16[128,2048]{1,0:T(8,128)(2,1)S(1)}, u32[]{:S(2)}, u32[]{:S(2)}) collective-permute-start(bf16[128,2048]{1,0:T(8,128)(2,1)S(1)} %convert_add_fusion.14), channel_id=1, source_target_pairs={{0,16},{8,24},{16,0},{24,8},{1,17},{9,25},{17,1},{25,9},{2,18},{10... | collective-permute-start | bytes 1572872 | tf_op jit(solution)/shard_map/ppermute | solution.py:65
  256.3 25.2 %collective-permute-start.49 = (bf16[128,2048]{1,0:T(8,128)(2,1)S(1)}, bf16[128,2048]{1,0:T(8,128)(2,1)S(1)}, u32[]{:S(2)}, u32[]{:S(2)}) collective-permute-start(bf16[128,2048]{1,0:T(8,128)(2,1)S(1)} %convert_add_fusion.15), channel_id=1, source_target_pairs={{0,8},{8,0},{16,24},{24,16},{1,9},{9,1},{17,25},{25,17},{2,10},{10... | collective-permute-start | bytes 1572872 | tf_op jit(solution)/shard_map/ppermute | solution.py:65
  303.8 24.8 %collective-permute-start.59 = (bf16[128,2048]{1,0:T(8,128)(2,1)S(1)}, bf16[128,2048]{1,0:T(8,128)(2,1)}, u32[]{:S(2)}, u32[]{:S(2)}) collective-permute-start(bf16[128,2048]{1,0:T(8,128)(2,1)S(1)} %get-tuple-element.641.refs_0_), channel_id=1, source_target_pairs={{0,6},{1,7},{2,4},{3,5},{4,2},{5,3},{6,0},{7,1},{8,14},{9,15},{10,... | collective-permute-start | bytes 1572872 | tf_op jit(solution)/shard_map/ppermute | solution.py:60
  305.4 24.3 %collective-permute-start.58 = (bf16[128,2048]{1,0:T(8,128)(2,1)S(1)}, bf16[128,2048]{1,0:T(8,128)(2,1)}, u32[]{:S(2)}, u32[]{:S(2)}) collective-permute-start(bf16[128,2048]{1,0:T(8,128)(2,1)S(1)} %get-tuple-element.641.refs_0_), channel_id=1, source_target_pairs={{0,4},{1,5},{2,6},{3,7},{4,0},{5,1},{6,2},{7,3},{8,12},{9,13},{10,... | collective-permute-start | bytes 1572872 | tf_op jit(solution)/shard_map/ppermute | solution.py:60
  306.6 23.1 %collective-permute-start.57 = (bf16[128,2048]{1,0:T(8,128)(2,1)S(1)}, bf16[128,2048]{1,0:T(8,128)(2,1)}, u32[]{:S(2)}, u32[]{:S(2)}) collective-permute-start(bf16[128,2048]{1,0:T(8,128)(2,1)S(1)} %get-tuple-element.641.refs_0_), channel_id=1, source_target_pairs={{0,2},{1,3},{2,0},{3,1},{4,6},{5,7},{6,4},{7,5},{8,10},{9,11},{10,... | collective-permute-start | bytes 1572872 | tf_op jit(solution)/shard_map/ppermute | solution.py:60
  307.3 20.1 %collective-permute-start.60 = (bf16[128,2048]{1,0:T(8,128)(2,1)}, bf16[128,2048]{1,0:T(8,128)(2,1)}, u32[]{:S(2)}, u32[]{:S(2)}) collective-permute-start(bf16[128,2048]{1,0:T(8,128)(2,1)} %convert_add_fusion.8), channel_id=1, source_target_pairs={{0,8},{8,0},{16,24},{24,16},{1,9},{9,1},{17,25},{25,17},{2,10},{10... | collective-permute-start | bytes 1572872 | tf_op jit(solution)/shard_map/ppermute | solution.py:65
  334.9 32.9 %collective-permute-start.65 = (bf16[128,2048]{1,0:T(8,128)(2,1)S(1)}, bf16[128,2048]{1,0:T(8,128)(2,1)S(1)}, u32[]{:S(2)}, u32[]{:S(2)}) collective-permute-start(bf16[128,2048]{1,0:T(8,128)(2,1)S(1)} %convert_add_fusion.6), channel_id=1, source_target_pairs={{0,16},{8,24},{16,0},{24,8},{1,17},{9,25},{17,1},{25,9},{2,18},{10... | collective-permute-start | bytes 1572872 | tf_op jit(solution)/shard_map/ppermute | solution.py:65
  344.3 23.5 %collective-permute-start.66 = (bf16[128,2048]{1,0:T(8,128)(2,1)S(1)}, bf16[128,2048]{1,0:T(8,128)(2,1)S(1)}, u32[]{:S(2)}, u32[]{:S(2)}) collective-permute-start(bf16[128,2048]{1,0:T(8,128)(2,1)S(1)} %copy-done.35), channel_id=1, source_target_pairs={{0,8},{8,0},{16,24},{24,16},{1,9},{9,1},{17,25},{25,17},{2,10},{10... | collective-permute-start | bytes 1572872 | tf_op jit(solution)/shard_map/ppermute | solution.py:65
  344.3 23.7 %collective-permute-start.67 = (bf16[512,768]{1,0:T(8,128)(2,1)}, bf16[512,768]{1,0:T(8,128)(2,1)S(1)}, u32[]{:S(2)}, u32[]{:S(2)}) collective-permute-start(bf16[512,768]{1,0:T(8,128)(2,1)} %get-tuple-element.619), channel_id=1, source_target_pairs={{0,4},{1,5},{2,6},{3,7},{4,0},{5,1},{6,2},{7,3},{8,12},{9,13},{10,... | collective-permute-start | bytes 2359304 | tf_op jit(solution)/shard_map/ppermute | solution.py:60
  345.3 25.2 %collective-permute-start.68 = (bf16[512,768]{1,0:T(8,128)(2,1)}, bf16[512,768]{1,0:T(8,128)(2,1)S(1)}, u32[]{:S(2)}, u32[]{:S(2)}) collective-permute-start(bf16[512,768]{1,0:T(8,128)(2,1)} %get-tuple-element.621), channel_id=1, source_target_pairs={{0,2},{1,3},{2,0},{3,1},{4,6},{5,7},{6,4},{7,5},{8,10},{9,11},{10,... | collective-permute-start | bytes 2359304 | tf_op jit(solution)/shard_map/ppermute | solution.py:60
  372.9 38.2 %collective-permute-start.69 = (bf16[2,512,768]{2,1,0:T(8,128)(2,1)}, bf16[2,512,768]{2,1,0:T(8,128)(2,1)}, u32[]{:S(2)}, u32[]{:S(2)}) collective-permute-start(bf16[2,512,768]{2,1,0:T(8,128)(2,1)} %pad_maximum_fusion.2), channel_id=1, source_target_pairs={{0,2},{1,3},{2,0},{3,1},{4,6},{5,7},{6,4},{7,5},{8,10},{9,11},{10,... | collective-permute-start | bytes 4718600 | tf_op jit(solution)/shard_map/ppermute | solution.py:60
  374.1 37.0 %collective-permute-start.70 = (bf16[2,512,768]{2,1,0:T(8,128)(2,1)}, bf16[2,512,768]{2,1,0:T(8,128)(2,1)}, u32[]{:S(2)}, u32[]{:S(2)}) collective-permute-start(bf16[2,512,768]{2,1,0:T(8,128)(2,1)} %pad_maximum_fusion.3), channel_id=1, source_target_pairs={{0,4},{1,5},{2,6},{3,7},{4,0},{5,1},{6,2},{7,3},{8,12},{9,13},{10,... | collective-permute-start | bytes 4718600 | tf_op jit(solution)/shard_map/ppermute | solution.py:60
  382.3 24.2 %collective-permute-start.73 = (bf16[512,384]{1,0:T(8,128)(2,1)}, bf16[512,384]{1,0:T(8,128)(2,1)S(1)}, u32[]{:S(2)}, u32[]{:S(2)}) collective-permute-start(bf16[512,384]{1,0:T(8,128)(2,1)} %get-tuple-element.632), channel_id=1, source_target_pairs={{0,8},{8,0},{16,24},{24,16},{1,9},{9,1},{17,25},{25,17},{2,10},{10... | collective-permute-start | bytes 1179656 | tf_op jit(solution)/shard_map/ppermute | solution.py:65
  392.9 17.2 %collective-permute-start.72 = (bf16[512,384]{1,0:T(8,128)(2,1)S(1)}, bf16[512,384]{1,0:T(8,128)(2,1)S(1)}, u32[]{:S(2)}, u32[]{:S(2)}) collective-permute-start(bf16[512,384]{1,0:T(8,128)(2,1)S(1)} %add_convert_fusion.7), channel_id=1, source_target_pairs={{0,16},{8,24},{16,0},{24,8},{1,17},{9,25},{17,1},{25,9},{2,18},{10... | collective-permute-start | bytes 1179656 | tf_op jit(solution)/shard_map/ppermute | solution.py:65
  430.6 18.7 %collective-permute-start.79 = (bf16[2,2,64,768]{3,2,1,0:T(8,128)(2,1)S(1)}, bf16[2,2,64,768]{3,2,1,0:T(8,128)(2,1)S(1)}, u32[]{:S(2)}, u32[]{:S(2)}) collective-permute-start(bf16[2,2,64,768]{3,2,1,0:T(8,128)(2,1)S(1)} %pad_maximum_fusion.14), channel_id=1, source_target_pairs={{0,8},{8,0},{16,24},{24,16},{1,9},{9,1},{17,25},{25,17},{2,10},{10... | collective-permute-start | bytes 1179656 | tf_op jit(solution)/shard_map/ppermute | solution.py:65
  430.8 19.6 %collective-permute-start.80 = (bf16[2,2,64,768]{3,2,1,0:T(8,128)(2,1)S(1)}, bf16[2,2,64,768]{3,2,1,0:T(8,128)(2,1)S(1)}, u32[]{:S(2)}, u32[]{:S(2)}) collective-permute-start(bf16[2,2,64,768]{3,2,1,0:T(8,128)(2,1)S(1)} %pad_maximum_fusion.15), channel_id=1, source_target_pairs={{0,16},{8,24},{16,0},{24,8},{1,17},{9,25},{17,1},{25,9},{2,18},{10... | collective-permute-start | bytes 1179656 | tf_op jit(solution)/shard_map/ppermute | solution.py:65
  451.9 28.8 %collective-permute-start.84 = (bf16[2,2,64,768]{3,2,1,0:T(8,128)(2,1)}, bf16[2,2,64,768]{3,2,1,0:T(8,128)(2,1)}, u32[]{:S(2)}, u32[]{:S(2)}) collective-permute-start(bf16[2,2,64,768]{3,2,1,0:T(8,128)(2,1)} %pad_maximum_fusion.12), channel_id=1, source_target_pairs={{0,24},{8,16},{16,8},{24,0},{1,25},{9,17},{17,9},{25,1},{2,26},{10... | collective-permute-start | bytes 1179656 | tf_op jit(solution)/shard_map/ppermute | solution.py:65
  480.8 17.1 %collective-permute-start.93 = (bf16[64,2048]{1,0:T(8,128)(2,1)S(1)}, bf16[64,2048]{1,0:T(8,128)(2,1)S(1)}, u32[]{:S(2)}, u32[]{:S(2)}) collective-permute-start(bf16[64,2048]{1,0:T(8,128)(2,1)S(1)} %copy-done.45), channel_id=1, source_target_pairs={{0,16},{8,24},{16,0},{24,8},{1,17},{9,25},{17,1},{25,9},{2,18},{10... | collective-permute-start | bytes 786440 | tf_op jit(solution)/shard_map/ppermute | solution.py:65
  (139 other events, 1343.4 us)
Sparse Core Ops, SparseCore 0:
  10.5 67.7 all-gather.1
  411.2 55.9 reduce-scatter.1
